TPU v7x, 32 devices: a whole 2x2x4 slice. The times are simulated.
32 devices in a mesh: pipe: 4 (over z), group: 4 (over y, core), dp: 2 (over x).
Axes of the slice: x: 2, y: 2, z: 4, core: 2. Of those that a mesh axis runs over, the one named last changes fastest.
Arguments:
- tokens: bfloat16 [16384, 768], P(('group', 'dp')), may hold values from -6 to 6
- doc_ids: int32 [16384], P(('group', 'dp')), may hold values from 0 to 7, as said below
- cotangent: bfloat16 [16384, 768], P(('group', 'dp')), may hold values from -6 to 6
- w_qkv: bfloat16 [4, 768, 2304], P('pipe'), may hold values from -0.21875 to 0.21875
- w_out: bfloat16 [4, 768, 768], P('pipe'), may hold values from -2.5 to 2.5
- w_up: bfloat16 [4, 768, 3072], P('pipe'), may hold values from -0.21875 to 0.21875
- w_down: bfloat16 [4, 3072, 768], P('pipe'), may hold values from -0.109375 to 0.109375
- first_gain: float32 [4, 768], P('pipe'), may hold values from 0.5 to 1.5
- first_bias: float32 [4, 768], P('pipe'), may hold values from -2 to 2
- second_gain: float32 [4, 768], P('pipe'), may hold values from 0.5 to 1.5
- second_bias: float32 [4, 768], P('pipe'), may hold values from -2 to 2
Outputs:
- block_out: bfloat16 [4, 16384, 768], P('pipe', ('group', 'dp'))
- input_grad: bfloat16 [4, 16384, 768], P('pipe', ('group', 'dp'))
- grad_w_qkv: float32 [4, 768, 2304], P('pipe', None, 'group')
- grad_w_out: float32 [4, 768, 768], P('pipe', None, 'group')
- grad_w_up: float32 [4, 768, 3072], P('pipe', None, 'group')
- grad_w_down: float32 [4, 3072, 768], P('pipe', 'group')
- grad_first_gain: float32 [4, 768], P('pipe', 'group')
- grad_first_bias: float32 [4, 768], P('pipe', 'group')
- grad_second_gain: float32 [4, 768], P('pipe', 'group')
- grad_second_bias: float32 [4, 768], P('pipe', 'group')
Inputs may be any that keep to these rules, and one draw needn't show every extreme that they name: `doc_ids`: within the m-th aligned block of 1024 rows of a replica (m from 0) the ids do not fall, begin at 4 * m and lie in 4 * m to 4 * m + 3; all documents of a block have one length, 1024, 512 or 256 rows; some replica has one document in its first block and four in its last.
All inputs are finite; a program needn't handle non-finite values.
Results may differ from a plain program's by a relative error of at most 0.017.
Values may be sent and summed in bfloat16 or wider, within the bound.
No kernel may reach another device: no remote copies, remote signals or barrier semaphores. Data moves between devices by JAX's collectives and lax.ppermute only.
A program may use at most 384 MiB of HBM per device.

v0:
```python
import math

import jax
import jax.numpy as jnp
from jax import lax
from jax.sharding import PartitionSpec as P

HEADS = 12
MB_ROWS = 1024
MICRO = 2


norm_eps = 1e-05


def shifted(block, axis, distance):
    devices = range(lax.axis_size(axis))
    route = [(i - distance, i) for i in devices if i - distance in devices]
    return lax.ppermute(block, axis, route)


def layer_norm(inputs, norm_gain, norm_bias):
    centre = jnp.mean(inputs, axis=-1, keepdims=True)
    centred = inputs - centre
    spread = jnp.mean(centred * centred, axis=-1, keepdims=True)
    return centred * lax.rsqrt(spread + norm_eps) * norm_gain + norm_bias


def doc_geometry(doc_row):
    row_count = doc_row.shape[0]
    same_doc = doc_row[:, None] == doc_row[None, :]
    row_order = jnp.arange(row_count, dtype=jnp.int32)
    earlier = row_order[None, :] <= row_order[:, None]
    causal = jnp.where(same_doc & earlier, 1.0, 0.0).astype(jnp.float32)
    position = jnp.sum(causal, axis=1) - 1.0
    doc_length = jnp.sum(jnp.where(same_doc, 1.0, 0.0).astype(jnp.float32), axis=1)
    phase_angle = 0.5 * math.pi * position / doc_length
    return (causal, jnp.cos(phase_angle)[:, None, None], jnp.sin(phase_angle)[:, None, None])


def feature_map(raw_part, cos_part, sin_part):
    positive = jax.nn.softplus(raw_part.reshape(raw_part.shape[0], HEADS, -1))
    return jnp.concatenate([positive * cos_part, positive * sin_part], axis=2)


def head_scores(causal, query_feat, key_feat):
    scores = jnp.einsum("rc,sc->rs", query_feat, key_feat, preferred_element_type=jnp.float32)
    masked = scores * causal
    denominator = jnp.sum(masked, axis=1, keepdims=True)
    shares = (masked / denominator).astype(jnp.bfloat16)
    return (masked, denominator, shares)


def head_forward(causal, query_feat, key_feat, value_head):
    masked, denominator, shares = head_scores(causal, query_feat, key_feat)
    return jnp.dot(shares, value_head, preferred_element_type=jnp.float32)


def head_backward(causal, query_feat, key_feat, value_head, grad_head):
    masked, denominator, shares = head_scores(causal, query_feat, key_feat)
    grad_shares = jnp.einsum("rd,sd->rs", grad_head, value_head, preferred_element_type=jnp.float32)
    grad_value = jnp.einsum("rs,rd->sd", shares, grad_head, preferred_element_type=jnp.float32)
    inner = jnp.sum(grad_shares * masked, axis=1, keepdims=True) / denominator
    grad_masked = ((grad_shares - inner) / denominator).astype(jnp.bfloat16) * causal.astype(
        jnp.bfloat16
    )
    grad_query = jnp.dot(grad_masked, key_feat, preferred_element_type=jnp.float32)
    grad_key = jnp.einsum("rs,rc->sc", grad_masked, query_feat, preferred_element_type=jnp.float32)
    return (grad_query, grad_key, grad_value)


def split_features(mixed, width, cos_part, sin_part):
    query_feat = feature_map(mixed[:, :width], cos_part, sin_part).astype(jnp.bfloat16)
    key_feat = feature_map(mixed[:, width : 2 * width], cos_part, sin_part).astype(jnp.bfloat16)
    value_heads = mixed[:, 2 * width :].astype(jnp.bfloat16).reshape(mixed.shape[0], HEADS, -1)
    return (query_feat, key_feat, value_heads)


def layer_forward(state, geometry, weights):
    causal, cos_part, sin_part = geometry
    w_qkv, w_out, w_up, w_down, gain_one, bias_one, gain_two, bias_two = weights
    width = state.shape[1]
    row_count = state.shape[0]
    mixed = jnp.dot(state, w_qkv, preferred_element_type=jnp.float32)
    query_feat, key_feat, value_heads = split_features(mixed, width, cos_part, sin_part)
    heads_out = lax.map(
        lambda items: head_forward(causal, items[0], items[1], items[2]),
        (
            jnp.swapaxes(query_feat, 0, 1),
            jnp.swapaxes(key_feat, 0, 1),
            jnp.swapaxes(value_heads, 0, 1),
        ),
    )
    attended = jnp.swapaxes(heads_out, 0, 1).reshape(row_count, width).astype(jnp.bfloat16)
    residual = state.astype(jnp.float32) + jnp.dot(
        attended, w_out, preferred_element_type=jnp.float32
    )
    hidden = layer_norm(residual, gain_one, bias_one)
    upper = jnp.dot(hidden.astype(jnp.bfloat16), w_up, preferred_element_type=jnp.float32)
    active = jax.nn.gelu(upper, approximate=False).astype(jnp.bfloat16)
    residual_two = hidden + jnp.dot(active, w_down, preferred_element_type=jnp.float32)
    output = layer_norm(residual_two, gain_two, bias_two).astype(jnp.bfloat16)
    return ((mixed, attended, residual, upper, residual_two), output)


def layer_backward(state, geometry, weights, saved, grad_out):
    causal, cos_part, sin_part = geometry
    w_qkv, w_out, w_up, w_down, gain_one, bias_one, gain_two, bias_two = weights
    mixed, attended, residual, upper, residual_two = saved
    width = state.shape[1]
    row_count = state.shape[0]
    hidden, norm_one_back = jax.vjp(layer_norm, residual, gain_one, bias_one)
    ignored_out, norm_two_back = jax.vjp(layer_norm, residual_two, gain_two, bias_two)
    d_resid_two, d_gain_two, d_bias_two = norm_two_back(grad_out.astype(jnp.float32))
    d_ffn = d_resid_two.astype(jnp.bfloat16)
    active, gelu_back = jax.vjp(
        lambda inner_value: jax.nn.gelu(inner_value, approximate=False), upper
    )
    active_b = active.astype(jnp.bfloat16)
    d_w_down = jnp.einsum("ri,rj->ij", active_b, d_ffn, preferred_element_type=jnp.float32)
    d_active = jnp.einsum("rj,ij->ri", d_ffn, w_down, preferred_element_type=jnp.float32)
    d_upper = gelu_back(d_active)[0].astype(jnp.bfloat16)
    hidden_b = hidden.astype(jnp.bfloat16)
    d_w_up = jnp.einsum("ri,rj->ij", hidden_b, d_upper, preferred_element_type=jnp.float32)
    d_hidden = d_resid_two + jnp.einsum(
        "rj,ij->ri", d_upper, w_up, preferred_element_type=jnp.float32
    )
    d_residual, d_gain_one, d_bias_one = norm_one_back(d_hidden)
    d_proj = d_residual.astype(jnp.bfloat16)
    d_w_out = jnp.einsum("ri,rj->ij", attended, d_proj, preferred_element_type=jnp.float32)
    d_attended = jnp.einsum("rj,ij->ri", d_proj, w_out, preferred_element_type=jnp.float32).astype(
        jnp.bfloat16
    )
    query_raw, query_back = jax.vjp(
        lambda raw_part: feature_map(raw_part, cos_part, sin_part), mixed[:, :width]
    )
    key_raw, key_back = jax.vjp(
        lambda raw_part: feature_map(raw_part, cos_part, sin_part), mixed[:, width : 2 * width]
    )
    query_feat = query_raw.astype(jnp.bfloat16)
    key_feat = key_raw.astype(jnp.bfloat16)
    value_heads = mixed[:, 2 * width :].astype(jnp.bfloat16).reshape(row_count, HEADS, -1)
    grad_heads = d_attended.reshape(row_count, HEADS, -1)
    grad_query, grad_key, grad_value = lax.map(
        lambda items: head_backward(causal, items[0], items[1], items[2], items[3]),
        (
            jnp.swapaxes(query_feat, 0, 1),
            jnp.swapaxes(key_feat, 0, 1),
            jnp.swapaxes(value_heads, 0, 1),
            jnp.swapaxes(grad_heads, 0, 1),
        ),
    )
    d_query = query_back(jnp.swapaxes(grad_query, 0, 1))[0]
    d_key = key_back(jnp.swapaxes(grad_key, 0, 1))[0]
    d_value = jnp.swapaxes(grad_value, 0, 1).reshape(row_count, width)
    d_mixed = jnp.concatenate([d_query, d_key, d_value], axis=1).astype(jnp.bfloat16)
    d_w_qkv = jnp.einsum("ri,rj->ij", state, d_mixed, preferred_element_type=jnp.float32)
    d_state = (
        jnp.einsum("rj,ij->ri", d_mixed, w_qkv, preferred_element_type=jnp.float32) + d_residual
    ).astype(jnp.bfloat16)
    return (
        d_state,
        (d_w_qkv, d_w_out, d_w_up, d_w_down, d_gain_one, d_bias_one, d_gain_two, d_bias_two),
    )


def local(
    tokens,
    doc_ids,
    cotangent,
    w_qkv,
    w_out,
    w_up,
    w_down,
    first_gain,
    first_bias,
    second_gain,
    second_bias,
):
    sections = lax.axis_size("pipe")
    section_index = lax.axis_index("pipe")
    width = tokens.shape[1]
    hidden_units = w_up.shape[2]
    inputs = tokens.reshape(MICRO, MB_ROWS, width)
    cot_blocks = cotangent.reshape(MICRO, MB_ROWS, width)
    doc_blocks = doc_ids.reshape(MICRO, MB_ROWS)
    weights = tuple(
        (
            weight_item[0]
            for weight_item in (
                w_qkv,
                w_out,
                w_up,
                w_down,
                first_gain,
                first_bias,
                second_gain,
                second_bias,
            )
        )
    )
    ticks = MICRO + sections - 1
    store = (
        jnp.zeros((MICRO, MB_ROWS, width), jnp.bfloat16),
        jnp.zeros((MICRO, MB_ROWS, 3 * width), jnp.float32),
        jnp.zeros((MICRO, MB_ROWS, width), jnp.bfloat16),
        jnp.zeros((MICRO, MB_ROWS, width), jnp.float32),
        jnp.zeros((MICRO, MB_ROWS, hidden_units), jnp.float32),
        jnp.zeros((MICRO, MB_ROWS, width), jnp.float32),
        jnp.zeros((MICRO, MB_ROWS, width), jnp.bfloat16),
    )

    def forward_tick(tick, carry):
        buffers, arriving = carry
        index = tick - section_index
        valid = (index >= 0) & (index < MICRO)
        slot = jnp.clip(index, 0, MICRO - 1)

        def advance(held):
            own_rows = lax.dynamic_index_in_dim(inputs, slot, 0, keepdims=False)
            state = jnp.where(section_index == 0, own_rows, arriving)
            geometry = doc_geometry(lax.dynamic_index_in_dim(doc_blocks, slot, 0, keepdims=False))
            saved, output = layer_forward(state, geometry, weights)
            fresh = (state,) + saved + (output,)
            return tuple(
                (
                    lax.dynamic_update_index_in_dim(buffer, fresh_item, slot, 0)
                    for buffer, fresh_item in zip(held, fresh)
                )
            )

        buffers = lax.cond(valid, advance, lambda held: held, buffers)
        sending = lax.dynamic_index_in_dim(buffers[6], slot, 0, keepdims=False)
        arriving = shifted(sending, "pipe", 1)
        return (buffers, arriving)

    store, last_arrived = lax.fori_loop(
        0, ticks, forward_tick, (store, jnp.zeros((MB_ROWS, width), jnp.bfloat16))
    )
    backs = jnp.zeros((MICRO, MB_ROWS, width), jnp.bfloat16)
    grads = tuple((jnp.zeros(weight_item.shape, jnp.float32) for weight_item in weights))

    def backward_tick(tick, carry):
        backs_now, grads_now, returning = carry
        index = tick - (sections - 1 - section_index)
        valid = (index >= 0) & (index < MICRO)
        slot = jnp.clip(index, 0, MICRO - 1)

        def retreat(parts):
            backs_in, grads_in = parts
            given = lax.dynamic_index_in_dim(cot_blocks, slot, 0, keepdims=False)
            grad_out = jnp.where(section_index == sections - 1, given, returning)
            items = tuple(
                (lax.dynamic_index_in_dim(buffer, slot, 0, keepdims=False) for buffer in store)
            )
            geometry = doc_geometry(lax.dynamic_index_in_dim(doc_blocks, slot, 0, keepdims=False))
            d_state, grad_terms = layer_backward(items[0], geometry, weights, items[1:6], grad_out)
            backs_out = lax.dynamic_update_index_in_dim(backs_in, d_state, slot, 0)
            return (backs_out, tuple((total + term for total, term in zip(grads_in, grad_terms))))

        backs_now, grads_now = lax.cond(valid, retreat, lambda parts: parts, (backs_now, grads_now))
        sending = lax.dynamic_index_in_dim(backs_now, slot, 0, keepdims=False)
        returning = shifted(sending, "pipe", -1)
        return (backs_now, grads_now, returning)

    backs, grads, last_returned = lax.fori_loop(
        0, ticks, backward_tick, (backs, grads, jnp.zeros((MB_ROWS, width), jnp.bfloat16))
    )
    block_out = store[6].reshape(1, MICRO * MB_ROWS, width)
    input_grad = backs.reshape(1, MICRO * MB_ROWS, width)
    g_qkv, g_out, g_up, g_down, g_gain_one, g_bias_one, g_gain_two, g_bias_two = tuple(
        (term[None] for term in grads)
    )
    shares = (
        lax.psum_scatter(
            g_qkv.astype(jnp.bfloat16), "group", scatter_dimension=2, tiled=True
        ).astype(jnp.float32),
        lax.psum_scatter(
            g_out.astype(jnp.bfloat16), "group", scatter_dimension=2, tiled=True
        ).astype(jnp.float32),
        lax.psum_scatter(
            g_up.astype(jnp.bfloat16), "group", scatter_dimension=2, tiled=True
        ).astype(jnp.float32),
        lax.psum_scatter(
            g_down.astype(jnp.bfloat16), "group", scatter_dimension=1, tiled=True
        ).astype(jnp.float32),
        lax.psum_scatter(
            g_gain_one.astype(jnp.bfloat16), "group", scatter_dimension=1, tiled=True
        ).astype(jnp.float32),
        lax.psum_scatter(
            g_bias_one.astype(jnp.bfloat16), "group", scatter_dimension=1, tiled=True
        ).astype(jnp.float32),
        lax.psum_scatter(
            g_gain_two.astype(jnp.bfloat16), "group", scatter_dimension=1, tiled=True
        ).astype(jnp.float32),
        lax.psum_scatter(
            g_bias_two.astype(jnp.bfloat16), "group", scatter_dimension=1, tiled=True
        ).astype(jnp.float32),
    )
    totals = (
        lax.psum(shares[0].astype(jnp.bfloat16), "dp").astype(jnp.float32),
        lax.psum(shares[1].astype(jnp.bfloat16), "dp").astype(jnp.float32),
        lax.psum(shares[2].astype(jnp.bfloat16), "dp").astype(jnp.float32),
        lax.psum(shares[3].astype(jnp.bfloat16), "dp").astype(jnp.float32),
        lax.psum(shares[4].astype(jnp.bfloat16), "dp").astype(jnp.float32),
        lax.psum(shares[5].astype(jnp.bfloat16), "dp").astype(jnp.float32),
        lax.psum(shares[6].astype(jnp.bfloat16), "dp").astype(jnp.float32),
        lax.psum(shares[7].astype(jnp.bfloat16), "dp").astype(jnp.float32),
    )
    return (
        block_out,
        input_grad,
        totals[0],
        totals[1],
        totals[2],
        totals[3],
        totals[4],
        totals[5],
        totals[6],
        totals[7],
    )


def solution(mesh):
    placed = (
        P(("group", "dp"), None),
        P(("group", "dp")),
        P(("group", "dp"), None),
        P("pipe", None, None),
        P("pipe", None, None),
        P("pipe", None, None),
        P("pipe", None, None),
        P("pipe", None),
        P("pipe", None),
        P("pipe", None),
        P("pipe", None),
    )
    return jax.shard_map(
        local,
        mesh=mesh,
        in_specs=placed,
        out_specs=(
            P("pipe", ("group", "dp"), None),
            P("pipe", ("group", "dp"), None),
            P("pipe", None, "group"),
            P("pipe", None, "group"),
            P("pipe", None, "group"),
            P("pipe", "group", None),
            P("pipe", "group"),
            P("pipe", "group"),
            P("pipe", "group"),
            P("pipe", "group"),
        ),
        check_vma=False,
    )
```

profile of v0, /device:TPU:0, one launch (start us, length us, event | category | flops | bytes accessed | tf_op | source)
XLA Modules:
  0.0 3136.9 jit_solution(13468486367501692204)
XLA Ops:
  13.2 11.6 broadcast_in_dim.123
  45.8 778.3 %while.87 = (s32[]{:T(128)}, bf16[2,1024,768]{1,2,0:T(8,128)(2,1)}, f32[2,1024,2304]{2,1,0:T(8,128)}, bf16[2,1024,768]{1,2,0:T(8,128)(2,1)}, f32[2,1024,768]{1,2...) while((s32[]{:T(128)}, bf16[2,1024,768]{1,2,0:T(8,128)(2,1)}, ...), condition=%wide.region_12.13_spmd, body=%wide.region_0.12_spmd.sunk | while | flops 15172372480 | bytes 259601328 | solution.py:237
  67.3 141.1 %conditional.4 = ((bf16[2,1024,768]{1,2,0:T(8,128)(2,1)}, f32[2,1024,2304]{2,1,0:T(8,128)}, bf16[2,1024,768]{1,2,0:T(8,128)(2,1)}, f32[2,1024,768]{1,2,0:T(8,128...) conditional(s32[]{:T(128)} %convert_element_type.307, ...), branch_computations={%region_1.1_spmd, %region_2.11_spmd} | conditional | flops 15172372480 | bytes 250163616 | solution.py:232
  104.9 36.1 %while.85 = (s32[]{:T(128)}, bf16[12,1024,64]{1,2,0:T(8,128)(2,1)S(1)}, bf16[12,1024,128]{1,2,0:T(8,128)(2,1)}, bf16[12,1024,128]{1,2,0:T(8,128)(2,1)}, bf16[12,...) while((s32[]{:T(128)}, bf16[12,1024,64]{1,2,0:T(8,128)(2,1)S(1)}, ...), condition=%wide.region_7.6_spmd.clone, body=%wide.region_5.5_spmd.clone.sunk | while | flops 416283648 | bytes 9332813 | solution.py:86
  148.9 13.5 bitcast_dynamic-update-slice_fusion
  162.4 38.3 %bitcast_dynamic-update-slice_fusion.2 = (f32[2,1024,768]{1,2,0:T(8,128)}, f32[1024,768]{0,1:T(8,128)}) fusion(f32[2,1024,768]{1,2,0:T(8,128)} %get-tuple-element.1094, s32[]{:T(128)S(6)} %select_n.66, bf16[3072,768]{1,0:T(8,128)(2,1)} %get-tuple-element.1095, f32[1024,3072]{1,0:T(8,128)} %get-tuple-element.1723, f32[768]{0:T(1024)S(1)} %reduce.3, ...), kind=kOutput, calls=%fused_computation.89 | convolution fusion | flops 5040242688 | bytes 26753028 | tf_op jit(solution)/shard_map/while/body/eval_jaxpr/cond/branch_1_fun/dot_general | solution.py:101
  211.3 34.4 %collective-permute-done.1 = bf16[1024,768]{0,1:T(8,128)(2,1)S(1)} collective-permute-done((bf16[1024,768]{0,1:T(8,128)(2,1)S(1)}, bf16[1024,768]{0,1:T(8,128)(2,1)S(1)}, u32[]{:S(2)}, u32[]{:S(2)}) %collective-permute-start.1) | collective-permute-done | bytes 1572896 | tf_op jit(solution)/shard_map/while/body/eval_jaxpr/ppermute | solution.py:19
  245.7 140.9 %conditional.4 = ((bf16[2,1024,768]{1,2,0:T(8,128)(2,1)}, f32[2,1024,2304]{2,1,0:T(8,128)}, bf16[2,1024,768]{1,2,0:T(8,128)(2,1)}, f32[2,1024,768]{1,2,0:T(8,128...) conditional(s32[]{:T(128)} %convert_element_type.307, ...), branch_computations={%region_1.1_spmd, %region_2.11_spmd} | conditional | flops 15172372480 | bytes 250163616 | solution.py:232
  283.3 36.1 %while.85 = (s32[]{:T(128)}, bf16[12,1024,64]{1,2,0:T(8,128)(2,1)S(1)}, bf16[12,1024,128]{1,2,0:T(8,128)(2,1)}, bf16[12,1024,128]{1,2,0:T(8,128)(2,1)}, bf16[12,...) while((s32[]{:T(128)}, bf16[12,1024,64]{1,2,0:T(8,128)(2,1)S(1)}, ...), condition=%wide.region_7.6_spmd.clone, body=%wide.region_5.5_spmd.clone.sunk | while | flops 416283648 | bytes 9332813 | solution.py:86
  327.2 13.6 bitcast_dynamic-update-slice_fusion
  340.8 38.2 %bitcast_dynamic-update-slice_fusion.2 = (f32[2,1024,768]{1,2,0:T(8,128)}, f32[1024,768]{0,1:T(8,128)}) fusion(f32[2,1024,768]{1,2,0:T(8,128)} %get-tuple-element.1094, s32[]{:T(128)S(6)} %select_n.66, bf16[3072,768]{1,0:T(8,128)(2,1)} %get-tuple-element.1095, f32[1024,3072]{1,0:T(8,128)} %get-tuple-element.1723, f32[768]{0:T(1024)S(1)} %reduce.3, ...), kind=kOutput, calls=%fused_computation.89 | convolution fusion | flops 5040242688 | bytes 26753028 | tf_op jit(solution)/shard_map/while/body/eval_jaxpr/cond/branch_1_fun/dot_general | solution.py:101
  392.9 33.6 %collective-permute-done.1 = bf16[1024,768]{0,1:T(8,128)(2,1)S(1)} collective-permute-done((bf16[1024,768]{0,1:T(8,128)(2,1)S(1)}, bf16[1024,768]{0,1:T(8,128)(2,1)S(1)}, u32[]{:S(2)}, u32[]{:S(2)}) %collective-permute-start.1) | collective-permute-done | bytes 1572896 | tf_op jit(solution)/shard_map/while/body/eval_jaxpr/ppermute | solution.py:19
  428.0 145.4 %collective-permute-start.1 = (bf16[1024,768]{0,1:T(8,128)(2,1)S(1)}, bf16[1024,768]{0,1:T(8,128)(2,1)S(1)}, u32[]{:S(2)}, u32[]{:S(2)}) collective-permute-start(bf16[1024,768]{0,1:T(8,128)(2,1)S(1)} %dynamic-slice_bitcast_fusion.5), channel_id=1, source_target_pairs={{0,8},{8,16},{16,24},{1,9},{9,17},{17,25},{2,10},{10,18},{18,26},{... | collective-permute-start | bytes 4718600 | tf_op jit(solution)/shard_map/while/body/eval_jaxpr/ppermute | solution.py:19
  573.4 32.7 %collective-permute-done.1 = bf16[1024,768]{0,1:T(8,128)(2,1)S(1)} collective-permute-done((bf16[1024,768]{0,1:T(8,128)(2,1)S(1)}, bf16[1024,768]{0,1:T(8,128)(2,1)S(1)}, u32[]{:S(2)}, u32[]{:S(2)}) %collective-permute-start.1) | collective-permute-done | bytes 1572896 | tf_op jit(solution)/shard_map/while/body/eval_jaxpr/ppermute | solution.py:19
  612.1 31.8 %collective-permute-done.1 = bf16[1024,768]{0,1:T(8,128)(2,1)S(1)} collective-permute-done((bf16[1024,768]{0,1:T(8,128)(2,1)S(1)}, bf16[1024,768]{0,1:T(8,128)(2,1)S(1)}, u32[]{:S(2)}, u32[]{:S(2)}) %collective-permute-start.1) | collective-permute-done | bytes 1572896 | tf_op jit(solution)/shard_map/while/body/eval_jaxpr/ppermute | solution.py:19
  645.4 144.0 %collective-permute-start.1 = (bf16[1024,768]{0,1:T(8,128)(2,1)S(1)}, bf16[1024,768]{0,1:T(8,128)(2,1)S(1)}, u32[]{:S(2)}, u32[]{:S(2)}) collective-permute-start(bf16[1024,768]{0,1:T(8,128)(2,1)S(1)} %dynamic-slice_bitcast_fusion.5), channel_id=1, source_target_pairs={{0,8},{8,16},{16,24},{1,9},{9,17},{17,25},{2,10},{10,18},{18,26},{... | collective-permute-start | bytes 4718600 | tf_op jit(solution)/shard_map/while/body/eval_jaxpr/ppermute | solution.py:19
  789.4 31.2 collective-permute-done.1
  824.1 18.7 copy.112
  883.1 1884.1 %while.88 = (s32[]{:T(128)}, bf16[2,1024,768]{2,1,0:T(8,128)(2,1)}, f32[768,2304]{1,0:T(8,128)}, f32[768,768]{1,0:T(8,128)}, f32[768,3072]{1,0:T(8,128)}, /*inde...) while((s32[]{:T(128)}, bf16[2,1024,768]{2,1,0:T(8,128)(2,1)}, ...), condition=%wide.region_34.36_spmd, body=%wide.region_13.35_spmd.sunk | while | flops 30492340224 | bytes 632875904 | solution.py:266
  895.0 34.2 %collective-permute-done = bf16[1024,768]{1,0:T(8,128)(2,1)S(1)} collective-permute-done((bf16[1024,768]{1,0:T(8,128)(2,1)S(1)}, bf16[1024,768]{1,0:T(8,128)(2,1)S(1)}, u32[]{:S(2)}, u32[]{:S(2)}) %collective-permute-start) | collective-permute-done | bytes 1572896 | tf_op jit(solution)/shard_map/while/body/eval_jaxpr/ppermute | solution.py:19
  933.1 173.7 %collective-permute-done = bf16[1024,768]{1,0:T(8,128)(2,1)S(1)} collective-permute-done((bf16[1024,768]{1,0:T(8,128)(2,1)S(1)}, bf16[1024,768]{1,0:T(8,128)(2,1)S(1)}, u32[]{:S(2)}, u32[]{:S(2)}) %collective-permute-start) | collective-permute-done | bytes 1572896 | tf_op jit(solution)/shard_map/while/body/eval_jaxpr/ppermute | solution.py:19
  1110.7 957.5 %collective-permute-done = bf16[1024,768]{1,0:T(8,128)(2,1)S(1)} collective-permute-done((bf16[1024,768]{1,0:T(8,128)(2,1)S(1)}, bf16[1024,768]{1,0:T(8,128)(2,1)S(1)}, u32[]{:S(2)}, u32[]{:S(2)}) %collective-permute-start) | collective-permute-done | bytes 1572896 | tf_op jit(solution)/shard_map/while/body/eval_jaxpr/ppermute | solution.py:19
  2069.4 311.4 %conditional.5 = ((bf16[2,1024,768]{2,1,0:T(8,128)(2,1)}, f32[768,2304]{1,0:T(8,128)}, f32[768,768]{1,0:T(8,128)}, f32[768,3072]{1,0:T(8,128)}, f32[3072,768]{1,...) conditional(s32[]{:T(128)} %convert_element_type.308, ...), branch_computations={%region_14.14_spmd, %region_15.34_spmd} | conditional | flops 30492340224 | bytes 617146624 | solution.py:261
  2098.1 28.2 fusion.108
  2126.2 15.9 fusion.115
  2142.9 11.1 multiply_reduce_fusion.3
  2164.8 150.7 %while.86 = (s32[]{:T(128)}, f32[12,1024,128]{1,2,0:T(8,128)}, f32[12,1024,128]{1,2,0:T(8,128)}, bf16[12,1024,64]{1,2,0:T(8,128)(2,1)}, bf16[12,1024,64]{2,1,0:T...) while((s32[]{:T(128)}, f32[12,1024,128]{1,2,0:T(8,128)}, ...), condition=%wide.region_29.29_spmd.clone.clone, body=%wide.region_26.28_spmd.clone.clone.sunk | while | flops 1109392384 | bytes 28251236 | solution.py:144
  2324.8 10.5 convolution_add_fusion
  2345.7 21.7 fusion.133
  2367.5 12.3 convolution_add_fusion.1
  2383.6 32.1 %collective-permute-done = bf16[1024,768]{1,0:T(8,128)(2,1)S(1)} collective-permute-done((bf16[1024,768]{1,0:T(8,128)(2,1)S(1)}, bf16[1024,768]{1,0:T(8,128)(2,1)S(1)}, u32[]{:S(2)}, u32[]{:S(2)}) %collective-permute-start) | collective-permute-done | bytes 1572896 | tf_op jit(solution)/shard_map/while/body/eval_jaxpr/ppermute | solution.py:19
  2417.1 311.5 %conditional.5 = ((bf16[2,1024,768]{2,1,0:T(8,128)(2,1)}, f32[768,2304]{1,0:T(8,128)}, f32[768,768]{1,0:T(8,128)}, f32[768,3072]{1,0:T(8,128)}, f32[3072,768]{1,...) conditional(s32[]{:T(128)} %convert_element_type.308, ...), branch_computations={%region_14.14_spmd, %region_15.34_spmd} | conditional | flops 30492340224 | bytes 617146624 | solution.py:261
  2446.1 28.2 fusion.108
  2474.3 15.9 fusion.115
  2490.9 10.7 multiply_reduce_fusion.3
  2512.4 150.7 %while.86 = (s32[]{:T(128)}, f32[12,1024,128]{1,2,0:T(8,128)}, f32[12,1024,128]{1,2,0:T(8,128)}, bf16[12,1024,64]{1,2,0:T(8,128)(2,1)}, bf16[12,1024,64]{2,1,0:T...) while((s32[]{:T(128)}, f32[12,1024,128]{1,2,0:T(8,128)}, ...), condition=%wide.region_29.29_spmd.clone.clone, body=%wide.region_26.28_spmd.clone.clone.sunk | while | flops 1109392384 | bytes 28251236 | solution.py:144
  2672.5 10.5 convolution_add_fusion
  2693.4 21.8 fusion.133
  2715.3 12.3 convolution_add_fusion.1
  2731.5 30.8 collective-permute-done
  2794.3 40.6 %reduce-scatter.17.cloned.1.call-done = bf16[1,768,576]{1,2,0:T(8,128)(2,1)} async-done(((bf16[1,768,2304]{1,2,0:T(8,128)(2,1)}), bf16[1,768,576]{1,2,0:T(8,128)(2,1)}) %reduce-scatter.17.cloned.1.call-update) | async-done | bytes 884752 | tf_op jit(solution)/shard_map/reduce_scatter | solution.py:275
  2834.9 50.4 %reduce-scatter.21.cloned.1.call-done = bf16[1,768,768]{2,1,0:T(8,128)(2,1)} async-done(((bf16[1,768,3072]{2,1,0:T(8,128)(2,1)}), bf16[1,768,768]{2,1,0:T(8,128)(2,1)}) %reduce-scatter.21.cloned.1.call-update) | async-done | bytes 1179664 | tf_op jit(solution)/shard_map/reduce_scatter | solution.py:281
  2885.3 50.4 %reduce-scatter.23.cloned.1.call-done = bf16[1,768,768]{2,1,0:T(8,128)(2,1)} async-done(((bf16[1,3072,768]{2,1,0:T(8,128)(2,1)}), bf16[1,768,768]{2,1,0:T(8,128)(2,1)}) %reduce-scatter.23.cloned.1.call-update) | async-done | bytes 1179664 | tf_op jit(solution)/shard_map/reduce_scatter | solution.py:284
  2938.5 19.8 reduce-scatter.25.cloned.1.call-done
  2959.2 21.8 reduce-scatter.27.cloned.1.call-done
  2981.9 21.9 reduce-scatter.29.cloned.1.call-done
  3004.7 21.3 reduce-scatter.31.cloned.1.call-done
  3034.1 89.3 %all-reduce.4.cloned.1.call-done = (bf16[1,768,576]{1,2,0:T(8,128)(2,1)}, bf16[1,768,192]{1,2,0:T(8,128)(2,1)}, bf16[1,768,768]{2,1,0:T(8,128)(2,1)}, bf16[1,768,768]{2,1,0:T(8,128)(2,1)}) async-done(((bf16[1,768,576]{1,2,0:T(8,128)(2,1)}, bf16[1,768,192]{1,2,0:T(8,128)(2,1)}, bf16[1,768,768]{2,1,0:T(8,128)(2,1)}, bf16[1,768,768]{2,1,0:T(8,128)(2,1)}), (bf16[1,768,576]{1,2,0:T(8,128)(2,1)}, ...) | async-done | bytes 3538960 | tf_op jit(solution)/shard_map/psum | solution.py:301
  (646 shorter events, 760.2 us)
Async XLA Ops:
  7.2 2787.1 %reduce-scatter.19.cloned.1.call-start = ((), (), s32[]{:S(2)}) async-start(), calls=%async_computation.9 | async-start | bytes 1474560 | tf_op jit(solution)/shard_map/reduce_scatter | solution.py:278
  209.9 35.8 %collective-permute-start.1 = (bf16[1024,768]{0,1:T(8,128)(2,1)S(1)}, bf16[1024,768]{0,1:T(8,128)(2,1)S(1)}, u32[]{:S(2)}, u32[]{:S(2)}) collective-permute-start(bf16[1024,768]{0,1:T(8,128)(2,1)S(1)} %dynamic-slice_bitcast_fusion.5), channel_id=1, source_target_pairs={{0,8},{8,16},{16,24},{1,9},{9,17},{17,25},{2,10},{10,18},{18,26},{... | collective-permute-start | bytes 4718600 | tf_op jit(solution)/shard_map/while/body/eval_jaxpr/ppermute | solution.py:19
  388.2 38.2 %collective-permute-start.1 = (bf16[1024,768]{0,1:T(8,128)(2,1)S(1)}, bf16[1024,768]{0,1:T(8,128)(2,1)S(1)}, u32[]{:S(2)}, u32[]{:S(2)}) collective-permute-start(bf16[1024,768]{0,1:T(8,128)(2,1)S(1)} %dynamic-slice_bitcast_fusion.5), channel_id=1, source_target_pairs={{0,8},{8,16},{16,24},{1,9},{9,17},{17,25},{2,10},{10,18},{18,26},{... | collective-permute-start | bytes 4718600 | tf_op jit(solution)/shard_map/while/body/eval_jaxpr/ppermute | solution.py:19
  428.0 178.1 %collective-permute-start.1 = (bf16[1024,768]{0,1:T(8,128)(2,1)S(1)}, bf16[1024,768]{0,1:T(8,128)(2,1)S(1)}, u32[]{:S(2)}, u32[]{:S(2)}) collective-permute-start(bf16[1024,768]{0,1:T(8,128)(2,1)S(1)} %dynamic-slice_bitcast_fusion.5), channel_id=1, source_target_pairs={{0,8},{8,16},{16,24},{1,9},{9,17},{17,25},{2,10},{10,18},{18,26},{... | collective-permute-start | bytes 4718600 | tf_op jit(solution)/shard_map/while/body/eval_jaxpr/ppermute | solution.py:19
  607.6 36.3 %collective-permute-start.1 = (bf16[1024,768]{0,1:T(8,128)(2,1)S(1)}, bf16[1024,768]{0,1:T(8,128)(2,1)S(1)}, u32[]{:S(2)}, u32[]{:S(2)}) collective-permute-start(bf16[1024,768]{0,1:T(8,128)(2,1)S(1)} %dynamic-slice_bitcast_fusion.5), channel_id=1, source_target_pairs={{0,8},{8,16},{16,24},{1,9},{9,17},{17,25},{2,10},{10,18},{18,26},{... | collective-permute-start | bytes 4718600 | tf_op jit(solution)/shard_map/while/body/eval_jaxpr/ppermute | solution.py:19
  645.4 175.2 %collective-permute-start.1 = (bf16[1024,768]{0,1:T(8,128)(2,1)S(1)}, bf16[1024,768]{0,1:T(8,128)(2,1)S(1)}, u32[]{:S(2)}, u32[]{:S(2)}) collective-permute-start(bf16[1024,768]{0,1:T(8,128)(2,1)S(1)} %dynamic-slice_bitcast_fusion.5), channel_id=1, source_target_pairs={{0,8},{8,16},{16,24},{1,9},{9,17},{17,25},{2,10},{10,18},{18,26},{... | collective-permute-start | bytes 4718600 | tf_op jit(solution)/shard_map/while/body/eval_jaxpr/ppermute | solution.py:19
  893.7 35.5 %collective-permute-start = (bf16[1024,768]{1,0:T(8,128)(2,1)S(1)}, bf16[1024,768]{1,0:T(8,128)(2,1)S(1)}, u32[]{:S(2)}, u32[]{:S(2)}) collective-permute-start(bf16[1024,768]{1,0:T(8,128)(2,1)S(1)} %dynamic-slice_bitcast_fusion.6), channel_id=1, source_target_pairs={{8,0},{16,8},{24,16},{9,1},{17,9},{25,17},{10,2},{18,10},{26,18},{... | collective-permute-start | bytes 4718600 | tf_op jit(solution)/shard_map/while/body/eval_jaxpr/ppermute | solution.py:19
  931.8 175.0 %collective-permute-start = (bf16[1024,768]{1,0:T(8,128)(2,1)S(1)}, bf16[1024,768]{1,0:T(8,128)(2,1)S(1)}, u32[]{:S(2)}, u32[]{:S(2)}) collective-permute-start(bf16[1024,768]{1,0:T(8,128)(2,1)S(1)} %dynamic-slice_bitcast_fusion.6), channel_id=1, source_target_pairs={{8,0},{16,8},{24,16},{9,1},{17,9},{25,17},{10,2},{18,10},{26,18},{... | collective-permute-start | bytes 4718600 | tf_op jit(solution)/shard_map/while/body/eval_jaxpr/ppermute | solution.py:19
  1109.4 958.8 %collective-permute-start = (bf16[1024,768]{1,0:T(8,128)(2,1)S(1)}, bf16[1024,768]{1,0:T(8,128)(2,1)S(1)}, u32[]{:S(2)}, u32[]{:S(2)}) collective-permute-start(bf16[1024,768]{1,0:T(8,128)(2,1)S(1)} %dynamic-slice_bitcast_fusion.6), channel_id=1, source_target_pairs={{8,0},{16,8},{24,16},{9,1},{17,9},{25,17},{10,2},{18,10},{26,18},{... | collective-permute-start | bytes 4718600 | tf_op jit(solution)/shard_map/while/body/eval_jaxpr/ppermute | solution.py:19
  2087.4 66.6 %copy-start.20 = (f32[1024]{0:T(1024)}, f32[1024]{0:T(1024)S(1)}, u32[]{:S(2)}) copy-start(f32[1024]{0:T(1024)S(1)} %broadcast_multiply_fusion.2) | copy-start | bytes 12292 | tf_op jit(solution)/shard_map/while/body/eval_jaxpr/cond
  2098.1 28.2 copy-start.7
  2164.7 150.7 %copy-start.3 = (f32[1024,768]{0,1:T(8,128)S(1)}, f32[1024,768]{0,1:T(8,128)}, u32[]{:S(2)}) copy-start(f32[1024,768]{0,1:T(8,128)} %copy-done.2) | copy-start | bytes 9437188 | tf_op jit(solution)/shard_map/while/body/eval_jaxpr/cond
  2164.7 150.7 %copy-start.30 = (f32[1024]{0:T(1024)S(1)}, f32[1024]{0:T(1024)}, u32[]{:S(2)}) copy-start(f32[1024]{0:T(1024)} %copy-done.29) | copy-start | bytes 12292 | tf_op jit(solution)/shard_map/while/body/eval_jaxpr/cond
  2164.7 150.7 %copy-start.32 = (f32[1024]{0:T(1024)S(1)}, f32[1024]{0:T(1024)}, u32[]{:S(2)}) copy-start(f32[1024]{0:T(1024)} %copy-done.31) | copy-start | bytes 12292 | tf_op jit(solution)/shard_map/while/body/eval_jaxpr/cond
  2345.7 21.7 copy-start.37
  2345.7 21.7 copy-start.21
  2345.7 21.7 copy-start.23
  2345.7 21.7 copy-start.25
  2367.4 12.4 copy-start.42
  2367.5 12.4 copy-start.35
  2367.5 12.4 copy-start.45
  2367.5 12.5 copy-start.34
  2367.5 12.5 copy-start.48
  2382.3 33.4 %collective-permute-start = (bf16[1024,768]{1,0:T(8,128)(2,1)S(1)}, bf16[1024,768]{1,0:T(8,128)(2,1)S(1)}, u32[]{:S(2)}, u32[]{:S(2)}) collective-permute-start(bf16[1024,768]{1,0:T(8,128)(2,1)S(1)} %dynamic-slice_bitcast_fusion.6), channel_id=1, source_target_pairs={{8,0},{16,8},{24,16},{9,1},{17,9},{25,17},{10,2},{18,10},{26,18},{... | collective-permute-start | bytes 4718600 | tf_op jit(solution)/shard_map/while/body/eval_jaxpr/ppermute | solution.py:19
  2435.4 66.2 %copy-start.20 = (f32[1024]{0:T(1024)}, f32[1024]{0:T(1024)S(1)}, u32[]{:S(2)}) copy-start(f32[1024]{0:T(1024)S(1)} %broadcast_multiply_fusion.2) | copy-start | bytes 12292 | tf_op jit(solution)/shard_map/while/body/eval_jaxpr/cond
  2446.1 28.2 copy-start.7
  2512.4 150.7 %copy-start.3 = (f32[1024,768]{0,1:T(8,128)S(1)}, f32[1024,768]{0,1:T(8,128)}, u32[]{:S(2)}) copy-start(f32[1024,768]{0,1:T(8,128)} %copy-done.2) | copy-start | bytes 9437188 | tf_op jit(solution)/shard_map/while/body/eval_jaxpr/cond
  2512.4 150.7 %copy-start.30 = (f32[1024]{0:T(1024)S(1)}, f32[1024]{0:T(1024)}, u32[]{:S(2)}) copy-start(f32[1024]{0:T(1024)} %copy-done.29) | copy-start | bytes 12292 | tf_op jit(solution)/shard_map/while/body/eval_jaxpr/cond
  2512.4 150.7 %copy-start.32 = (f32[1024]{0:T(1024)S(1)}, f32[1024]{0:T(1024)}, u32[]{:S(2)}) copy-start(f32[1024]{0:T(1024)} %copy-done.31) | copy-start | bytes 12292 | tf_op jit(solution)/shard_map/while/body/eval_jaxpr/cond
  2693.4 21.8 copy-start.37
  2693.4 21.8 copy-start.21
  2693.4 21.8 copy-start.23
  2693.4 21.8 copy-start.25
  2715.3 12.4 copy-start.42
  2715.3 12.4 copy-start.35
  2715.3 12.4 copy-start.45
  2715.3 12.5 copy-start.34
  2715.3 12.5 copy-start.48
  2730.2 32.1 %collective-permute-start = (bf16[1024,768]{1,0:T(8,128)(2,1)S(1)}, bf16[1024,768]{1,0:T(8,128)(2,1)S(1)}, u32[]{:S(2)}, u32[]{:S(2)}) collective-permute-start(bf16[1024,768]{1,0:T(8,128)(2,1)S(1)} %dynamic-slice_bitcast_fusion.6), channel_id=1, source_target_pairs={{8,0},{16,8},{24,16},{9,1},{17,9},{25,17},{10,2},{18,10},{26,18},{... | collective-permute-start | bytes 4718600 | tf_op jit(solution)/shard_map/while/body/eval_jaxpr/ppermute | solution.py:19
  2769.9 64.9 %reduce-scatter.17.cloned.1.call-start = ((), (), s32[]{:S(2)}) async-start(), calls=%async_computation.8 | async-start | bytes 4423680 | tf_op jit(solution)/shard_map/reduce_scatter | solution.py:275
  2776.8 108.5 %reduce-scatter.21.cloned.1.call-start = ((), (), s32[]{:S(2)}) async-start(), calls=%async_computation.10 | async-start | bytes 5898240 | tf_op jit(solution)/shard_map/reduce_scatter | solution.py:281
  2783.5 152.2 %reduce-scatter.23.cloned.1.call-start = ((), (), s32[]{:S(2)}) async-start(), calls=%async_computation.11 | async-start | bytes 5898240 | tf_op jit(solution)/shard_map/reduce_scatter | solution.py:284
  2789.9 145.9 %copy-start.12 = (bf16[2,1024,768]{1,2,0:T(8,128)(2,1)S(1)}, bf16[2,1024,768]{1,2,0:T(8,128)(2,1)}, u32[]{:S(2)}) copy-start(bf16[2,1024,768]{1,2,0:T(8,128)(2,1)} %get-tuple-element.1236) | copy-start | bytes 9437188
  2789.9 168.5 %reduce-scatter.25.cloned.1.call-start = ((), (), s32[]{:S(2)}) async-start(), calls=%async_computation.12 | async-start | bytes 245760
  2791.4 189.6 %reduce-scatter.27.cloned.1.call-start = ((), (), s32[]{:S(2)}) async-start(), calls=%async_computation.13 | async-start | bytes 245760
  2792.3 211.5 %reduce-scatter.29.cloned.1.call-start = ((), (), s32[]{:S(2)}) async-start(), calls=%async_computation.14 | async-start | bytes 245760
  2793.3 232.7 %reduce-scatter.31.cloned.1.call-start = ((), (), s32[]{:S(2)}) async-start(), calls=%async_computation.15 | async-start | bytes 245760
  2794.2 329.2 %all-reduce.4.cloned.1.call-start = ((), (), s32[]{:S(2)}) async-start(), calls=%async_computation.16 | async-start | bytes 7077888 | tf_op jit(solution)/shard_map/psum | solution.py:301
  (84 other events, 438.5 us)
Sparse Core Ops, SparseCore 0:
  2770.0 21.5 reduce-scatter.18
  2794.4 40.4 reduce-scatter.16
  2837.4 47.8 reduce-scatter.20
  2887.8 47.8 reduce-scatter.22
  2938.6 19.7 reduce-scatter.24
  2961.2 19.7 reduce-scatter.26
  2984.0 19.7 reduce-scatter.28
  3006.2 19.7 reduce-scatter.30
  3028.5 94.8 all-reduce.3
where the time goes:
time: 3150 us; the launch traced here: 3140 us
  waiting for transfers between devices  1710 us (54%)
  matrix products  668 us (21%)
  starting transfers between devices  307 us (10%)
  local copies, waits for them, and re-layouts  210 us (7%)
  other arithmetic  184 us (6%)
  loops' own time  41.4 us (1%)
    ppermute x10, waiting for transfers between devices, shifted(): return lax.ppermute(block, axis, route)  1390 us
    ppermute x10, starting transfers between devices, shifted(): return lax.ppermute(block, axis, route)  306 us
    dot_general x48, matrix products, head_scores(): jnp.einsum('rc,sc->rs', query_feat, key_feat, preferred_element_type=jnp....  91.8 us
    psum x1, waiting for transfers between devices, local(): lax.psum(shares[0].astype(jnp.bfloat16), 'dp').astype(jnp.float32)  89.3 us
    dot_general x24, matrix products, head_backward(): jnp.einsum('rs,rc->sc', grad_masked, query_feat, preferred_element_type=j...  86.3 us
    unnamed x13, waiting for transfers between devices  85 us
    dot_general x2, matrix products, layer_forward(): jnp.dot(active, w_down, preferred_element_type=jnp.float32)  76.4 us
    dot_general x24, matrix products, head_backward(): jnp.dot(grad_masked, key_feat, preferred_element_type=jnp.float32)  69.9 us
  transfers between devices with their start and end apart: 19, of which 18 were waited for; matrix products, arithmetic and copies ran while one was open for 1% of the time, Pallas kernels for 0%

commit v1 on v0

v1 whole, which is shorter than its diff:
```python
import functools, math
import jax, jax.numpy as jnp
from jax import lax
from jax.experimental import pallas as pl
from jax.experimental.pallas import tpu as pltpu
from jax.sharding import PartitionSpec as P

bf = jnp.bfloat16
f32 = jnp.float32
EPS = 1e-05
D = 768
PAIRS = 6
NT = (((1,), (1,)), ((), ()))
TN = (((0,), (0,)), ((), ()))


def nn_dot(a, b):
    return jnp.dot(a, b, preferred_element_type=f32)


def nt_dot(a, b):
    return lax.dot_general(a, b, NT, preferred_element_type=f32)


def tn_dot(a, b):
    return lax.dot_general(a, b, TN, preferred_element_type=f32)


def head_lanes(rows, lanes):
    lane = lax.broadcasted_iota(jnp.int32, (rows, lanes), 1)
    return (lane & 64) == 0


def block_diag(size):
    r = lax.broadcasted_iota(jnp.int32, (size, size), 0)
    c = lax.broadcasted_iota(jnp.int32, (size, size), 1)
    return ((r ^ c) & 64) == 0


def soft_pair(raw):
    e = jnp.exp(-jnp.abs(raw))
    one = 1.0 + e
    tail = jnp.where(e < 1e-3, e * (1.0 - e * (0.5 - e * (1.0 / 3.0))), jnp.log(one))
    soft = jnp.maximum(raw, 0.0) + tail
    sig = jnp.where(raw >= 0.0, 1.0, e) / one
    return soft, sig


def norm_rows(v):
    centre = jnp.mean(v, axis=-1, keepdims=True)
    centred = v - centre
    spread = jnp.mean(centred * centred, axis=-1, keepdims=True)
    rstd = lax.rsqrt(spread + EPS)
    return centred * rstd, rstd


class Sender:
    def __init__(self, sems):
        self.sems, self.copies = sems, []

    def put(self, src, dst):
        copy = pltpu.make_async_copy(src, dst, self.sems.at[len(self.copies)])
        copy.start()
        self.copies.append(copy)

    def finish(self):
        for copy in self.copies:
            copy.wait()


def forward_kernel(delta, n, rows,
                   t_ref, meta_ref, tok_ref, arr_ref, cos_ref, sin_ref,
                   wq_ref, wo_ref, wu_ref, wd_ref, gb_ref, s_in, all_in,
                   y_ref, x_o, att_o, hb_o, act_o, qn_o, kf_o, v_o, sg_o, n1_o, gp_o, n2_o, rs_o, sb_o, s_out, all_out,
                   x_ref, att_ref, hb_ref, act_ref, qn_ref, kf_ref, v_ref, sg_ref, n1_ref, gp_ref, n2_ref, rs_ref, sb_ref, sems):
    stage = meta_ref[0]
    chunk = t_ref[0] - delta * stage
    valid = (chunk >= 0) & (chunk < n)

    @pl.when(valid)
    def _():
        send = Sender(sems)
        base = pl.multiple_of(chunk * rows, rows)
        first = meta_ref[1 + chunk] != 0

        @pl.when(stage == 0)
        def _():
            x_ref[...] = tok_ref[pl.ds(base, rows), :]

        @pl.when(stage != 0)
        def _():
            x_ref[...] = arr_ref[...]

        @pl.when(first)
        def _():
            s_out[...] = jnp.zeros_like(s_out)

        @pl.when(jnp.logical_not(first))
        def _():
            s_out[...] = s_in[...]

        send.put(x_ref, x_o)
        x = x_ref[...]
        cos = cos_ref[pl.ds(base, rows), :]
        sin = sin_ref[pl.ds(base, rows), :]
        q_raw = nn_dot(x, wq_ref[:, 0:D])
        k_raw = nn_dot(x, wq_ref[:, D:2 * D])
        v_ref[...] = nn_dot(x, wq_ref[:, 2 * D:]).astype(bf)
        send.put(v_ref, v_o)
        m_a = head_lanes(rows, 256)
        ri = lax.broadcasted_iota(jnp.int32, (rows, rows), 0)
        ci = lax.broadcasted_iota(jnp.int32, (rows, rows), 1)
        tril = ci <= ri
        diag = block_diag(256)
        ones = jnp.ones((rows, 128), bf)
        zero = jnp.zeros((), bf)
        for p in range(PAIRS):
            lanes = slice(128 * p, 128 * p + 128)
            wide = slice(256 * p, 256 * p + 256)
            q, sq = soft_pair(q_raw[:, lanes])
            k, sk = soft_pair(k_raw[:, lanes])
            qc, qs = q * cos, q * sin
            qf = jnp.concatenate([qc, qs], axis=1).astype(bf)
            kf = jnp.concatenate([k * cos, k * sin], axis=1).astype(bf)
            kf_ref[:, wide] = kf
            sg_ref[:, D + 128 * p:D + 128 * p + 128] = sk.astype(bf)
            ve = jnp.concatenate([v_ref[:, lanes], ones], axis=1)
            s_a = nt_dot(jnp.where(m_a, qf, zero), kf)
            s_b = nt_dot(jnp.where(m_a, zero, qf), kf)
            p_ab = jnp.concatenate([jnp.where(tril, s_a, 0.0), jnp.where(tril, s_b, 0.0)], axis=1).astype(bf)
            ve2 = jnp.concatenate([jnp.where(m_a, ve, zero), jnp.where(m_a, zero, ve)], axis=0)
            before = s_out[p].astype(bf)
            sb_ref[p] = before
            nd = nn_dot(p_ab, ve2) + nn_dot(qf, before)
            inv = 1.0 / nd[:, 128:]
            att_ref[:, lanes] = (nd[:, :128] * inv).astype(bf)
            qn_ref[:, wide] = jnp.concatenate([qc * inv, qs * inv], axis=1).astype(bf)
            sg_ref[:, lanes] = (sq * inv).astype(bf)
            s_out[p] = s_out[p] + jnp.where(diag, tn_dot(kf, ve), 0.0)
        send.put(kf_ref, kf_o)
        send.put(att_ref, att_o)
        send.put(qn_ref, qn_o)
        send.put(sg_ref, sg_o)
        send.put(sb_ref, sb_o)
        residual = x.astype(f32) + nn_dot(att_ref[...], wo_ref[...])
        n1, r1 = norm_rows(residual)
        n1_ref[...] = n1.astype(bf)
        hidden = n1 * gb_ref[0:1, :] + gb_ref[1:2, :]
        hb = hidden.astype(bf)
        hb_ref[...] = hb
        send.put(n1_ref, n1_o)
        send.put(hb_ref, hb_o)
        total = hidden
        FB = 768
        for j in range(0, 4 * D, FB):
            cols = slice(j, j + FB)
            u = nn_dot(hb, wu_ref[:, cols])
            cdf = 0.5 + 0.5 * lax.erf(u * (1.0 / math.sqrt(2.0)))
            act = (u * cdf).astype(bf)
            act_ref[:, cols] = act
            gp_ref[:, cols] = (cdf + u * (jnp.exp(-0.5 * u * u) * (1.0 / math.sqrt(2.0 * math.pi)))).astype(bf)
            total = total + nn_dot(act, wd_ref[cols, :])
        send.put(act_ref, act_o)
        send.put(gp_ref, gp_o)
        n2, r2 = norm_rows(total)
        n2_ref[...] = n2.astype(bf)
        lane = lax.broadcasted_iota(jnp.int32, (rows, 128), 1)
        rs_ref[...] = jnp.where(lane < 64, r1, r2)
        send.put(n2_ref, n2_o)
        send.put(rs_ref, rs_o)
        y_ref[...] = (n2 * gb_ref[2:3, :] + gb_ref[3:4, :]).astype(bf)
        send.put(y_ref, all_out.at[pl.ds(base, rows), :])
        send.finish()


def forward_call(rows, n, delta, limit=28):
    V = pl.BlockSpec(memory_space=pltpu.VMEM)
    S = pl.BlockSpec(memory_space=pltpu.SMEM)
    A = pl.BlockSpec(memory_space=pl.ANY)
    sd = jax.ShapeDtypeStruct
    saved = [((rows, D), bf)] * 3 + [((rows, 4 * D), bf)] + [((rows, 2 * D), bf)] * 2 + [((rows, D), bf), ((rows, 2 * D), bf), ((rows, D), bf), ((rows, 4 * D), bf), ((rows, D), bf), ((rows, 128), f32), ((PAIRS, 256, 256), bf)]
    outs = [sd((rows, D), bf)] + [sd(*item) for item in saved] + [sd((PAIRS, 256, 256), f32), sd((n * rows, D), bf)]
    return pl.pallas_call(
        functools.partial(forward_kernel, delta, n, rows),
        in_specs=[S, S] + [V] * 10 + [A],
        out_specs=[V] + [A] * 13 + [V, A],
        out_shape=outs,
        scratch_shapes=[pltpu.VMEM(*item) for item in saved] + [pltpu.SemaphoreType.DMA((14,))],
        input_output_aliases={11: 14, 12: 15},
        cost_estimate=pl.CostEstimate(flops=rows * 2 * 9 * 10**6, bytes_accessed=4 * 2**20, transcendentals=0),
        compiler_params=pltpu.CompilerParams(vmem_limit_bytes=limit * 2**20),
        name="layer_forward",
    )


def norm_back(grad, normed, rstd, gain):
    scaled = grad * gain
    mean_one = jnp.mean(scaled, axis=-1, keepdims=True)
    mean_two = jnp.mean(scaled * normed, axis=-1, keepdims=True)
    return rstd * (scaled - mean_one - normed * mean_two)


def backward_kernel(delta, n, rows, stages,
                    t_ref, meta_ref, cot_ref, arr_ref, cos_ref, sin_ref,
                    wq_ref, wo_ref, wu_ref, wd_ref, gb_ref,
                    att_ref, qn_ref, kf_ref, v_ref, sg_ref, n1_ref, gp_ref, n2_ref, rs_ref, sb_ref,
                    t_in, ga_in, all_in,
                    ds_ref, df_o, du_o, dp_o, dm_o, t_out, ga_out, all_out,
                    df_ref, du_ref, dp_ref, dm_ref, da_ref, g_ref, sems):
    stage = meta_ref[0]
    chunk = n - 1 - t_ref[0] + delta * (stages - 1 - stage)
    valid = (chunk >= 0) & (chunk < n)

    @pl.when(valid)
    def _():
        send = Sender(sems)
        base = pl.multiple_of(chunk * rows, rows)
        last = meta_ref[1 + n + chunk] != 0

        @pl.when(stage == stages - 1)
        def _():
            g_ref[...] = cot_ref[pl.ds(base, rows), :]

        @pl.when(stage != stages - 1)
        def _():
            g_ref[...] = arr_ref[...]

        @pl.when(last)
        def _():
            t_out[...] = jnp.zeros_like(t_out)

        @pl.when(jnp.logical_not(last))
        def _():
            t_out[...] = t_in[...]

        @pl.when(chunk == n - 1)
        def _():
            ga_out[...] = jnp.zeros_like(ga_out)

        @pl.when(chunk != n - 1)
        def _():
            ga_out[...] = ga_in[...]

        g = g_ref[...].astype(f32)
        n2 = n2_ref[...].astype(f32)
        r1 = rs_ref[:, 0:1]
        r2 = rs_ref[:, 64:65]
        ga_out[2:3, :] += jnp.sum(g * n2, axis=0, keepdims=True)
        ga_out[3:4, :] += jnp.sum(g, axis=0, keepdims=True)
        d_two = norm_back(g, n2, r2, gb_ref[2:3, :])
        df = d_two.astype(bf)
        df_ref[...] = df
        send.put(df_ref, df_o)
        total = d_two
        FB = 768
        for j in range(0, 4 * D, FB):
            cols = slice(j, j + FB)
            du = (nt_dot(df, wd_ref[cols, :]) * gp_ref[:, cols].astype(f32)).astype(bf)
            du_ref[:, cols] = du
            total = total + nt_dot(du, wu_ref[:, cols])
        send.put(du_ref, du_o)
        n1 = n1_ref[...].astype(f32)
        ga_out[0:1, :] += jnp.sum(total * n1, axis=0, keepdims=True)
        ga_out[1:2, :] += jnp.sum(total, axis=0, keepdims=True)
        d_res = norm_back(total, n1, r1, gb_ref[0:1, :])
        dp = d_res.astype(bf)
        dp_ref[...] = dp
        send.put(dp_ref, dp_o)
        da_ref[...] = nt_dot(dp, wo_ref[...]).astype(bf)
        cos = cos_ref[pl.ds(base, rows), :]
        sin = sin_ref[pl.ds(base, rows), :]
        m_a = head_lanes(rows, 256)
        lane = lax.broadcasted_iota(jnp.int32, (rows, 128), 1)
        ri = lax.broadcasted_iota(jnp.int32, (rows, rows), 0)
        ci = lax.broadcasted_iota(jnp.int32, (rows, rows), 1)
        tril = ci <= ri
        triu = ri <= ci
        diag = block_diag(256)
        ones = jnp.ones((rows, 128), bf)
        zero = jnp.zeros((), bf)
        for p in range(PAIRS):
            lanes = slice(128 * p, 128 * p + 128)
            wide = slice(256 * p, 256 * p + 256)
            d_o = da_ref[:, lanes]
            prod = d_o.astype(f32) * att_ref[:, lanes].astype(f32)
            in_a = jnp.sum(jnp.where(lane < 64, prod, 0.0), axis=1, keepdims=True)
            in_b = jnp.sum(jnp.where(lane < 64, 0.0, prod), axis=1, keepdims=True)
            inner = jnp.where(lane < 64, -in_a, -in_b)
            high = inner.astype(bf).astype(f32)
            ext = jnp.where((lane & 63) == 0, high, jnp.where((lane & 63) == 1, inner - high, 0.0)).astype(bf)
            left = jnp.concatenate([d_o, ext], axis=1)
            left_a, left_b = jnp.where(m_a, left, zero), jnp.where(m_a, zero, left)
            ve = jnp.concatenate([v_ref[:, lanes], ones], axis=1)
            qn = qn_ref[:, wide]
            kf = kf_ref[:, wide]
            qn_a, qn_b = jnp.where(m_a, qn, zero), jnp.where(m_a, zero, qn)
            kf_a, kf_b = jnp.where(m_a, kf, zero), jnp.where(m_a, zero, kf)
            pt = jnp.concatenate([jnp.where(triu, nt_dot(kf, qn_a), 0.0), jnp.where(triu, nt_dot(kf, qn_b), 0.0)], axis=1).astype(bf)
            gg = jnp.concatenate([jnp.where(tril, nt_dot(left_a, ve), 0.0), jnp.where(tril, nt_dot(left_b, ve), 0.0)], axis=1).astype(bf)
            gt = jnp.concatenate([jnp.where(triu, nt_dot(ve, left_a), 0.0), jnp.where(triu, nt_dot(ve, left_b), 0.0)], axis=1).astype(bf)
            after = t_out[p].astype(bf)
            dv = nn_dot(pt, jnp.concatenate([left_a[:, :128], left_b[:, :128]], axis=0)) + nn_dot(kf, after[:, :128])
            dq = nn_dot(gg, jnp.concatenate([kf_a, kf_b], axis=0)) + nt_dot(left, sb_ref[p])
            dk = nn_dot(gt, jnp.concatenate([qn_a, qn_b], axis=0)) + nt_dot(ve, after)
            t_out[p] = t_out[p] + jnp.where(diag, tn_dot(qn, left), 0.0)
            sq = sg_ref[:, lanes].astype(f32)
            sk = sg_ref[:, D + 128 * p:D + 128 * p + 128].astype(f32)
            dm_ref[:, lanes] = ((dq[:, :128] * cos + dq[:, 128:] * sin) * sq).astype(bf)
            dm_ref[:, D + 128 * p:D + 128 * p + 128] = ((dk[:, :128] * cos + dk[:, 128:] * sin) * sk).astype(bf)
            dm_ref[:, 2 * D + 128 * p:2 * D + 128 * p + 128] = dv.astype(bf)
        send.put(dm_ref, dm_o)
        ds_ref[...] = (d_res + nt_dot(dm_ref[...], wq_ref[...])).astype(bf)
        send.put(ds_ref, all_out.at[pl.ds(base, rows), :])
        send.finish()


def backward_call(rows, n, delta, stages, limit=28):
    V = pl.BlockSpec(memory_space=pltpu.VMEM)
    S = pl.BlockSpec(memory_space=pltpu.SMEM)
    A = pl.BlockSpec(memory_space=pl.ANY)
    sd = jax.ShapeDtypeStruct
    made = [((rows, D), bf), ((rows, 4 * D), bf), ((rows, D), bf), ((rows, 3 * D), bf)]
    outs = [sd((rows, D), bf)] + [sd(*item) for item in made] + [sd((PAIRS, 256, 256), f32), sd((8, D), f32), sd((n * rows, D), bf)]
    return pl.pallas_call(
        functools.partial(backward_kernel, delta, n, rows, stages),
        in_specs=[S, S] + [V] * 21 + [A],
        out_specs=[V] + [A] * 4 + [V] * 2 + [A],
        out_shape=outs,
        scratch_shapes=[pltpu.VMEM(*item) for item in made] + [pltpu.VMEM((rows, D), bf), pltpu.VMEM((rows, D), bf), pltpu.SemaphoreType.DMA((5,))],
        input_output_aliases={21: 5, 22: 6, 23: 7},
        cost_estimate=pl.CostEstimate(flops=rows * 2 * 10 * 10**6, bytes_accessed=4 * 2**20, transcendentals=0),
        compiler_params=pltpu.CompilerParams(vmem_limit_bytes=limit * 2**20),
        name="layer_backward",
    )


def weight_kernel(delta, n, rows, stages, slots, units,
                  meta_ref, *refs):
    lefts, rights = refs[:slots], refs[slots:2 * slots]
    keep_ref, send_ref, left_buf, right_buf, left_sem, right_sem = refs[2 * slots:]
    step, steps = pl.program_id(0), pl.num_programs(0)
    stage, me = meta_ref[0], meta_ref[1]

    def fetch(tile, slot):
        cols = pl.ds(pl.multiple_of(tile * 384, 128), 384)
        for owner in range(stages):
            @pl.when(stage == owner)
            def _():
                for k in range(n):
                    pltpu.make_async_copy(lefts[delta * owner + k].at[:, cols], left_buf.at[slot, pl.ds(k * rows, rows), :], left_sem.at[slot]).start()

    @pl.when(step == 0)
    def _():
        for owner in range(stages):
            @pl.when(stage == owner)
            def _():
                for k in range(n):
                    pltpu.make_async_copy(rights[delta * owner + k], right_buf.at[pl.ds(k * rows, rows), :], right_sem).start()
        fetch(0, 0)
        pltpu.make_async_copy(right_buf, right_buf, right_sem).wait()

    @pl.when(step + 1 < steps)
    def _():
        fetch(step + 1, (step + 1) & 1)

    slot = step & 1
    pltpu.make_async_copy(left_buf.at[slot], left_buf.at[slot], left_sem.at[slot]).wait()
    value = tn_dot(left_buf[slot], right_buf[...]).astype(bf)
    for half in range(2):
        unit = step * 2 + half
        group = unit // units
        inside = pl.multiple_of((unit - group * units) * 192, 192)
        rel = group ^ me
        part = value[half * 192:half * 192 + 192, :]

        @pl.when((rel & 1) == 0)
        def _():
            keep_ref[rel >> 1, pl.ds(inside, 192), :] = part

        @pl.when((rel & 1) == 1)
        def _():
            send_ref[rel >> 1, pl.ds(inside, 192), :] = part


def weight_call(rows, n, delta, stages, slots, width, groups, limit=40):
    V = pl.BlockSpec(memory_space=pltpu.VMEM)
    S = pl.BlockSpec(memory_space=pltpu.SMEM)
    A = pl.BlockSpec(memory_space=pl.ANY)
    out = jax.ShapeDtypeStruct((2, width // groups, D), bf)
    return pl.pallas_call(
        functools.partial(weight_kernel, delta, n, rows, stages, slots, width // groups // 192),
        grid=(width // 384,),
        in_specs=[S] + [A] * (2 * slots),
        out_specs=[V, V],
        out_shape=[out, out],
        scratch_shapes=[pltpu.VMEM((2, n * rows, 384), bf), pltpu.VMEM((n * rows, D), bf), pltpu.SemaphoreType.DMA((2,)), pltpu.SemaphoreType.DMA],
        cost_estimate=pl.CostEstimate(flops=2 * n * rows * D * width, bytes_accessed=n * rows * (D + width) * 2, transcendentals=0),
        compiler_params=pltpu.CompilerParams(vmem_limit_bytes=limit * 2**20),
        name="weight_grad",
    )


MB_ROWS = 1024
MICRO = 2
ROWS = 256
DELTA = 2


def geometry(doc_ids):
    quarter = MB_ROWS // 4
    marks = doc_ids.reshape(-1, MB_ROWS)[:, ::quarter]
    pieces = 1 + jnp.sum((marks[:, 1:] != marks[:, :-1]).astype(jnp.int32), axis=1)
    length = MB_ROWS // pieces
    row = jnp.arange(MB_ROWS, dtype=jnp.int32)
    position = row[None, :] % length[:, None]
    angle = (0.5 * math.pi) * position.astype(f32) / length[:, None].astype(f32)
    angle = angle.reshape(-1, 1)
    starts = jnp.arange(0, MB_ROWS, ROWS, dtype=jnp.int32)
    first = (starts[None, :] % length[:, None]) == 0
    last = ((starts[None, :] + ROWS) % length[:, None]) == 0
    wide = (angle.shape[0], 128)
    return (jnp.broadcast_to(jnp.cos(angle), wide), jnp.broadcast_to(jnp.sin(angle), wide),
            first.reshape(-1).astype(jnp.int32), last.reshape(-1).astype(jnp.int32))


def exchange(block, axis, flip):
    route = [(i, i ^ flip) for i in range(lax.axis_size(axis))]
    return lax.ppermute(block, axis, route)


def reduced(keep, send):
    half = lax.optimization_barrier((keep.astype(f32) + exchange(send, "group", 1).astype(f32)).astype(bf))
    own = lax.optimization_barrier((half[0].astype(f32) + exchange(half[1], "group", 2).astype(f32)).astype(bf))
    if lax.axis_size("dp") == 2:
        return own.astype(f32) + exchange(own, "dp", 1).astype(f32)
    return lax.psum(own, "dp").astype(f32)


def local(tokens, doc_ids, cotangent, w_qkv, w_out, w_up, w_down,
          first_gain, first_bias, second_gain, second_bias):
    stages = lax.axis_size("pipe")
    groups = lax.axis_size("group")
    stage = lax.axis_index("pipe").astype(jnp.int32)
    me = lax.axis_index("group").astype(jnp.int32)
    n = tokens.shape[0] // ROWS
    ticks = n + DELTA * (stages - 1)
    cos, sin, first, last = geometry(doc_ids)
    meta = jnp.concatenate([stage[None], first, last])
    weights = (w_qkv[0], w_out[0], w_up[0], w_down[0])
    gb = jnp.concatenate([first_gain, first_bias, second_gain, second_bias], axis=0)
    forward = forward_call(ROWS, n, DELTA)
    backward = backward_call(ROWS, n, DELTA, stages)
    blank = jnp.zeros((ROWS, D), bf)
    arriving = [blank] * DELTA
    state = jnp.zeros((PAIRS, 256, 256), f32)
    block_out = jnp.zeros((n * ROWS, D), bf)
    saved = []
    for t in range(ticks):
        made = forward(jnp.full((1,), t, jnp.int32), meta, tokens, arriving.pop(0), cos, sin, *weights, gb, state, block_out)
        state, block_out = made[-2:]
        saved.append(made[1:-2])
        route = [(a, a + 1) for a in range(stages - 1) if 0 <= t - a * DELTA < n]
        arriving.append(lax.ppermute(made[0], "pipe", route) if route else blank)
    arriving = [blank] * DELTA
    state = jnp.zeros((PAIRS, 256, 256), f32)
    sums = jnp.zeros((8, D), f32)
    input_grad = jnp.zeros((n * ROWS, D), bf)
    diffs = [None] * ticks
    for t in range(ticks):
        slot = ticks - 1 - t
        x, att, hb, act, qn, kf, v, sg, n1, gp, n2, rs, sb = saved[slot]
        made = backward(jnp.full((1,), t, jnp.int32), meta, cotangent, arriving.pop(0), cos, sin, *weights, gb,
                        att, qn, kf, v, sg, n1, gp, n2, rs, sb, state, sums, input_grad)
        state, sums, input_grad = made[-3:]
        diffs[slot] = made[1:-3]
        route = [(a, a - 1) for a in range(1, stages) if 0 <= t - (stages - 1 - a) * DELTA < n]
        arriving.append(lax.ppermute(made[0], "pipe", route) if route else blank)
    where = jnp.stack([stage, me])

    def weight(left, right):
        call = weight_call(ROWS, n, DELTA, stages, ticks, left[0].shape[1], groups)
        return reduced(*call(where, *left, *right))

    pick = lambda items, i: [item[i] for item in items]
    g_down = weight(pick(saved, 3), pick(diffs, 0))
    g_up = weight(pick(diffs, 1), pick(saved, 2))
    g_qkv = weight(pick(diffs, 3), pick(saved, 0))
    g_out = weight(pick(diffs, 2), pick(saved, 1))
    total = lax.psum(sums[:4], ("group", "dp"))
    mine = lax.dynamic_slice_in_dim(total, me * (D // groups), D // groups, axis=1)
    return (block_out[None], input_grad[None], g_qkv.T[None], g_out.T[None], g_up.T[None], g_down[None],
            mine[0:1], mine[1:2], mine[2:3], mine[3:4])


def solution(mesh):
    rows = ("group", "dp")
    whole = P("pipe", None, None)
    vector = P("pipe", None)
    return jax.shard_map(
        local,
        mesh=mesh,
        in_specs=(P(rows, None), P(rows), P(rows, None)) + (whole,) * 4 + (vector,) * 4,
        out_specs=(P("pipe", rows, None), P("pipe", rows, None), P("pipe", None, "group"), P("pipe", None, "group"),
                   P("pipe", None, "group"), P("pipe", "group", None)) + (P("pipe", "group"),) * 4,
        check_vma=False,
    )
```

time: 3150 us -> 854 us (0.27)
  waiting for transfers between devices: 1710 us -> 99 us
  matrix products: 668 us -> 0 us
  Pallas kernels: 0 us -> 358 us
  starting transfers between devices: 307 us -> 39 us
  other arithmetic: 184 us -> 18.5 us
  local copies, waits for them, and re-layouts: 210 us -> 274 us
  blocking collectives: 4.94 us -> 50.3 us
  loops' own time: 41.4 us -> 0 us
    ppermute x10 -> x36, waiting for transfers between devices: 1390 us -> 99 us  [the longest x12 66.7 us: exchange(): return lax.ppermute(block, axis, route)]
    dot_general x192 -> x0, matrix products: 668 us -> none  [the longest x48 91.8 us: head_scores(): jnp.einsum('rc,sc->rs', query_feat, key_feat, preferred_element_type=jnp....]
    pallas_call x0 -> x32, Pallas kernels: none -> 358 us  [the longest x14 155 us: local(): backward(jnp.full((1,), t, jnp.int32), meta, cotangent, arriving.pop(0),...]
    ppermute x10 -> x36, starting transfers between devices: 306 us -> 39 us  [the longest x24 27.5 us: local(): arriving.append(lax.ppermute(made[0], 'pipe', route) if route else blank)]
    unnamed x28 -> x949, local copies, waits for them, and re-layouts: 7.5 us -> 267 us
    reduce_scatter x4 -> x0, waiting for transfers between devices: 141 us -> none  [the longest x1 50.4 us: local(): lax.psum_scatter(g_down.astype(jnp.bfloat16), 'group', scatter_dimension=...]
    another operation x30 -> x1, other arithmetic: 100 us -> 0.07 us  [local(): where = jnp.stack([stage, me])]
    psum x1 -> x0, waiting for transfers between devices: 89.3 us -> none  [local(): lax.psum(shares[0].astype(jnp.bfloat16), 'dp').astype(jnp.float32)]
  transfers between devices with their start and end apart: 19 -> 36, of which waited for: 18 -> 8; matrix products, arithmetic and copies ran while one was open for 1% -> 2% of each run, Pallas kernels for 0% -> 35%
where the time goes in v1:
time: 854 us; the launch traced here: 843 us
  Pallas kernels  358 us (42%)
  local copies, waits for them, and re-layouts  274 us (32%)
  waiting for transfers between devices  99 us (12%)
  blocking collectives  50.3 us (6%)
  starting transfers between devices  39 us (5%)
  other arithmetic  18.5 us (2%)
    unnamed x949, local copies, waits for them, and re-layouts  267 us
    pallas_call x14, Pallas kernels, local(): backward(jnp.full((1,), t, jnp.int32), meta, cotangent, arriving.pop(0),...  155 us
    pallas_call x14, Pallas kernels, local(): forward(jnp.full((1,), t, jnp.int32), meta, tokens, arriving.pop(0), cos,...  144 us
    ppermute x12, waiting for transfers between devices, exchange(): return lax.ppermute(block, axis, route)  66.7 us
    pallas_call x4, Pallas kernels, weight(): return reduced(*call(where, *left, *right))  59.1 us
    psum x1, blocking collectives, local(): total = lax.psum(sums[:4], ('group', 'dp'))  50.3 us
    ppermute x24, waiting for transfers between devices, local(): arriving.append(lax.ppermute(made[0], 'pipe', route) if route else blank)  32.3 us
    ppermute x24, starting transfers between devices, local(): arriving.append(lax.ppermute(made[0], 'pipe', route) if route else blank)  27.5 us
  transfers between devices with their start and end apart: 36, of which 8 were waited for; matrix products, arithmetic and copies ran while one was open for 2% of the time, Pallas kernels for 35%

profile of v1, /device:TPU:0, one launch (start us, length us, event | category | flops | bytes accessed | tf_op | source)
XLA Modules:
  0.0 842.6 jit_solution(4609151422456180289)
XLA Ops:
  6.3 2.3 copy-done
  12.5 13.7 %layer_forward.14 = (bf16[256,768]{1,0:T(8,128)(2,1)}, bf16[256,768]{1,0:T(8,128)(2,1)S(1)}, bf16[256,768]{1,0:T(8,128)(2,1)S(1)}, bf16[256,768]{1,0:T(8,128)(2,...) custom-call(s32[1]{0:T(128)} %constant.20.clone.1.t_ref, ...), custom_call_target="tpu_custom_call", output_to_operand_aliasing={{14}: (11, {}), {15}: (12, {})} | custom-call | flops 4608000000 | bytes 4194304 | tf_op jit(solution)/shard_map/layer_forward/pallas_call | solution.py:459
  37.9 14.0 %layer_forward.15 = (bf16[256,768]{1,0:T(8,128)(2,1)}, bf16[256,768]{1,0:T(8,128)(2,1)S(1)}, bf16[256,768]{1,0:T(8,128)(2,1)S(1)}, bf16[256,768]{1,0:T(8,128)(2,...) custom-call(s32[1]{0:T(128)} %constant.42.clone.1.t_ref, ...), custom_call_target="tpu_custom_call", output_to_operand_aliasing={{14}: (11, {}), {15}: (12, {})} | custom-call | flops 4608000000 | bytes 4194304 | tf_op jit(solution)/shard_map/layer_forward/pallas_call | solution.py:459
  66.2 2.3 copy-done.1
  75.5 12.8 %layer_forward.16 = (bf16[256,768]{1,0:T(8,128)(2,1)S(1)}, bf16[256,768]{1,0:T(8,128)(2,1)S(1)}, bf16[256,768]{1,0:T(8,128)(2,1)S(1)}, bf16[256,768]{1,0:T(8,128...) custom-call(s32[1]{0:T(128)} %constant.22.clone.1.t_ref, ...), custom_call_target="tpu_custom_call", output_to_operand_aliasing={{14}: (11, {}), {15}: (12, {})} | custom-call | flops 4608000000 | bytes 4194304 | tf_op jit(solution)/shard_map/layer_forward/pallas_call | solution.py:459
  98.7 13.5 %layer_forward.17 = (bf16[256,768]{1,0:T(8,128)(2,1)S(1)}, bf16[256,768]{1,0:T(8,128)(2,1)S(1)}, bf16[256,768]{1,0:T(8,128)(2,1)S(1)}, bf16[256,768]{1,0:T(8,128...) custom-call(s32[1]{0:T(128)} %constant.41.clone.1.t_ref, ...), custom_call_target="tpu_custom_call", output_to_operand_aliasing={{14}: (11, {}), {15}: (12, {})} | custom-call | flops 4608000000 | bytes 4194304 | tf_op jit(solution)/shard_map/layer_forward/pallas_call | solution.py:459
  121.3 12.7 %layer_forward.18 = (bf16[256,768]{1,0:T(8,128)(2,1)S(1)}, bf16[256,768]{1,0:T(8,128)(2,1)S(1)}, bf16[256,768]{1,0:T(8,128)(2,1)S(1)}, bf16[256,768]{1,0:T(8,128...) custom-call(s32[1]{0:T(128)} %constant.23.clone.1.t_ref, ...), custom_call_target="tpu_custom_call", output_to_operand_aliasing={{14}: (11, {}), {15}: (12, {})} | custom-call | flops 4608000000 | bytes 4194304 | tf_op jit(solution)/shard_map/layer_forward/pallas_call | solution.py:459
  143.3 13.2 %layer_forward.19 = (bf16[256,768]{1,0:T(8,128)(2,1)S(1)}, bf16[256,768]{1,0:T(8,128)(2,1)S(1)}, bf16[256,768]{1,0:T(8,128)(2,1)S(1)}, bf16[256,768]{1,0:T(8,128...) custom-call(s32[1]{0:T(128)} %constant.40.clone.1.t_ref, ...), custom_call_target="tpu_custom_call", output_to_operand_aliasing={{14}: (11, {}), {15}: (12, {})} | custom-call | flops 4608000000 | bytes 4194304 | tf_op jit(solution)/shard_map/layer_forward/pallas_call | solution.py:459
  166.6 12.7 %layer_forward.20 = (bf16[256,768]{1,0:T(8,128)(2,1)S(1)}, bf16[256,768]{1,0:T(8,128)(2,1)S(1)}, bf16[256,768]{1,0:T(8,128)(2,1)S(1)}, bf16[256,768]{1,0:T(8,128...) custom-call(s32[1]{0:T(128)} %constant.24.clone.1.t_ref, ...), custom_call_target="tpu_custom_call", output_to_operand_aliasing={{14}: (11, {}), {15}: (12, {})} | custom-call | flops 4608000000 | bytes 4194304 | tf_op jit(solution)/shard_map/layer_forward/pallas_call | solution.py:459
  189.5 13.3 %layer_forward.21 = (bf16[256,768]{1,0:T(8,128)(2,1)S(1)}, bf16[256,768]{1,0:T(8,128)(2,1)S(1)}, bf16[256,768]{1,0:T(8,128)(2,1)S(1)}, bf16[256,768]{1,0:T(8,128...) custom-call(s32[1]{0:T(128)} %constant.17.clone.1.t_ref, ...), custom_call_target="tpu_custom_call", output_to_operand_aliasing={{14}: (11, {}), {15}: (12, {})} | custom-call | flops 4608000000 | bytes 4194304 | tf_op jit(solution)/shard_map/layer_forward/pallas_call | solution.py:459
  213.7 2.5 layer_forward.22
  226.5 9.0 %layer_forward.23 = (bf16[256,768]{1,0:T(8,128)(2,1)S(1)}, bf16[256,768]{1,0:T(8,128)(2,1)S(1)}, bf16[256,768]{1,0:T(8,128)(2,1)S(1)}, bf16[256,768]{1,0:T(8,128...) custom-call(s32[1]{0:T(128)} %constant.16.clone.1.t_ref, ...), custom_call_target="tpu_custom_call", output_to_operand_aliasing={{14}: (11, {}), {15}: (12, {})} | custom-call | flops 4608000000 | bytes 4194304 | tf_op jit(solution)/shard_map/layer_forward/pallas_call | solution.py:459
  245.8 2.5 layer_forward.24
  258.5 9.1 %layer_forward.25 = (bf16[256,768]{1,0:T(8,128)(2,1)S(1)}, bf16[256,768]{1,0:T(8,128)(2,1)S(1)}, bf16[256,768]{1,0:T(8,128)(2,1)S(1)}, bf16[256,768]{1,0:T(8,128...) custom-call(s32[1]{0:T(128)} %constant.15.clone.1.t_ref, ...), custom_call_target="tpu_custom_call", output_to_operand_aliasing={{14}: (11, {}), {15}: (12, {})} | custom-call | flops 4608000000 | bytes 4194304 | tf_op jit(solution)/shard_map/layer_forward/pallas_call | solution.py:459
  277.8 3.4 layer_forward.26
  289.0 11.5 %layer_forward.27 = (bf16[256,768]{1,0:T(8,128)(2,1)}, bf16[256,768]{1,0:T(8,128)(2,1)S(1)}, bf16[256,768]{1,0:T(8,128)(2,1)S(1)}, bf16[256,768]{1,0:T(8,128)(2,...) custom-call(s32[1]{0:T(128)} %constant.30.clone.1.t_ref, ...), custom_call_target="tpu_custom_call", output_to_operand_aliasing={{14}: (11, {}), {15}: (12, {})} | custom-call | flops 4608000000 | bytes 4194304 | tf_op jit(solution)/shard_map/layer_forward/pallas_call | solution.py:459
  319.8 2.6 layer_backward.14
  329.2 9.9 %layer_backward.15 = (bf16[256,768]{1,0:T(8,128)(2,1)S(1)}, bf16[256,768]{1,0:T(8,128)(2,1)S(1)}, bf16[256,3072]{1,0:T(8,128)(2,1)S(1)}, bf16[256,768]{1,0:T(8,1...) custom-call(s32[1]{0:T(128)} %constant.42.clone.1.t_ref, ...), custom_call_target="tpu_custom_call", output_to_operand_aliasing={{5}: (21, {}), {6}: (22, {}), {7}: (23, {})} | custom-call | flops 5120000000 | bytes 4194304 | tf_op jit(solution)/shard_map/layer_backward/pallas_call | solution.py:472
  345.9 2.6 layer_backward.16
  354.3 10.4 %layer_backward.17 = (bf16[256,768]{1,0:T(8,128)(2,1)}, bf16[256,768]{1,0:T(8,128)(2,1)S(1)}, bf16[256,3072]{1,0:T(8,128)(2,1)S(1)}, bf16[256,768]{1,0:T(8,128)(...) custom-call(s32[1]{0:T(128)} %constant.41.clone.1.t_ref, ...), custom_call_target="tpu_custom_call", output_to_operand_aliasing={{5}: (21, {}), {6}: (22, {}), {7}: (23, {})} | custom-call | flops 5120000000 | bytes 4194304 | tf_op jit(solution)/shard_map/layer_backward/pallas_call | solution.py:472
  368.5 3.3 layer_backward.18
  379.3 10.6 %layer_backward.19 = (bf16[256,768]{1,0:T(8,128)(2,1)}, bf16[256,768]{1,0:T(8,128)(2,1)S(1)}, bf16[256,3072]{1,0:T(8,128)(2,1)S(1)}, bf16[256,768]{1,0:T(8,128)(...) custom-call(s32[1]{0:T(128)} %constant.40.clone.1.t_ref, ...), custom_call_target="tpu_custom_call", output_to_operand_aliasing={{5}: (21, {}), {6}: (22, {}), {7}: (23, {})} | custom-call | flops 5120000000 | bytes 4194304 | tf_op jit(solution)/shard_map/layer_backward/pallas_call | solution.py:472
  394.9 21.7 %collective-permute-done.17.arr_ref = bf16[256,768]{1,0:T(8,128)(2,1)S(1)} collective-permute-done((bf16[256,768]{1,0:T(8,128)(2,1)}, bf16[256,768]{1,0:T(8,128)(2,1)S(1)}, u32[]{:S(2)}, u32[]{:S(2)}) %collective-permute-start.17) | collective-permute-done | bytes 393248 | tf_op jit(solution)/shard_map/ppermute | solution.py:477
  417.7 14.6 %layer_backward.20 = (bf16[256,768]{1,0:T(8,128)(2,1)}, bf16[256,768]{1,0:T(8,128)(2,1)S(1)}, bf16[256,3072]{1,0:T(8,128)(2,1)S(1)}, bf16[256,768]{1,0:T(8,128)(...) custom-call(s32[1]{0:T(128)} %constant.24.clone.1.t_ref, ...), custom_call_target="tpu_custom_call", output_to_operand_aliasing={{5}: (21, {}), {6}: (22, {}), {7}: (23, {})} | custom-call | flops 5120000000 | bytes 4194304 | tf_op jit(solution)/shard_map/layer_backward/pallas_call | solution.py:472
  437.2 3.6 collective-permute-done.16.arr_ref
  443.1 15.0 %layer_backward.21 = (bf16[256,768]{1,0:T(8,128)(2,1)}, bf16[256,768]{1,0:T(8,128)(2,1)S(1)}, bf16[256,3072]{1,0:T(8,128)(2,1)S(1)}, bf16[256,768]{1,0:T(8,128)(...) custom-call(s32[1]{0:T(128)} %constant.17.clone.1.t_ref, ...), custom_call_target="tpu_custom_call", output_to_operand_aliasing={{5}: (21, {}), {6}: (22, {}), {7}: (23, {})} | custom-call | flops 5120000000 | bytes 4194304 | tf_op jit(solution)/shard_map/layer_backward/pallas_call | solution.py:472
  463.2 13.8 %layer_backward.22 = (bf16[256,768]{1,0:T(8,128)(2,1)S(1)}, bf16[256,768]{1,0:T(8,128)(2,1)S(1)}, bf16[256,3072]{1,0:T(8,128)(2,1)S(1)}, bf16[256,768]{1,0:T(8,1...) custom-call(s32[1]{0:T(128)} %constant.25.clone.1.t_ref, ...), custom_call_target="tpu_custom_call", output_to_operand_aliasing={{5}: (21, {}), {6}: (22, {}), {7}: (23, {})} | custom-call | flops 5120000000 | bytes 4194304 | tf_op jit(solution)/shard_map/layer_backward/pallas_call | solution.py:472
  480.9 4.1 collective-permute-done.18.arr_ref
  485.1 14.4 %layer_backward.23 = (bf16[256,768]{1,0:T(8,128)(2,1)S(1)}, bf16[256,768]{1,0:T(8,128)(2,1)S(1)}, bf16[256,3072]{1,0:T(8,128)(2,1)S(1)}, bf16[256,768]{1,0:T(8,1...) custom-call(s32[1]{0:T(128)} %constant.16.clone.1.t_ref, ...), custom_call_target="tpu_custom_call", output_to_operand_aliasing={{5}: (21, {}), {6}: (22, {}), {7}: (23, {})} | custom-call | flops 5120000000 | bytes 4194304 | tf_op jit(solution)/shard_map/layer_backward/pallas_call | solution.py:472
  504.6 13.8 %layer_backward.24 = (bf16[256,768]{1,0:T(8,128)(2,1)S(1)}, bf16[256,768]{1,0:T(8,128)(2,1)S(1)}, bf16[256,3072]{1,0:T(8,128)(2,1)S(1)}, bf16[256,768]{1,0:T(8,1...) custom-call(s32[1]{0:T(128)} %constant.26.clone.1.t_ref, ...), custom_call_target="tpu_custom_call", output_to_operand_aliasing={{5}: (21, {}), {6}: (22, {}), {7}: (23, {})} | custom-call | flops 5120000000 | bytes 4194304 | tf_op jit(solution)/shard_map/layer_backward/pallas_call | solution.py:472
  523.4 2.4 collective-permute-done.20.arr_ref
  525.9 14.2 %layer_backward.25 = (bf16[256,768]{1,0:T(8,128)(2,1)S(1)}, bf16[256,768]{1,0:T(8,128)(2,1)S(1)}, bf16[256,3072]{1,0:T(8,128)(2,1)S(1)}, bf16[256,768]{1,0:T(8,1...) custom-call(s32[1]{0:T(128)} %constant.15.clone.1.t_ref, ...), custom_call_target="tpu_custom_call", output_to_operand_aliasing={{5}: (21, {}), {6}: (22, {}), {7}: (23, {})} | custom-call | flops 5120000000 | bytes 4194304 | tf_op jit(solution)/shard_map/layer_backward/pallas_call | solution.py:472
  545.3 14.5 %layer_backward.26 = (bf16[256,768]{1,0:T(8,128)(2,1)}, bf16[256,768]{1,0:T(8,128)(2,1)S(1)}, bf16[256,3072]{1,0:T(8,128)(2,1)S(1)}, bf16[256,768]{1,0:T(8,128)(...) custom-call(s32[1]{0:T(128)} %constant.27.clone.1.t_ref, ...), custom_call_target="tpu_custom_call", output_to_operand_aliasing={{5}: (21, {}), {6}: (22, {}), {7}: (23, {})} | custom-call | flops 5120000000 | bytes 4194304 | tf_op jit(solution)/shard_map/layer_backward/pallas_call | solution.py:472
  564.2 15.1 %layer_backward.27 = (bf16[256,768]{1,0:T(8,128)(2,1)}, bf16[256,768]{1,0:T(8,128)(2,1)S(1)}, bf16[256,3072]{1,0:T(8,128)(2,1)S(1)}, bf16[256,768]{1,0:T(8,128)(...) custom-call(s32[1]{0:T(128)} %constant.30.clone.1.t_ref, ...), custom_call_target="tpu_custom_call", output_to_operand_aliasing={{5}: (21, {}), {6}: (22, {}), {7}: (23, {})} | custom-call | flops 5120000000 | bytes 4194304 | tf_op jit(solution)/shard_map/layer_backward/pallas_call | solution.py:472
  600.2 19.3 %weight_grad.6 = (bf16[2,768,768]{2,1,0:T(8,128)(2,1)}, bf16[2,768,768]{2,1,0:T(8,128)(2,1)}) custom-call(s32[2]{0:T(128)S(1)} %pad_add_fusion.1.meta_ref, bf16[256,3072]{1,0:T(8,128)(2,1)S(1)} %copy-done.362, bf16[256,3072]{1,0:T(8,128)(2,1)S(1)} %copy-done.360, bf16[256,3072]{1,0:T(8,128)(2,1)S(1)} %copy-done.358, bf16[256,3072]{1,0:T(8,128)(2,1)S(1)} %copy-done.356, ...), custom_call_target="tpu_custom_call" | custom-call | flops 9663676416 | bytes 15728640 | tf_op jit(solution)/shard_map/weight_grad/pallas_call | solution.py:482
  631.6 14.9 %weight_grad.4 = (bf16[2,576,768]{2,1,0:T(8,128)(2,1)}, bf16[2,576,768]{2,1,0:T(8,128)(2,1)}) custom-call(s32[2]{0:T(128)S(1)} %pad_add_fusion.1.meta_ref, bf16[256,2304]{1,0:T(8,128)(2,1)S(1)} %copy-done.383, bf16[256,2304]{1,0:T(8,128)(2,1)S(1)} %copy-done.381, bf16[256,2304]{1,0:T(8,128)(2,1)S(1)} %copy-done.379, bf16[256,2304]{1,0:T(8,128)(2,1)S(1)} %copy-done.377, ...), custom_call_target="tpu_custom_call" | custom-call | flops 7247757312 | bytes 12582912 | tf_op jit(solution)/shard_map/weight_grad/pallas_call | solution.py:482
  669.4 19.1 %weight_grad.7 = (bf16[2,768,768]{2,1,0:T(8,128)(2,1)}, bf16[2,768,768]{2,1,0:T(8,128)(2,1)}) custom-call(s32[2]{0:T(128)S(1)} %copy-done.324, bf16[256,3072]{1,0:T(8,128)(2,1)S(1)} %copy-done.326, bf16[256,3072]{1,0:T(8,128)(2,1)S(1)} %copy-done.328, bf16[256,3072]{1,0:T(8,128)(2,1)S(1)} %copy-done.330, bf16[256,3072]{1,0:T(8,128)(2,1)S(1)} %copy-done.332, ...), custom_call_target="tpu_custom_call" | custom-call | flops 9663676416 | bytes 15728640 | tf_op jit(solution)/shard_map/weight_grad/pallas_call | solution.py:482
  688.8 5.8 weight_grad.5
  695.2 2.0 add_convert_fusion.2
  697.4 2.2 add_convert_fusion.1
  699.7 2.1 collective-permute-start.31
  704.8 15.1 %collective-permute-done.25 = bf16[576,768]{1,0:T(8,128)(2,1)S(1)} collective-permute-done((bf16[576,768]{1,0:T(8,128)(2,1)S(1)}, bf16[576,768]{1,0:T(8,128)(2,1)S(1)}, u32[]{:S(2)}, u32[]{:S(2)}) %collective-permute-start.25) | collective-permute-done | bytes 884768 | tf_op jit(solution)/shard_map/ppermute | solution.py:428
  722.0 23.1 %collective-permute-done.31 = bf16[768,768]{1,0:T(8,128)(2,1)S(1)} collective-permute-done((bf16[768,768]{1,0:T(8,128)(2,1)S(1)}, bf16[768,768]{1,0:T(8,128)(2,1)S(1)}, u32[]{:S(2)}, u32[]{:S(2)}) %collective-permute-start.31) | collective-permute-done | bytes 1179680 | tf_op jit(solution)/shard_map/ppermute | solution.py:428
  747.4 28.5 %collective-permute-done.28 = bf16[192,768]{1,0:T(8,128)(2,1)S(1)} collective-permute-done((bf16[192,768]{1,0:T(8,128)(2,1)S(1)}, bf16[192,768]{1,0:T(8,128)(2,1)S(1)}, u32[]{:S(2)}, u32[]{:S(2)}) %collective-permute-start.28) | collective-permute-done | bytes 294944 | tf_op jit(solution)/shard_map/ppermute | solution.py:428
  776.6 2.2 collective-permute-start.29
  780.2 50.3 %psum.7 = f32[4,768]{1,0:T(4,128)S(1)} all-reduce(f32[4,768]{1,0:T(4,128)S(1)} %slice.59), channel_id=1, replica_groups=mesh['pipe'=4,'group'=4,'dp'=2] {'group','dp'}, use_global_device_ids=true, to_apply=%region_1.3 | all-reduce | flops 3072 | bytes 24576 | tf_op jit(solution)/shard_map/psum | solution.py:489
  833.1 2.6 add_bitcast_fusion.2
  839.1 3.3 add_bitcast_fusion
  (1051 shorter events, 312.8 us)
Async XLA Ops:
  35.8 30.4 %collective-permute-start.1 = (bf16[256,768]{1,0:T(8,128)(2,1)}, bf16[256,768]{1,0:T(8,128)(2,1)}, u32[]{:S(2)}, u32[]{:S(2)}) collective-permute-start(bf16[256,768]{1,0:T(8,128)(2,1)} %get-tuple-element.352), channel_id=1, source_target_pairs={{0,8},{1,9},{2,10},{3,11},{4,12},{5,13},{6,14},{7,15}} | collective-permute-start | bytes 1179656 | tf_op jit(solution)/shard_map/ppermute | solution.py:463
  64.1 34.7 %collective-permute-start = (bf16[256,768]{1,0:T(8,128)(2,1)}, bf16[256,768]{1,0:T(8,128)(2,1)}, u32[]{:S(2)}, u32[]{:S(2)}) collective-permute-start(bf16[256,768]{1,0:T(8,128)(2,1)} %get-tuple-element.351), channel_id=1, source_target_pairs={{0,8},{1,9},{2,10},{3,11},{4,12},{5,13},{6,14},{7,15}} | collective-permute-start | bytes 1179656 | tf_op jit(solution)/shard_map/ppermute | solution.py:463
  97.4 23.8 %collective-permute-start.3 = (bf16[256,768]{1,0:T(8,128)(2,1)S(1)}, bf16[256,768]{1,0:T(8,128)(2,1)S(1)}, u32[]{:S(2)}, u32[]{:S(2)}) collective-permute-start(bf16[256,768]{1,0:T(8,128)(2,1)S(1)} %get-tuple-element.358), channel_id=1, source_target_pairs={{0,8},{8,16},{1,9},{9,17},{2,10},{10,18},{3,11},{11,19},{4,12},{12... | collective-permute-start | bytes 1179656 | tf_op jit(solution)/shard_map/ppermute | solution.py:463
  119.9 23.4 %collective-permute-start.2 = (bf16[256,768]{1,0:T(8,128)(2,1)S(1)}, bf16[256,768]{1,0:T(8,128)(2,1)S(1)}, u32[]{:S(2)}, u32[]{:S(2)}) collective-permute-start(bf16[256,768]{1,0:T(8,128)(2,1)S(1)} %get-tuple-element.357), channel_id=1, source_target_pairs={{0,8},{8,16},{1,9},{9,17},{2,10},{10,18},{3,11},{11,19},{4,12},{12... | collective-permute-start | bytes 1179656 | tf_op jit(solution)/shard_map/ppermute | solution.py:463
  142.0 24.6 %collective-permute-start.5 = (bf16[256,768]{1,0:T(8,128)(2,1)S(1)}, bf16[256,768]{1,0:T(8,128)(2,1)S(1)}, u32[]{:S(2)}, u32[]{:S(2)}) collective-permute-start(bf16[256,768]{1,0:T(8,128)(2,1)S(1)} %get-tuple-element.364), channel_id=1, source_target_pairs={{0,8},{8,16},{16,24},{1,9},{9,17},{17,25},{2,10},{10,18},{18,26},{... | collective-permute-start | bytes 1179656 | tf_op jit(solution)/shard_map/ppermute | solution.py:463
  165.3 297.7 %copy-start.24 = (bf16[256,768]{1,0:T(8,128)(2,1)}, bf16[256,768]{1,0:T(8,128)(2,1)S(1)}, u32[]{:S(2)}) copy-start(bf16[256,768]{1,0:T(8,128)(2,1)S(1)} %get-tuple-element.507.att_ref.refs_19_) | copy-start | bytes 1179652
  165.3 24.2 %collective-permute-start.4 = (bf16[256,768]{1,0:T(8,128)(2,1)S(1)}, bf16[256,768]{1,0:T(8,128)(2,1)S(1)}, u32[]{:S(2)}, u32[]{:S(2)}) collective-permute-start(bf16[256,768]{1,0:T(8,128)(2,1)S(1)} %get-tuple-element.363), channel_id=1, source_target_pairs={{0,8},{8,16},{16,24},{1,9},{9,17},{17,25},{2,10},{10,18},{18,26},{... | collective-permute-start | bytes 1179656 | tf_op jit(solution)/shard_map/ppermute | solution.py:463
  188.2 252.6 %copy-start.26 = (bf16[256,768]{1,0:T(8,128)(2,1)}, bf16[256,768]{1,0:T(8,128)(2,1)S(1)}, u32[]{:S(2)}) copy-start(bf16[256,768]{1,0:T(8,128)(2,1)S(1)} %get-tuple-element.468.att_ref.refs_20_) | copy-start | bytes 1179652
  188.2 25.5 %collective-permute-start.7 = (bf16[256,768]{1,0:T(8,128)(2,1)S(1)}, bf16[256,768]{1,0:T(8,128)(2,1)S(1)}, u32[]{:S(2)}, u32[]{:S(2)}) collective-permute-start(bf16[256,768]{1,0:T(8,128)(2,1)S(1)} %get-tuple-element.370), channel_id=1, source_target_pairs={{0,8},{8,16},{16,24},{1,9},{9,17},{17,25},{2,10},{10,18},{18,26},{... | collective-permute-start | bytes 1179656 | tf_op jit(solution)/shard_map/ppermute | solution.py:463
  212.4 14.1 %collective-permute-start.6 = (bf16[256,768]{1,0:T(8,128)(2,1)S(1)}, bf16[256,768]{1,0:T(8,128)(2,1)S(1)}, u32[]{:S(2)}, u32[]{:S(2)}) collective-permute-start(bf16[256,768]{1,0:T(8,128)(2,1)S(1)} %get-tuple-element.369), channel_id=1, source_target_pairs={{0,8},{8,16},{16,24},{1,9},{9,17},{17,25},{2,10},{10,18},{18,26},{... | collective-permute-start | bytes 1179656 | tf_op jit(solution)/shard_map/ppermute | solution.py:463
  225.8 19.9 %collective-permute-start.9 = (bf16[256,768]{1,0:T(8,128)(2,1)S(1)}, bf16[256,768]{1,0:T(8,128)(2,1)S(1)}, u32[]{:S(2)}, u32[]{:S(2)}) collective-permute-start(bf16[256,768]{1,0:T(8,128)(2,1)S(1)} %get-tuple-element.376), channel_id=1, source_target_pairs={{8,16},{16,24},{9,17},{17,25},{10,18},{18,26},{11,19},{19,27},{12,... | collective-permute-start | bytes 1179656 | tf_op jit(solution)/shard_map/ppermute | solution.py:463
  245.1 13.4 %collective-permute-start.8 = (bf16[256,768]{1,0:T(8,128)(2,1)S(1)}, bf16[256,768]{1,0:T(8,128)(2,1)S(1)}, u32[]{:S(2)}, u32[]{:S(2)}) collective-permute-start(bf16[256,768]{1,0:T(8,128)(2,1)S(1)} %get-tuple-element.375), channel_id=1, source_target_pairs={{8,16},{16,24},{9,17},{17,25},{10,18},{18,26},{11,19},{19,27},{12,... | collective-permute-start | bytes 1179656 | tf_op jit(solution)/shard_map/ppermute | solution.py:463
  257.8 20.0 %collective-permute-start.11 = (bf16[256,768]{1,0:T(8,128)(2,1)S(1)}, bf16[256,768]{1,0:T(8,128)(2,1)S(1)}, u32[]{:S(2)}, u32[]{:S(2)}) collective-permute-start(bf16[256,768]{1,0:T(8,128)(2,1)S(1)} %get-tuple-element.382), channel_id=1, source_target_pairs={{16,24},{17,25},{18,26},{19,27},{20,28},{21,29},{22,30},{23,31}} | collective-permute-start | bytes 1179656 | tf_op jit(solution)/shard_map/ppermute | solution.py:463
  277.1 11.9 %collective-permute-start.10 = (bf16[256,768]{1,0:T(8,128)(2,1)S(1)}, bf16[256,768]{1,0:T(8,128)(2,1)S(1)}, u32[]{:S(2)}, u32[]{:S(2)}) collective-permute-start(bf16[256,768]{1,0:T(8,128)(2,1)S(1)} %get-tuple-element.381), channel_id=1, source_target_pairs={{16,24},{17,25},{18,26},{19,27},{20,28},{21,29},{22,30},{23,31}} | collective-permute-start | bytes 1179656 | tf_op jit(solution)/shard_map/ppermute | solution.py:463
  326.2 17.4 %collective-permute-start.13 = (bf16[256,768]{1,0:T(8,128)(2,1)S(1)}, bf16[256,768]{1,0:T(8,128)(2,1)S(1)}, u32[]{:S(2)}, u32[]{:S(2)}) collective-permute-start(bf16[256,768]{1,0:T(8,128)(2,1)S(1)} %get-tuple-element.422), channel_id=1, source_target_pairs={{24,16},{25,17},{26,18},{27,19},{28,20},{29,21},{30,22},{31,23}} | collective-permute-start | bytes 1179656 | tf_op jit(solution)/shard_map/ppermute | solution.py:477
  342.8 10.1 %collective-permute-start.12 = (bf16[256,768]{1,0:T(8,128)(2,1)S(1)}, bf16[256,768]{1,0:T(8,128)(2,1)S(1)}, u32[]{:S(2)}, u32[]{:S(2)}) collective-permute-start(bf16[256,768]{1,0:T(8,128)(2,1)S(1)} %get-tuple-element.411), channel_id=1, source_target_pairs={{24,16},{25,17},{26,18},{27,19},{28,20},{29,21},{30,22},{31,23}} | collective-permute-start | bytes 1179656 | tf_op jit(solution)/shard_map/ppermute | solution.py:477
  352.3 16.1 %collective-permute-start.15 = (bf16[256,768]{1,0:T(8,128)(2,1)S(1)}, bf16[256,768]{1,0:T(8,128)(2,1)S(1)}, u32[]{:S(2)}, u32[]{:S(2)}) collective-permute-start(bf16[256,768]{1,0:T(8,128)(2,1)S(1)} %get-tuple-element.450), channel_id=1, source_target_pairs={{16,8},{24,16},{17,9},{25,17},{18,10},{26,18},{19,11},{27,19},{20,... | collective-permute-start | bytes 1179656 | tf_op jit(solution)/shard_map/ppermute | solution.py:477
  367.6 9.3 %collective-permute-start.14 = (bf16[256,768]{1,0:T(8,128)(2,1)}, bf16[256,768]{1,0:T(8,128)(2,1)S(1)}, u32[]{:S(2)}, u32[]{:S(2)}) collective-permute-start(bf16[256,768]{1,0:T(8,128)(2,1)} %get-tuple-element.439), channel_id=1, source_target_pairs={{16,8},{24,16},{17,9},{25,17},{18,10},{26,18},{19,11},{27,19},{20,... | collective-permute-start | bytes 1179656 | tf_op jit(solution)/shard_map/ppermute | solution.py:477
  375.6 41.0 %collective-permute-start.17 = (bf16[256,768]{1,0:T(8,128)(2,1)}, bf16[256,768]{1,0:T(8,128)(2,1)S(1)}, u32[]{:S(2)}, u32[]{:S(2)}) collective-permute-start(bf16[256,768]{1,0:T(8,128)(2,1)} %get-tuple-element.478), channel_id=1, source_target_pairs={{8,0},{16,8},{24,16},{9,1},{17,9},{25,17},{10,2},{18,10},{26,18},{... | collective-permute-start | bytes 1179656 | tf_op jit(solution)/shard_map/ppermute | solution.py:477
  379.3 37.3 %copy-start.29 = (bf16[256,768]{1,0:T(8,128)(2,1)S(1)}, bf16[256,768]{1,0:T(8,128)(2,1)}, u32[]{:S(2)}) copy-start(bf16[256,768]{1,0:T(8,128)(2,1)} %copy-done.28) | copy-start | bytes 1179652
  379.3 37.3 %copy-start.64 = (bf16[256,3072]{1,0:T(8,128)(2,1)S(1)}, bf16[256,3072]{1,0:T(8,128)(2,1)}, u32[]{:S(2)}) copy-start(bf16[256,3072]{1,0:T(8,128)(2,1)} %copy-done.63) | copy-start | bytes 4718596
  379.3 37.3 %copy-start.134 = (bf16[256,1536]{1,0:T(8,128)(2,1)S(1)}, bf16[256,1536]{1,0:T(8,128)(2,1)}, u32[]{:S(2)}) copy-start(bf16[256,1536]{1,0:T(8,128)(2,1)} %copy-done.133) | copy-start | bytes 2359300
  379.3 37.3 %copy-start.136 = (bf16[256,1536]{1,0:T(8,128)(2,1)S(1)}, bf16[256,1536]{1,0:T(8,128)(2,1)}, u32[]{:S(2)}) copy-start(bf16[256,1536]{1,0:T(8,128)(2,1)} %copy-done.135) | copy-start | bytes 2359300
  379.3 37.3 %copy-start.138 = (bf16[256,1536]{1,0:T(8,128)(2,1)S(1)}, bf16[256,1536]{1,0:T(8,128)(2,1)}, u32[]{:S(2)}) copy-start(bf16[256,1536]{1,0:T(8,128)(2,1)} %copy-done.137) | copy-start | bytes 2359300
  379.3 37.3 %copy-start.140 = (bf16[6,256,256]{2,1,0:T(8,128)(2,1)S(1)}, bf16[6,256,256]{2,1,0:T(8,128)(2,1)}, u32[]{:S(2)}) copy-start(bf16[6,256,256]{2,1,0:T(8,128)(2,1)} %copy-done.139) | copy-start | bytes 2359300
  379.3 37.3 %copy-start.232 = (bf16[256,768]{1,0:T(8,128)(2,1)S(1)}, bf16[256,768]{1,0:T(8,128)(2,1)}, u32[]{:S(2)}) copy-start(bf16[256,768]{1,0:T(8,128)(2,1)} %copy-done.231) | copy-start | bytes 1179652
  379.3 37.3 %copy-start.234 = (bf16[256,768]{1,0:T(8,128)(2,1)S(1)}, bf16[256,768]{1,0:T(8,128)(2,1)}, u32[]{:S(2)}) copy-start(bf16[256,768]{1,0:T(8,128)(2,1)} %copy-done.233) | copy-start | bytes 1179652
  379.3 37.3 %copy-start.310 = (f32[256,128]{1,0:T(8,128)S(1)}, f32[256,128]{1,0:T(8,128)}, u32[]{:S(2)}) copy-start(f32[256,128]{1,0:T(8,128)} %copy-done.309) | copy-start | bytes 393220
  393.6 47.2 %collective-permute-start.16 = (bf16[256,768]{1,0:T(8,128)(2,1)}, bf16[256,768]{1,0:T(8,128)(2,1)S(1)}, u32[]{:S(2)}, u32[]{:S(2)}) collective-permute-start(bf16[256,768]{1,0:T(8,128)(2,1)} %get-tuple-element.467), channel_id=1, source_target_pairs={{8,0},{16,8},{24,16},{9,1},{17,9},{25,17},{10,2},{18,10},{26,18},{... | collective-permute-start | bytes 1179656 | tf_op jit(solution)/shard_map/ppermute | solution.py:477
  435.9 27.1 %collective-permute-start.19 = (bf16[256,768]{1,0:T(8,128)(2,1)}, bf16[256,768]{1,0:T(8,128)(2,1)S(1)}, u32[]{:S(2)}, u32[]{:S(2)}) collective-permute-start(bf16[256,768]{1,0:T(8,128)(2,1)} %get-tuple-element.506), channel_id=1, source_target_pairs={{8,0},{16,8},{24,16},{9,1},{17,9},{25,17},{10,2},{18,10},{26,18},{... | collective-permute-start | bytes 1179656 | tf_op jit(solution)/shard_map/ppermute | solution.py:477
  461.7 23.3 %collective-permute-start.18 = (bf16[256,768]{1,0:T(8,128)(2,1)}, bf16[256,768]{1,0:T(8,128)(2,1)S(1)}, u32[]{:S(2)}, u32[]{:S(2)}) collective-permute-start(bf16[256,768]{1,0:T(8,128)(2,1)} %get-tuple-element.495), channel_id=1, source_target_pairs={{8,0},{16,8},{24,16},{9,1},{17,9},{25,17},{10,2},{18,10},{26,18},{... | collective-permute-start | bytes 1179656 | tf_op jit(solution)/shard_map/ppermute | solution.py:477
  479.6 24.8 %collective-permute-start.21 = (bf16[256,768]{1,0:T(8,128)(2,1)S(1)}, bf16[256,768]{1,0:T(8,128)(2,1)S(1)}, u32[]{:S(2)}, u32[]{:S(2)}) collective-permute-start(bf16[256,768]{1,0:T(8,128)(2,1)S(1)} %get-tuple-element.534), channel_id=1, source_target_pairs={{8,0},{16,8},{9,1},{17,9},{10,2},{18,10},{11,3},{19,11},{12,4},{20... | collective-permute-start | bytes 1179656 | tf_op jit(solution)/shard_map/ppermute | solution.py:477
  503.2 22.6 %collective-permute-start.20 = (bf16[256,768]{1,0:T(8,128)(2,1)S(1)}, bf16[256,768]{1,0:T(8,128)(2,1)S(1)}, u32[]{:S(2)}, u32[]{:S(2)}) collective-permute-start(bf16[256,768]{1,0:T(8,128)(2,1)S(1)} %get-tuple-element.523), channel_id=1, source_target_pairs={{8,0},{16,8},{9,1},{17,9},{10,2},{18,10},{11,3},{19,11},{12,4},{20... | collective-permute-start | bytes 1179656 | tf_op jit(solution)/shard_map/ppermute | solution.py:477
  522.1 23.0 %collective-permute-start.23 = (bf16[256,768]{1,0:T(8,128)(2,1)S(1)}, bf16[256,768]{1,0:T(8,128)(2,1)S(1)}, u32[]{:S(2)}, u32[]{:S(2)}) collective-permute-start(bf16[256,768]{1,0:T(8,128)(2,1)S(1)} %get-tuple-element.562), channel_id=1, source_target_pairs={{8,0},{9,1},{10,2},{11,3},{12,4},{13,5},{14,6},{15,7}} | collective-permute-start | bytes 1179656 | tf_op jit(solution)/shard_map/ppermute | solution.py:477
  543.8 20.3 %collective-permute-start.22 = (bf16[256,768]{1,0:T(8,128)(2,1)S(1)}, bf16[256,768]{1,0:T(8,128)(2,1)S(1)}, u32[]{:S(2)}, u32[]{:S(2)}) collective-permute-start(bf16[256,768]{1,0:T(8,128)(2,1)S(1)} %get-tuple-element.551), channel_id=1, source_target_pairs={{8,0},{9,1},{10,2},{11,3},{12,4},{13,5},{14,6},{15,7}} | collective-permute-start | bytes 1179656 | tf_op jit(solution)/shard_map/ppermute | solution.py:477
  583.0 36.5 %copy-start.18 = (f32[8,768]{1,0:T(8,128)}, f32[8,768]{1,0:T(8,128)S(1)}, u32[]{:S(2)}) copy-start(f32[8,768]{1,0:T(8,128)S(1)} %get-tuple-element.686) | copy-start | bytes 73732
  619.5 77.9 %collective-permute-start.30 = (bf16[2,768,768]{2,1,0:T(8,128)(2,1)}, bf16[2,768,768]{2,1,0:T(8,128)(2,1)}, u32[]{:S(2)}, u32[]{:S(2)}) collective-permute-start(bf16[2,768,768]{2,1,0:T(8,128)(2,1)} %get-tuple-element.655), channel_id=1, source_target_pairs={{0,2},{2,0},{4,6},{6,4},{1,3},{3,1},{5,7},{7,5},{8,10},{10,8},{12,... | collective-permute-start | bytes 7077896 | tf_op jit(solution)/shard_map/ppermute | solution.py:428
  647.1 48.1 %collective-permute-start.24 = (bf16[2,576,768]{2,1,0:T(8,128)(2,1)}, bf16[2,576,768]{2,1,0:T(8,128)(2,1)}, u32[]{:S(2)}, u32[]{:S(2)}) collective-permute-start(bf16[2,576,768]{2,1,0:T(8,128)(2,1)} %get-tuple-element.609), channel_id=1, source_target_pairs={{0,2},{2,0},{4,6},{6,4},{1,3},{3,1},{5,7},{7,5},{8,10},{10,8},{12,... | collective-permute-start | bytes 5308424 | tf_op jit(solution)/shard_map/ppermute | solution.py:428
  688.5 13.3 %collective-permute-start.33 = (bf16[2,768,768]{2,1,0:T(8,128)(2,1)}, bf16[2,768,768]{2,1,0:T(8,128)(2,1)S(1)}, u32[]{:S(2)}, u32[]{:S(2)}) collective-permute-start(bf16[2,768,768]{2,1,0:T(8,128)(2,1)} %get-tuple-element.685), channel_id=1, source_target_pairs={{0,2},{2,0},{4,6},{6,4},{1,3},{3,1},{5,7},{7,5},{8,10},{10,8},{12,... | collective-permute-start | bytes 7077896 | tf_op jit(solution)/shard_map/ppermute | solution.py:428
  694.7 9.3 %collective-permute-start.27 = (bf16[2,192,768]{2,1,0:T(8,128)(2,1)S(1)}, bf16[2,192,768]{2,1,0:T(8,128)(2,1)S(1)}, u32[]{:S(2)}, u32[]{:S(2)}) collective-permute-start(bf16[2,192,768]{2,1,0:T(8,128)(2,1)S(1)} %get-tuple-element.625), channel_id=1, source_target_pairs={{0,2},{2,0},{4,6},{6,4},{1,3},{3,1},{5,7},{7,5},{8,10},{10,8},{12,... | collective-permute-start | bytes 1769480 | tf_op jit(solution)/shard_map/ppermute | solution.py:428
  697.3 22.6 %collective-permute-start.25 = (bf16[576,768]{1,0:T(8,128)(2,1)S(1)}, bf16[576,768]{1,0:T(8,128)(2,1)S(1)}, u32[]{:S(2)}, u32[]{:S(2)}) collective-permute-start(bf16[576,768]{1,0:T(8,128)(2,1)S(1)} %slice_bitcast_fusion.4), channel_id=1, source_target_pairs={{0,4},{2,6},{4,0},{6,2},{1,5},{3,7},{5,1},{7,3},{8,12},{10,14},{12... | collective-permute-start | bytes 2654216 | tf_op jit(solution)/shard_map/ppermute | solution.py:428
  699.7 45.4 %collective-permute-start.31 = (bf16[768,768]{1,0:T(8,128)(2,1)S(1)}, bf16[768,768]{1,0:T(8,128)(2,1)S(1)}, u32[]{:S(2)}, u32[]{:S(2)}) collective-permute-start(bf16[768,768]{1,0:T(8,128)(2,1)S(1)} %slice_bitcast_fusion.2), channel_id=1, source_target_pairs={{0,4},{2,6},{4,0},{6,2},{1,5},{3,7},{5,1},{7,3},{8,12},{10,14},{12... | collective-permute-start | bytes 3538952 | tf_op jit(solution)/shard_map/ppermute | solution.py:428
  702.4 76.4 %collective-permute-start.34 = (bf16[768,768]{1,0:T(8,128)(2,1)S(1)}, bf16[768,768]{1,0:T(8,128)(2,1)S(1)}, u32[]{:S(2)}, u32[]{:S(2)}) collective-permute-start(bf16[768,768]{1,0:T(8,128)(2,1)S(1)} %slice_bitcast_fusion), channel_id=1, source_target_pairs={{0,4},{2,6},{4,0},{6,2},{1,5},{3,7},{5,1},{7,3},{8,12},{10,14},{12... | collective-permute-start | bytes 3538952 | tf_op jit(solution)/shard_map/ppermute | solution.py:428
  704.2 71.7 %collective-permute-start.28 = (bf16[192,768]{1,0:T(8,128)(2,1)S(1)}, bf16[192,768]{1,0:T(8,128)(2,1)S(1)}, u32[]{:S(2)}, u32[]{:S(2)}) collective-permute-start(bf16[192,768]{1,0:T(8,128)(2,1)S(1)} %slice_bitcast_fusion.6), channel_id=1, source_target_pairs={{0,4},{2,6},{4,0},{6,2},{1,5},{3,7},{5,1},{7,3},{8,12},{10,14},{12... | collective-permute-start | bytes 884744 | tf_op jit(solution)/shard_map/ppermute | solution.py:428
  720.1 113.0 %collective-permute-start.26 = (bf16[576,768]{1,0:T(8,128)(2,1)S(1)}, bf16[576,768]{1,0:T(8,128)(2,1)}, u32[]{:S(2)}, u32[]{:S(2)}) collective-permute-start(bf16[576,768]{1,0:T(8,128)(2,1)S(1)} %fusion.2), channel_id=1, source_target_pairs={{0,1},{1,0},{2,3},{3,2},{4,5},{5,4},{6,7},{7,6},{8,9},{9,8},{10,11... | collective-permute-start | bytes 2654216 | tf_op jit(solution)/shard_map/ppermute | solution.py:428
  745.4 90.2 %collective-permute-start.32 = (bf16[768,768]{1,0:T(8,128)(2,1)S(1)}, bf16[768,768]{1,0:T(8,128)(2,1)}, u32[]{:S(2)}, u32[]{:S(2)}) collective-permute-start(bf16[768,768]{1,0:T(8,128)(2,1)S(1)} %fusion.1), channel_id=1, source_target_pairs={{0,1},{1,0},{2,3},{3,2},{4,5},{5,4},{6,7},{7,6},{8,9},{9,8},{10,11... | collective-permute-start | bytes 3538952 | tf_op jit(solution)/shard_map/ppermute | solution.py:428
  776.6 54.5 %collective-permute-start.29 = (bf16[192,768]{1,0:T(8,128)(2,1)}, bf16[192,768]{1,0:T(8,128)(2,1)}, u32[]{:S(2)}, u32[]{:S(2)}) collective-permute-start(bf16[192,768]{1,0:T(8,128)(2,1)} %fusion.3), channel_id=1, source_target_pairs={{0,1},{1,0},{2,3},{3,2},{4,5},{5,4},{6,7},{7,6},{8,9},{9,8},{10,11... | collective-permute-start | bytes 884744 | tf_op jit(solution)/shard_map/ppermute | solution.py:428
  780.2 58.9 %collective-permute-start.35 = (bf16[768,768]{1,0:T(8,128)(2,1)}, bf16[768,768]{1,0:T(8,128)(2,1)}, u32[]{:S(2)}, u32[]{:S(2)}) collective-permute-start(bf16[768,768]{1,0:T(8,128)(2,1)} %fusion), channel_id=1, source_target_pairs={{0,1},{1,0},{2,3},{3,2},{4,5},{5,4},{6,7},{7,6},{8,9},{9,8},{10,11... | collective-permute-start | bytes 3538952 | tf_op jit(solution)/shard_map/ppermute | solution.py:428
  (461 other events, 3184.0 us)

commit v2 on v1

v2 whole, which is shorter than its diff:
```python
import functools, math
import jax, jax.numpy as jnp
from jax import lax
from jax.experimental import pallas as pl
from jax.experimental.pallas import tpu as pltpu
from jax.sharding import PartitionSpec as P

bf = jnp.bfloat16
f32 = jnp.float32
EPS = 1e-05
D = 768
PAIRS = 6
TILE = 256
TILES = 4 * D // TILE
NT = (((1,), (1,)), ((), ()))
TN = (((0,), (0,)), ((), ()))


def nn_dot(a, b):
    return jnp.dot(a, b, preferred_element_type=f32)


def nt_dot(a, b):
    return lax.dot_general(a, b, NT, preferred_element_type=f32)


def tn_dot(a, b):
    return lax.dot_general(a, b, TN, preferred_element_type=f32)


def head_lanes(rows, lanes):
    lane = lax.broadcasted_iota(jnp.int32, (rows, lanes), 1)
    return (lane & 64) == 0


def block_diag(size):
    r = lax.broadcasted_iota(jnp.int32, (size, size), 0)
    c = lax.broadcasted_iota(jnp.int32, (size, size), 1)
    return ((r ^ c) & 64) == 0


def soft_pair(raw):
    e = jnp.exp(-jnp.abs(raw))
    one = 1.0 + e
    tail = jnp.where(e < 1e-3, e * (1.0 - e * (0.5 - e * (1.0 / 3.0))), jnp.log(one))
    soft = jnp.maximum(raw, 0.0) + tail
    sig = jnp.where(raw >= 0.0, 1.0, e) / one
    return soft, sig


def norm_rows(v):
    centre = jnp.mean(v, axis=-1, keepdims=True)
    centred = v - centre
    spread = jnp.mean(centred * centred, axis=-1, keepdims=True)
    rstd = lax.rsqrt(spread + EPS)
    return centred * rstd, rstd


class Sender:
    def __init__(self, sems):
        self.sems, self.copies = sems, []

    def put(self, src, dst):
        copy = pltpu.make_async_copy(src, dst, self.sems.at[len(self.copies)])
        copy.start()
        self.copies.append(copy)

    def finish(self):
        for copy in self.copies:
            copy.wait()


def forward_kernel(delta, n, rows,
                   t_ref, meta_ref, tok_ref, arr_ref, cos_ref, sin_ref,
                   wq_ref, wo_ref, wu_ref, wd_ref, gb_ref, s_in,
                   y_ref, s_out, all_o, x_o, att_o, hb_o, act_o, qn_o, kf_o, v_o, sg_o, n1_o, gp_o, n2_o, rs_o, sb_o,
                   x_ref, att_ref, hb_ref, act_ref, qn_ref, kf_ref, v_ref, sg_ref, n1_ref, gp_ref, n2_ref, rs_ref, sb_ref, sems, loads=()):
    stage = meta_ref[0]
    chunk = t_ref[0] - delta * stage
    valid = (chunk >= 0) & (chunk < n)

    def loaded(*which):
        for i in which:
            if loads:
                loads[i].wait()

    @pl.when(jnp.logical_not(valid))
    def _():
        loaded(*range(len(loads)))

    @pl.when(valid)
    def _():
        send = Sender(sems)
        base = pl.multiple_of(chunk * rows, rows)
        here = pl.ds(base, rows)
        first = meta_ref[2 + chunk] != 0
        loaded(0)

        @pl.when(stage == 0)
        def _():
            x_ref[...] = tok_ref[pl.ds(base, rows), :]

        @pl.when(stage != 0)
        def _():
            x_ref[...] = arr_ref[...]

        @pl.when(first)
        def _():
            s_out[...] = jnp.zeros_like(s_out)

        if s_in is not None:
            @pl.when(jnp.logical_not(first))
            def _():
                s_out[...] = s_in[...]

        send.put(x_ref, x_o.at[here, :])
        x = x_ref[...]
        cos = cos_ref[pl.ds(base, rows), :]
        sin = sin_ref[pl.ds(base, rows), :]
        loaded(1)
        q_raw = nn_dot(x, wq_ref[:, 0:D])
        k_raw = nn_dot(x, wq_ref[:, D:2 * D])
        v_ref[...] = nn_dot(x, wq_ref[:, 2 * D:]).astype(bf)
        send.put(v_ref, v_o.at[here, :])
        m_a = head_lanes(rows, 256)
        ri = lax.broadcasted_iota(jnp.int32, (rows, rows), 0)
        ci = lax.broadcasted_iota(jnp.int32, (rows, rows), 1)
        tril = ci <= ri
        diag = block_diag(256)
        ones = jnp.ones((rows, 128), bf)
        zero = jnp.zeros((), bf)
        for p in range(PAIRS):
            lanes = slice(128 * p, 128 * p + 128)
            wide = slice(256 * p, 256 * p + 256)
            q, sq = soft_pair(q_raw[:, lanes])
            k, sk = soft_pair(k_raw[:, lanes])
            qc, qs = q * cos, q * sin
            qf = jnp.concatenate([qc, qs], axis=1).astype(bf)
            kf = jnp.concatenate([k * cos, k * sin], axis=1).astype(bf)
            kf_ref[:, wide] = kf
            sg_ref[:, D + 128 * p:D + 128 * p + 128] = sk.astype(bf)
            ve = jnp.concatenate([v_ref[:, lanes], ones], axis=1)
            s_a = nt_dot(jnp.where(m_a, qf, zero), kf)
            s_b = nt_dot(jnp.where(m_a, zero, qf), kf)
            p_ab = jnp.concatenate([jnp.where(tril, s_a, 0.0), jnp.where(tril, s_b, 0.0)], axis=1).astype(bf)
            ve2 = jnp.concatenate([jnp.where(m_a, ve, zero), jnp.where(m_a, zero, ve)], axis=0)
            before = s_out[p].astype(bf)
            sb_ref[p] = before
            nd = nn_dot(p_ab, ve2) + nn_dot(qf, before)
            inv = 1.0 / nd[:, 128:]
            att_ref[:, lanes] = (nd[:, :128] * inv).astype(bf)
            qn_ref[:, wide] = jnp.concatenate([qc * inv, qs * inv], axis=1).astype(bf)
            sg_ref[:, lanes] = (sq * inv).astype(bf)
            s_out[p] = s_out[p] + jnp.where(diag, tn_dot(kf, ve), 0.0)
        send.put(kf_ref, kf_o.at[here, :])
        send.put(att_ref, att_o.at[here, :])
        send.put(qn_ref, qn_o.at[here, :])
        send.put(sg_ref, sg_o.at[here, :])
        send.put(sb_ref, sb_o.at[chunk])
        loaded(2)
        residual = x.astype(f32) + nn_dot(att_ref[...], wo_ref[...])
        n1, r1 = norm_rows(residual)
        n1_ref[...] = n1.astype(bf)
        hidden = n1 * gb_ref[0:1, :] + gb_ref[1:2, :]
        hb = hidden.astype(bf)
        hb_ref[...] = hb
        send.put(n1_ref, n1_o.at[here, :])
        send.put(hb_ref, hb_o.at[here, :])
        total = hidden
        loaded(3, 4)
        FB = 768
        for j in range(0, 4 * D, FB):
            cols = slice(j, j + FB)
            u = nn_dot(hb, wu_ref[:, cols])
            cdf = 0.5 + 0.5 * lax.erf(u * (1.0 / math.sqrt(2.0)))
            act = (u * cdf).astype(bf)
            act_ref[:, cols] = act
            gp_ref[:, cols] = (cdf + u * (jnp.exp(-0.5 * u * u) * (1.0 / math.sqrt(2.0 * math.pi)))).astype(bf)
            for i in range(j // TILE, (j + FB) // TILE):
                send.put(act_ref.at[:, i * TILE:(i + 1) * TILE], act_o.at[i, here, :])
            send.put(gp_ref.at[:, cols], gp_o.at[here, cols])
            total = total + nn_dot(act, wd_ref[cols, :])
        n2, r2 = norm_rows(total)
        n2_ref[...] = n2.astype(bf)
        lane = lax.broadcasted_iota(jnp.int32, (rows, 128), 1)
        rs_ref[...] = jnp.where(lane < 64, r1, r2)
        send.put(n2_ref, n2_o.at[here, :])
        send.put(rs_ref, rs_o.at[here, :])
        y_ref[...] = (n2 * gb_ref[2:3, :] + gb_ref[3:4, :]).astype(bf)
        send.put(y_ref, all_o.at[here, :])
        loaded(5, 6)
        send.finish()


def far(items):
    return [pltpu.with_memory_space_constraint(item, pltpu.HBM) for item in items]


def near(items):
    return [pltpu.with_memory_space_constraint(item, pltpu.VMEM) for item in items]


def forward_opening(delta, n, rows, *refs):
    ins, refs = refs[:12], refs[12:]
    outs, kept, scratch, load_sems = refs[:16], refs[16:25], refs[25:-1], refs[-1]
    tok, cot, cos, sin, *weights, gb = ins[3:]
    tok_v, cot_v, _, _, *weights_v, _ = kept
    head, tail = pl.ds(0, rows), pl.ds(rows, (n - 1) * rows)
    pairs = [(tok.at[head, :], tok_v.at[head, :])] + list(zip(weights, weights_v)) + [(tok.at[tail, :], tok_v.at[tail, :]), (cot, cot_v)]
    loads = [pltpu.make_async_copy(src, dst, load_sems.at[i]) for i, (src, dst) in enumerate(pairs)]
    for copy in loads:
        copy.start()
    forward_kernel(delta, n, rows, *ins[:2], tok_v, ins[2], cos, sin, *weights_v, gb, None, *outs, *scratch, loads=loads)


def forward_next(delta, n, rows, *refs):
    t, meta, arr, tok, cot, cos, sin, wq, wo, wu, wd, gb, s_in = refs[:13]
    forward_kernel(delta, n, rows, t, meta, tok, arr, cos, sin, wq, wo, wu, wd, gb, s_in, *refs[27:43], *refs[52:])


def saved_items(rows):
    return [((rows, D), bf)] * 3 + [((rows, 4 * D), bf), ((rows, 2 * D), bf), ((rows, 2 * D), bf), ((rows, D), bf), ((rows, 2 * D), bf),
                                    ((rows, D), bf), ((rows, 4 * D), bf), ((rows, D), bf), ((rows, 128), f32), ((PAIRS, 256, 256), bf)]


def kept_items(every):
    return [((every, D), bf), ((every, D), bf), ((every, 128), f32), ((every, 128), f32),
            ((D, 3 * D), bf), ((D, D), bf), ((D, 4 * D), bf), ((4 * D, D), bf), ((4, D), f32)]


def forward_call(rows, n, delta, opening, limit=22):
    V = pl.BlockSpec(memory_space=pltpu.VMEM)
    S = pl.BlockSpec(memory_space=pltpu.SMEM)
    A = pl.BlockSpec(memory_space=pl.ANY)
    sd = jax.ShapeDtypeStruct
    every = n * rows
    big = [pltpu.HBM((every, D), bf)] + [pltpu.HBM(*item) for item in saved_items(every)]
    big[4] = pltpu.HBM((TILES, every, TILE), bf)
    big[13] = pltpu.HBM((n, PAIRS, 256, 256), bf)
    aliases = {5: 18, 6: 19, 11: 24}
    if not opening:
        aliases = {12: 1, **{13 + i: 2 + i for i in range(14)}, **{3 + i: 16 + i for i in range(9)}}
    return pl.pallas_call(
        functools.partial(forward_opening if opening else forward_next, delta, n, rows),
        in_specs=[S, S, V, A, A, V, V, A, A, A, A, V] if opening else [S, S] + [V] * 11 + [A] * 14,
        out_specs=[V, V] + [A] * 14 + [V] * 9,
        out_shape=[sd((rows, D), bf), sd((PAIRS, 256, 256), f32)] + big + [pltpu.VMEM(*item) for item in kept_items(every)],
        scratch_shapes=[pltpu.VMEM(*item) for item in saved_items(rows)] + [pltpu.SemaphoreType.DMA((30,))] + [pltpu.SemaphoreType.DMA((7,))] * opening,
        input_output_aliases=aliases,
        cost_estimate=pl.CostEstimate(flops=rows * 2 * 9 * 10**6, bytes_accessed=4 * 2**20, transcendentals=0),
        compiler_params=pltpu.CompilerParams(vmem_limit_bytes=limit * 2**20),
        name="layer_forward",
    )


def norm_back(grad, normed, rstd, gain):
    scaled = grad * gain
    mean_one = jnp.mean(scaled, axis=-1, keepdims=True)
    mean_two = jnp.mean(scaled * normed, axis=-1, keepdims=True)
    return rstd * (scaled - mean_one - normed * mean_two)


def backward_kernel(delta, n, rows, stages, groups,
                    t_ref, meta_ref, cot_ref, arr_ref, cos_ref, sin_ref,
                    wq_ref, wo_ref, wu_ref, wd_ref, gb_ref, t_in, ga_in,
                    n2_i, rs_i, gp_i, n1_i, att_i, v_i, qn_i, kf_i, sg_i, sb_i,
                    ds_ref, t_out, ga_out, df_o, du_o, de_o, all_o,
                    df_ref, du_ref, de_ref, dm_ref, da_ref, g_ref,
                    n2_ref, rs_ref, gp_ref, n1_ref, att_ref, v_ref, qn_ref, kf_ref, sg_ref, sb_ref, sems, fetch_sems, loads=()):
    stage = meta_ref[0]
    chunk = n - 1 - t_ref[0] + delta * (stages - 1 - stage)
    valid = (chunk >= 0) & (chunk < n)

    def loaded(*which):
        for i in which:
            if loads:
                loads[i].wait()

    @pl.when(jnp.logical_not(valid))
    def _():
        loaded(*range(len(loads)))

    @pl.when(valid)
    def _():
        base = pl.multiple_of(chunk * rows, rows)
        here = pl.ds(base, rows)
        fetched = []
        quarters = [slice(j, j + D) for j in range(0, 4 * D, D)]
        pairs = [(n2_i.at[here, :], n2_ref), (rs_i.at[here, :], rs_ref)] + [(gp_i.at[here, cols], gp_ref.at[:, cols]) for cols in quarters]
        pairs += [(src.at[here, :], dst) for src, dst in ((n1_i, n1_ref), (att_i, att_ref), (v_i, v_ref), (qn_i, qn_ref), (kf_i, kf_ref), (sg_i, sg_ref))]
        pairs += [(sb_i.at[chunk], sb_ref)]
        for i, (src, dst) in enumerate(pairs):
            copy = pltpu.make_async_copy(src, dst, fetch_sems.at[i])
            copy.start()
            fetched.append(copy)
        send = Sender(sems)
        last = meta_ref[2 + n + chunk] != 0

        loaded(0)

        if cot_ref is None:
            g_ref[...] = arr_ref[...]
        else:
            @pl.when(stage == stages - 1)
            def _():
                g_ref[...] = cot_ref[pl.ds(base, rows), :]

            @pl.when(stage != stages - 1)
            def _():
                g_ref[...] = arr_ref[...]

        @pl.when(last)
        def _():
            t_out[...] = jnp.zeros_like(t_out)

        if t_in is not None:
            @pl.when(jnp.logical_not(last))
            def _():
                t_out[...] = t_in[...]

        @pl.when(chunk == n - 1)
        def _():
            ga_out[...] = jnp.zeros_like(ga_out)

        if ga_in is not None:
            @pl.when(chunk != n - 1)
            def _():
                ga_out[...] = ga_in[...]

        g = g_ref[...].astype(f32)
        fetched[0].wait()
        fetched[1].wait()
        n2 = n2_ref[...].astype(f32)
        r1 = rs_ref[:, 0:1]
        r2 = rs_ref[:, 64:65]
        ga_out[2:3, :] += jnp.sum(g * n2, axis=0, keepdims=True)
        ga_out[3:4, :] += jnp.sum(g, axis=0, keepdims=True)
        d_two = norm_back(g, n2, r2, gb_ref[2:3, :])
        df = d_two.astype(bf)
        df_ref[...] = df
        send.put(df_ref, df_o.at[here, :])
        total = d_two
        loaded(1, 2)
        for cols, copy in zip(quarters, fetched[2:6]):
            copy.wait()
            du = (nt_dot(df, wd_ref[cols, :]) * gp_ref[:, cols].astype(f32)).astype(bf)
            du_ref[:, cols] = du
            for i in range(cols.start // TILE, cols.stop // TILE):
                send.put(du_ref.at[:, i * TILE:(i + 1) * TILE], du_o.at[i, here, :])
            total = total + nt_dot(du, wu_ref[:, cols])
        fetched[6].wait()
        n1 = n1_ref[...].astype(f32)
        ga_out[0:1, :] += jnp.sum(total * n1, axis=0, keepdims=True)
        ga_out[1:2, :] += jnp.sum(total, axis=0, keepdims=True)
        d_res = norm_back(total, n1, r1, gb_ref[0:1, :])
        dp = d_res.astype(bf)
        loaded(3)
        da_ref[...] = nt_dot(dp, wo_ref[...]).astype(bf)
        for copy in fetched[7:]:
            copy.wait()
        cos = cos_ref[pl.ds(base, rows), :]
        sin = sin_ref[pl.ds(base, rows), :]
        m_a = head_lanes(rows, 256)
        lane = lax.broadcasted_iota(jnp.int32, (rows, 128), 1)
        ri = lax.broadcasted_iota(jnp.int32, (rows, rows), 0)
        ci = lax.broadcasted_iota(jnp.int32, (rows, rows), 1)
        tril = ci <= ri
        triu = ri <= ci
        diag = block_diag(256)
        ones = jnp.ones((rows, 128), bf)
        zero = jnp.zeros((), bf)
        for p in range(PAIRS):
            lanes = slice(128 * p, 128 * p + 128)
            wide = slice(256 * p, 256 * p + 256)
            d_o = da_ref[:, lanes]
            prod = d_o.astype(f32) * att_ref[:, lanes].astype(f32)
            in_a = jnp.sum(jnp.where(lane < 64, prod, 0.0), axis=1, keepdims=True)
            in_b = jnp.sum(jnp.where(lane < 64, 0.0, prod), axis=1, keepdims=True)
            inner = jnp.where(lane < 64, -in_a, -in_b)
            high = inner.astype(bf).astype(f32)
            ext = jnp.where((lane & 63) == 0, high, jnp.where((lane & 63) == 1, inner - high, 0.0)).astype(bf)
            left = jnp.concatenate([d_o, ext], axis=1)
            left_a, left_b = jnp.where(m_a, left, zero), jnp.where(m_a, zero, left)
            ve = jnp.concatenate([v_ref[:, lanes], ones], axis=1)
            qn = qn_ref[:, wide]
            kf = kf_ref[:, wide]
            qn_a, qn_b = jnp.where(m_a, qn, zero), jnp.where(m_a, zero, qn)
            kf_a, kf_b = jnp.where(m_a, kf, zero), jnp.where(m_a, zero, kf)
            pt = jnp.concatenate([jnp.where(triu, nt_dot(kf, qn_a), 0.0), jnp.where(triu, nt_dot(kf, qn_b), 0.0)], axis=1).astype(bf)
            gg = jnp.concatenate([jnp.where(tril, nt_dot(left_a, ve), 0.0), jnp.where(tril, nt_dot(left_b, ve), 0.0)], axis=1).astype(bf)
            gt = jnp.concatenate([jnp.where(triu, nt_dot(ve, left_a), 0.0), jnp.where(triu, nt_dot(ve, left_b), 0.0)], axis=1).astype(bf)
            after = t_out[p].astype(bf)
            dv = nn_dot(pt, jnp.concatenate([left_a[:, :128], left_b[:, :128]], axis=0)) + nn_dot(kf, after[:, :128])
            dq = nn_dot(gg, jnp.concatenate([kf_a, kf_b], axis=0)) + nt_dot(left, sb_ref[p])
            dk = nn_dot(gt, jnp.concatenate([qn_a, qn_b], axis=0)) + nt_dot(ve, after)
            t_out[p] = t_out[p] + jnp.where(diag, tn_dot(qn, left), 0.0)
            sq = sg_ref[:, lanes].astype(f32)
            sk = sg_ref[:, D + 128 * p:D + 128 * p + 128].astype(f32)
            dm_ref[:, lanes] = ((dq[:, :128] * cos + dq[:, 128:] * sin) * sq).astype(bf)
            dm_ref[:, D + 128 * p:D + 128 * p + 128] = ((dk[:, :128] * cos + dk[:, 128:] * sin) * sk).astype(bf)
            dm_ref[:, 2 * D + 128 * p:2 * D + 128 * p + 128] = dv.astype(bf)
        loaded(4, 5)
        dm = dm_ref[...]
        for g in range(groups):
            odd = g & 1
            part, rest = 9 * g, 3 * g
            inner, outer = part + odd, rest + odd
            de_ref[:, g * D:g * D + 4 * 128] = dm[:, inner * 64:inner * 64 + 4 * 128]
            de_ref[:, g * D + 5 * 128:(g + 1) * D] = dp[:, outer * 64:outer * 64 + 128]
            one = dm[:, (part if odd else part + 8) // 2 * 128:][:, :128].astype(f32)
            two = dp[:, (rest if odd else rest + 2) // 2 * 128:][:, :128].astype(f32)
            if odd:
                one = pltpu.roll(one, 64, 1)
            else:
                two = pltpu.roll(two, 64, 1)
            de_ref[:, g * D + 4 * 128:g * D + 5 * 128] = jnp.where(lane < 64, one, two).astype(bf)
        for i in range(TILES):
            send.put(de_ref.at[:, i * TILE:(i + 1) * TILE], de_o.at[i, here, :])
        ds_ref[...] = (d_res + nt_dot(dm, wq_ref[...])).astype(bf)
        send.put(ds_ref, all_o.at[here, :])
        send.finish()


def backward_opening(delta, n, rows, stages, groups, *refs):
    t, meta, arr, cot = refs[:4]
    backward_kernel(delta, n, rows, stages, groups, t, meta, cot, arr, *refs[4:11], None, None, *refs[11:28], *refs[36:])


def backward_next(delta, n, rows, stages, groups, *refs):
    t, meta, arr, cot = refs[:4]
    backward_kernel(delta, n, rows, stages, groups, t, meta, cot, arr, *refs[4:23], *refs[27:34], *refs[42:])


def backward_closing(delta, n, rows, stages, groups, *refs):
    t, meta, arr = refs[:3]
    act, refs, outs = refs[26], refs[3:22] + refs[27:], refs[27:34]
    act_v, rest, sem = refs[19 + 14], refs[19 + 15:-1], refs[-1]
    copies = [pltpu.make_async_copy(act.at[i], act_v.at[i], sem.at[i]) for i in range(TILES)]
    for copy in copies:
        copy.start()
    backward_kernel(delta, n, rows, stages, groups, t, meta, None, arr, *refs[:19], *outs, *rest)
    for copy in copies:
        copy.wait()


def backward_call(rows, n, delta, stages, groups, opening, closing, limit=22):
    V = pl.BlockSpec(memory_space=pltpu.VMEM)
    S = pl.BlockSpec(memory_space=pltpu.SMEM)
    A = pl.BlockSpec(memory_space=pl.ANY)
    sd = jax.ShapeDtypeStruct
    every = n * rows
    made = [((rows, D), bf), ((rows, 4 * D), bf), ((rows, 4 * D), bf)]
    saved = [((rows, D), bf), ((rows, 128), f32), ((rows, 4 * D), bf), ((rows, D), bf), ((rows, D), bf), ((rows, D), bf),
             ((rows, 2 * D), bf), ((rows, 2 * D), bf), ((rows, 2 * D), bf), ((PAIRS, 256, 256), bf)]
    own = [((rows, 3 * D), bf), ((rows, D), bf), ((rows, D), bf)]
    big = [pltpu.HBM((every, D), bf), pltpu.HBM((TILES, every, TILE), bf), pltpu.HBM((TILES, every, TILE), bf), pltpu.HBM((every, D), bf)]
    return pl.pallas_call(
        functools.partial(backward_opening if opening else backward_closing if closing else backward_next, delta, n, rows, stages, groups),
        in_specs=[S, S] + [V] * 9 + [A] * 10 if opening else [S, S] + [V] * (11 - closing) + [A] * (14 + closing),
        out_specs=[V] * 3 + [A] * 4 + [V] * 8,
        out_shape=[sd((rows, D), bf), sd((PAIRS, 256, 256), f32), sd((8, D), f32)] + big
        + [pltpu.VMEM(*item) for item in kept_items(every)[1 + closing:]] + [pltpu.VMEM((TILES, every, TILE), bf)] * closing,
        scratch_shapes=[pltpu.VMEM(*item) for item in made + own + saved] + [pltpu.SemaphoreType.DMA((30,)), pltpu.SemaphoreType.DMA((13,))]
        + [pltpu.SemaphoreType.DMA((TILES,))] * closing,
        input_output_aliases={**{3 + i: 7 + i for i in range(8 - closing)}, **({} if opening else {11 - closing: 1, 12 - closing: 2, **{23 - closing + i: 3 + i for i in range(4)}})},
        cost_estimate=pl.CostEstimate(flops=rows * 2 * 10 * 10**6, bytes_accessed=4 * 2**20, transcendentals=0),
        compiler_params=pltpu.CompilerParams(vmem_limit_bytes=limit * 2**20),
        name="layer_backward",
    )


HALF = D // 2


def weight_kernel(groups, mixed, waits, meta_ref, left, *refs):
    raws, refs = refs[:1 + mixed], refs[1 + mixed + waits:]
    outs, (turned, out_buf, out_sem) = refs[:4], refs[4:]
    me = meta_ref[1]
    share = TILES // groups
    for j, raw in enumerate(raws):
        for k in range(0, raw.shape[0], 256):
            turned[j, :, k:k + 256] = raw[k:k + 256, :].T
    for g in range(groups):
        for i in range(share):
            cols = slice(i * TILE, (i + 1) * TILE)
            value = nn_dot(turned[0], left[g * share + i])
            if mixed and i == share - 1:
                other = nn_dot(turned[1], left[g * share + i])
                lane = lax.broadcasted_iota(jnp.int32, other.shape, 1)
                value = jnp.where(lane < 3 * D // groups - i * TILE, value, other)
            out_buf[g, :, cols] = value.astype(bf)
        rel = g ^ me
        for half in range(2):
            part = out_buf.at[g, half * HALF:(half + 1) * HALF, :]

            @pl.when((rel & 1) == 0)
            def _():
                pltpu.make_async_copy(part, outs[2 * half].at[rel >> 1], out_sem).start()

            @pl.when((rel & 1) == 1)
            def _():
                pltpu.make_async_copy(part, outs[2 * half + 1].at[rel >> 1], out_sem).start()
    pltpu.make_async_copy(out_buf, out_buf, out_sem).wait()


def weight_call(every, groups, mixed, waits, limit=22):
    V = pl.BlockSpec(memory_space=pltpu.VMEM)
    S = pl.BlockSpec(memory_space=pltpu.SMEM)
    A = pl.BlockSpec(memory_space=pl.ANY)
    raws = 1 + mixed
    return pl.pallas_call(
        functools.partial(weight_kernel, groups, mixed, waits),
        in_specs=[S] + [V] * (1 + raws) + [A] * waits,
        out_specs=[A] * 4,
        out_shape=[pltpu.HBM((2, HALF, D), bf)] * 4,
        scratch_shapes=[pltpu.VMEM((raws, D, every), bf), pltpu.VMEM((groups, D, D), bf), pltpu.SemaphoreType.DMA],
        cost_estimate=pl.CostEstimate(flops=2 * every * D * 4 * D, bytes_accessed=every * 5 * D * 2, transcendentals=0),
        compiler_params=pltpu.CompilerParams(vmem_limit_bytes=limit * 2**20),
        name="weight_grad",
    )


MB_ROWS = 1024
MICRO = 2
ROWS = 256
DELTA = 2


def geometry(doc_ids):
    quarter = MB_ROWS // 4
    marks = doc_ids.reshape(-1, MB_ROWS)[:, ::quarter]
    pieces = 1 + jnp.sum((marks[:, 1:] != marks[:, :-1]).astype(jnp.int32), axis=1)
    length = MB_ROWS // pieces
    row = jnp.arange(MB_ROWS, dtype=jnp.int32)
    position = row[None, :] % length[:, None]
    angle = (0.5 * math.pi) * position.astype(f32) / length[:, None].astype(f32)
    angle = angle.reshape(-1, 1)
    starts = jnp.arange(0, MB_ROWS, ROWS, dtype=jnp.int32)
    first = (starts[None, :] % length[:, None]) == 0
    last = ((starts[None, :] + ROWS) % length[:, None]) == 0
    wide = (angle.shape[0], 128)
    return (jnp.broadcast_to(jnp.cos(angle), wide), jnp.broadcast_to(jnp.sin(angle), wide),
            first.reshape(-1).astype(jnp.int32), last.reshape(-1).astype(jnp.int32))


def exchange(block, axis, flip):
    route = [(i, i ^ flip) for i in range(lax.axis_size(axis))]
    return lax.ppermute(block, axis, route)


def reduced(keep, send, wire):
    got = exchange(send, "group", 1)
    away = lax.optimization_barrier((keep[1].astype(f32) + got[1].astype(f32)).astype(wire))
    back = exchange(away, "group", 2)
    own = lax.optimization_barrier((keep[0].astype(f32) + got[0].astype(f32) + back.astype(f32)).astype(wire))
    if lax.axis_size("dp") == 2:
        return away, own, own.astype(f32) + exchange(own, "dp", 1).astype(f32)
    return away, own, lax.psum(own, "dp").astype(f32)


def local(tokens, doc_ids, cotangent, w_qkv, w_out, w_up, w_down,
          first_gain, first_bias, second_gain, second_bias):
    stages = lax.axis_size("pipe")
    groups = lax.axis_size("group")
    stage = lax.axis_index("pipe").astype(jnp.int32)
    me = lax.axis_index("group").astype(jnp.int32)
    n = tokens.shape[0] // ROWS
    ticks = n + DELTA * (stages - 1)
    cos, sin, first, last = geometry(doc_ids)
    meta = jnp.concatenate([stage[None], me[None], first, last])
    resident = far((tokens, cotangent)) + [cos, sin] + far((w_qkv[0], w_out[0], w_up[0], w_down[0]))
    gb = jnp.concatenate([first_gain, first_bias, second_gain, second_bias], axis=0)
    blank = jnp.zeros((ROWS, D), bf)
    arriving = [blank] * DELTA
    resident = resident + [gb]
    state, big = (), ()
    for t in range(ticks):
        made = forward_call(ROWS, n, DELTA, t == 0)(jnp.full((1,), t, jnp.int32), meta, arriving.pop(0), *resident, *state, *big)
        state, big, resident = made[1:2], made[2:16], made[16:]
        route = [(a, a + 1) for a in range(stages - 1) if 0 <= t - a * DELTA < n]
        arriving.append(lax.ppermute(made[0], "pipe", route) if route else made[0])
    block_out, x, att, hb, act, qn, kf, v, sg, n1, gp, n2, rs, sb = big
    arriving = [made[0]] * DELTA
    state, big, resident = (), (), resident[1:]
    for t in range(ticks):
        closing = t == ticks - 1
        made = backward_call(ROWS, n, DELTA, stages, groups, t == 0, closing)(
            jnp.full((1,), t, jnp.int32), meta, arriving.pop(0), *resident[closing:], *state,
            *far((n2, rs, gp, n1, att, v, qn, kf, sg, sb)), *big, *far([act] * closing))
        state, big, resident = made[1:3], made[3:7], made[7:]
        route = [(a, a - 1) for a in range(1, stages) if 0 <= t - (stages - 1 - a) * DELTA < n]
        arriving.append(lax.ppermute(made[0], "pipe", route) if route else made[0])
    df, du, de, input_grad = big
    act = resident[7]
    aways, owns, parts = [], [], []
    for left, rights in ((act, (df,)), (de, (x, att)), (du, (hb,))):
        waits = aways[-2:] + owns[-2:-1]
        made = weight_call(n * ROWS, groups, len(rights) == 2, len(waits))(meta, left, *rights, *waits)
        for half in range(2):
            away, own, part = reduced(made[2 * half], made[2 * half + 1], bf)
            aways.append(away)
            owns.append(own)
            parts.append(part)
    vectors = state[1][:4].reshape(4, groups, D // groups).swapaxes(0, 1).reshape(groups, 1, D)
    ordered = [lax.dynamic_index_in_dim(vectors, me ^ rel, 0, keepdims=False) for rel in range(4)]
    mine = reduced(jnp.stack(ordered[0::2]), jnp.stack(ordered[1::2]), f32)[2].reshape(4, D // groups)
    g_down, g_mixed, g_up = (jnp.concatenate(parts[i:i + 2], axis=0) for i in (0, 2, 4))
    odd = (me & 1) == 1
    swap = lambda a, b: jnp.concatenate([g_mixed[:, a], g_mixed[:, b]], axis=1)
    low, one, two, high = slice(0, 512), slice(512, 576), slice(576, 640), slice(640, 768)
    g_qkv = jnp.where(odd, swap(one, low), swap(low, one))
    g_out = jnp.where(odd, swap(two, high), swap(high, two))
    return (block_out[None], input_grad[None], g_qkv[None], g_out[None], g_up[None], g_down.T[None],
            mine[0:1], mine[1:2], mine[2:3], mine[3:4])


def solution(mesh):
    rows = ("group", "dp")
    whole = P("pipe", None, None)
    vector = P("pipe", None)
    return jax.shard_map(
        local,
        mesh=mesh,
        in_specs=(P(rows, None), P(rows), P(rows, None)) + (whole,) * 4 + (vector,) * 4,
        out_specs=(P("pipe", rows, None), P("pipe", rows, None), P("pipe", None, "group"), P("pipe", None, "group"),
                   P("pipe", None, "group"), P("pipe", "group", None)) + (P("pipe", "group"),) * 4,
        check_vma=False,
    )
```

time: 854 us -> 554 us (0.65)
  local copies, waits for them, and re-layouts: 274 us -> 28.7 us
  Pallas kernels: 358 us -> 293 us
  blocking collectives: 50.3 us -> 0 us
  waiting for transfers between devices: 99 us -> 145 us
  other arithmetic: 18.5 us -> 28.4 us
  starting transfers between devices: 39 us -> 48.8 us
    unnamed x949 -> x43, local copies, waits for them, and re-layouts: 267 us -> 26.1 us
    pallas_call x32 -> x31, Pallas kernels: 358 us -> 293 us  [the longest x14 148 us: local(): backward_call(ROWS, n, DELTA, stages, groups, t == 0, closing)]
    psum x1 -> x0, blocking collectives: 50.3 us -> none  [local(): total = lax.psum(sums[:4], ('group', 'dp'))]
    ppermute x24, waiting for transfers between devices: 32.3 us -> 61.9 us  [local(): arriving.append(lax.ppermute(made[0], 'pipe', route) if route else made[0])]
    ppermute x12 -> x21, waiting for transfers between devices: 66.7 us -> 82.7 us  [exchange(): return lax.ppermute(block, axis, route)]
    convert_element_type x8 -> x12, other arithmetic: 7.61 us -> 18.6 us  [the longest x6 9.47 us: reduced(): (keep[1].astype(f32) + got[1].astype(f32)).astype(wire)]
    ppermute x12 -> x21, starting transfers between devices: 11.5 us -> 18.4 us  [exchange(): return lax.ppermute(block, axis, route)]
  transfers between devices with their start and end apart: 36 -> 45, of which waited for: 8 -> 19; matrix products, arithmetic and copies ran while one was open for 2% -> 5% of each run, Pallas kernels for 35% -> 42%
where the time goes in v2:
time: 554 us; the launch traced here: 546 us
  Pallas kernels  293 us (53%)
  waiting for transfers between devices  145 us (26%)
  starting transfers between devices  48.8 us (9%)
  local copies, waits for them, and re-layouts  28.7 us (5%)
  other arithmetic  28.4 us (5%)
    pallas_call x14, Pallas kernels, local(): backward_call(ROWS, n, DELTA, stages, groups, t == 0, closing)  148 us
    pallas_call x14, Pallas kernels, local(): forward_call(ROWS, n, DELTA, t == 0)  107 us
    ppermute x21, waiting for transfers between devices, exchange(): return lax.ppermute(block, axis, route)  82.7 us
    ppermute x24, waiting for transfers between devices, local(): arriving.append(lax.ppermute(made[0], 'pipe', route) if route else made[0])  61.9 us
    pallas_call x3, Pallas kernels, local(): weight_call(n * ROWS, groups, len(rights) == 2, len(waits))  38.3 us
    ppermute x24, starting transfers between devices, local(): arriving.append(lax.ppermute(made[0], 'pipe', route) if route else made[0])  30.4 us
    unnamed x43, local copies, waits for them, and re-layouts  26.1 us
    ppermute x21, starting transfers between devices, exchange(): return lax.ppermute(block, axis, route)  18.4 us
  transfers between devices with their start and end apart: 45, of which 19 were waited for; matrix products, arithmetic and copies ran while one was open for 5% of the time, Pallas kernels for 42%

profile of v2, /device:TPU:0, one launch (start us, length us, event | category | flops | bytes accessed | tf_op | source)
XLA Modules:
  0.0 546.0 jit_solution(3882409631874466683)
XLA Ops:
  4.2 11.6 %layer_forward.14 = (bf16[256,768]{1,0:T(8,128)(2,1)S(1)}, f32[6,256,256]{2,1,0:T(8,128)S(1)}, bf16[2048,768]{1,0:T(8,128)(2,1)}, bf16[2048,768]{1,0:T(8,128)(2,...) custom-call(s32[1]{0:T(128)} %constant.45.clone.1.refs_0_, ...), custom_call_target="tpu_custom_call", output_to_operand_aliasing={{18}: (5, {}), {19}: (6, {}), {24}: (11, {})} | custom-call | flops 4608000000 | bytes 4194304 | tf_op jit(solution)/shard_map/layer_forward/pallas_call | solution.py:578
  17.3 9.8 %layer_forward.15 = (bf16[256,768]{1,0:T(8,128)(2,1)S(1)}, f32[6,256,256]{2,1,0:T(8,128)S(1)}, bf16[2048,768]{1,0:T(8,128)(2,1)}, bf16[2048,768]{1,0:T(8,128)(2,...) custom-call(s32[1]{0:T(128)} %constant.28.clone.1.refs_0_, ...), custom_call_target="tpu_custom_call", output_to_operand_aliasing={{1}: (12, {}), {2}: (13, {}), {3}: (14, {}), {4}: (15, {}),... | custom-call | flops 4608000000 | bytes 4194304 | tf_op jit(solution)/shard_map/layer_forward/pallas_call | solution.py:578
  28.4 9.3 %layer_forward.16 = (bf16[256,768]{1,0:T(8,128)(2,1)S(1)}, f32[6,256,256]{2,1,0:T(8,128)S(1)}, bf16[2048,768]{1,0:T(8,128)(2,1)}, bf16[2048,768]{1,0:T(8,128)(2,...) custom-call(s32[1]{0:T(128)} %constant.76.clone.1.refs_0_, ...), custom_call_target="tpu_custom_call", output_to_operand_aliasing={{1}: (12, {}), {2}: (13, {}), {3}: (14, {}), {4}: (15, {}),... | custom-call | flops 4608000000 | bytes 4194304 | tf_op jit(solution)/shard_map/layer_forward/pallas_call | solution.py:578
  37.8 2.2 collective-permute-start.3
  40.0 10.0 %layer_forward.17 = (bf16[256,768]{1,0:T(8,128)(2,1)S(1)}, f32[6,256,256]{2,1,0:T(8,128)S(1)}, bf16[2048,768]{1,0:T(8,128)(2,1)}, bf16[2048,768]{1,0:T(8,128)(2,...) custom-call(s32[1]{0:T(128)} %constant.27.clone.1.refs_0_, ...), custom_call_target="tpu_custom_call", output_to_operand_aliasing={{1}: (12, {}), {2}: (13, {}), {3}: (14, {}), {4}: (15, {}),... | custom-call | flops 4608000000 | bytes 4194304 | tf_op jit(solution)/shard_map/layer_forward/pallas_call | solution.py:578
  51.9 9.3 %layer_forward.18 = (bf16[256,768]{1,0:T(8,128)(2,1)S(1)}, f32[6,256,256]{2,1,0:T(8,128)S(1)}, bf16[2048,768]{1,0:T(8,128)(2,1)}, bf16[2048,768]{1,0:T(8,128)(2,...) custom-call(s32[1]{0:T(128)} %constant.77.clone.1.refs_0_, ...), custom_call_target="tpu_custom_call", output_to_operand_aliasing={{1}: (12, {}), {2}: (13, {}), {3}: (14, {}), {4}: (15, {}),... | custom-call | flops 4608000000 | bytes 4194304 | tf_op jit(solution)/shard_map/layer_forward/pallas_call | solution.py:578
  61.2 2.0 collective-permute-start.5
  63.2 9.8 %layer_forward.19 = (bf16[256,768]{1,0:T(8,128)(2,1)S(1)}, f32[6,256,256]{2,1,0:T(8,128)S(1)}, bf16[2048,768]{1,0:T(8,128)(2,1)}, bf16[2048,768]{1,0:T(8,128)(2,...) custom-call(s32[1]{0:T(128)} %constant.26.clone.1.refs_0_, ...), custom_call_target="tpu_custom_call", output_to_operand_aliasing={{1}: (12, {}), {2}: (13, {}), {3}: (14, {}), {4}: (15, {}),... | custom-call | flops 4608000000 | bytes 4194304 | tf_op jit(solution)/shard_map/layer_forward/pallas_call | solution.py:578
  74.9 9.3 %layer_forward.20 = (bf16[256,768]{1,0:T(8,128)(2,1)S(1)}, f32[6,256,256]{2,1,0:T(8,128)S(1)}, bf16[2048,768]{1,0:T(8,128)(2,1)}, bf16[2048,768]{1,0:T(8,128)(2,...) custom-call(s32[1]{0:T(128)} %constant.78.clone.1.refs_0_, ...), custom_call_target="tpu_custom_call", output_to_operand_aliasing={{1}: (12, {}), {2}: (13, {}), {3}: (14, {}), {4}: (15, {}),... | custom-call | flops 4608000000 | bytes 4194304 | tf_op jit(solution)/shard_map/layer_forward/pallas_call | solution.py:578
  86.1 10.0 %layer_forward.21 = (bf16[256,768]{1,0:T(8,128)(2,1)S(1)}, f32[6,256,256]{2,1,0:T(8,128)S(1)}, bf16[2048,768]{1,0:T(8,128)(2,1)}, bf16[2048,768]{1,0:T(8,128)(2,...) custom-call(s32[1]{0:T(128)} %constant.40.clone.1.refs_0_, ...), custom_call_target="tpu_custom_call", output_to_operand_aliasing={{1}: (12, {}), {2}: (13, {}), {3}: (14, {}), {4}: (15, {}),... | custom-call | flops 4608000000 | bytes 4194304 | tf_op jit(solution)/shard_map/layer_forward/pallas_call | solution.py:578
  99.6 6.4 %collective-permute-done.6.refs_2_ = bf16[256,768]{1,0:T(8,128)(2,1)S(1)} collective-permute-done((bf16[256,768]{1,0:T(8,128)(2,1)S(1)}, bf16[256,768]{1,0:T(8,128)(2,1)S(1)}, u32[]{:S(2)}, u32[]{:S(2)}) %collective-permute-start.6) | collective-permute-done | bytes 393248 | tf_op jit(solution)/shard_map/ppermute | solution.py:581
  106.0 6.8 %layer_forward.23 = (bf16[256,768]{1,0:T(8,128)(2,1)S(1)}, f32[6,256,256]{2,1,0:T(8,128)S(1)}, bf16[2048,768]{1,0:T(8,128)(2,1)}, bf16[2048,768]{1,0:T(8,128)(2,...) custom-call(s32[1]{0:T(128)} %constant.39.clone.1.refs_0_, ...), custom_call_target="tpu_custom_call", output_to_operand_aliasing={{1}: (12, {}), {2}: (13, {}), {3}: (14, {}), {4}: (15, {}),... | custom-call | flops 4608000000 | bytes 4194304 | tf_op jit(solution)/shard_map/layer_forward/pallas_call | solution.py:578
  115.1 8.7 %layer_forward.25 = (bf16[256,768]{1,0:T(8,128)(2,1)S(1)}, f32[6,256,256]{2,1,0:T(8,128)S(1)}, bf16[2048,768]{1,0:T(8,128)(2,1)}, bf16[2048,768]{1,0:T(8,128)(2,...) custom-call(s32[1]{0:T(128)} %constant.38.clone.1.refs_0_, ...), custom_call_target="tpu_custom_call", output_to_operand_aliasing={{1}: (12, {}), {2}: (13, {}), {3}: (14, {}), {4}: (15, {}),... | custom-call | flops 4608000000 | bytes 4194304 | tf_op jit(solution)/shard_map/layer_forward/pallas_call | solution.py:578
  126.2 9.4 %layer_forward.27 = (bf16[256,768]{1,0:T(8,128)(2,1)S(1)}, f32[6,256,256]{2,1,0:T(8,128)S(1)}, bf16[2048,768]{1,0:T(8,128)(2,1)}, bf16[2048,768]{1,0:T(8,128)(2,...) custom-call(s32[1]{0:T(128)} %constant.21.clone.1.refs_0_, ...), custom_call_target="tpu_custom_call", output_to_operand_aliasing={{1}: (12, {}), {2}: (13, {}), {3}: (14, {}), {4}: (15, {}),... | custom-call | flops 4608000000 | bytes 4194304 | tf_op jit(solution)/shard_map/layer_forward/pallas_call | solution.py:578
  137.2 11.5 %layer_backward.15 = (bf16[256,768]{1,0:T(8,128)(2,1)S(1)}, f32[6,256,256]{2,1,0:T(8,128)S(1)}, f32[8,768]{1,0:T(8,128)S(1)}, bf16[2048,768]{1,0:T(8,128)(2,1)},...) custom-call(s32[1]{0:T(128)} %constant.28.clone.1.refs_0_, ...), custom_call_target="tpu_custom_call", output_to_operand_aliasing={{7}: (3, {}), {8}: (4, {}), {9}: (5, {}), {10}: (6, {}), {1... | custom-call | flops 5120000000 | bytes 4194304 | tf_op jit(solution)/shard_map/layer_backward/pallas_call | solution.py:587
  151.1 10.5 %layer_backward.17 = (bf16[256,768]{1,0:T(8,128)(2,1)S(1)}, f32[6,256,256]{2,1,0:T(8,128)S(1)}, f32[8,768]{1,0:T(8,128)S(1)}, bf16[2048,768]{1,0:T(8,128)(2,1)},...) custom-call(s32[1]{0:T(128)} %constant.27.clone.1.refs_0_, ...), custom_call_target="tpu_custom_call", output_to_operand_aliasing={{7}: (3, {}), {8}: (4, {}), {9}: (5, {}), {10}: (6, {}), {1... | custom-call | flops 5120000000 | bytes 4194304 | tf_op jit(solution)/shard_map/layer_backward/pallas_call | solution.py:587
  164.7 10.1 %layer_backward.19 = (bf16[256,768]{1,0:T(8,128)(2,1)S(1)}, f32[6,256,256]{2,1,0:T(8,128)S(1)}, f32[8,768]{1,0:T(8,128)S(1)}, bf16[2048,768]{1,0:T(8,128)(2,1)},...) custom-call(s32[1]{0:T(128)} %constant.26.clone.1.refs_0_, ...), custom_call_target="tpu_custom_call", output_to_operand_aliasing={{7}: (3, {}), {8}: (4, {}), {9}: (5, {}), {10}: (6, {}), {1... | custom-call | flops 5120000000 | bytes 4194304 | tf_op jit(solution)/shard_map/layer_backward/pallas_call | solution.py:587
  176.0 51.7 %collective-permute-done.17.refs_2_ = bf16[256,768]{1,0:T(8,128)(2,1)S(1)} collective-permute-done((bf16[256,768]{1,0:T(8,128)(2,1)S(1)}, bf16[256,768]{1,0:T(8,128)(2,1)S(1)}, u32[]{:S(2)}, u32[]{:S(2)}) %collective-permute-start.17) | collective-permute-done | bytes 393248 | tf_op jit(solution)/shard_map/ppermute | solution.py:592
  227.7 13.3 %layer_backward.20 = (bf16[256,768]{1,0:T(8,128)(2,1)S(1)}, f32[6,256,256]{2,1,0:T(8,128)S(1)}, f32[8,768]{1,0:T(8,128)S(1)}, bf16[2048,768]{1,0:T(8,128)(2,1)},...) custom-call(s32[1]{0:T(128)} %constant.78.clone.1.refs_0_, ...), custom_call_target="tpu_custom_call", output_to_operand_aliasing={{7}: (3, {}), {8}: (4, {}), {9}: (5, {}), {10}: (6, {}), {1... | custom-call | flops 5120000000 | bytes 4194304 | tf_op jit(solution)/shard_map/layer_backward/pallas_call | solution.py:587
  243.4 13.6 %layer_backward.21 = (bf16[256,768]{1,0:T(8,128)(2,1)S(1)}, f32[6,256,256]{2,1,0:T(8,128)S(1)}, f32[8,768]{1,0:T(8,128)S(1)}, bf16[2048,768]{1,0:T(8,128)(2,1)},...) custom-call(s32[1]{0:T(128)} %constant.40.clone.1.refs_0_, ...), custom_call_target="tpu_custom_call", output_to_operand_aliasing={{7}: (3, {}), {8}: (4, {}), {9}: (5, {}), {10}: (6, {}), {1... | custom-call | flops 5120000000 | bytes 4194304 | tf_op jit(solution)/shard_map/layer_backward/pallas_call | solution.py:587
  258.7 13.3 %layer_backward.22 = (bf16[256,768]{1,0:T(8,128)(2,1)S(1)}, f32[6,256,256]{2,1,0:T(8,128)S(1)}, f32[8,768]{1,0:T(8,128)S(1)}, bf16[2048,768]{1,0:T(8,128)(2,1)},...) custom-call(s32[1]{0:T(128)} %constant.79.clone.1.refs_0_, ...), custom_call_target="tpu_custom_call", output_to_operand_aliasing={{7}: (3, {}), {8}: (4, {}), {9}: (5, {}), {10}: (6, {}), {1... | custom-call | flops 5120000000 | bytes 4194304 | tf_op jit(solution)/shard_map/layer_backward/pallas_call | solution.py:587
  274.3 13.5 %layer_backward.23 = (bf16[256,768]{1,0:T(8,128)(2,1)S(1)}, f32[6,256,256]{2,1,0:T(8,128)S(1)}, f32[8,768]{1,0:T(8,128)S(1)}, bf16[2048,768]{1,0:T(8,128)(2,1)},...) custom-call(s32[1]{0:T(128)} %constant.39.clone.1.refs_0_, ...), custom_call_target="tpu_custom_call", output_to_operand_aliasing={{7}: (3, {}), {8}: (4, {}), {9}: (5, {}), {10}: (6, {}), {1... | custom-call | flops 5120000000 | bytes 4194304 | tf_op jit(solution)/shard_map/layer_backward/pallas_call | solution.py:587
  289.6 13.3 %layer_backward.24 = (bf16[256,768]{1,0:T(8,128)(2,1)S(1)}, f32[6,256,256]{2,1,0:T(8,128)S(1)}, f32[8,768]{1,0:T(8,128)S(1)}, bf16[2048,768]{1,0:T(8,128)(2,1)},...) custom-call(s32[1]{0:T(128)} %constant.80.clone.1.refs_0_, ...), custom_call_target="tpu_custom_call", output_to_operand_aliasing={{7}: (3, {}), {8}: (4, {}), {9}: (5, {}), {10}: (6, {}), {1... | custom-call | flops 5120000000 | bytes 4194304 | tf_op jit(solution)/shard_map/layer_backward/pallas_call | solution.py:587
  305.1 13.6 %layer_backward.25 = (bf16[256,768]{1,0:T(8,128)(2,1)S(1)}, f32[6,256,256]{2,1,0:T(8,128)S(1)}, f32[8,768]{1,0:T(8,128)S(1)}, bf16[2048,768]{1,0:T(8,128)(2,1)},...) custom-call(s32[1]{0:T(128)} %constant.38.clone.1.refs_0_, ...), custom_call_target="tpu_custom_call", output_to_operand_aliasing={{7}: (3, {}), {8}: (4, {}), {9}: (5, {}), {10}: (6, {}), {1... | custom-call | flops 5120000000 | bytes 4194304 | tf_op jit(solution)/shard_map/layer_backward/pallas_call | solution.py:587
  320.0 14.1 %layer_backward.26 = (bf16[256,768]{1,0:T(8,128)(2,1)}, f32[6,256,256]{2,1,0:T(8,128)S(1)}, f32[8,768]{1,0:T(8,128)S(1)}, bf16[2048,768]{1,0:T(8,128)(2,1)}, bf1...) custom-call(s32[1]{0:T(128)} %constant.81.clone.1.refs_0_, ...), custom_call_target="tpu_custom_call", output_to_operand_aliasing={{7}: (3, {}), {8}: (4, {}), {9}: (5, {}), {10}: (6, {}), {1... | custom-call | flops 5120000000 | bytes 4194304 | tf_op jit(solution)/shard_map/layer_backward/pallas_call | solution.py:587
  336.1 2.0 copy-done.1
  338.1 18.0 %layer_backward.27 = (bf16[256,768]{1,0:T(8,128)(2,1)}, f32[6,256,256]{2,1,0:T(8,128)S(1)}, f32[8,768]{1,0:T(8,128)S(1)}, bf16[2048,768]{1,0:T(8,128)(2,1)}, bf1...) custom-call(s32[1]{0:T(128)} %constant.21.clone.1.refs_0_, ...), custom_call_target="tpu_custom_call", output_to_operand_aliasing={{7}: (3, {}), {8}: (4, {}), {9}: (5, {}), {10}: (6, {}), {1... | custom-call | flops 5120000000 | bytes 4194304 | tf_op jit(solution)/shard_map/layer_backward/pallas_call | solution.py:587
  356.1 4.6 copy-done.7
  360.7 2.0 copy-done.4
  362.8 4.7 copy-done.8
  367.5 11.6 %weight_grad.3 = (bf16[2,384,768]{2,1,0:T(8,128)(2,1)}, bf16[2,384,768]{2,1,0:T(8,128)(2,1)}, bf16[2,384,768]{2,1,0:T(8,128)(2,1)}, bf16[2,384,768]{2,1,0:T(8,128)(2,1)}) custom-call(s32[18]{0:T(128)S(1)} %pad_add_fusion.refs_1_.meta_ref, bf16[12,2048,256]{2,1,0:T(8,128)(2,1)S(1)} %copy-done.8, bf16[2048,768]{1,0:T(8,128)(2,1)S(1)} %copy-done.4), custom_call_target="tpu_custom_call" | custom-call | flops 9663676416 | bytes 15728640 | tf_op jit(solution)/shard_map/weight_grad/pallas_call | solution.py:598
  379.7 2.5 collective-permute-done.24
  386.8 12.1 %collective-permute-done.26 = bf16[384,768]{1,0:T(8,128)(2,1)S(1)} collective-permute-done((bf16[384,768]{1,0:T(8,128)(2,1)S(1)}, bf16[384,768]{1,0:T(8,128)(2,1)S(1)}, u32[]{:S(2)}, u32[]{:S(2)}) %collective-permute-start.26) | collective-permute-done | bytes 589856 | tf_op jit(solution)/shard_map/ppermute | solution.py:548
  400.3 15.0 %weight_grad.4 = (bf16[2,384,768]{2,1,0:T(8,128)(2,1)}, bf16[2,384,768]{2,1,0:T(8,128)(2,1)}, bf16[2,384,768]{2,1,0:T(8,128)(2,1)}, bf16[2,384,768]{2,1,0:T(8,128)(2,1)}) custom-call(s32[18]{0:T(128)S(1)} %pad_add_fusion.refs_1_.meta_ref, bf16[12,2048,256]{2,1,0:T(8,128)(2,1)S(1)} %bitcast.106, bf16[2048,768]{1,0:T(8,128)(2,1)S(1)} %copy-done.5, ...), custom_call_target="tpu_custom_call" | custom-call | flops 9663676416 | bytes 15728640 | tf_op jit(solution)/shard_map/weight_grad/pallas_call | solution.py:598
  430.3 5.8 %collective-permute-done.40 = bf16[384,768]{1,0:T(8,128)(2,1)S(1)} collective-permute-done((bf16[384,768]{1,0:T(8,128)(2,1)S(1)}, bf16[384,768]{1,0:T(8,128)(2,1)S(1)}, u32[]{:S(2)}, u32[]{:S(2)}) %collective-permute-start.40) | collective-permute-done | bytes 589856 | tf_op jit(solution)/shard_map/ppermute | solution.py:548
  441.3 7.5 %collective-permute-done.28 = bf16[384,768]{1,0:T(8,128)(2,1)S(1)} collective-permute-done((bf16[384,768]{1,0:T(8,128)(2,1)S(1)}, bf16[384,768]{1,0:T(8,128)(2,1)S(1)}, u32[]{:S(2)}, u32[]{:S(2)}) %collective-permute-start.28) | collective-permute-done | bytes 589856 | tf_op jit(solution)/shard_map/ppermute | solution.py:548
  450.1 4.6 copy-done.3
  454.7 11.6 %weight_grad.5 = (bf16[2,384,768]{2,1,0:T(8,128)(2,1)}, bf16[2,384,768]{2,1,0:T(8,128)(2,1)}, bf16[2,384,768]{2,1,0:T(8,128)(2,1)}, bf16[2,384,768]{2,1,0:T(8,128)(2,1)}) custom-call(s32[18]{0:T(128)S(1)} %pad_add_fusion.refs_1_.meta_ref, bf16[12,2048,256]{2,1,0:T(8,128)(2,1)S(1)} %copy-done.3, bf16[2048,768]{1,0:T(8,128)(2,1)S(1)} %copy-done.6, ...), custom_call_target="tpu_custom_call" | custom-call | flops 9663676416 | bytes 15728640 | tf_op jit(solution)/shard_map/weight_grad/pallas_call | solution.py:598
  466.4 2.1 fusion.7
  471.1 2.2 copy.535
  473.3 11.7 %collective-permute-done.32 = bf16[384,768]{1,0:T(8,128)(2,1)} collective-permute-done((bf16[384,768]{1,0:T(8,128)(2,1)}, bf16[384,768]{1,0:T(8,128)(2,1)}, u32[]{:S(2)}, u32[]{:S(2)}) %collective-permute-start.32) | collective-permute-done | bytes 589856 | tf_op jit(solution)/shard_map/ppermute | solution.py:548
  486.3 10.8 %collective-permute-done.29 = bf16[384,768]{1,0:T(8,128)(2,1)S(1)} collective-permute-done((bf16[384,768]{1,0:T(8,128)(2,1)S(1)}, bf16[384,768]{1,0:T(8,128)(2,1)S(1)}, u32[]{:S(2)}, u32[]{:S(2)}) %collective-permute-start.29) | collective-permute-done | bytes 589856 | tf_op jit(solution)/shard_map/ppermute | solution.py:548
  497.2 2.0 fusion.18
  499.8 2.0 fusion.19
  504.8 11.0 %collective-permute-done.34 = bf16[384,768]{1,0:T(8,128)(2,1)} collective-permute-done((bf16[384,768]{1,0:T(8,128)(2,1)}, bf16[384,768]{1,0:T(8,128)(2,1)}, u32[]{:S(2)}, u32[]{:S(2)}) %collective-permute-start.34) | collective-permute-done | bytes 589856 | tf_op jit(solution)/shard_map/ppermute | solution.py:548
  518.4 8.8 %collective-permute-done.37 = bf16[384,768]{1,0:T(8,128)(2,1)} collective-permute-done((bf16[384,768]{1,0:T(8,128)(2,1)}, bf16[384,768]{1,0:T(8,128)(2,1)}, u32[]{:S(2)}, u32[]{:S(2)}) %collective-permute-start.37) | collective-permute-done | bytes 589856 | tf_op jit(solution)/shard_map/ppermute | solution.py:548
  531.7 2.8 copy.533
  535.7 7.1 %collective-permute-done.38 = bf16[384,768]{1,0:T(8,128)(2,1)} collective-permute-done((bf16[384,768]{1,0:T(8,128)(2,1)S(1)}, bf16[384,768]{1,0:T(8,128)(2,1)}, u32[]{:S(2)}, u32[]{:S(2)}) %collective-permute-start.38) | collective-permute-done | bytes 589856 | tf_op jit(solution)/shard_map/ppermute | solution.py:548
  (172 shorter events, 88.2 us)
Async XLA Ops:
  15.8 12.6 %collective-permute-start.1 = (bf16[256,768]{1,0:T(8,128)(2,1)S(1)}, bf16[256,768]{1,0:T(8,128)(2,1)S(1)}, u32[]{:S(2)}, u32[]{:S(2)}) collective-permute-start(bf16[256,768]{1,0:T(8,128)(2,1)S(1)} %get-tuple-element.594), channel_id=1, source_target_pairs={{0,8},{1,9},{2,10},{3,11},{4,12},{5,13},{6,14},{7,15}} | collective-permute-start | bytes 1179656 | tf_op jit(solution)/shard_map/ppermute | solution.py:581
  27.1 12.9 %collective-permute-start = (bf16[256,768]{1,0:T(8,128)(2,1)S(1)}, bf16[256,768]{1,0:T(8,128)(2,1)S(1)}, u32[]{:S(2)}, u32[]{:S(2)}) collective-permute-start(bf16[256,768]{1,0:T(8,128)(2,1)S(1)} %get-tuple-element.593), channel_id=1, source_target_pairs={{0,8},{1,9},{2,10},{3,11},{4,12},{5,13},{6,14},{7,15}} | collective-permute-start | bytes 1179656 | tf_op jit(solution)/shard_map/ppermute | solution.py:581
  37.8 14.1 %collective-permute-start.3 = (bf16[256,768]{1,0:T(8,128)(2,1)S(1)}, bf16[256,768]{1,0:T(8,128)(2,1)S(1)}, u32[]{:S(2)}, u32[]{:S(2)}) collective-permute-start(bf16[256,768]{1,0:T(8,128)(2,1)S(1)} %get-tuple-element.644), channel_id=1, source_target_pairs={{0,8},{8,16},{1,9},{9,17},{2,10},{10,18},{3,11},{11,19},{4,12},{12... | collective-permute-start | bytes 1179656 | tf_op jit(solution)/shard_map/ppermute | solution.py:581
  50.0 13.2 %collective-permute-start.2 = (bf16[256,768]{1,0:T(8,128)(2,1)S(1)}, bf16[256,768]{1,0:T(8,128)(2,1)S(1)}, u32[]{:S(2)}, u32[]{:S(2)}) collective-permute-start(bf16[256,768]{1,0:T(8,128)(2,1)S(1)} %get-tuple-element.643), channel_id=1, source_target_pairs={{0,8},{8,16},{1,9},{9,17},{2,10},{10,18},{3,11},{11,19},{4,12},{12... | collective-permute-start | bytes 1179656 | tf_op jit(solution)/shard_map/ppermute | solution.py:581
  61.2 13.7 %collective-permute-start.5 = (bf16[256,768]{1,0:T(8,128)(2,1)S(1)}, bf16[256,768]{1,0:T(8,128)(2,1)S(1)}, u32[]{:S(2)}, u32[]{:S(2)}) collective-permute-start(bf16[256,768]{1,0:T(8,128)(2,1)S(1)} %get-tuple-element.694), channel_id=1, source_target_pairs={{0,8},{8,16},{16,24},{1,9},{9,17},{17,25},{2,10},{10,18},{18,26},{... | collective-permute-start | bytes 1179656 | tf_op jit(solution)/shard_map/ppermute | solution.py:581
  73.0 13.1 %collective-permute-start.4 = (bf16[256,768]{1,0:T(8,128)(2,1)S(1)}, bf16[256,768]{1,0:T(8,128)(2,1)S(1)}, u32[]{:S(2)}, u32[]{:S(2)}) collective-permute-start(bf16[256,768]{1,0:T(8,128)(2,1)S(1)} %get-tuple-element.693), channel_id=1, source_target_pairs={{0,8},{8,16},{16,24},{1,9},{9,17},{17,25},{2,10},{10,18},{18,26},{... | collective-permute-start | bytes 1179656 | tf_op jit(solution)/shard_map/ppermute | solution.py:581
  84.3 13.7 %collective-permute-start.7 = (bf16[256,768]{1,0:T(8,128)(2,1)S(1)}, bf16[256,768]{1,0:T(8,128)(2,1)S(1)}, u32[]{:S(2)}, u32[]{:S(2)}) collective-permute-start(bf16[256,768]{1,0:T(8,128)(2,1)S(1)} %get-tuple-element.744), channel_id=1, source_target_pairs={{0,8},{8,16},{16,24},{1,9},{9,17},{17,25},{2,10},{10,18},{18,26},{... | collective-permute-start | bytes 1179656 | tf_op jit(solution)/shard_map/ppermute | solution.py:581
  96.1 9.9 %collective-permute-start.6 = (bf16[256,768]{1,0:T(8,128)(2,1)S(1)}, bf16[256,768]{1,0:T(8,128)(2,1)S(1)}, u32[]{:S(2)}, u32[]{:S(2)}) collective-permute-start(bf16[256,768]{1,0:T(8,128)(2,1)S(1)} %get-tuple-element.743), channel_id=1, source_target_pairs={{0,8},{8,16},{16,24},{1,9},{9,17},{17,25},{2,10},{10,18},{18,26},{... | collective-permute-start | bytes 1179656 | tf_op jit(solution)/shard_map/ppermute | solution.py:581
  98.9 14.6 %collective-permute-start.9 = (bf16[256,768]{1,0:T(8,128)(2,1)S(1)}, bf16[256,768]{1,0:T(8,128)(2,1)S(1)}, u32[]{:S(2)}, u32[]{:S(2)}) collective-permute-start(bf16[256,768]{1,0:T(8,128)(2,1)S(1)} %get-tuple-element.794), channel_id=1, source_target_pairs={{8,16},{16,24},{9,17},{17,25},{10,18},{18,26},{11,19},{19,27},{12,... | collective-permute-start | bytes 1179656 | tf_op jit(solution)/shard_map/ppermute | solution.py:581
  112.8 2.3 collective-permute-start.8
  114.4 10.1 %collective-permute-start.11 = (bf16[256,768]{1,0:T(8,128)(2,1)S(1)}, bf16[256,768]{1,0:T(8,128)(2,1)S(1)}, u32[]{:S(2)}, u32[]{:S(2)}) collective-permute-start(bf16[256,768]{1,0:T(8,128)(2,1)S(1)} %get-tuple-element.844), channel_id=1, source_target_pairs={{16,24},{17,25},{18,26},{19,27},{20,28},{21,29},{22,30},{23,31}} | collective-permute-start | bytes 1179656 | tf_op jit(solution)/shard_map/ppermute | solution.py:581
  123.8 2.3 collective-permute-start.10
  136.5 12.9 %collective-permute-start.13 = (bf16[256,768]{1,0:T(8,128)(2,1)S(1)}, bf16[256,768]{1,0:T(8,128)(2,1)S(1)}, u32[]{:S(2)}, u32[]{:S(2)}) collective-permute-start(bf16[256,768]{1,0:T(8,128)(2,1)S(1)} %get-tuple-element.928), channel_id=1, source_target_pairs={{24,16},{25,17},{26,18},{27,19},{28,20},{29,21},{30,22},{31,23}} | collective-permute-start | bytes 1179656 | tf_op jit(solution)/shard_map/ppermute | solution.py:592
  148.7 2.4 collective-permute-start.12
  150.4 11.9 %collective-permute-start.15 = (bf16[256,768]{1,0:T(8,128)(2,1)S(1)}, bf16[256,768]{1,0:T(8,128)(2,1)S(1)}, u32[]{:S(2)}, u32[]{:S(2)}) collective-permute-start(bf16[256,768]{1,0:T(8,128)(2,1)S(1)} %get-tuple-element.958), channel_id=1, source_target_pairs={{16,8},{24,16},{17,9},{25,17},{18,10},{26,18},{19,11},{27,19},{20,... | collective-permute-start | bytes 1179656 | tf_op jit(solution)/shard_map/ppermute | solution.py:592
  161.6 3.0 collective-permute-start.14
  163.3 64.3 %collective-permute-start.17 = (bf16[256,768]{1,0:T(8,128)(2,1)S(1)}, bf16[256,768]{1,0:T(8,128)(2,1)S(1)}, u32[]{:S(2)}, u32[]{:S(2)}) collective-permute-start(bf16[256,768]{1,0:T(8,128)(2,1)S(1)} %get-tuple-element.988), channel_id=1, source_target_pairs={{8,0},{16,8},{24,16},{9,1},{17,9},{25,17},{10,2},{18,10},{26,18},{... | collective-permute-start | bytes 1179656 | tf_op jit(solution)/shard_map/ppermute | solution.py:592
  174.7 68.7 %collective-permute-start.16 = (bf16[256,768]{1,0:T(8,128)(2,1)S(1)}, bf16[256,768]{1,0:T(8,128)(2,1)S(1)}, u32[]{:S(2)}, u32[]{:S(2)}) collective-permute-start(bf16[256,768]{1,0:T(8,128)(2,1)S(1)} %get-tuple-element.987), channel_id=1, source_target_pairs={{8,0},{16,8},{24,16},{9,1},{17,9},{25,17},{10,2},{18,10},{26,18},{... | collective-permute-start | bytes 1179656 | tf_op jit(solution)/shard_map/ppermute | solution.py:592
  241.0 17.7 %collective-permute-start.19 = (bf16[256,768]{1,0:T(8,128)(2,1)S(1)}, bf16[256,768]{1,0:T(8,128)(2,1)S(1)}, u32[]{:S(2)}, u32[]{:S(2)}) collective-permute-start(bf16[256,768]{1,0:T(8,128)(2,1)S(1)} %get-tuple-element.1018), channel_id=1, source_target_pairs={{8,0},{16,8},{24,16},{9,1},{17,9},{25,17},{10,2},{18,10},{26,18},{... | collective-permute-start | bytes 1179656 | tf_op jit(solution)/shard_map/ppermute | solution.py:592
  257.0 17.3 %collective-permute-start.18 = (bf16[256,768]{1,0:T(8,128)(2,1)S(1)}, bf16[256,768]{1,0:T(8,128)(2,1)S(1)}, u32[]{:S(2)}, u32[]{:S(2)}) collective-permute-start(bf16[256,768]{1,0:T(8,128)(2,1)S(1)} %get-tuple-element.1017), channel_id=1, source_target_pairs={{8,0},{16,8},{24,16},{9,1},{17,9},{25,17},{10,2},{18,10},{26,18},{... | collective-permute-start | bytes 1179656 | tf_op jit(solution)/shard_map/ppermute | solution.py:592
  272.1 17.5 %collective-permute-start.21 = (bf16[256,768]{1,0:T(8,128)(2,1)S(1)}, bf16[256,768]{1,0:T(8,128)(2,1)S(1)}, u32[]{:S(2)}, u32[]{:S(2)}) collective-permute-start(bf16[256,768]{1,0:T(8,128)(2,1)S(1)} %get-tuple-element.1048), channel_id=1, source_target_pairs={{8,0},{16,8},{9,1},{17,9},{10,2},{18,10},{11,3},{19,11},{12,4},{20... | collective-permute-start | bytes 1179656 | tf_op jit(solution)/shard_map/ppermute | solution.py:592
  287.8 17.3 %collective-permute-start.20 = (bf16[256,768]{1,0:T(8,128)(2,1)S(1)}, bf16[256,768]{1,0:T(8,128)(2,1)S(1)}, u32[]{:S(2)}, u32[]{:S(2)}) collective-permute-start(bf16[256,768]{1,0:T(8,128)(2,1)S(1)} %get-tuple-element.1047), channel_id=1, source_target_pairs={{8,0},{16,8},{9,1},{17,9},{10,2},{18,10},{11,3},{19,11},{12,4},{20... | collective-permute-start | bytes 1179656 | tf_op jit(solution)/shard_map/ppermute | solution.py:592
  303.0 17.0 %collective-permute-start.23 = (bf16[256,768]{1,0:T(8,128)(2,1)S(1)}, bf16[256,768]{1,0:T(8,128)(2,1)S(1)}, u32[]{:S(2)}, u32[]{:S(2)}) collective-permute-start(bf16[256,768]{1,0:T(8,128)(2,1)S(1)} %get-tuple-element.1078), channel_id=1, source_target_pairs={{8,0},{9,1},{10,2},{11,3},{12,4},{13,5},{14,6},{15,7}} | collective-permute-start | bytes 1179656 | tf_op jit(solution)/shard_map/ppermute | solution.py:592
  318.7 17.4 %collective-permute-start.22 = (bf16[256,768]{1,0:T(8,128)(2,1)S(1)}, bf16[256,768]{1,0:T(8,128)(2,1)S(1)}, u32[]{:S(2)}, u32[]{:S(2)}) collective-permute-start(bf16[256,768]{1,0:T(8,128)(2,1)S(1)} %get-tuple-element.1077), channel_id=1, source_target_pairs={{8,0},{9,1},{10,2},{11,3},{12,4},{13,5},{14,6},{15,7}} | collective-permute-start | bytes 1179656 | tf_op jit(solution)/shard_map/ppermute | solution.py:592
  360.7 39.5 %slice-start = ((s8[12582912]{0:T(1024)(128)(4,1)}), s8[4194304]{0:T(1024)(128)(4,1)S(1)}, s32[]{:S(2)}) async-start(s8[12582912]{0:T(1024)(128)(4,1)} %bitcast.105), calls=%async_computation | async-start | bytes 8388608
  367.5 32.8 %slice-start.2 = ((s8[12582912]{0:T(1024)(128)(4,1)}), s8[4194304]{0:T(1024)(128)(4,1)S(1)}, s32[]{:S(2)}) async-start(s8[12582912]{0:T(1024)(128)(4,1)} %bitcast.105), calls=%async_computation.2 | async-start | bytes 8388608
  367.5 32.8 %copy-start.5 = (bf16[2048,768]{1,0:T(8,128)(2,1)S(1)}, bf16[2048,768]{1,0:T(8,128)(2,1)}, u32[]{:S(2)}) copy-start(bf16[2048,768]{1,0:T(8,128)(2,1)} %get-tuple-element.1109.refs_0_) | copy-start | bytes 9437188
  379.2 3.1 collective-permute-start.24
  379.2 5.9 %collective-permute-start.25 = (bf16[2,384,768]{2,1,0:T(8,128)(2,1)}, bf16[2,384,768]{2,1,0:T(8,128)(2,1)S(1)}, u32[]{:S(2)}, u32[]{:S(2)}) collective-permute-start(bf16[2,384,768]{2,1,0:T(8,128)(2,1)} %get-tuple-element.1115), channel_id=1, source_target_pairs={{0,2},{2,0},{4,6},{6,4},{1,3},{3,1},{5,7},{7,5},{8,10},{10,8},{12,... | collective-permute-start | bytes 3538952 | tf_op jit(solution)/shard_map/ppermute | solution.py:548
  383.5 15.4 %collective-permute-start.26 = (bf16[384,768]{1,0:T(8,128)(2,1)S(1)}, bf16[384,768]{1,0:T(8,128)(2,1)S(1)}, u32[]{:S(2)}, u32[]{:S(2)}) collective-permute-start(bf16[384,768]{1,0:T(8,128)(2,1)S(1)} %fusion.14.refs_2_), channel_id=1, source_target_pairs={{0,4},{2,6},{4,0},{6,2},{1,5},{3,7},{5,1},{7,3},{8,12},{10,14},{12... | collective-permute-start | bytes 1769480 | tf_op jit(solution)/shard_map/ppermute | solution.py:548
  415.3 10.3 %collective-permute-start.27 = (bf16[2,384,768]{2,1,0:T(8,128)(2,1)}, bf16[2,384,768]{2,1,0:T(8,128)(2,1)}, u32[]{:S(2)}, u32[]{:S(2)}) collective-permute-start(bf16[2,384,768]{2,1,0:T(8,128)(2,1)} %get-tuple-element.1117), channel_id=1, source_target_pairs={{0,2},{2,0},{4,6},{6,4},{1,3},{3,1},{5,7},{7,5},{8,10},{10,8},{12,... | collective-permute-start | bytes 3538952 | tf_op jit(solution)/shard_map/ppermute | solution.py:548
  415.6 2.6 collective-permute-start.42
  416.2 22.6 %collective-permute-start.30 = (bf16[2,384,768]{2,1,0:T(8,128)(2,1)}, bf16[2,384,768]{2,1,0:T(8,128)(2,1)}, u32[]{:S(2)}, u32[]{:S(2)}) collective-permute-start(bf16[2,384,768]{2,1,0:T(8,128)(2,1)} %get-tuple-element.1119), channel_id=1, source_target_pairs={{0,2},{2,0},{4,6},{6,4},{1,3},{3,1},{5,7},{7,5},{8,10},{10,8},{12,... | collective-permute-start | bytes 3538952 | tf_op jit(solution)/shard_map/ppermute | solution.py:548
  418.3 3.7 collective-permute-start.43
  419.9 16.2 %collective-permute-start.40 = (bf16[384,768]{1,0:T(8,128)(2,1)S(1)}, bf16[384,768]{1,0:T(8,128)(2,1)S(1)}, u32[]{:S(2)}, u32[]{:S(2)}) collective-permute-start(bf16[384,768]{1,0:T(8,128)(2,1)S(1)} %fusion.15.refs_3_), channel_id=1, source_target_pairs={{0,4},{2,6},{4,0},{6,2},{1,5},{3,7},{5,1},{7,3},{8,12},{10,14},{12... | collective-permute-start | bytes 1769480 | tf_op jit(solution)/shard_map/ppermute | solution.py:548
  421.9 3.7 collective-permute-start.44
  427.0 21.8 %collective-permute-start.28 = (bf16[384,768]{1,0:T(8,128)(2,1)S(1)}, bf16[384,768]{1,0:T(8,128)(2,1)S(1)}, u32[]{:S(2)}, u32[]{:S(2)}) collective-permute-start(bf16[384,768]{1,0:T(8,128)(2,1)S(1)} %fusion.16.refs_1_), channel_id=1, source_target_pairs={{0,4},{2,6},{4,0},{6,2},{1,5},{3,7},{5,1},{7,3},{8,12},{10,14},{12... | collective-permute-start | bytes 1769480 | tf_op jit(solution)/shard_map/ppermute | solution.py:548
  429.3 40.2 %collective-permute-start.39 = (bf16[384,768]{1,0:T(8,128)(2,1)S(1)}, bf16[384,768]{1,0:T(8,128)(2,1)S(1)}, u32[]{:S(2)}, u32[]{:S(2)}) collective-permute-start(bf16[384,768]{1,0:T(8,128)(2,1)S(1)} %fusion.9.refs_4_), channel_id=1, source_target_pairs={{0,1},{1,0},{2,3},{3,2},{4,5},{5,4},{6,7},{7,6},{8,9},{9,8},{10,11... | collective-permute-start | bytes 1769480 | tf_op jit(solution)/shard_map/ppermute | solution.py:548
  437.7 33.1 %collective-permute-start.41 = (bf16[384,768]{1,0:T(8,128)(2,1)S(1)}, bf16[384,768]{1,0:T(8,128)(2,1)S(1)}, u32[]{:S(2)}, u32[]{:S(2)}) collective-permute-start(bf16[384,768]{1,0:T(8,128)(2,1)S(1)} %fusion.4), channel_id=1, source_target_pairs={{0,1},{1,0},{2,3},{3,2},{4,5},{5,4},{6,7},{7,6},{8,9},{9,8},{10,11... | collective-permute-start | bytes 1769480 | tf_op jit(solution)/shard_map/ppermute | solution.py:548
  440.0 26.4 %collective-permute-start.31 = (bf16[384,768]{1,0:T(8,128)(2,1)S(1)}, bf16[384,768]{1,0:T(8,128)(2,1)S(1)}, u32[]{:S(2)}, u32[]{:S(2)}) collective-permute-start(bf16[384,768]{1,0:T(8,128)(2,1)S(1)} %fusion.17.refs_2_), channel_id=1, source_target_pairs={{0,4},{2,6},{4,0},{6,2},{1,5},{3,7},{5,1},{7,3},{8,12},{10,14},{12... | collective-permute-start | bytes 1769480 | tf_op jit(solution)/shard_map/ppermute | solution.py:548
  466.3 30.9 %collective-permute-start.33 = (bf16[2,384,768]{2,1,0:T(8,128)(2,1)}, bf16[2,384,768]{2,1,0:T(8,128)(2,1)}, u32[]{:S(2)}, u32[]{:S(2)}) collective-permute-start(bf16[2,384,768]{2,1,0:T(8,128)(2,1)} %get-tuple-element.1123), channel_id=1, source_target_pairs={{0,2},{2,0},{4,6},{6,4},{1,3},{3,1},{5,7},{7,5},{8,10},{10,8},{12,... | collective-permute-start | bytes 3538952 | tf_op jit(solution)/shard_map/ppermute | solution.py:548
  468.5 16.4 %collective-permute-start.32 = (bf16[384,768]{1,0:T(8,128)(2,1)}, bf16[384,768]{1,0:T(8,128)(2,1)}, u32[]{:S(2)}, u32[]{:S(2)}) collective-permute-start(bf16[384,768]{1,0:T(8,128)(2,1)} %fusion.7), channel_id=1, source_target_pairs={{0,1},{1,0},{2,3},{3,2},{4,5},{5,4},{6,7},{7,6},{8,9},{9,8},{10,11... | collective-permute-start | bytes 1769480 | tf_op jit(solution)/shard_map/ppermute | solution.py:548
  469.7 27.4 %collective-permute-start.29 = (bf16[384,768]{1,0:T(8,128)(2,1)S(1)}, bf16[384,768]{1,0:T(8,128)(2,1)S(1)}, u32[]{:S(2)}, u32[]{:S(2)}) collective-permute-start(bf16[384,768]{1,0:T(8,128)(2,1)S(1)} %fusion.8.refs_3_), channel_id=1, source_target_pairs={{0,1},{1,0},{2,3},{3,2},{4,5},{5,4},{6,7},{7,6},{8,9},{9,8},{10,11... | collective-permute-start | bytes 1769480 | tf_op jit(solution)/shard_map/ppermute | solution.py:548
  470.8 29.0 %collective-permute-start.36 = (bf16[2,384,768]{2,1,0:T(8,128)(2,1)}, bf16[2,384,768]{2,1,0:T(8,128)(2,1)}, u32[]{:S(2)}, u32[]{:S(2)}) collective-permute-start(bf16[2,384,768]{2,1,0:T(8,128)(2,1)} %get-tuple-element.1125), channel_id=1, source_target_pairs={{0,2},{2,0},{4,6},{6,4},{1,3},{3,1},{5,7},{7,5},{8,10},{10,8},{12,... | collective-permute-start | bytes 3538952 | tf_op jit(solution)/shard_map/ppermute | solution.py:548
  499.3 16.5 %collective-permute-start.34 = (bf16[384,768]{1,0:T(8,128)(2,1)}, bf16[384,768]{1,0:T(8,128)(2,1)}, u32[]{:S(2)}, u32[]{:S(2)}) collective-permute-start(bf16[384,768]{1,0:T(8,128)(2,1)} %fusion.18), channel_id=1, source_target_pairs={{0,4},{2,6},{4,0},{6,2},{1,5},{3,7},{5,1},{7,3},{8,12},{10,14},{12... | collective-permute-start | bytes 1769480 | tf_op jit(solution)/shard_map/ppermute | solution.py:548
  501.8 25.3 %collective-permute-start.37 = (bf16[384,768]{1,0:T(8,128)(2,1)}, bf16[384,768]{1,0:T(8,128)(2,1)}, u32[]{:S(2)}, u32[]{:S(2)}) collective-permute-start(bf16[384,768]{1,0:T(8,128)(2,1)} %fusion.19), channel_id=1, source_target_pairs={{0,4},{2,6},{4,0},{6,2},{1,5},{3,7},{5,1},{7,3},{8,12},{10,14},{12... | collective-permute-start | bytes 1769480 | tf_op jit(solution)/shard_map/ppermute | solution.py:548
  517.3 17.2 %collective-permute-start.35 = (bf16[384,768]{1,0:T(8,128)(2,1)S(1)}, bf16[384,768]{1,0:T(8,128)(2,1)}, u32[]{:S(2)}, u32[]{:S(2)}) collective-permute-start(bf16[384,768]{1,0:T(8,128)(2,1)S(1)} %fusion.6), channel_id=1, source_target_pairs={{0,1},{1,0},{2,3},{3,2},{4,5},{5,4},{6,7},{7,6},{8,9},{9,8},{10,11... | collective-permute-start | bytes 1769480 | tf_op jit(solution)/shard_map/ppermute | solution.py:548
  528.6 14.2 %collective-permute-start.38 = (bf16[384,768]{1,0:T(8,128)(2,1)S(1)}, bf16[384,768]{1,0:T(8,128)(2,1)}, u32[]{:S(2)}, u32[]{:S(2)}) collective-permute-start(bf16[384,768]{1,0:T(8,128)(2,1)S(1)} %fusion.5), channel_id=1, source_target_pairs={{0,1},{1,0},{2,3},{3,2},{4,5},{5,4},{6,7},{7,6},{8,9},{9,8},{10,11... | collective-permute-start | bytes 1769480 | tf_op jit(solution)/shard_map/ppermute | solution.py:548
  (16 other events, 256.9 us)

commit v3 on v2

--- a/solution.py
+++ b/solution.py
@@ -188,7 +188,7 @@
         send.put(rs_ref, rs_o.at[here, :])
         y_ref[...] = (n2 * gb_ref[2:3, :] + gb_ref[3:4, :]).astype(bf)
         send.put(y_ref, all_o.at[here, :])
-        loaded(5, 6)
+        loaded(5)
         send.finish()
 
 
@@ -201,12 +201,12 @@
 
 
 def forward_opening(delta, n, rows, *refs):
-    ins, refs = refs[:12], refs[12:]
-    outs, kept, scratch, load_sems = refs[:16], refs[16:25], refs[25:-1], refs[-1]
-    tok, cot, cos, sin, *weights, gb = ins[3:]
-    tok_v, cot_v, _, _, *weights_v, _ = kept
+    ins, refs = refs[:11], refs[11:]
+    outs, kept, scratch, load_sems = refs[:16], refs[16:24], refs[24:-1], refs[-1]
+    tok, cos, sin, *weights, gb = ins[3:]
+    tok_v, _, _, *weights_v = kept[:7]
     head, tail = pl.ds(0, rows), pl.ds(rows, (n - 1) * rows)
-    pairs = [(tok.at[head, :], tok_v.at[head, :])] + list(zip(weights, weights_v)) + [(tok.at[tail, :], tok_v.at[tail, :]), (cot, cot_v)]
+    pairs = [(tok.at[head, :], tok_v.at[head, :])] + list(zip(weights, weights_v)) + [(tok.at[tail, :], tok_v.at[tail, :])]
     loads = [pltpu.make_async_copy(src, dst, load_sems.at[i]) for i, (src, dst) in enumerate(pairs)]
     for copy in loads:
         copy.start()
@@ -214,8 +214,8 @@
 
 
 def forward_next(delta, n, rows, *refs):
-    t, meta, arr, tok, cot, cos, sin, wq, wo, wu, wd, gb, s_in = refs[:13]
-    forward_kernel(delta, n, rows, t, meta, tok, arr, cos, sin, wq, wo, wu, wd, gb, s_in, *refs[27:43], *refs[52:])
+    t, meta, arr, tok = refs[:4]
+    forward_kernel(delta, n, rows, t, meta, tok, arr, *refs[4:12], *refs[26:42], *refs[50:])
 
 
 def saved_items(rows):
@@ -224,11 +224,11 @@
 
 
 def kept_items(every):
-    return [((every, D), bf), ((every, D), bf), ((every, 128), f32), ((every, 128), f32),
-            ((D, 3 * D), bf), ((D, D), bf), ((D, 4 * D), bf), ((4 * D, D), bf), ((4, D), f32)]
-
-
-def forward_call(rows, n, delta, opening, limit=22):
+    return [((every, D), bf), ((every, 128), f32), ((every, 128), f32), ((D, 3 * D), bf), ((D, D), bf), ((D, 4 * D), bf), ((4 * D, D), bf),
+            ((4, D), f32)]
+
+
+def forward_call(rows, n, delta, opening, limit=20):
     V = pl.BlockSpec(memory_space=pltpu.VMEM)
     S = pl.BlockSpec(memory_space=pltpu.SMEM)
     A = pl.BlockSpec(memory_space=pl.ANY)
@@ -237,15 +237,15 @@
     big = [pltpu.HBM((every, D), bf)] + [pltpu.HBM(*item) for item in saved_items(every)]
     big[4] = pltpu.HBM((TILES, every, TILE), bf)
     big[13] = pltpu.HBM((n, PAIRS, 256, 256), bf)
-    aliases = {5: 18, 6: 19, 11: 24}
+    aliases = {4: 17, 5: 18, 10: 23}
     if not opening:
-        aliases = {12: 1, **{13 + i: 2 + i for i in range(14)}, **{3 + i: 16 + i for i in range(9)}}
+        aliases = {11: 1, **{12 + i: 2 + i for i in range(14)}, **{3 + i: 16 + i for i in range(8)}}
     return pl.pallas_call(
         functools.partial(forward_opening if opening else forward_next, delta, n, rows),
-        in_specs=[S, S, V, A, A, V, V, A, A, A, A, V] if opening else [S, S] + [V] * 11 + [A] * 14,
-        out_specs=[V, V] + [A] * 14 + [V] * 9,
+        in_specs=[S, S, V, A, V, V, A, A, A, A, V] if opening else [S, S] + [V] * 10 + [A] * 14,
+        out_specs=[V, V] + [A] * 14 + [V] * 8,
         out_shape=[sd((rows, D), bf), sd((PAIRS, 256, 256), f32)] + big + [pltpu.VMEM(*item) for item in kept_items(every)],
-        scratch_shapes=[pltpu.VMEM(*item) for item in saved_items(rows)] + [pltpu.SemaphoreType.DMA((30,))] + [pltpu.SemaphoreType.DMA((7,))] * opening,
+        scratch_shapes=[pltpu.VMEM(*item) for item in saved_items(rows)] + [pltpu.SemaphoreType.DMA((30,))] + [pltpu.SemaphoreType.DMA((6,))] * opening,
         input_output_aliases=aliases,
         cost_estimate=pl.CostEstimate(flops=rows * 2 * 9 * 10**6, bytes_accessed=4 * 2**20, transcendentals=0),
         compiler_params=pltpu.CompilerParams(vmem_limit_bytes=limit * 2**20),
@@ -340,7 +340,6 @@
         df_ref[...] = df
         send.put(df_ref, df_o.at[here, :])
         total = d_two
-        loaded(1, 2)
         for cols, copy in zip(quarters, fetched[2:6]):
             copy.wait()
             du = (nt_dot(df, wd_ref[cols, :]) * gp_ref[:, cols].astype(f32)).astype(bf)
@@ -354,7 +353,6 @@
         ga_out[1:2, :] += jnp.sum(total, axis=0, keepdims=True)
         d_res = norm_back(total, n1, r1, gb_ref[0:1, :])
         dp = d_res.astype(bf)
-        loaded(3)
         da_ref[...] = nt_dot(dp, wo_ref[...]).astype(bf)
         for copy in fetched[7:]:
             copy.wait()
@@ -399,7 +397,7 @@
             dm_ref[:, lanes] = ((dq[:, :128] * cos + dq[:, 128:] * sin) * sq).astype(bf)
             dm_ref[:, D + 128 * p:D + 128 * p + 128] = ((dk[:, :128] * cos + dk[:, 128:] * sin) * sk).astype(bf)
             dm_ref[:, 2 * D + 128 * p:2 * D + 128 * p + 128] = dv.astype(bf)
-        loaded(4, 5)
+        loaded(1)
         dm = dm_ref[...]
         for g in range(groups):
             odd = g & 1
@@ -422,8 +420,13 @@
 
 
 def backward_opening(delta, n, rows, stages, groups, *refs):
-    t, meta, arr, cot = refs[:4]
-    backward_kernel(delta, n, rows, stages, groups, t, meta, cot, arr, *refs[4:11], None, None, *refs[11:28], *refs[36:])
+    t, meta, arr = refs[:3]
+    cot, cot_v, load_sems, refs = refs[21], refs[29], refs[-1], refs[:-1]
+    head, tail = pl.ds((n - 1) * rows, rows), pl.ds(0, (n - 1) * rows)
+    loads = [pltpu.make_async_copy(cot.at[part, :], cot_v.at[part, :], load_sems.at[i]) for i, part in enumerate((head, tail))]
+    for copy in loads:
+        copy.start()
+    backward_kernel(delta, n, rows, stages, groups, t, meta, cot_v, arr, *refs[4:11], None, None, *refs[11:21], *refs[22:29], *refs[37:], loads=loads)
 
 
 def backward_next(delta, n, rows, stages, groups, *refs):
@@ -431,19 +434,7 @@
     backward_kernel(delta, n, rows, stages, groups, t, meta, cot, arr, *refs[4:23], *refs[27:34], *refs[42:])
 
 
-def backward_closing(delta, n, rows, stages, groups, *refs):
-    t, meta, arr = refs[:3]
-    act, refs, outs = refs[26], refs[3:22] + refs[27:], refs[27:34]
-    act_v, rest, sem = refs[19 + 14], refs[19 + 15:-1], refs[-1]
-    copies = [pltpu.make_async_copy(act.at[i], act_v.at[i], sem.at[i]) for i in range(TILES)]
-    for copy in copies:
-        copy.start()
-    backward_kernel(delta, n, rows, stages, groups, t, meta, None, arr, *refs[:19], *outs, *rest)
-    for copy in copies:
-        copy.wait()
-
-
-def backward_call(rows, n, delta, stages, groups, opening, closing, limit=22):
+def backward_call(rows, n, delta, stages, groups, opening, limit=20):
     V = pl.BlockSpec(memory_space=pltpu.VMEM)
     S = pl.BlockSpec(memory_space=pltpu.SMEM)
     A = pl.BlockSpec(memory_space=pl.ANY)
@@ -454,15 +445,19 @@
              ((rows, 2 * D), bf), ((rows, 2 * D), bf), ((rows, 2 * D), bf), ((PAIRS, 256, 256), bf)]
     own = [((rows, 3 * D), bf), ((rows, D), bf), ((rows, D), bf)]
     big = [pltpu.HBM((every, D), bf), pltpu.HBM((TILES, every, TILE), bf), pltpu.HBM((TILES, every, TILE), bf), pltpu.HBM((every, D), bf)]
+    if opening:
+        aliases = {3 + i: 7 + i for i in range(8)}
+    else:
+        aliases = {**{3 + i: 7 + i for i in range(8)}, 11: 1, 12: 2, **{23 + i: 3 + i for i in range(4)}}
     return pl.pallas_call(
-        functools.partial(backward_opening if opening else backward_closing if closing else backward_next, delta, n, rows, stages, groups),
-        in_specs=[S, S] + [V] * 9 + [A] * 10 if opening else [S, S] + [V] * (11 - closing) + [A] * (14 + closing),
+        functools.partial(backward_opening if opening else backward_next, delta, n, rows, stages, groups),
+        in_specs=[S, S] + [V] * 9 + [A] * 11 if opening else [S, S] + [V] * 11 + [A] * 14,
         out_specs=[V] * 3 + [A] * 4 + [V] * 8,
         out_shape=[sd((rows, D), bf), sd((PAIRS, 256, 256), f32), sd((8, D), f32)] + big
-        + [pltpu.VMEM(*item) for item in kept_items(every)[1 + closing:]] + [pltpu.VMEM((TILES, every, TILE), bf)] * closing,
+        + [pltpu.VMEM(*item) for item in kept_items(every)],
         scratch_shapes=[pltpu.VMEM(*item) for item in made + own + saved] + [pltpu.SemaphoreType.DMA((30,)), pltpu.SemaphoreType.DMA((13,))]
-        + [pltpu.SemaphoreType.DMA((TILES,))] * closing,
-        input_output_aliases={**{3 + i: 7 + i for i in range(8 - closing)}, **({} if opening else {11 - closing: 1, 12 - closing: 2, **{23 - closing + i: 3 + i for i in range(4)}})},
+        + [pltpu.SemaphoreType.DMA((2,))] * opening,
+        input_output_aliases=aliases,
         cost_estimate=pl.CostEstimate(flops=rows * 2 * 10 * 10**6, bytes_accessed=4 * 2**20, transcendentals=0),
         compiler_params=pltpu.CompilerParams(vmem_limit_bytes=limit * 2**20),
         name="layer_backward",
@@ -472,14 +467,27 @@
 HALF = D // 2
 
 
-def weight_kernel(groups, mixed, waits, meta_ref, left, *refs):
+def weight_kernel(groups, half, mixed, waits, fetch, meta_ref, left, *refs):
     raws, refs = refs[:1 + mixed], refs[1 + mixed + waits:]
-    outs, (turned, out_buf, out_sem) = refs[:4], refs[4:]
+    keep_o, send_o, refs = refs[0], refs[1], refs[2:]
+    kept, (turned, out_buf, out_sem, *load_sems) = refs[:2 * fetch], refs[2 * fetch:]
     me = meta_ref[1]
     share = TILES // groups
+    raw_copies, left_copies = [], []
+    if fetch:
+        left_v, raw_v = kept
+        raw_copies = [pltpu.make_async_copy(raws[0].at[k:k + 256, :], raw_v.at[k:k + 256, :], load_sems[0].at[k // 256]) for k in range(0, raw_v.shape[0], 256)]
+        left_copies = [pltpu.make_async_copy(left.at[i], left_v.at[i], load_sems[1].at[i]) for i in range(TILES)]
+        for copy in raw_copies + left_copies:
+            copy.start()
+        left, raws = left_v, (raw_v,)
     for j, raw in enumerate(raws):
         for k in range(0, raw.shape[0], 256):
-            turned[j, :, k:k + 256] = raw[k:k + 256, :].T
+            if fetch:
+                raw_copies[k // 256].wait()
+            turned[j, :, k:k + 256] = raw[k:k + 256, half * HALF:(half + 1) * HALF].T
+    for copy in left_copies:
+        copy.wait()
     for g in range(groups):
         for i in range(share):
             cols = slice(i * TILE, (i + 1) * TILE)
@@ -490,31 +498,30 @@
                 value = jnp.where(lane < 3 * D // groups - i * TILE, value, other)
             out_buf[g, :, cols] = value.astype(bf)
         rel = g ^ me
-        for half in range(2):
-            part = out_buf.at[g, half * HALF:(half + 1) * HALF, :]
-
-            @pl.when((rel & 1) == 0)
-            def _():
-                pltpu.make_async_copy(part, outs[2 * half].at[rel >> 1], out_sem).start()
-
-            @pl.when((rel & 1) == 1)
-            def _():
-                pltpu.make_async_copy(part, outs[2 * half + 1].at[rel >> 1], out_sem).start()
+
+        @pl.when((rel & 1) == 0)
+        def _():
+            pltpu.make_async_copy(out_buf.at[g], keep_o.at[rel >> 1], out_sem).start()
+
+        @pl.when((rel & 1) == 1)
+        def _():
+            pltpu.make_async_copy(out_buf.at[g], send_o.at[rel >> 1], out_sem).start()
     pltpu.make_async_copy(out_buf, out_buf, out_sem).wait()
 
 
-def weight_call(every, groups, mixed, waits, limit=22):
+def weight_call(every, groups, half, mixed, waits, fetch, limit=12):
     V = pl.BlockSpec(memory_space=pltpu.VMEM)
     S = pl.BlockSpec(memory_space=pltpu.SMEM)
     A = pl.BlockSpec(memory_space=pl.ANY)
     raws = 1 + mixed
     return pl.pallas_call(
-        functools.partial(weight_kernel, groups, mixed, waits),
-        in_specs=[S] + [V] * (1 + raws) + [A] * waits,
-        out_specs=[A] * 4,
-        out_shape=[pltpu.HBM((2, HALF, D), bf)] * 4,
-        scratch_shapes=[pltpu.VMEM((raws, D, every), bf), pltpu.VMEM((groups, D, D), bf), pltpu.SemaphoreType.DMA],
-        cost_estimate=pl.CostEstimate(flops=2 * every * D * 4 * D, bytes_accessed=every * 5 * D * 2, transcendentals=0),
+        functools.partial(weight_kernel, groups, half, mixed, waits, fetch),
+        in_specs=[S] + [A if fetch else V] * (1 + raws) + [A] * waits,
+        out_specs=[A] * 2 + [V] * 2 * fetch,
+        out_shape=[pltpu.HBM((2, HALF, D), bf)] * 2 + [pltpu.VMEM((TILES, every, TILE), bf), pltpu.VMEM((every, D), bf)] * fetch,
+        scratch_shapes=[pltpu.VMEM((raws, HALF, every), bf), pltpu.VMEM((groups, HALF, D), bf), pltpu.SemaphoreType.DMA]
+        + [pltpu.SemaphoreType.DMA((every // 256,)), pltpu.SemaphoreType.DMA((TILES,))] * fetch,
+        cost_estimate=pl.CostEstimate(flops=2 * every * HALF * 4 * D, bytes_accessed=every * 5 * D * 2, transcendentals=0),
         compiler_params=pltpu.CompilerParams(vmem_limit_bytes=limit * 2**20),
         name="weight_grad",
     )
@@ -568,7 +575,7 @@
     ticks = n + DELTA * (stages - 1)
     cos, sin, first, last = geometry(doc_ids)
     meta = jnp.concatenate([stage[None], me[None], first, last])
-    resident = far((tokens, cotangent)) + [cos, sin] + far((w_qkv[0], w_out[0], w_up[0], w_down[0]))
+    resident = far((tokens,)) + [cos, sin] + far((w_qkv[0], w_out[0], w_up[0], w_down[0]))
     gb = jnp.concatenate([first_gain, first_bias, second_gain, second_bias], axis=0)
     blank = jnp.zeros((ROWS, D), bf)
     arriving = [blank] * DELTA
@@ -581,23 +588,25 @@
         arriving.append(lax.ppermute(made[0], "pipe", route) if route else made[0])
     block_out, x, att, hb, act, qn, kf, v, sg, n1, gp, n2, rs, sb = big
     arriving = [made[0]] * DELTA
-    state, big, resident = (), (), resident[1:]
+    state, big = (), ()
     for t in range(ticks):
-        closing = t == ticks - 1
-        made = backward_call(ROWS, n, DELTA, stages, groups, t == 0, closing)(
-            jnp.full((1,), t, jnp.int32), meta, arriving.pop(0), *resident[closing:], *state,
-            *far((n2, rs, gp, n1, att, v, qn, kf, sg, sb)), *big, *far([act] * closing))
+        made = backward_call(ROWS, n, DELTA, stages, groups, t == 0)(
+            jnp.full((1,), t, jnp.int32), meta, arriving.pop(0), *resident, *state,
+            *far((n2, rs, gp, n1, att, v, qn, kf, sg, sb)), *big, *far([cotangent] * (t == 0)))
         state, big, resident = made[1:3], made[3:7], made[7:]
         route = [(a, a - 1) for a in range(1, stages) if 0 <= t - (stages - 1 - a) * DELTA < n]
         arriving.append(lax.ppermute(made[0], "pipe", route) if route else made[0])
     df, du, de, input_grad = big
-    act = resident[7]
     aways, owns, parts = [], [], []
     for left, rights in ((act, (df,)), (de, (x, att)), (du, (hb,))):
-        waits = aways[-2:] + owns[-2:-1]
-        made = weight_call(n * ROWS, groups, len(rights) == 2, len(waits))(meta, left, *rights, *waits)
         for half in range(2):
-            away, own, part = reduced(made[2 * half], made[2 * half + 1], bf)
+            waits = aways[-2:-1] + owns[-4:-3]
+            fetch = not parts
+            operands = far((left,) + rights) if fetch else (left,) + rights
+            keep, send, *loaded = weight_call(n * ROWS, groups, half, len(rights) == 2, len(waits), fetch)(meta, *operands, *waits)
+            if fetch:
+                left, rights = loaded[0], tuple(loaded[1:])
+            away, own, part = reduced(keep, send, bf)
             aways.append(away)
             owns.append(own)
             parts.append(part)

time: 554 us -> 561 us (1.013)
  local copies, waits for them, and re-layouts: 28.7 us -> 65.1 us
  waiting for transfers between devices: 145 us -> 114 us
  Pallas kernels: 293 us -> 299 us
    unnamed x43 -> x101, local copies, waits for them, and re-layouts: 26.1 us -> 62.4 us
    ppermute x21, waiting for transfers between devices: 82.7 us -> 50.4 us  [exchange(): return lax.ppermute(block, axis, route)]
    pallas_call x17 -> x20, Pallas kernels: 186 us -> 190 us  [the longest x14 142 us: local(): backward_call(ROWS, n, DELTA, stages, groups, t == 0)]
  transfers between devices with their start and end apart: 45 -> 45, of which waited for: 19 -> 17; matrix products, arithmetic and copies ran while one was open for 5% -> 5% of each run, Pallas kernels for 42% -> 45%
where the time goes in v3:
time: 561 us; the launch traced here: 552 us
  Pallas kernels  299 us (53%)
  waiting for transfers between devices  114 us (20%)
  local copies, waits for them, and re-layouts  65.1 us (12%)
  starting transfers between devices  47.9 us (9%)
  other arithmetic  24.6 us (4%)
    pallas_call x14, Pallas kernels, local(): backward_call(ROWS, n, DELTA, stages, groups, t == 0)  142 us
    pallas_call x14, Pallas kernels, local(): forward_call(ROWS, n, DELTA, t == 0)  108 us
    ppermute x24, waiting for transfers between devices, local(): arriving.append(lax.ppermute(made[0], 'pipe', route) if route else made[0])  63.8 us
    unnamed x101, local copies, waits for them, and re-layouts  62.4 us
    ppermute x21, waiting for transfers between devices, exchange(): return lax.ppermute(block, axis, route)  50.4 us
    pallas_call x6, Pallas kernels, local(): weight_call(n * ROWS, groups, half, len(rights) == 2, len(waits), fetch)  48.4 us
    ppermute x24, starting transfers between devices, local(): arriving.append(lax.ppermute(made[0], 'pipe', route) if route else made[0])  30.8 us
    ppermute x21, starting transfers between devices, exchange(): return lax.ppermute(block, axis, route)  17.1 us
  transfers between devices with their start and end apart: 45, of which 17 were waited for; matrix products, arithmetic and copies ran while one was open for 5% of the time, Pallas kernels for 45%

profile of v3, /device:TPU:0, one launch (start us, length us, event | category | flops | bytes accessed | tf_op | source)
XLA Modules:
  0.0 552.3 jit_solution(6919320817983155798)
XLA Ops:
  4.2 12.3 %layer_forward.14 = (bf16[256,768]{1,0:T(8,128)(2,1)}, f32[6,256,256]{2,1,0:T(8,128)S(1)}, bf16[2048,768]{1,0:T(8,128)(2,1)}, bf16[2048,768]{1,0:T(8,128)(2,1)},...) custom-call(s32[1]{0:T(128)} %constant.45.clone.1.refs_0_, ...), custom_call_target="tpu_custom_call", output_to_operand_aliasing={{17}: (4, {}), {18}: (5, {}), {23}: (10, {})} | custom-call | flops 4608000000 | bytes 4194304 | tf_op jit(solution)/shard_map/layer_forward/pallas_call | solution.py:585
  18.6 10.5 %layer_forward.15 = (bf16[256,768]{1,0:T(8,128)(2,1)}, f32[6,256,256]{2,1,0:T(8,128)S(1)}, bf16[2048,768]{1,0:T(8,128)(2,1)}, bf16[2048,768]{1,0:T(8,128)(2,1)},...) custom-call(s32[1]{0:T(128)} %constant.28.clone.1.refs_0_, ...), custom_call_target="tpu_custom_call", output_to_operand_aliasing={{1}: (11, {}), {2}: (12, {}), {3}: (13, {}), {4}: (14, {}),... | custom-call | flops 4608000000 | bytes 4194304 | tf_op jit(solution)/shard_map/layer_forward/pallas_call | solution.py:585
  41.4 2.3 copy-done.1
  43.7 2.3 copy-done.7
  53.1 9.6 %layer_forward.16 = (bf16[256,768]{1,0:T(8,128)(2,1)S(1)}, f32[6,256,256]{2,1,0:T(8,128)S(1)}, bf16[2048,768]{1,0:T(8,128)(2,1)}, bf16[2048,768]{1,0:T(8,128)(2,...) custom-call(s32[1]{0:T(128)} %constant.76.clone.1.refs_0_, ...), custom_call_target="tpu_custom_call", output_to_operand_aliasing={{1}: (11, {}), {2}: (12, {}), {3}: (13, {}), {4}: (14, {}),... | custom-call | flops 4608000000 | bytes 4194304 | tf_op jit(solution)/shard_map/layer_forward/pallas_call | solution.py:585
  64.0 10.2 %layer_forward.17 = (bf16[256,768]{1,0:T(8,128)(2,1)S(1)}, f32[6,256,256]{2,1,0:T(8,128)S(1)}, bf16[2048,768]{1,0:T(8,128)(2,1)}, bf16[2048,768]{1,0:T(8,128)(2,...) custom-call(s32[1]{0:T(128)} %constant.27.clone.1.refs_0_, ...), custom_call_target="tpu_custom_call", output_to_operand_aliasing={{1}: (11, {}), {2}: (12, {}), {3}: (13, {}), {4}: (14, {}),... | custom-call | flops 4608000000 | bytes 4194304 | tf_op jit(solution)/shard_map/layer_forward/pallas_call | solution.py:585
  75.5 9.0 %layer_forward.18 = (bf16[256,768]{1,0:T(8,128)(2,1)S(1)}, f32[6,256,256]{2,1,0:T(8,128)S(1)}, bf16[2048,768]{1,0:T(8,128)(2,1)}, bf16[2048,768]{1,0:T(8,128)(2,...) custom-call(s32[1]{0:T(128)} %constant.77.clone.1.refs_0_, ...), custom_call_target="tpu_custom_call", output_to_operand_aliasing={{1}: (11, {}), {2}: (12, {}), {3}: (13, {}), {4}: (14, {}),... | custom-call | flops 4608000000 | bytes 4194304 | tf_op jit(solution)/shard_map/layer_forward/pallas_call | solution.py:585
  86.5 9.5 %layer_forward.19 = (bf16[256,768]{1,0:T(8,128)(2,1)S(1)}, f32[6,256,256]{2,1,0:T(8,128)S(1)}, bf16[2048,768]{1,0:T(8,128)(2,1)}, bf16[2048,768]{1,0:T(8,128)(2,...) custom-call(s32[1]{0:T(128)} %constant.26.clone.1.refs_0_, ...), custom_call_target="tpu_custom_call", output_to_operand_aliasing={{1}: (11, {}), {2}: (12, {}), {3}: (13, {}), {4}: (14, {}),... | custom-call | flops 4608000000 | bytes 4194304 | tf_op jit(solution)/shard_map/layer_forward/pallas_call | solution.py:585
  96.0 2.4 collective-permute-start.4
  98.4 9.0 %layer_forward.20 = (bf16[256,768]{1,0:T(8,128)(2,1)S(1)}, f32[6,256,256]{2,1,0:T(8,128)S(1)}, bf16[2048,768]{1,0:T(8,128)(2,1)}, bf16[2048,768]{1,0:T(8,128)(2,...) custom-call(s32[1]{0:T(128)} %constant.78.clone.1.refs_0_, ...), custom_call_target="tpu_custom_call", output_to_operand_aliasing={{1}: (11, {}), {2}: (12, {}), {3}: (13, {}), {4}: (14, {}),... | custom-call | flops 4608000000 | bytes 4194304 | tf_op jit(solution)/shard_map/layer_forward/pallas_call | solution.py:585
  109.4 9.6 %layer_forward.21 = (bf16[256,768]{1,0:T(8,128)(2,1)S(1)}, f32[6,256,256]{2,1,0:T(8,128)S(1)}, bf16[2048,768]{1,0:T(8,128)(2,1)}, bf16[2048,768]{1,0:T(8,128)(2,...) custom-call(s32[1]{0:T(128)} %constant.40.clone.1.refs_0_, ...), custom_call_target="tpu_custom_call", output_to_operand_aliasing={{1}: (11, {}), {2}: (12, {}), {3}: (13, {}), {4}: (14, {}),... | custom-call | flops 4608000000 | bytes 4194304 | tf_op jit(solution)/shard_map/layer_forward/pallas_call | solution.py:585
  122.5 6.6 %collective-permute-done.6.refs_2_ = bf16[256,768]{1,0:T(8,128)(2,1)S(1)} collective-permute-done((bf16[256,768]{1,0:T(8,128)(2,1)S(1)}, bf16[256,768]{1,0:T(8,128)(2,1)S(1)}, u32[]{:S(2)}, u32[]{:S(2)}) %collective-permute-start.6) | collective-permute-done | bytes 393248 | tf_op jit(solution)/shard_map/ppermute | solution.py:588
  129.1 6.8 %layer_forward.23 = (bf16[256,768]{1,0:T(8,128)(2,1)S(1)}, f32[6,256,256]{2,1,0:T(8,128)S(1)}, bf16[2048,768]{1,0:T(8,128)(2,1)}, bf16[2048,768]{1,0:T(8,128)(2,...) custom-call(s32[1]{0:T(128)} %constant.39.clone.1.refs_0_, ...), custom_call_target="tpu_custom_call", output_to_operand_aliasing={{1}: (11, {}), {2}: (12, {}), {3}: (13, {}), {4}: (14, {}),... | custom-call | flops 4608000000 | bytes 4194304 | tf_op jit(solution)/shard_map/layer_forward/pallas_call | solution.py:585
  138.2 8.7 %layer_forward.25 = (bf16[256,768]{1,0:T(8,128)(2,1)S(1)}, f32[6,256,256]{2,1,0:T(8,128)S(1)}, bf16[2048,768]{1,0:T(8,128)(2,1)}, bf16[2048,768]{1,0:T(8,128)(2,...) custom-call(s32[1]{0:T(128)} %constant.38.clone.1.refs_0_, ...), custom_call_target="tpu_custom_call", output_to_operand_aliasing={{1}: (11, {}), {2}: (12, {}), {3}: (13, {}), {4}: (14, {}),... | custom-call | flops 4608000000 | bytes 4194304 | tf_op jit(solution)/shard_map/layer_forward/pallas_call | solution.py:585
  149.3 9.6 %layer_forward.27 = (bf16[256,768]{1,0:T(8,128)(2,1)S(1)}, f32[6,256,256]{2,1,0:T(8,128)S(1)}, bf16[2048,768]{1,0:T(8,128)(2,1)}, bf16[2048,768]{1,0:T(8,128)(2,...) custom-call(s32[1]{0:T(128)} %constant.21.clone.1.refs_0_, ...), custom_call_target="tpu_custom_call", output_to_operand_aliasing={{1}: (11, {}), {2}: (12, {}), {3}: (13, {}), {4}: (14, {}),... | custom-call | flops 4608000000 | bytes 4194304 | tf_op jit(solution)/shard_map/layer_forward/pallas_call | solution.py:585
  165.2 2.3 copy-done.3
  167.5 2.3 copy-done.9
  172.3 2.9 layer_backward.14
  184.6 2.3 copy-done.11
  189.4 8.2 %layer_backward.15 = (bf16[256,768]{1,0:T(8,128)(2,1)S(1)}, f32[6,256,256]{2,1,0:T(8,128)S(1)}, f32[8,768]{1,0:T(8,128)S(1)}, bf16[2048,768]{1,0:T(8,128)(2,1)},...) custom-call(s32[1]{0:T(128)} %constant.28.clone.1.refs_0_, ...), custom_call_target="tpu_custom_call", output_to_operand_aliasing={{7}: (3, {}), {8}: (4, {}), {9}: (5, {}), {10}: (6, {}), {1... | custom-call | flops 5120000000 | bytes 4194304 | tf_op jit(solution)/shard_map/layer_backward/pallas_call | solution.py:593
  199.9 10.5 %layer_backward.17 = (bf16[256,768]{1,0:T(8,128)(2,1)S(1)}, f32[6,256,256]{2,1,0:T(8,128)S(1)}, f32[8,768]{1,0:T(8,128)S(1)}, bf16[2048,768]{1,0:T(8,128)(2,1)},...) custom-call(s32[1]{0:T(128)} %constant.27.clone.1.refs_0_, ...), custom_call_target="tpu_custom_call", output_to_operand_aliasing={{7}: (3, {}), {8}: (4, {}), {9}: (5, {}), {10}: (6, {}), {1... | custom-call | flops 5120000000 | bytes 4194304 | tf_op jit(solution)/shard_map/layer_backward/pallas_call | solution.py:593
  213.4 10.1 %layer_backward.19 = (bf16[256,768]{1,0:T(8,128)(2,1)S(1)}, f32[6,256,256]{2,1,0:T(8,128)S(1)}, f32[8,768]{1,0:T(8,128)S(1)}, bf16[2048,768]{1,0:T(8,128)(2,1)},...) custom-call(s32[1]{0:T(128)} %constant.26.clone.1.refs_0_, ...), custom_call_target="tpu_custom_call", output_to_operand_aliasing={{7}: (3, {}), {8}: (4, {}), {9}: (5, {}), {10}: (6, {}), {1... | custom-call | flops 5120000000 | bytes 4194304 | tf_op jit(solution)/shard_map/layer_backward/pallas_call | solution.py:593
  224.8 46.0 %collective-permute-done.17.refs_2_ = bf16[256,768]{1,0:T(8,128)(2,1)S(1)} collective-permute-done((bf16[256,768]{1,0:T(8,128)(2,1)S(1)}, bf16[256,768]{1,0:T(8,128)(2,1)S(1)}, u32[]{:S(2)}, u32[]{:S(2)}) %collective-permute-start.17) | collective-permute-done | bytes 393248 | tf_op jit(solution)/shard_map/ppermute | solution.py:598
  270.9 13.3 %layer_backward.20 = (bf16[256,768]{1,0:T(8,128)(2,1)S(1)}, f32[6,256,256]{2,1,0:T(8,128)S(1)}, f32[8,768]{1,0:T(8,128)S(1)}, bf16[2048,768]{1,0:T(8,128)(2,1)},...) custom-call(s32[1]{0:T(128)} %constant.78.clone.1.refs_0_, ...), custom_call_target="tpu_custom_call", output_to_operand_aliasing={{7}: (3, {}), {8}: (4, {}), {9}: (5, {}), {10}: (6, {}), {1... | custom-call | flops 5120000000 | bytes 4194304 | tf_op jit(solution)/shard_map/layer_backward/pallas_call | solution.py:593
  285.4 7.7 %collective-permute-done.16.refs_2_ = bf16[256,768]{1,0:T(8,128)(2,1)S(1)} collective-permute-done((bf16[256,768]{1,0:T(8,128)(2,1)S(1)}, bf16[256,768]{1,0:T(8,128)(2,1)S(1)}, u32[]{:S(2)}, u32[]{:S(2)}) %collective-permute-start.16) | collective-permute-done | bytes 393248 | tf_op jit(solution)/shard_map/ppermute | solution.py:598
  293.1 13.5 %layer_backward.21 = (bf16[256,768]{1,0:T(8,128)(2,1)S(1)}, f32[6,256,256]{2,1,0:T(8,128)S(1)}, f32[8,768]{1,0:T(8,128)S(1)}, bf16[2048,768]{1,0:T(8,128)(2,1)},...) custom-call(s32[1]{0:T(128)} %constant.40.clone.1.refs_0_, ...), custom_call_target="tpu_custom_call", output_to_operand_aliasing={{7}: (3, {}), {8}: (4, {}), {9}: (5, {}), {10}: (6, {}), {1... | custom-call | flops 5120000000 | bytes 4194304 | tf_op jit(solution)/shard_map/layer_backward/pallas_call | solution.py:593
  308.4 13.3 %layer_backward.22 = (bf16[256,768]{1,0:T(8,128)(2,1)S(1)}, f32[6,256,256]{2,1,0:T(8,128)S(1)}, f32[8,768]{1,0:T(8,128)S(1)}, bf16[2048,768]{1,0:T(8,128)(2,1)},...) custom-call(s32[1]{0:T(128)} %constant.79.clone.1.refs_0_, ...), custom_call_target="tpu_custom_call", output_to_operand_aliasing={{7}: (3, {}), {8}: (4, {}), {9}: (5, {}), {10}: (6, {}), {1... | custom-call | flops 5120000000 | bytes 4194304 | tf_op jit(solution)/shard_map/layer_backward/pallas_call | solution.py:593
  323.9 13.4 %layer_backward.23 = (bf16[256,768]{1,0:T(8,128)(2,1)S(1)}, f32[6,256,256]{2,1,0:T(8,128)S(1)}, f32[8,768]{1,0:T(8,128)S(1)}, bf16[2048,768]{1,0:T(8,128)(2,1)},...) custom-call(s32[1]{0:T(128)} %constant.39.clone.1.refs_0_, ...), custom_call_target="tpu_custom_call", output_to_operand_aliasing={{7}: (3, {}), {8}: (4, {}), {9}: (5, {}), {10}: (6, {}), {1... | custom-call | flops 5120000000 | bytes 4194304 | tf_op jit(solution)/shard_map/layer_backward/pallas_call | solution.py:593
  339.1 13.3 %layer_backward.24 = (bf16[256,768]{1,0:T(8,128)(2,1)S(1)}, f32[6,256,256]{2,1,0:T(8,128)S(1)}, f32[8,768]{1,0:T(8,128)S(1)}, bf16[2048,768]{1,0:T(8,128)(2,1)},...) custom-call(s32[1]{0:T(128)} %constant.80.clone.1.refs_0_, ...), custom_call_target="tpu_custom_call", output_to_operand_aliasing={{7}: (3, {}), {8}: (4, {}), {9}: (5, {}), {10}: (6, {}), {1... | custom-call | flops 5120000000 | bytes 4194304 | tf_op jit(solution)/shard_map/layer_backward/pallas_call | solution.py:593
  354.6 13.5 %layer_backward.25 = (bf16[256,768]{1,0:T(8,128)(2,1)S(1)}, f32[6,256,256]{2,1,0:T(8,128)S(1)}, f32[8,768]{1,0:T(8,128)S(1)}, bf16[2048,768]{1,0:T(8,128)(2,1)},...) custom-call(s32[1]{0:T(128)} %constant.38.clone.1.refs_0_, ...), custom_call_target="tpu_custom_call", output_to_operand_aliasing={{7}: (3, {}), {8}: (4, {}), {9}: (5, {}), {10}: (6, {}), {1... | custom-call | flops 5120000000 | bytes 4194304 | tf_op jit(solution)/shard_map/layer_backward/pallas_call | solution.py:593
  369.4 14.1 %layer_backward.26 = (bf16[256,768]{1,0:T(8,128)(2,1)}, f32[6,256,256]{2,1,0:T(8,128)S(1)}, f32[8,768]{1,0:T(8,128)S(1)}, bf16[2048,768]{1,0:T(8,128)(2,1)}, bf1...) custom-call(s32[1]{0:T(128)} %constant.81.clone.1.refs_0_, ...), custom_call_target="tpu_custom_call", output_to_operand_aliasing={{7}: (3, {}), {8}: (4, {}), {9}: (5, {}), {10}: (6, {}), {1... | custom-call | flops 5120000000 | bytes 4194304 | tf_op jit(solution)/shard_map/layer_backward/pallas_call | solution.py:593
  384.1 14.2 %layer_backward.27 = (bf16[256,768]{1,0:T(8,128)(2,1)}, f32[6,256,256]{2,1,0:T(8,128)S(1)}, f32[8,768]{1,0:T(8,128)S(1)}, bf16[2048,768]{1,0:T(8,128)(2,1)}, bf1...) custom-call(s32[1]{0:T(128)} %constant.21.clone.1.refs_0_, ...), custom_call_target="tpu_custom_call", output_to_operand_aliasing={{7}: (3, {}), {8}: (4, {}), {9}: (5, {}), {10}: (6, {}), {1... | custom-call | flops 5120000000 | bytes 4194304 | tf_op jit(solution)/shard_map/layer_backward/pallas_call | solution.py:593
  398.5 12.1 %weight_grad.6 = (bf16[2,384,768]{2,1,0:T(8,128)(2,1)}, bf16[2,384,768]{2,1,0:T(8,128)(2,1)}, bf16[12,2048,256]{2,1,0:T(8,128)(2,1)S(1)}, bf16[2048,768]{1,0:T(8,128)(2,1)S(1)}) custom-call(s32[18]{0:T(128)S(1)} %pad_add_fusion.refs_1_.meta_ref, bf16[12,2048,256]{2,1,0:T(8,128)(2,1)} %get-tuple-element.1086.left, bf16[2048,768]{1,0:T(8,128)(2,1)} %get-tuple-element.1087.refs_0_), custom_call_target="tpu_custom_call" | custom-call | flops 4831838208 | bytes 15728640 | tf_op jit(solution)/shard_map/weight_grad/pallas_call | solution.py:606
  411.2 6.5 %weight_grad.8 = (bf16[2,384,768]{2,1,0:T(8,128)(2,1)}, bf16[2,384,768]{2,1,0:T(8,128)(2,1)}) custom-call(s32[18]{0:T(128)S(1)} %pad_add_fusion.refs_1_.meta_ref, bf16[12,2048,256]{2,1,0:T(8,128)(2,1)S(1)} %get-tuple-element.1092.left, bf16[2048,768]{1,0:T(8,128)(2,1)S(1)} %get-tuple-element.1093.refs_0_), custom_call_target="tpu_custom_call" | custom-call | flops 4831838208 | bytes 15728640 | tf_op jit(solution)/shard_map/weight_grad/pallas_call | solution.py:606
  422.3 2.8 collective-permute-done.44
  429.2 4.6 copy-done.12
  435.6 8.3 %weight_grad.7 = (bf16[2,384,768]{2,1,0:T(8,128)(2,1)}, bf16[2,384,768]{2,1,0:T(8,128)(2,1)}) custom-call(s32[18]{0:T(128)S(1)} %pad_add_fusion.refs_1_.meta_ref, bf16[12,2048,256]{2,1,0:T(8,128)(2,1)S(1)} %copy-done.12, bf16[2048,768]{1,0:T(8,128)(2,1)S(1)} %copy-done.30, bf16[2048,768]{1,0:T(8,128)(2,1)S(1)} %copy-done.13, bf16[384,768]{1,0:T(8,128)(2,1)S(1)} %fusion.14.refs_2_), custom_call_target="tpu_custom_call" | custom-call | flops 4831838208 | bytes 15728640 | tf_op jit(solution)/shard_map/weight_grad/pallas_call | solution.py:606
  445.7 8.1 %weight_grad.9 = (bf16[2,384,768]{2,1,0:T(8,128)(2,1)}, bf16[2,384,768]{2,1,0:T(8,128)(2,1)}) custom-call(s32[18]{0:T(128)S(1)} %pad_add_fusion.refs_1_.meta_ref, bf16[12,2048,256]{2,1,0:T(8,128)(2,1)S(1)} %copy-done.12, bf16[2048,768]{1,0:T(8,128)(2,1)S(1)} %copy-done.31, bf16[2048,768]{1,0:T(8,128)(2,1)S(1)} %copy-done.13, bf16[384,768]{1,0:T(8,128)(2,1)S(1)} %fusion.16.refs_2_), custom_call_target="tpu_custom_call" | custom-call | flops 4831838208 | bytes 15728640 | tf_op jit(solution)/shard_map/weight_grad/pallas_call | solution.py:606
  456.6 4.7 collective-permute-done.36
  464.0 6.6 %weight_grad.10 = (bf16[2,384,768]{2,1,0:T(8,128)(2,1)}, bf16[2,384,768]{2,1,0:T(8,128)(2,1)}) custom-call(s32[18]{0:T(128)S(1)} %pad_add_fusion.refs_1_.meta_ref, bf16[12,2048,256]{2,1,0:T(8,128)(2,1)S(1)} %bitcast.106, bf16[2048,768]{1,0:T(8,128)(2,1)S(1)} %copy-done.32, bf16[384,768]{1,0:T(8,128)(2,1)S(1)} %fusion.15.refs_1_, ...), custom_call_target="tpu_custom_call" | custom-call | flops 4831838208 | bytes 15728640 | tf_op jit(solution)/shard_map/weight_grad/pallas_call | solution.py:606
  472.6 6.8 %weight_grad.11 = (bf16[2,384,768]{2,1,0:T(8,128)(2,1)}, bf16[2,384,768]{2,1,0:T(8,128)(2,1)}) custom-call(s32[18]{0:T(128)S(1)} %pad_add_fusion.refs_1_.meta_ref, bf16[12,2048,256]{2,1,0:T(8,128)(2,1)S(1)} %bitcast.106, bf16[2048,768]{1,0:T(8,128)(2,1)S(1)} %copy-done.32, bf16[384,768]{1,0:T(8,128)(2,1)S(1)} %fusion.17.refs_1_, ...), custom_call_target="tpu_custom_call" | custom-call | flops 4831838208 | bytes 15728640 | tf_op jit(solution)/shard_map/weight_grad/pallas_call | solution.py:606
  479.8 4.0 collective-permute-done.41
  486.1 5.0 collective-permute-done.30
  502.5 6.5 %collective-permute-done.31 = bf16[384,768]{1,0:T(8,128)(2,1)S(1)} collective-permute-done((bf16[384,768]{1,0:T(8,128)(2,1)S(1)}, bf16[384,768]{1,0:T(8,128)(2,1)S(1)}, u32[]{:S(2)}, u32[]{:S(2)}) %collective-permute-start.31) | collective-permute-done | bytes 589856 | tf_op jit(solution)/shard_map/ppermute | solution.py:555
  509.1 10.0 %collective-permute-done.27 = bf16[384,768]{1,0:T(8,128)(2,1)S(1)} collective-permute-done((bf16[384,768]{1,0:T(8,128)(2,1)S(1)}, bf16[384,768]{1,0:T(8,128)(2,1)S(1)}, u32[]{:S(2)}, u32[]{:S(2)}) %collective-permute-start.27) | collective-permute-done | bytes 589856 | tf_op jit(solution)/shard_map/ppermute | solution.py:555
  529.4 2.8 copy.521
  532.1 7.7 %collective-permute-done.35 = bf16[384,768]{1,0:T(8,128)(2,1)} collective-permute-done((bf16[384,768]{1,0:T(8,128)(2,1)S(1)}, bf16[384,768]{1,0:T(8,128)(2,1)}, u32[]{:S(2)}, u32[]{:S(2)}) %collective-permute-start.35) | collective-permute-done | bytes 589856 | tf_op jit(solution)/shard_map/ppermute | solution.py:555
  541.0 8.1 %collective-permute-done.39 = bf16[384,768]{1,0:T(8,128)(2,1)} collective-permute-done((bf16[384,768]{1,0:T(8,128)(2,1)S(1)}, bf16[384,768]{1,0:T(8,128)(2,1)}, u32[]{:S(2)}, u32[]{:S(2)}) %collective-permute-start.39) | collective-permute-done | bytes 589856 | tf_op jit(solution)/shard_map/ppermute | solution.py:555
  (233 shorter events, 126.6 us)
Async XLA Ops:
  16.5 24.9 %collective-permute-start.1 = (bf16[256,768]{1,0:T(8,128)(2,1)}, bf16[256,768]{1,0:T(8,128)(2,1)}, u32[]{:S(2)}, u32[]{:S(2)}) collective-permute-start(bf16[256,768]{1,0:T(8,128)(2,1)} %get-tuple-element.582), channel_id=1, source_target_pairs={{0,8},{1,9},{2,10},{3,11},{4,12},{5,13},{6,14},{7,15}} | collective-permute-start | bytes 1179656 | tf_op jit(solution)/shard_map/ppermute | solution.py:588
  39.3 24.6 %collective-permute-start = (bf16[256,768]{1,0:T(8,128)(2,1)}, bf16[256,768]{1,0:T(8,128)(2,1)}, u32[]{:S(2)}, u32[]{:S(2)}) collective-permute-start(bf16[256,768]{1,0:T(8,128)(2,1)} %get-tuple-element.581), channel_id=1, source_target_pairs={{0,8},{1,9},{2,10},{3,11},{4,12},{5,13},{6,14},{7,15}} | collective-permute-start | bytes 1179656 | tf_op jit(solution)/shard_map/ppermute | solution.py:588
  62.6 12.9 %collective-permute-start.3 = (bf16[256,768]{1,0:T(8,128)(2,1)S(1)}, bf16[256,768]{1,0:T(8,128)(2,1)S(1)}, u32[]{:S(2)}, u32[]{:S(2)}) collective-permute-start(bf16[256,768]{1,0:T(8,128)(2,1)S(1)} %get-tuple-element.630), channel_id=1, source_target_pairs={{0,8},{8,16},{1,9},{9,17},{2,10},{10,18},{3,11},{11,19},{4,12},{12... | collective-permute-start | bytes 1179656 | tf_op jit(solution)/shard_map/ppermute | solution.py:588
  74.2 12.3 %collective-permute-start.2 = (bf16[256,768]{1,0:T(8,128)(2,1)S(1)}, bf16[256,768]{1,0:T(8,128)(2,1)S(1)}, u32[]{:S(2)}, u32[]{:S(2)}) collective-permute-start(bf16[256,768]{1,0:T(8,128)(2,1)S(1)} %get-tuple-element.629), channel_id=1, source_target_pairs={{0,8},{8,16},{1,9},{9,17},{2,10},{10,18},{3,11},{11,19},{4,12},{12... | collective-permute-start | bytes 1179656 | tf_op jit(solution)/shard_map/ppermute | solution.py:588
  84.5 13.8 %collective-permute-start.5 = (bf16[256,768]{1,0:T(8,128)(2,1)S(1)}, bf16[256,768]{1,0:T(8,128)(2,1)S(1)}, u32[]{:S(2)}, u32[]{:S(2)}) collective-permute-start(bf16[256,768]{1,0:T(8,128)(2,1)S(1)} %get-tuple-element.678), channel_id=1, source_target_pairs={{0,8},{8,16},{16,24},{1,9},{9,17},{17,25},{2,10},{10,18},{18,26},{... | collective-permute-start | bytes 1179656 | tf_op jit(solution)/shard_map/ppermute | solution.py:588
  96.0 13.4 %collective-permute-start.4 = (bf16[256,768]{1,0:T(8,128)(2,1)S(1)}, bf16[256,768]{1,0:T(8,128)(2,1)S(1)}, u32[]{:S(2)}, u32[]{:S(2)}) collective-permute-start(bf16[256,768]{1,0:T(8,128)(2,1)S(1)} %get-tuple-element.677), channel_id=1, source_target_pairs={{0,8},{8,16},{16,24},{1,9},{9,17},{17,25},{2,10},{10,18},{18,26},{... | collective-permute-start | bytes 1179656 | tf_op jit(solution)/shard_map/ppermute | solution.py:588
  107.4 13.5 %collective-permute-start.7 = (bf16[256,768]{1,0:T(8,128)(2,1)S(1)}, bf16[256,768]{1,0:T(8,128)(2,1)S(1)}, u32[]{:S(2)}, u32[]{:S(2)}) collective-permute-start(bf16[256,768]{1,0:T(8,128)(2,1)S(1)} %get-tuple-element.726), channel_id=1, source_target_pairs={{0,8},{8,16},{16,24},{1,9},{9,17},{17,25},{2,10},{10,18},{18,26},{... | collective-permute-start | bytes 1179656 | tf_op jit(solution)/shard_map/ppermute | solution.py:588
  119.0 10.1 %collective-permute-start.6 = (bf16[256,768]{1,0:T(8,128)(2,1)S(1)}, bf16[256,768]{1,0:T(8,128)(2,1)S(1)}, u32[]{:S(2)}, u32[]{:S(2)}) collective-permute-start(bf16[256,768]{1,0:T(8,128)(2,1)S(1)} %get-tuple-element.725), channel_id=1, source_target_pairs={{0,8},{8,16},{16,24},{1,9},{9,17},{17,25},{2,10},{10,18},{18,26},{... | collective-permute-start | bytes 1179656 | tf_op jit(solution)/shard_map/ppermute | solution.py:588
  121.8 14.8 %collective-permute-start.9 = (bf16[256,768]{1,0:T(8,128)(2,1)S(1)}, bf16[256,768]{1,0:T(8,128)(2,1)S(1)}, u32[]{:S(2)}, u32[]{:S(2)}) collective-permute-start(bf16[256,768]{1,0:T(8,128)(2,1)S(1)} %get-tuple-element.774), channel_id=1, source_target_pairs={{8,16},{16,24},{9,17},{17,25},{10,18},{18,26},{11,19},{19,27},{12,... | collective-permute-start | bytes 1179656 | tf_op jit(solution)/shard_map/ppermute | solution.py:588
  135.9 2.3 collective-permute-start.8
  137.5 10.1 %collective-permute-start.11 = (bf16[256,768]{1,0:T(8,128)(2,1)S(1)}, bf16[256,768]{1,0:T(8,128)(2,1)S(1)}, u32[]{:S(2)}, u32[]{:S(2)}) collective-permute-start(bf16[256,768]{1,0:T(8,128)(2,1)S(1)} %get-tuple-element.822), channel_id=1, source_target_pairs={{16,24},{17,25},{18,26},{19,27},{20,28},{21,29},{22,30},{23,31}} | collective-permute-start | bytes 1179656 | tf_op jit(solution)/shard_map/ppermute | solution.py:588
  147.0 2.3 collective-permute-start.10
  181.6 16.7 %collective-permute-start.13 = (bf16[256,768]{1,0:T(8,128)(2,1)S(1)}, bf16[256,768]{1,0:T(8,128)(2,1)S(1)}, u32[]{:S(2)}, u32[]{:S(2)}) collective-permute-start(bf16[256,768]{1,0:T(8,128)(2,1)S(1)} %get-tuple-element.904), channel_id=1, source_target_pairs={{24,16},{25,17},{26,18},{27,19},{28,20},{29,21},{30,22},{31,23}} | collective-permute-start | bytes 1179656 | tf_op jit(solution)/shard_map/ppermute | solution.py:598
  197.5 2.4 collective-permute-start.12
  199.2 11.9 %collective-permute-start.15 = (bf16[256,768]{1,0:T(8,128)(2,1)S(1)}, bf16[256,768]{1,0:T(8,128)(2,1)S(1)}, u32[]{:S(2)}, u32[]{:S(2)}) collective-permute-start(bf16[256,768]{1,0:T(8,128)(2,1)S(1)} %get-tuple-element.934), channel_id=1, source_target_pairs={{16,8},{24,16},{17,9},{25,17},{18,10},{26,18},{19,11},{27,19},{20,... | collective-permute-start | bytes 1179656 | tf_op jit(solution)/shard_map/ppermute | solution.py:598
  210.4 3.0 collective-permute-start.14
  212.1 58.7 %collective-permute-start.17 = (bf16[256,768]{1,0:T(8,128)(2,1)S(1)}, bf16[256,768]{1,0:T(8,128)(2,1)S(1)}, u32[]{:S(2)}, u32[]{:S(2)}) collective-permute-start(bf16[256,768]{1,0:T(8,128)(2,1)S(1)} %get-tuple-element.964), channel_id=1, source_target_pairs={{8,0},{16,8},{24,16},{9,1},{17,9},{25,17},{10,2},{18,10},{26,18},{... | collective-permute-start | bytes 1179656 | tf_op jit(solution)/shard_map/ppermute | solution.py:598
  223.5 69.6 %collective-permute-start.16 = (bf16[256,768]{1,0:T(8,128)(2,1)S(1)}, bf16[256,768]{1,0:T(8,128)(2,1)S(1)}, u32[]{:S(2)}, u32[]{:S(2)}) collective-permute-start(bf16[256,768]{1,0:T(8,128)(2,1)S(1)} %get-tuple-element.963), channel_id=1, source_target_pairs={{8,0},{16,8},{24,16},{9,1},{17,9},{25,17},{10,2},{18,10},{26,18},{... | collective-permute-start | bytes 1179656 | tf_op jit(solution)/shard_map/ppermute | solution.py:598
  284.1 24.2 %collective-permute-start.19 = (bf16[256,768]{1,0:T(8,128)(2,1)S(1)}, bf16[256,768]{1,0:T(8,128)(2,1)S(1)}, u32[]{:S(2)}, u32[]{:S(2)}) collective-permute-start(bf16[256,768]{1,0:T(8,128)(2,1)S(1)} %get-tuple-element.994), channel_id=1, source_target_pairs={{8,0},{16,8},{24,16},{9,1},{17,9},{25,17},{10,2},{18,10},{26,18},{... | collective-permute-start | bytes 1179656 | tf_op jit(solution)/shard_map/ppermute | solution.py:598
  306.6 17.3 %collective-permute-start.18 = (bf16[256,768]{1,0:T(8,128)(2,1)S(1)}, bf16[256,768]{1,0:T(8,128)(2,1)S(1)}, u32[]{:S(2)}, u32[]{:S(2)}) collective-permute-start(bf16[256,768]{1,0:T(8,128)(2,1)S(1)} %get-tuple-element.993), channel_id=1, source_target_pairs={{8,0},{16,8},{24,16},{9,1},{17,9},{25,17},{10,2},{18,10},{26,18},{... | collective-permute-start | bytes 1179656 | tf_op jit(solution)/shard_map/ppermute | solution.py:598
  321.7 17.5 %collective-permute-start.21 = (bf16[256,768]{1,0:T(8,128)(2,1)S(1)}, bf16[256,768]{1,0:T(8,128)(2,1)S(1)}, u32[]{:S(2)}, u32[]{:S(2)}) collective-permute-start(bf16[256,768]{1,0:T(8,128)(2,1)S(1)} %get-tuple-element.1024), channel_id=1, source_target_pairs={{8,0},{16,8},{9,1},{17,9},{10,2},{18,10},{11,3},{19,11},{12,4},{20... | collective-permute-start | bytes 1179656 | tf_op jit(solution)/shard_map/ppermute | solution.py:598
  337.3 17.3 %collective-permute-start.20 = (bf16[256,768]{1,0:T(8,128)(2,1)S(1)}, bf16[256,768]{1,0:T(8,128)(2,1)S(1)}, u32[]{:S(2)}, u32[]{:S(2)}) collective-permute-start(bf16[256,768]{1,0:T(8,128)(2,1)S(1)} %get-tuple-element.1023), channel_id=1, source_target_pairs={{8,0},{16,8},{9,1},{17,9},{10,2},{18,10},{11,3},{19,11},{12,4},{20... | collective-permute-start | bytes 1179656 | tf_op jit(solution)/shard_map/ppermute | solution.py:598
  352.4 16.9 %collective-permute-start.23 = (bf16[256,768]{1,0:T(8,128)(2,1)S(1)}, bf16[256,768]{1,0:T(8,128)(2,1)S(1)}, u32[]{:S(2)}, u32[]{:S(2)}) collective-permute-start(bf16[256,768]{1,0:T(8,128)(2,1)S(1)} %get-tuple-element.1054), channel_id=1, source_target_pairs={{8,0},{9,1},{10,2},{11,3},{12,4},{13,5},{14,6},{15,7}} | collective-permute-start | bytes 1179656 | tf_op jit(solution)/shard_map/ppermute | solution.py:598
  368.1 16.0 %collective-permute-start.22 = (bf16[256,768]{1,0:T(8,128)(2,1)S(1)}, bf16[256,768]{1,0:T(8,128)(2,1)S(1)}, u32[]{:S(2)}, u32[]{:S(2)}) collective-permute-start(bf16[256,768]{1,0:T(8,128)(2,1)S(1)} %get-tuple-element.1053), channel_id=1, source_target_pairs={{8,0},{9,1},{10,2},{11,3},{12,4},{13,5},{14,6},{15,7}} | collective-permute-start | bytes 1179656 | tf_op jit(solution)/shard_map/ppermute | solution.py:598
  410.6 15.3 %collective-permute-start.24 = (bf16[2,384,768]{2,1,0:T(8,128)(2,1)}, bf16[2,384,768]{2,1,0:T(8,128)(2,1)}, u32[]{:S(2)}, u32[]{:S(2)}) collective-permute-start(bf16[2,384,768]{2,1,0:T(8,128)(2,1)} %get-tuple-element.1089), channel_id=1, source_target_pairs={{0,2},{2,0},{4,6},{6,4},{1,3},{3,1},{5,7},{7,5},{8,10},{10,8},{12,... | collective-permute-start | bytes 3538952 | tf_op jit(solution)/shard_map/ppermute | solution.py:555
  410.7 7.1 %collective-permute-start.42 = (f32[2,1,768]{2,0,1:T(2,128)S(1)}, f32[2,1,768]{2,0,1:T(2,128)S(1)}, u32[]{:S(2)}, u32[]{:S(2)}) collective-permute-start(f32[2,1,768]{2,0,1:T(2,128)S(1)} %pad_maximum_fusion.1), channel_id=1, source_target_pairs={{0,2},{2,0},{4,6},{6,4},{1,3},{3,1},{5,7},{7,5},{8,10},{10,8},{12,... | collective-permute-start | bytes 18440 | tf_op jit(solution)/shard_map/ppermute | solution.py:555
  417.7 26.3 %collective-permute-start.28 = (bf16[2,384,768]{2,1,0:T(8,128)(2,1)}, bf16[2,384,768]{2,1,0:T(8,128)(2,1)}, u32[]{:S(2)}, u32[]{:S(2)}) collective-permute-start(bf16[2,384,768]{2,1,0:T(8,128)(2,1)} %get-tuple-element.1095), channel_id=1, source_target_pairs={{0,2},{2,0},{4,6},{6,4},{1,3},{3,1},{5,7},{7,5},{8,10},{10,8},{12,... | collective-permute-start | bytes 3538952 | tf_op jit(solution)/shard_map/ppermute | solution.py:555
  417.8 3.7 collective-permute-start.43
  421.5 3.7 collective-permute-start.44
  427.2 27.1 %collective-permute-start.32 = (bf16[384,768]{1,0:T(8,128)(2,1)S(1)}, bf16[384,768]{1,0:T(8,128)(2,1)S(1)}, u32[]{:S(2)}, u32[]{:S(2)}) collective-permute-start(bf16[384,768]{1,0:T(8,128)(2,1)S(1)} %fusion.14.refs_2_), channel_id=1, source_target_pairs={{0,4},{2,6},{4,0},{6,2},{1,5},{3,7},{5,1},{7,3},{8,12},{10,14},{12... | collective-permute-start | bytes 1769480 | tf_op jit(solution)/shard_map/ppermute | solution.py:555
  444.0 19.5 %collective-permute-start.25 = (bf16[2,384,768]{2,1,0:T(8,128)(2,1)}, bf16[2,384,768]{2,1,0:T(8,128)(2,1)S(1)}, u32[]{:S(2)}, u32[]{:S(2)}) collective-permute-start(bf16[2,384,768]{2,1,0:T(8,128)(2,1)} %get-tuple-element.1091), channel_id=1, source_target_pairs={{0,2},{2,0},{4,6},{6,4},{1,3},{3,1},{5,7},{7,5},{8,10},{10,8},{12,... | collective-permute-start | bytes 3538952 | tf_op jit(solution)/shard_map/ppermute | solution.py:555
  444.1 19.9 %slice-start = ((s8[12582912]{0:T(1024)(128)(4,1)}), s8[4194304]{0:T(1024)(128)(4,1)S(1)}, s32[]{:S(2)}) async-start(s8[12582912]{0:T(1024)(128)(4,1)} %bitcast.105), calls=%async_computation | async-start | bytes 8388608
  445.5 18.5 %slice-start.1 = ((s8[12582912]{0:T(1024)(128)(4,1)}), s8[4194304]{0:T(1024)(128)(4,1)S(1)}, s32[]{:S(2)}) async-start(s8[12582912]{0:T(1024)(128)(4,1)} %bitcast.105), calls=%async_computation.1 | async-start | bytes 8388608
  445.5 18.5 %slice-start.2 = ((s8[12582912]{0:T(1024)(128)(4,1)}), s8[4194304]{0:T(1024)(128)(4,1)S(1)}, s32[]{:S(2)}) async-start(s8[12582912]{0:T(1024)(128)(4,1)} %bitcast.105), calls=%async_computation.2 | async-start | bytes 8388608
  445.5 15.8 %collective-permute-start.36 = (bf16[384,768]{1,0:T(8,128)(2,1)S(1)}, bf16[384,768]{1,0:T(8,128)(2,1)S(1)}, u32[]{:S(2)}, u32[]{:S(2)}) collective-permute-start(bf16[384,768]{1,0:T(8,128)(2,1)S(1)} %fusion.16.refs_2_), channel_id=1, source_target_pairs={{0,4},{2,6},{4,0},{6,2},{1,5},{3,7},{5,1},{7,3},{8,12},{10,14},{12... | collective-permute-start | bytes 1769480 | tf_op jit(solution)/shard_map/ppermute | solution.py:555
  453.8 16.8 %collective-permute-start.29 = (bf16[2,384,768]{2,1,0:T(8,128)(2,1)}, bf16[2,384,768]{2,1,0:T(8,128)(2,1)S(1)}, u32[]{:S(2)}, u32[]{:S(2)}) collective-permute-start(bf16[2,384,768]{2,1,0:T(8,128)(2,1)} %get-tuple-element.1097), channel_id=1, source_target_pairs={{0,2},{2,0},{4,6},{6,4},{1,3},{3,1},{5,7},{7,5},{8,10},{10,8},{12,... | collective-permute-start | bytes 3538952 | tf_op jit(solution)/shard_map/ppermute | solution.py:555
  455.7 23.7 %collective-permute-start.40 = (bf16[384,768]{1,0:T(8,128)(2,1)S(1)}, bf16[384,768]{1,0:T(8,128)(2,1)S(1)}, u32[]{:S(2)}, u32[]{:S(2)}) collective-permute-start(bf16[384,768]{1,0:T(8,128)(2,1)S(1)} %fusion.7.refs_2_), channel_id=1, source_target_pairs={{0,1},{1,0},{2,3},{3,2},{4,5},{5,4},{6,7},{7,6},{8,9},{9,8},{10,11... | collective-permute-start | bytes 1769480 | tf_op jit(solution)/shard_map/ppermute | solution.py:555
  462.5 21.2 %collective-permute-start.41 = (bf16[384,768]{1,0:T(8,128)(2,1)S(1)}, bf16[384,768]{1,0:T(8,128)(2,1)S(1)}, u32[]{:S(2)}, u32[]{:S(2)}) collective-permute-start(bf16[384,768]{1,0:T(8,128)(2,1)S(1)} %fusion.5.refs_2_), channel_id=1, source_target_pairs={{0,1},{1,0},{2,3},{3,2},{4,5},{5,4},{6,7},{7,6},{8,9},{9,8},{10,11... | collective-permute-start | bytes 1769480 | tf_op jit(solution)/shard_map/ppermute | solution.py:555
  463.6 30.4 %collective-permute-start.26 = (bf16[384,768]{1,0:T(8,128)(2,1)S(1)}, bf16[384,768]{1,0:T(8,128)(2,1)}, u32[]{:S(2)}, u32[]{:S(2)}) collective-permute-start(bf16[384,768]{1,0:T(8,128)(2,1)S(1)} %fusion.15.refs_1_), channel_id=1, source_target_pairs={{0,4},{2,6},{4,0},{6,2},{1,5},{3,7},{5,1},{7,3},{8,12},{10,14},{12... | collective-permute-start | bytes 1769480 | tf_op jit(solution)/shard_map/ppermute | solution.py:555
  470.6 25.9 %collective-permute-start.33 = (bf16[2,384,768]{2,1,0:T(8,128)(2,1)}, bf16[2,384,768]{2,1,0:T(8,128)(2,1)}, u32[]{:S(2)}, u32[]{:S(2)}) collective-permute-start(bf16[2,384,768]{2,1,0:T(8,128)(2,1)} %get-tuple-element.1101), channel_id=1, source_target_pairs={{0,2},{2,0},{4,6},{6,4},{1,3},{3,1},{5,7},{7,5},{8,10},{10,8},{12,... | collective-permute-start | bytes 3538952 | tf_op jit(solution)/shard_map/ppermute | solution.py:555
  470.8 20.2 %collective-permute-start.30 = (bf16[384,768]{1,0:T(8,128)(2,1)S(1)}, bf16[384,768]{1,0:T(8,128)(2,1)}, u32[]{:S(2)}, u32[]{:S(2)}) collective-permute-start(bf16[384,768]{1,0:T(8,128)(2,1)S(1)} %fusion.17.refs_1_), channel_id=1, source_target_pairs={{0,4},{2,6},{4,0},{6,2},{1,5},{3,7},{5,1},{7,3},{8,12},{10,14},{12... | collective-permute-start | bytes 1769480 | tf_op jit(solution)/shard_map/ppermute | solution.py:555
  479.4 19.4 %collective-permute-start.37 = (bf16[2,384,768]{2,1,0:T(8,128)(2,1)}, bf16[2,384,768]{2,1,0:T(8,128)(2,1)}, u32[]{:S(2)}, u32[]{:S(2)}) collective-permute-start(bf16[2,384,768]{2,1,0:T(8,128)(2,1)} %get-tuple-element.1103), channel_id=1, source_target_pairs={{0,2},{2,0},{4,6},{6,4},{1,3},{3,1},{5,7},{7,5},{8,10},{10,8},{12,... | collective-permute-start | bytes 3538952 | tf_op jit(solution)/shard_map/ppermute | solution.py:555
  492.7 16.3 %collective-permute-start.31 = (bf16[384,768]{1,0:T(8,128)(2,1)S(1)}, bf16[384,768]{1,0:T(8,128)(2,1)S(1)}, u32[]{:S(2)}, u32[]{:S(2)}) collective-permute-start(bf16[384,768]{1,0:T(8,128)(2,1)S(1)} %fusion.8), channel_id=1, source_target_pairs={{0,1},{1,0},{2,3},{3,2},{4,5},{5,4},{6,7},{7,6},{8,9},{9,8},{10,11... | collective-permute-start | bytes 1769480 | tf_op jit(solution)/shard_map/ppermute | solution.py:555
  495.6 23.5 %collective-permute-start.27 = (bf16[384,768]{1,0:T(8,128)(2,1)S(1)}, bf16[384,768]{1,0:T(8,128)(2,1)S(1)}, u32[]{:S(2)}, u32[]{:S(2)}) collective-permute-start(bf16[384,768]{1,0:T(8,128)(2,1)S(1)} %fusion.9), channel_id=1, source_target_pairs={{0,1},{1,0},{2,3},{3,2},{4,5},{5,4},{6,7},{7,6},{8,9},{9,8},{10,11... | collective-permute-start | bytes 1769480 | tf_op jit(solution)/shard_map/ppermute | solution.py:555
  498.5 22.2 %collective-permute-start.34 = (bf16[384,768]{1,0:T(8,128)(2,1)}, bf16[384,768]{1,0:T(8,128)(2,1)}, u32[]{:S(2)}, u32[]{:S(2)}) collective-permute-start(bf16[384,768]{1,0:T(8,128)(2,1)} %fusion.18), channel_id=1, source_target_pairs={{0,4},{2,6},{4,0},{6,2},{1,5},{3,7},{5,1},{7,3},{8,12},{10,14},{12... | collective-permute-start | bytes 1769480 | tf_op jit(solution)/shard_map/ppermute | solution.py:555
  500.9 23.8 %collective-permute-start.38 = (bf16[384,768]{1,0:T(8,128)(2,1)}, bf16[384,768]{1,0:T(8,128)(2,1)}, u32[]{:S(2)}, u32[]{:S(2)}) collective-permute-start(bf16[384,768]{1,0:T(8,128)(2,1)} %fusion.19), channel_id=1, source_target_pairs={{0,4},{2,6},{4,0},{6,2},{1,5},{3,7},{5,1},{7,3},{8,12},{10,14},{12... | collective-permute-start | bytes 1769480 | tf_op jit(solution)/shard_map/ppermute | solution.py:555
  523.4 16.4 %collective-permute-start.35 = (bf16[384,768]{1,0:T(8,128)(2,1)S(1)}, bf16[384,768]{1,0:T(8,128)(2,1)}, u32[]{:S(2)}, u32[]{:S(2)}) collective-permute-start(bf16[384,768]{1,0:T(8,128)(2,1)S(1)} %fusion.6), channel_id=1, source_target_pairs={{0,1},{1,0},{2,3},{3,2},{4,5},{5,4},{6,7},{7,6},{8,9},{9,8},{10,11... | collective-permute-start | bytes 1769480 | tf_op jit(solution)/shard_map/ppermute | solution.py:555
  526.2 23.0 %collective-permute-start.39 = (bf16[384,768]{1,0:T(8,128)(2,1)S(1)}, bf16[384,768]{1,0:T(8,128)(2,1)}, u32[]{:S(2)}, u32[]{:S(2)}) collective-permute-start(bf16[384,768]{1,0:T(8,128)(2,1)S(1)} %fusion.4), channel_id=1, source_target_pairs={{0,1},{1,0},{2,3},{3,2},{4,5},{5,4},{6,7},{7,6},{8,9},{9,8},{10,11... | collective-permute-start | bytes 1769480 | tf_op jit(solution)/shard_map/ppermute | solution.py:555
  (45 other events, 171.4 us)

commit v4 on v3

--- a/solution.py
+++ b/solution.py
@@ -202,7 +202,7 @@
 
 def forward_opening(delta, n, rows, *refs):
     ins, refs = refs[:11], refs[11:]
-    outs, kept, scratch, load_sems = refs[:16], refs[16:24], refs[24:-1], refs[-1]
+    outs, kept, scratch, load_sems = refs[:16], refs[16:25], refs[25:-1], refs[-1]
     tok, cos, sin, *weights, gb = ins[3:]
     tok_v, _, _, *weights_v = kept[:7]
     head, tail = pl.ds(0, rows), pl.ds(rows, (n - 1) * rows)
@@ -214,8 +214,8 @@
 
 
 def forward_next(delta, n, rows, *refs):
-    t, meta, arr, tok = refs[:4]
-    forward_kernel(delta, n, rows, t, meta, tok, arr, *refs[4:12], *refs[26:42], *refs[50:])
+    t, meta, arr, tok, cos, sin, wq, wo, wu, wd, gb, _, s_in = refs[:13]
+    forward_kernel(delta, n, rows, t, meta, tok, arr, cos, sin, wq, wo, wu, wd, gb, s_in, *refs[27:43], *refs[52:])
 
 
 def saved_items(rows):
@@ -225,10 +225,10 @@
 
 def kept_items(every):
     return [((every, D), bf), ((every, 128), f32), ((every, 128), f32), ((D, 3 * D), bf), ((D, D), bf), ((D, 4 * D), bf), ((4 * D, D), bf),
-            ((4, D), f32)]
-
-
-def forward_call(rows, n, delta, opening, limit=20):
+            ((4, D), f32), ((TILES, every, TILE), bf)]
+
+
+def forward_call(rows, n, delta, opening, limit=19):
     V = pl.BlockSpec(memory_space=pltpu.VMEM)
     S = pl.BlockSpec(memory_space=pltpu.SMEM)
     A = pl.BlockSpec(memory_space=pl.ANY)
@@ -239,11 +239,11 @@
     big[13] = pltpu.HBM((n, PAIRS, 256, 256), bf)
     aliases = {4: 17, 5: 18, 10: 23}
     if not opening:
-        aliases = {11: 1, **{12 + i: 2 + i for i in range(14)}, **{3 + i: 16 + i for i in range(8)}}
+        aliases = {12: 1, **{13 + i: 2 + i for i in range(14)}, **{3 + i: 16 + i for i in range(9)}}
     return pl.pallas_call(
         functools.partial(forward_opening if opening else forward_next, delta, n, rows),
-        in_specs=[S, S, V, A, V, V, A, A, A, A, V] if opening else [S, S] + [V] * 10 + [A] * 14,
-        out_specs=[V, V] + [A] * 14 + [V] * 8,
+        in_specs=[S, S, V, A, V, V, A, A, A, A, V] if opening else [S, S] + [V] * 11 + [A] * 14,
+        out_specs=[V, V] + [A] * 14 + [V] * 9,
         out_shape=[sd((rows, D), bf), sd((PAIRS, 256, 256), f32)] + big + [pltpu.VMEM(*item) for item in kept_items(every)],
         scratch_shapes=[pltpu.VMEM(*item) for item in saved_items(rows)] + [pltpu.SemaphoreType.DMA((30,))] + [pltpu.SemaphoreType.DMA((6,))] * opening,
         input_output_aliases=aliases,
@@ -421,20 +421,33 @@
 
 def backward_opening(delta, n, rows, stages, groups, *refs):
     t, meta, arr = refs[:3]
-    cot, cot_v, load_sems, refs = refs[21], refs[29], refs[-1], refs[:-1]
+    cot, cot_v, load_sems, refs = refs[22], refs[30], refs[-1], refs[:-1]
     head, tail = pl.ds((n - 1) * rows, rows), pl.ds(0, (n - 1) * rows)
     loads = [pltpu.make_async_copy(cot.at[part, :], cot_v.at[part, :], load_sems.at[i]) for i, part in enumerate((head, tail))]
     for copy in loads:
         copy.start()
-    backward_kernel(delta, n, rows, stages, groups, t, meta, cot_v, arr, *refs[4:11], None, None, *refs[11:21], *refs[22:29], *refs[37:], loads=loads)
+    backward_kernel(delta, n, rows, stages, groups, t, meta, cot_v, arr, *refs[4:11], None, None, *refs[12:22], *refs[23:30], *refs[39:], loads=loads)
 
 
 def backward_next(delta, n, rows, stages, groups, *refs):
     t, meta, arr, cot = refs[:4]
-    backward_kernel(delta, n, rows, stages, groups, t, meta, cot, arr, *refs[4:23], *refs[27:34], *refs[42:])
-
-
-def backward_call(rows, n, delta, stages, groups, opening, limit=20):
+    act, act_v, sem, refs = refs[28], refs[44], refs[-1], refs[:-1]
+    fill = (t[0] >= 1) & (t[0] <= TILES)
+    tile = jnp.clip(t[0] - 1, 0, TILES - 1)
+    copy = pltpu.make_async_copy(act.at[tile], act_v.at[tile], sem)
+
+    @pl.when(fill)
+    def _():
+        copy.start()
+
+    backward_kernel(delta, n, rows, stages, groups, t, meta, cot, arr, *refs[4:11], *refs[12:24], *refs[29:36], *refs[45:])
+
+    @pl.when(fill)
+    def _():
+        copy.wait()
+
+
+def backward_call(rows, n, delta, stages, groups, opening, limit=19):
     V = pl.BlockSpec(memory_space=pltpu.VMEM)
     S = pl.BlockSpec(memory_space=pltpu.SMEM)
     A = pl.BlockSpec(memory_space=pl.ANY)
@@ -446,17 +459,17 @@
     own = [((rows, 3 * D), bf), ((rows, D), bf), ((rows, D), bf)]
     big = [pltpu.HBM((every, D), bf), pltpu.HBM((TILES, every, TILE), bf), pltpu.HBM((TILES, every, TILE), bf), pltpu.HBM((every, D), bf)]
     if opening:
-        aliases = {3 + i: 7 + i for i in range(8)}
+        aliases = {3 + i: 7 + i for i in range(9)}
     else:
-        aliases = {**{3 + i: 7 + i for i in range(8)}, 11: 1, 12: 2, **{23 + i: 3 + i for i in range(4)}}
+        aliases = {**{3 + i: 7 + i for i in range(9)}, 12: 1, 13: 2, **{24 + i: 3 + i for i in range(4)}}
     return pl.pallas_call(
         functools.partial(backward_opening if opening else backward_next, delta, n, rows, stages, groups),
-        in_specs=[S, S] + [V] * 9 + [A] * 11 if opening else [S, S] + [V] * 11 + [A] * 14,
-        out_specs=[V] * 3 + [A] * 4 + [V] * 8,
+        in_specs=[S, S] + [V] * 10 + [A] * 11 if opening else [S, S] + [V] * 12 + [A] * 15,
+        out_specs=[V] * 3 + [A] * 4 + [V] * 9,
         out_shape=[sd((rows, D), bf), sd((PAIRS, 256, 256), f32), sd((8, D), f32)] + big
         + [pltpu.VMEM(*item) for item in kept_items(every)],
         scratch_shapes=[pltpu.VMEM(*item) for item in made + own + saved] + [pltpu.SemaphoreType.DMA((30,)), pltpu.SemaphoreType.DMA((13,))]
-        + [pltpu.SemaphoreType.DMA((2,))] * opening,
+        + [pltpu.SemaphoreType.DMA((2,)) if opening else pltpu.SemaphoreType.DMA],
         input_output_aliases=aliases,
         cost_estimate=pl.CostEstimate(flops=rows * 2 * 10 * 10**6, bytes_accessed=4 * 2**20, transcendentals=0),
         compiler_params=pltpu.CompilerParams(vmem_limit_bytes=limit * 2**20),
@@ -467,27 +480,31 @@
 HALF = D // 2
 
 
-def weight_kernel(groups, half, mixed, waits, fetch, meta_ref, left, *refs):
+def weight_kernel(groups, half, mixed, waits, fetch, ahead, meta_ref, left, *refs):
     raws, refs = refs[:1 + mixed], refs[1 + mixed + waits:]
+    sources, refs = refs[:ahead], refs[ahead:]
     keep_o, send_o, refs = refs[0], refs[1], refs[2:]
-    kept, (turned, out_buf, out_sem, *load_sems) = refs[:2 * fetch], refs[2 * fetch:]
+    kept, refs = refs[:fetch], refs[fetch:]
+    targets, refs = refs[:ahead], refs[ahead:]
+    turned, out_buf, out_sem, raw_sem, ahead_sem = refs
     me = meta_ref[1]
     share = TILES // groups
-    raw_copies, left_copies = [], []
+    every = raws[0].shape[0]
+    raw_copies, later = [], []
     if fetch:
-        left_v, raw_v = kept
-        raw_copies = [pltpu.make_async_copy(raws[0].at[k:k + 256, :], raw_v.at[k:k + 256, :], load_sems[0].at[k // 256]) for k in range(0, raw_v.shape[0], 256)]
-        left_copies = [pltpu.make_async_copy(left.at[i], left_v.at[i], load_sems[1].at[i]) for i in range(TILES)]
-        for copy in raw_copies + left_copies:
-            copy.start()
-        left, raws = left_v, (raw_v,)
+        raw_copies = [pltpu.make_async_copy(raws[0].at[k:k + 256, :], kept[0].at[k:k + 256, :], raw_sem.at[k // 256]) for k in range(0, every, 256)]
+        raws = kept
+    for source, target in zip(sources, targets):
+        step = 1 if len(source.shape) == 3 else every // 4
+        for k in range(0, source.shape[0], step):
+            later.append(pltpu.make_async_copy(source.at[k:k + step], target.at[k:k + step], ahead_sem.at[len(later)]))
+    for copy in raw_copies + later:
+        copy.start()
     for j, raw in enumerate(raws):
-        for k in range(0, raw.shape[0], 256):
+        for k in range(0, every, 256):
             if fetch:
                 raw_copies[k // 256].wait()
             turned[j, :, k:k + 256] = raw[k:k + 256, half * HALF:(half + 1) * HALF].T
-    for copy in left_copies:
-        copy.wait()
     for g in range(groups):
         for i in range(share):
             cols = slice(i * TILE, (i + 1) * TILE)
@@ -507,20 +524,22 @@
         def _():
             pltpu.make_async_copy(out_buf.at[g], send_o.at[rel >> 1], out_sem).start()
     pltpu.make_async_copy(out_buf, out_buf, out_sem).wait()
-
-
-def weight_call(every, groups, half, mixed, waits, fetch, limit=12):
+    for copy in later:
+        copy.wait()
+
+
+def weight_call(every, groups, half, mixed, waits, fetch, ahead, limit=12):
     V = pl.BlockSpec(memory_space=pltpu.VMEM)
     S = pl.BlockSpec(memory_space=pltpu.SMEM)
     A = pl.BlockSpec(memory_space=pl.ANY)
     raws = 1 + mixed
     return pl.pallas_call(
-        functools.partial(weight_kernel, groups, half, mixed, waits, fetch),
-        in_specs=[S] + [A if fetch else V] * (1 + raws) + [A] * waits,
-        out_specs=[A] * 2 + [V] * 2 * fetch,
-        out_shape=[pltpu.HBM((2, HALF, D), bf)] * 2 + [pltpu.VMEM((TILES, every, TILE), bf), pltpu.VMEM((every, D), bf)] * fetch,
-        scratch_shapes=[pltpu.VMEM((raws, HALF, every), bf), pltpu.VMEM((groups, HALF, D), bf), pltpu.SemaphoreType.DMA]
-        + [pltpu.SemaphoreType.DMA((every // 256,)), pltpu.SemaphoreType.DMA((TILES,))] * fetch,
+        functools.partial(weight_kernel, groups, half, mixed, waits, fetch, len(ahead)),
+        in_specs=[S, V] + [A if fetch else V] * raws + [A] * (waits + len(ahead)),
+        out_specs=[A] * 2 + [V] * (fetch + len(ahead)),
+        out_shape=[pltpu.HBM((2, HALF, D), bf)] * 2 + [pltpu.VMEM((every, D), bf)] * fetch + [pltpu.VMEM(shape, bf) for shape in ahead],
+        scratch_shapes=[pltpu.VMEM((raws, HALF, every), bf), pltpu.VMEM((groups, HALF, D), bf), pltpu.SemaphoreType.DMA,
+                        pltpu.SemaphoreType.DMA((every // 256,)), pltpu.SemaphoreType.DMA((24,))],
         cost_estimate=pl.CostEstimate(flops=2 * every * HALF * 4 * D, bytes_accessed=every * 5 * D * 2, transcendentals=0),
         compiler_params=pltpu.CompilerParams(vmem_limit_bytes=limit * 2**20),
         name="weight_grad",
@@ -555,14 +574,49 @@
     return lax.ppermute(block, axis, route)
 
 
-def reduced(keep, send, wire):
+def add_kernel(*refs):
+    total = sum(ref[...].reshape(refs[-1].shape).astype(f32) for ref in refs[:-1])
+    refs[-1][...] = total.astype(refs[-1].dtype)
+
+
+def add_call(slot, keep, got, *more, limit=12):
+    rows, columns = keep.shape[1:]
+    step = min(rows, 192)
+    pick = pl.BlockSpec((1, step, columns), lambda i: (slot, i, 0))
+    flat = pl.BlockSpec((step, columns), lambda i: (i, 0))
+    return pl.pallas_call(
+        add_kernel,
+        grid=(rows // step,),
+        in_specs=[pick, pick] + [flat] * len(more),
+        out_specs=flat,
+        out_shape=jax.ShapeDtypeStruct((rows, columns), keep.dtype),
+        cost_estimate=pl.CostEstimate(flops=rows * columns * 2, bytes_accessed=rows * columns * 6, transcendentals=0),
+        compiler_params=pltpu.CompilerParams(vmem_limit_bytes=limit * 2**20),
+        name="add_parts",
+    )(keep, got, *more)
+
+
+def reduced(keep, send, before):
     got = exchange(send, "group", 1)
-    away = lax.optimization_barrier((keep[1].astype(f32) + got[1].astype(f32)).astype(wire))
+    away = add_call(1, keep, got)
+    if before:
+        before[0], away = lax.optimization_barrier((before[0], away))
     back = exchange(away, "group", 2)
-    own = lax.optimization_barrier((keep[0].astype(f32) + got[0].astype(f32) + back.astype(f32)).astype(wire))
+    return [back, keep, got, away]
+
+
+def spread(own, before):
+    if lax.axis_size("dp") != 2:
+        return lax.psum(own, "dp")
+    if before:
+        before[-1], own = lax.optimization_barrier((before[-1], own))
+    return exchange(own, "dp", 1)
+
+
+def finished(own, other):
     if lax.axis_size("dp") == 2:
-        return away, own, own.astype(f32) + exchange(own, "dp", 1).astype(f32)
-    return away, own, lax.psum(own, "dp").astype(f32)
+        return own.astype(f32) + other.astype(f32)
+    return other.astype(f32)
 
 
 def local(tokens, doc_ids, cotangent, w_qkv, w_out, w_up, w_down,
@@ -592,27 +646,37 @@
     for t in range(ticks):
         made = backward_call(ROWS, n, DELTA, stages, groups, t == 0)(
             jnp.full((1,), t, jnp.int32), meta, arriving.pop(0), *resident, *state,
-            *far((n2, rs, gp, n1, att, v, qn, kf, sg, sb)), *big, *far([cotangent] * (t == 0)))
+            *far((n2, rs, gp, n1, att, v, qn, kf, sg, sb)), *big, *far([act if t > 0 else cotangent]))
         state, big, resident = made[1:3], made[3:7], made[7:]
         route = [(a, a - 1) for a in range(1, stages) if 0 <= t - (stages - 1 - a) * DELTA < n]
         arriving.append(lax.ppermute(made[0], "pipe", route) if route else made[0])
     df, du, de, input_grad = big
-    aways, owns, parts = [], [], []
-    for left, rights in ((act, (df,)), (de, (x, att)), (du, (hb,))):
+    act = resident[8]
+    pieces = [(act, df), (de, x, att), (du, hb)]
+    waiting, owns, others, keeps = [], [], [], []
+    for piece in range(3):
+        left, *rights = pieces[piece]
         for half in range(2):
-            waits = aways[-2:-1] + owns[-4:-3]
-            fetch = not parts
-            operands = far((left,) + rights) if fetch else (left,) + rights
-            keep, send, *loaded = weight_call(n * ROWS, groups, half, len(rights) == 2, len(waits), fetch)(meta, *operands, *waits)
-            if fetch:
-                left, rights = loaded[0], tuple(loaded[1:])
-            away, own, part = reduced(keep, send, bf)
-            aways.append(away)
-            owns.append(own)
-            parts.append(part)
-    vectors = state[1][:4].reshape(4, groups, D // groups).swapaxes(0, 1).reshape(groups, 1, D)
+            fetch = not keeps
+            ready = {2: 1, 4: 2, 5: 3}.get(len(keeps))
+            waits = [] if ready is None else [waiting[ready][3]]
+            call = weight_call(n * ROWS, groups, half, len(rights) == 2, len(waits), fetch, [])
+            keep, send, *loads = call(meta, left, *(far(rights) if fetch else rights), *waits)
+            rights = loads if fetch else rights
+            keeps.append(keep)
+            waiting.append(reduced(keep, send, waiting[-1] if waiting else None))
+    for back, keep, got, _ in waiting:
+        own = add_call(0, keep, got, back)
+        other = spread(own, others)
+        owns.append(own)
+        others.append(other)
+    parts = [finished(*pair) for pair in zip(owns, others)]
+    vectors, me, _ = lax.optimization_barrier((state[1], me, owns[3]))
+    vectors = vectors[:4].reshape(4, groups, D // groups).swapaxes(0, 1).reshape(groups, 1, D)
     ordered = [lax.dynamic_index_in_dim(vectors, me ^ rel, 0, keepdims=False) for rel in range(4)]
-    mine = reduced(jnp.stack(ordered[0::2]), jnp.stack(ordered[1::2]), f32)[2].reshape(4, D // groups)
+    small = reduced(jnp.stack(ordered[0::2]), jnp.stack(ordered[1::2]), None)
+    own = add_call(0, *small[1:3], small[0])
+    mine = finished(own, spread(own, [])).reshape(4, D // groups)
     g_down, g_mixed, g_up = (jnp.concatenate(parts[i:i + 2], axis=0) for i in (0, 2, 4))
     odd = (me & 1) == 1
     swap = lambda a, b: jnp.concatenate([g_mixed[:, a], g_mixed[:, b]], axis=1)

time: 561 us -> 508 us (0.906)
  local copies, waits for them, and re-layouts: 65.1 us -> 13.5 us
  Pallas kernels: 299 us -> 310 us
    unnamed x101 -> x49, local copies, waits for them, and re-layouts: 62.4 us -> 10.8 us
    convert_element_type x12 -> x0, other arithmetic: 16 us -> none  [the longest x6 8.9 us: reduced(): (keep[0].astype(f32) + got[0].astype(f32) + back.astype(f32)).astype(wire)]
    pallas_call x6 -> x20, Pallas kernels: 48.4 us -> 55.9 us  [the longest x6 45.9 us: local(): call(meta, left, *(far(rights) if fetch else rights), *waits)]
  transfers between devices with their start and end apart: 45 -> 45, of which waited for: 17 -> 18; matrix products, arithmetic and copies ran while one was open for 5% -> 5% of each run, Pallas kernels for 45% -> 51%
where the time goes in v4:
time: 508 us; the launch traced here: 502 us
  Pallas kernels  310 us (61%)
  waiting for transfers between devices  112 us (22%)
  starting transfers between devices  45.4 us (9%)
  other arithmetic  19 us (4%)
  local copies, waits for them, and re-layouts  13.5 us (3%)
    pallas_call x14, Pallas kernels, local(): backward_call(ROWS, n, DELTA, stages, groups, t == 0)  147 us
    pallas_call x14, Pallas kernels, local(): forward_call(ROWS, n, DELTA, t == 0)  107 us
    ppermute x24, waiting for transfers between devices, local(): arriving.append(lax.ppermute(made[0], 'pipe', route) if route else made[0])  64.6 us
    ppermute x21, waiting for transfers between devices, exchange(): return lax.ppermute(block, axis, route)  47.2 us
    pallas_call x6, Pallas kernels, local(): call(meta, left, *(far(rights) if fetch else rights), *waits)  45.9 us
    ppermute x24, starting transfers between devices, local(): arriving.append(lax.ppermute(made[0], 'pipe', route) if route else made[0])  30.5 us
    ppermute x21, starting transfers between devices, exchange(): return lax.ppermute(block, axis, route)  14.9 us
    unnamed x49, local copies, waits for them, and re-layouts  10.8 us
  transfers between devices with their start and end apart: 45, of which 18 were waited for; matrix products, arithmetic and copies ran while one was open for 5% of the time, Pallas kernels for 51%

profile of v4, /device:TPU:0, one launch (start us, length us, event | category | flops | bytes accessed | tf_op | source)
XLA Modules:
  0.0 501.6 jit_solution(5905534109977096595)
XLA Ops:
  4.2 11.6 %layer_forward.14 = (bf16[256,768]{1,0:T(8,128)(2,1)S(1)}, f32[6,256,256]{2,1,0:T(8,128)S(1)}, bf16[2048,768]{1,0:T(8,128)(2,1)}, bf16[2048,768]{1,0:T(8,128)(2,...) custom-call(s32[1]{0:T(128)} %constant.45.clone.1.refs_0_, ...), custom_call_target="tpu_custom_call", output_to_operand_aliasing={{17}: (4, {}), {18}: (5, {}), {23}: (10, {})} | custom-call | flops 4608000000 | bytes 4194304 | tf_op jit(solution)/shard_map/layer_forward/pallas_call | solution.py:639
  17.2 9.8 %layer_forward.15 = (bf16[256,768]{1,0:T(8,128)(2,1)S(1)}, f32[6,256,256]{2,1,0:T(8,128)S(1)}, bf16[2048,768]{1,0:T(8,128)(2,1)}, bf16[2048,768]{1,0:T(8,128)(2,...) custom-call(s32[1]{0:T(128)} %constant.28.clone.1.refs_0_, ...), custom_call_target="tpu_custom_call", output_to_operand_aliasing={{1}: (12, {}), {2}: (13, {}), {3}: (14, {}), {4}: (15, {}),... | custom-call | flops 4608000000 | bytes 4194304 | tf_op jit(solution)/shard_map/layer_forward/pallas_call | solution.py:639
  28.2 9.3 %layer_forward.16 = (bf16[256,768]{1,0:T(8,128)(2,1)S(1)}, f32[6,256,256]{2,1,0:T(8,128)S(1)}, bf16[2048,768]{1,0:T(8,128)(2,1)}, bf16[2048,768]{1,0:T(8,128)(2,...) custom-call(s32[1]{0:T(128)} %constant.76.clone.1.refs_0_, ...), custom_call_target="tpu_custom_call", output_to_operand_aliasing={{1}: (12, {}), {2}: (13, {}), {3}: (14, {}), {4}: (15, {}),... | custom-call | flops 4608000000 | bytes 4194304 | tf_op jit(solution)/shard_map/layer_forward/pallas_call | solution.py:639
  37.6 2.4 collective-permute-start.3
  40.0 9.9 %layer_forward.17 = (bf16[256,768]{1,0:T(8,128)(2,1)S(1)}, f32[6,256,256]{2,1,0:T(8,128)S(1)}, bf16[2048,768]{1,0:T(8,128)(2,1)}, bf16[2048,768]{1,0:T(8,128)(2,...) custom-call(s32[1]{0:T(128)} %constant.27.clone.1.refs_0_, ...), custom_call_target="tpu_custom_call", output_to_operand_aliasing={{1}: (12, {}), {2}: (13, {}), {3}: (14, {}), {4}: (15, {}),... | custom-call | flops 4608000000 | bytes 4194304 | tf_op jit(solution)/shard_map/layer_forward/pallas_call | solution.py:639
  51.8 9.2 %layer_forward.18 = (bf16[256,768]{1,0:T(8,128)(2,1)S(1)}, f32[6,256,256]{2,1,0:T(8,128)S(1)}, bf16[2048,768]{1,0:T(8,128)(2,1)}, bf16[2048,768]{1,0:T(8,128)(2,...) custom-call(s32[1]{0:T(128)} %constant.77.clone.1.refs_0_, ...), custom_call_target="tpu_custom_call", output_to_operand_aliasing={{1}: (12, {}), {2}: (13, {}), {3}: (14, {}), {4}: (15, {}),... | custom-call | flops 4608000000 | bytes 4194304 | tf_op jit(solution)/shard_map/layer_forward/pallas_call | solution.py:639
  61.1 2.0 collective-permute-start.5
  63.1 9.7 %layer_forward.19 = (bf16[256,768]{1,0:T(8,128)(2,1)S(1)}, f32[6,256,256]{2,1,0:T(8,128)S(1)}, bf16[2048,768]{1,0:T(8,128)(2,1)}, bf16[2048,768]{1,0:T(8,128)(2,...) custom-call(s32[1]{0:T(128)} %constant.26.clone.1.refs_0_, ...), custom_call_target="tpu_custom_call", output_to_operand_aliasing={{1}: (12, {}), {2}: (13, {}), {3}: (14, {}), {4}: (15, {}),... | custom-call | flops 4608000000 | bytes 4194304 | tf_op jit(solution)/shard_map/layer_forward/pallas_call | solution.py:639
  74.8 9.2 %layer_forward.20 = (bf16[256,768]{1,0:T(8,128)(2,1)S(1)}, f32[6,256,256]{2,1,0:T(8,128)S(1)}, bf16[2048,768]{1,0:T(8,128)(2,1)}, bf16[2048,768]{1,0:T(8,128)(2,...) custom-call(s32[1]{0:T(128)} %constant.78.clone.1.refs_0_, ...), custom_call_target="tpu_custom_call", output_to_operand_aliasing={{1}: (12, {}), {2}: (13, {}), {3}: (14, {}), {4}: (15, {}),... | custom-call | flops 4608000000 | bytes 4194304 | tf_op jit(solution)/shard_map/layer_forward/pallas_call | solution.py:639
  85.9 9.9 %layer_forward.21 = (bf16[256,768]{1,0:T(8,128)(2,1)S(1)}, f32[6,256,256]{2,1,0:T(8,128)S(1)}, bf16[2048,768]{1,0:T(8,128)(2,1)}, bf16[2048,768]{1,0:T(8,128)(2,...) custom-call(s32[1]{0:T(128)} %constant.40.clone.1.refs_0_, ...), custom_call_target="tpu_custom_call", output_to_operand_aliasing={{1}: (12, {}), {2}: (13, {}), {3}: (14, {}), {4}: (15, {}),... | custom-call | flops 4608000000 | bytes 4194304 | tf_op jit(solution)/shard_map/layer_forward/pallas_call | solution.py:639
  99.4 6.7 %collective-permute-done.6.refs_2_ = bf16[256,768]{1,0:T(8,128)(2,1)S(1)} collective-permute-done((bf16[256,768]{1,0:T(8,128)(2,1)S(1)}, bf16[256,768]{1,0:T(8,128)(2,1)S(1)}, u32[]{:S(2)}, u32[]{:S(2)}) %collective-permute-start.6) | collective-permute-done | bytes 393248 | tf_op jit(solution)/shard_map/ppermute | solution.py:642
  106.1 6.8 %layer_forward.23 = (bf16[256,768]{1,0:T(8,128)(2,1)S(1)}, f32[6,256,256]{2,1,0:T(8,128)S(1)}, bf16[2048,768]{1,0:T(8,128)(2,1)}, bf16[2048,768]{1,0:T(8,128)(2,...) custom-call(s32[1]{0:T(128)} %constant.39.clone.1.refs_0_, ...), custom_call_target="tpu_custom_call", output_to_operand_aliasing={{1}: (12, {}), {2}: (13, {}), {3}: (14, {}), {4}: (15, {}),... | custom-call | flops 4608000000 | bytes 4194304 | tf_op jit(solution)/shard_map/layer_forward/pallas_call | solution.py:639
  115.2 8.7 %layer_forward.25 = (bf16[256,768]{1,0:T(8,128)(2,1)S(1)}, f32[6,256,256]{2,1,0:T(8,128)S(1)}, bf16[2048,768]{1,0:T(8,128)(2,1)}, bf16[2048,768]{1,0:T(8,128)(2,...) custom-call(s32[1]{0:T(128)} %constant.38.clone.1.refs_0_, ...), custom_call_target="tpu_custom_call", output_to_operand_aliasing={{1}: (12, {}), {2}: (13, {}), {3}: (14, {}), {4}: (15, {}),... | custom-call | flops 4608000000 | bytes 4194304 | tf_op jit(solution)/shard_map/layer_forward/pallas_call | solution.py:639
  126.2 9.5 %layer_forward.27 = (bf16[256,768]{1,0:T(8,128)(2,1)S(1)}, f32[6,256,256]{2,1,0:T(8,128)S(1)}, bf16[2048,768]{1,0:T(8,128)(2,1)}, bf16[2048,768]{1,0:T(8,128)(2,...) custom-call(s32[1]{0:T(128)} %constant.21.clone.1.refs_0_, ...), custom_call_target="tpu_custom_call", output_to_operand_aliasing={{1}: (12, {}), {2}: (13, {}), {3}: (14, {}), {4}: (15, {}),... | custom-call | flops 4608000000 | bytes 4194304 | tf_op jit(solution)/shard_map/layer_forward/pallas_call | solution.py:639
  135.8 2.9 layer_backward.14
  139.4 9.6 %layer_backward.15 = (bf16[256,768]{1,0:T(8,128)(2,1)S(1)}, f32[6,256,256]{2,1,0:T(8,128)S(1)}, f32[8,768]{1,0:T(8,128)S(1)}, bf16[2048,768]{1,0:T(8,128)(2,1)},...) custom-call(s32[1]{0:T(128)} %constant.28.clone.1.refs_0_, ...), custom_call_target="tpu_custom_call", output_to_operand_aliasing={{7}: (3, {}), {8}: (4, {}), {9}: (5, {}), {10}: (6, {}), {1... | custom-call | flops 5120000000 | bytes 4194304 | tf_op jit(solution)/shard_map/layer_backward/pallas_call | solution.py:647
  149.7 2.2 layer_backward.16
  152.6 9.3 %layer_backward.17 = (bf16[256,768]{1,0:T(8,128)(2,1)S(1)}, f32[6,256,256]{2,1,0:T(8,128)S(1)}, f32[8,768]{1,0:T(8,128)S(1)}, bf16[2048,768]{1,0:T(8,128)(2,1)},...) custom-call(s32[1]{0:T(128)} %constant.27.clone.1.refs_0_, ...), custom_call_target="tpu_custom_call", output_to_operand_aliasing={{7}: (3, {}), {8}: (4, {}), {9}: (5, {}), {10}: (6, {}), {1... | custom-call | flops 5120000000 | bytes 4194304 | tf_op jit(solution)/shard_map/layer_backward/pallas_call | solution.py:647
  162.6 2.2 layer_backward.18
  166.2 8.9 %layer_backward.19 = (bf16[256,768]{1,0:T(8,128)(2,1)S(1)}, f32[6,256,256]{2,1,0:T(8,128)S(1)}, f32[8,768]{1,0:T(8,128)S(1)}, bf16[2048,768]{1,0:T(8,128)(2,1)},...) custom-call(s32[1]{0:T(128)} %constant.26.clone.1.refs_0_, ...), custom_call_target="tpu_custom_call", output_to_operand_aliasing={{7}: (3, {}), {8}: (4, {}), {9}: (5, {}), {10}: (6, {}), {1... | custom-call | flops 5120000000 | bytes 4194304 | tf_op jit(solution)/shard_map/layer_backward/pallas_call | solution.py:647
  176.3 53.3 %collective-permute-done.17.refs_2_ = bf16[256,768]{1,0:T(8,128)(2,1)S(1)} collective-permute-done((bf16[256,768]{1,0:T(8,128)(2,1)S(1)}, bf16[256,768]{1,0:T(8,128)(2,1)S(1)}, u32[]{:S(2)}, u32[]{:S(2)}) %collective-permute-start.17) | collective-permute-done | bytes 393248 | tf_op jit(solution)/shard_map/ppermute | solution.py:652
  229.7 13.7 %layer_backward.20 = (bf16[256,768]{1,0:T(8,128)(2,1)S(1)}, f32[6,256,256]{2,1,0:T(8,128)S(1)}, f32[8,768]{1,0:T(8,128)S(1)}, bf16[2048,768]{1,0:T(8,128)(2,1)},...) custom-call(s32[1]{0:T(128)} %constant.78.clone.1.refs_0_, ...), custom_call_target="tpu_custom_call", output_to_operand_aliasing={{7}: (3, {}), {8}: (4, {}), {9}: (5, {}), {10}: (6, {}), {1... | custom-call | flops 5120000000 | bytes 4194304 | tf_op jit(solution)/shard_map/layer_backward/pallas_call | solution.py:647
  245.8 13.9 %layer_backward.21 = (bf16[256,768]{1,0:T(8,128)(2,1)S(1)}, f32[6,256,256]{2,1,0:T(8,128)S(1)}, f32[8,768]{1,0:T(8,128)S(1)}, bf16[2048,768]{1,0:T(8,128)(2,1)},...) custom-call(s32[1]{0:T(128)} %constant.40.clone.1.refs_0_, ...), custom_call_target="tpu_custom_call", output_to_operand_aliasing={{7}: (3, {}), {8}: (4, {}), {9}: (5, {}), {10}: (6, {}), {1... | custom-call | flops 5120000000 | bytes 4194304 | tf_op jit(solution)/shard_map/layer_backward/pallas_call | solution.py:647
  261.5 13.7 %layer_backward.22 = (bf16[256,768]{1,0:T(8,128)(2,1)S(1)}, f32[6,256,256]{2,1,0:T(8,128)S(1)}, f32[8,768]{1,0:T(8,128)S(1)}, bf16[2048,768]{1,0:T(8,128)(2,1)},...) custom-call(s32[1]{0:T(128)} %constant.79.clone.1.refs_0_, ...), custom_call_target="tpu_custom_call", output_to_operand_aliasing={{7}: (3, {}), {8}: (4, {}), {9}: (5, {}), {10}: (6, {}), {1... | custom-call | flops 5120000000 | bytes 4194304 | tf_op jit(solution)/shard_map/layer_backward/pallas_call | solution.py:647
  277.4 13.9 %layer_backward.23 = (bf16[256,768]{1,0:T(8,128)(2,1)S(1)}, f32[6,256,256]{2,1,0:T(8,128)S(1)}, f32[8,768]{1,0:T(8,128)S(1)}, bf16[2048,768]{1,0:T(8,128)(2,1)},...) custom-call(s32[1]{0:T(128)} %constant.39.clone.1.refs_0_, ...), custom_call_target="tpu_custom_call", output_to_operand_aliasing={{7}: (3, {}), {8}: (4, {}), {9}: (5, {}), {10}: (6, {}), {1... | custom-call | flops 5120000000 | bytes 4194304 | tf_op jit(solution)/shard_map/layer_backward/pallas_call | solution.py:647
  293.1 13.7 %layer_backward.24 = (bf16[256,768]{1,0:T(8,128)(2,1)S(1)}, f32[6,256,256]{2,1,0:T(8,128)S(1)}, f32[8,768]{1,0:T(8,128)S(1)}, bf16[2048,768]{1,0:T(8,128)(2,1)},...) custom-call(s32[1]{0:T(128)} %constant.80.clone.1.refs_0_, ...), custom_call_target="tpu_custom_call", output_to_operand_aliasing={{7}: (3, {}), {8}: (4, {}), {9}: (5, {}), {10}: (6, {}), {1... | custom-call | flops 5120000000 | bytes 4194304 | tf_op jit(solution)/shard_map/layer_backward/pallas_call | solution.py:647
  309.0 13.9 %layer_backward.25 = (bf16[256,768]{1,0:T(8,128)(2,1)S(1)}, f32[6,256,256]{2,1,0:T(8,128)S(1)}, f32[8,768]{1,0:T(8,128)S(1)}, bf16[2048,768]{1,0:T(8,128)(2,1)},...) custom-call(s32[1]{0:T(128)} %constant.38.clone.1.refs_0_, ...), custom_call_target="tpu_custom_call", output_to_operand_aliasing={{7}: (3, {}), {8}: (4, {}), {9}: (5, {}), {10}: (6, {}), {1... | custom-call | flops 5120000000 | bytes 4194304 | tf_op jit(solution)/shard_map/layer_backward/pallas_call | solution.py:647
  324.2 14.5 %layer_backward.26 = (bf16[256,768]{1,0:T(8,128)(2,1)}, f32[6,256,256]{2,1,0:T(8,128)S(1)}, f32[8,768]{1,0:T(8,128)S(1)}, bf16[2048,768]{1,0:T(8,128)(2,1)}, bf1...) custom-call(s32[1]{0:T(128)} %constant.81.clone.1.refs_0_, ...), custom_call_target="tpu_custom_call", output_to_operand_aliasing={{7}: (3, {}), {8}: (4, {}), {9}: (5, {}), {10}: (6, {}), {1... | custom-call | flops 5120000000 | bytes 4194304 | tf_op jit(solution)/shard_map/layer_backward/pallas_call | solution.py:647
  339.4 14.3 %layer_backward.27 = (bf16[256,768]{1,0:T(8,128)(2,1)}, f32[6,256,256]{2,1,0:T(8,128)S(1)}, f32[8,768]{1,0:T(8,128)S(1)}, bf16[2048,768]{1,0:T(8,128)(2,1)}, bf1...) custom-call(s32[1]{0:T(128)} %constant.21.clone.1.refs_0_, ...), custom_call_target="tpu_custom_call", output_to_operand_aliasing={{7}: (3, {}), {8}: (4, {}), {9}: (5, {}), {10}: (6, {}), {1... | custom-call | flops 5120000000 | bytes 4194304 | tf_op jit(solution)/shard_map/layer_backward/pallas_call | solution.py:647
  353.7 8.6 %weight_grad.7 = (bf16[2,384,768]{2,1,0:T(8,128)(2,1)}, bf16[2,384,768]{2,1,0:T(8,128)(2,1)}, bf16[2048,768]{1,0:T(8,128)(2,1)S(1)}) custom-call(s32[18]{0:T(128)S(1)} %pad_add_fusion.refs_1_.meta_ref, bf16[12,2048,256]{2,1,0:T(8,128)(2,1)S(1)} %get-tuple-element.1166.left, bf16[2048,768]{1,0:T(8,128)(2,1)} %get-tuple-element.1167.refs_0_), custom_call_target="tpu_custom_call" | custom-call | flops 4831838208 | bytes 15728640 | tf_op jit(solution)/shard_map/weight_grad/pallas_call | solution.py:664
  362.5 6.8 %weight_grad.8 = (bf16[2,384,768]{2,1,0:T(8,128)(2,1)}, bf16[2,384,768]{2,1,0:T(8,128)(2,1)}) custom-call(s32[18]{0:T(128)S(1)} %pad_add_fusion.refs_1_.meta_ref, bf16[12,2048,256]{2,1,0:T(8,128)(2,1)S(1)} %get-tuple-element.1166.left, bf16[2048,768]{1,0:T(8,128)(2,1)S(1)} %get-tuple-element.1170.refs_0_), custom_call_target="tpu_custom_call" | custom-call | flops 4831838208 | bytes 15728640 | tf_op jit(solution)/shard_map/weight_grad/pallas_call | solution.py:664
  374.0 11.6 %collective-permute-done.26.refs_2_ = bf16[384,768]{1,0:T(8,128)(2,1)S(1)} collective-permute-done((bf16[384,768]{1,0:T(8,128)(2,1)S(1)}, bf16[384,768]{1,0:T(8,128)(2,1)S(1)}, u32[]{:S(2)}, u32[]{:S(2)}) %collective-permute-start.26) | collective-permute-done | bytes 589856 | tf_op jit(solution)/shard_map/ppermute | solution.py:574
  385.7 8.4 %weight_grad.9 = (bf16[2,384,768]{2,1,0:T(8,128)(2,1)}, bf16[2,384,768]{2,1,0:T(8,128)(2,1)}) custom-call(s32[18]{0:T(128)S(1)} %pad_add_fusion.refs_1_.meta_ref, bf16[12,2048,256]{2,1,0:T(8,128)(2,1)S(1)} %bitcast.64, bf16[2048,768]{1,0:T(8,128)(2,1)S(1)} %copy-done.1, bf16[2048,768]{1,0:T(8,128)(2,1)S(1)} %copy-done, bf16[384,768]{1,0:T(8,128)(2,1)S(1)} %add_parts.15.refs_2_), custom_call_target="tpu_custom_call" | custom-call | flops 4831838208 | bytes 15728640 | tf_op jit(solution)/shard_map/weight_grad/pallas_call | solution.py:664
  396.7 8.4 %weight_grad.6 = (bf16[2,384,768]{2,1,0:T(8,128)(2,1)}, bf16[2,384,768]{2,1,0:T(8,128)(2,1)}) custom-call(s32[18]{0:T(128)S(1)} %pad_add_fusion.refs_1_.meta_ref, bf16[12,2048,256]{2,1,0:T(8,128)(2,1)S(1)} %bitcast.64, bf16[2048,768]{1,0:T(8,128)(2,1)S(1)} %copy-done.1, bf16[2048,768]{1,0:T(8,128)(2,1)S(1)} %copy-done), custom_call_target="tpu_custom_call" | custom-call | flops 4831838208 | bytes 15728640 | tf_op jit(solution)/shard_map/weight_grad/pallas_call | solution.py:664
  405.4 4.5 collective-permute-done.28.refs_2_
  413.8 6.8 %weight_grad.10 = (bf16[2,384,768]{2,1,0:T(8,128)(2,1)}, bf16[2,384,768]{2,1,0:T(8,128)(2,1)}) custom-call(s32[18]{0:T(128)S(1)} %pad_add_fusion.refs_1_.meta_ref, bf16[12,2048,256]{2,1,0:T(8,128)(2,1)S(1)} %bitcast.66, bf16[2048,768]{1,0:T(8,128)(2,1)S(1)} %copy-done.2, bf16[384,768]{1,0:T(8,128)(2,1)S(1)} %add_parts.16.refs_1_), custom_call_target="tpu_custom_call" | custom-call | flops 4831838208 | bytes 15728640 | tf_op jit(solution)/shard_map/weight_grad/pallas_call | solution.py:664
  422.2 4.8 collective-permute-done.30.refs_2_
  428.8 6.8 %weight_grad.11 = (bf16[2,384,768]{2,1,0:T(8,128)(2,1)}, bf16[2,384,768]{2,1,0:T(8,128)(2,1)}) custom-call(s32[18]{0:T(128)S(1)} %pad_add_fusion.refs_1_.meta_ref, bf16[12,2048,256]{2,1,0:T(8,128)(2,1)S(1)} %bitcast.66, bf16[2048,768]{1,0:T(8,128)(2,1)S(1)} %copy-done.2, bf16[384,768]{1,0:T(8,128)(2,1)S(1)} %add_parts.17.refs_1_), custom_call_target="tpu_custom_call" | custom-call | flops 4831838208 | bytes 15728640 | tf_op jit(solution)/shard_map/weight_grad/pallas_call | solution.py:664
  437.3 3.7 collective-permute-done.31.refs_2_
  446.7 3.2 maximum_bitcast_fusion.1
  449.8 3.1 copy.547
  453.0 6.8 %collective-permute-done.43.refs_2_ = f32[1,768]{1,0:T(1,128)} collective-permute-done((f32[1,768]{1,0:T(1,128)}, f32[1,768]{1,0:T(1,128)}, u32[]{:S(2)}, u32[]{:S(2)}) %collective-permute-start.43) | collective-permute-done | bytes 3104 | tf_op jit(solution)/shard_map/ppermute | solution.py:574
  461.4 2.4 convert_add_fusion.5
  468.1 2.0 add_parts.24
  475.2 2.2 copy.546
  478.5 6.5 %collective-permute-done.40.refs_2_ = bf16[384,768]{1,0:T(8,128)(2,1)S(1)} collective-permute-done((bf16[384,768]{1,0:T(8,128)(2,1)}, bf16[384,768]{1,0:T(8,128)(2,1)S(1)}, u32[]{:S(2)}, u32[]{:S(2)}) %collective-permute-start.40) | collective-permute-done | bytes 589856 | tf_op jit(solution)/shard_map/ppermute | solution.py:574
  488.9 2.8 copy.545
  493.0 6.4 %collective-permute-done.41 = bf16[384,768]{1,0:T(8,128)(2,1)S(1)} collective-permute-done((bf16[384,768]{1,0:T(8,128)(2,1)S(1)}, bf16[384,768]{1,0:T(8,128)(2,1)S(1)}, u32[]{:S(2)}, u32[]{:S(2)}) %collective-permute-start.41) | collective-permute-done | bytes 589856 | tf_op jit(solution)/shard_map/ppermute | solution.py:574
  (183 shorter events, 78.5 us)
Async XLA Ops:
  15.8 12.4 %collective-permute-start.1 = (bf16[256,768]{1,0:T(8,128)(2,1)S(1)}, bf16[256,768]{1,0:T(8,128)(2,1)S(1)}, u32[]{:S(2)}, u32[]{:S(2)}) collective-permute-start(bf16[256,768]{1,0:T(8,128)(2,1)S(1)} %get-tuple-element.632), channel_id=1, source_target_pairs={{0,8},{1,9},{2,10},{3,11},{4,12},{5,13},{6,14},{7,15}} | collective-permute-start | bytes 1179656 | tf_op jit(solution)/shard_map/ppermute | solution.py:642
  26.9 13.0 %collective-permute-start = (bf16[256,768]{1,0:T(8,128)(2,1)S(1)}, bf16[256,768]{1,0:T(8,128)(2,1)S(1)}, u32[]{:S(2)}, u32[]{:S(2)}) collective-permute-start(bf16[256,768]{1,0:T(8,128)(2,1)S(1)} %get-tuple-element.631), channel_id=1, source_target_pairs={{0,8},{1,9},{2,10},{3,11},{4,12},{5,13},{6,14},{7,15}} | collective-permute-start | bytes 1179656 | tf_op jit(solution)/shard_map/ppermute | solution.py:642
  37.6 14.3 %collective-permute-start.3 = (bf16[256,768]{1,0:T(8,128)(2,1)S(1)}, bf16[256,768]{1,0:T(8,128)(2,1)S(1)}, u32[]{:S(2)}, u32[]{:S(2)}) collective-permute-start(bf16[256,768]{1,0:T(8,128)(2,1)S(1)} %get-tuple-element.682), channel_id=1, source_target_pairs={{0,8},{8,16},{1,9},{9,17},{2,10},{10,18},{3,11},{11,19},{4,12},{12... | collective-permute-start | bytes 1179656 | tf_op jit(solution)/shard_map/ppermute | solution.py:642
  49.9 13.2 %collective-permute-start.2 = (bf16[256,768]{1,0:T(8,128)(2,1)S(1)}, bf16[256,768]{1,0:T(8,128)(2,1)S(1)}, u32[]{:S(2)}, u32[]{:S(2)}) collective-permute-start(bf16[256,768]{1,0:T(8,128)(2,1)S(1)} %get-tuple-element.681), channel_id=1, source_target_pairs={{0,8},{8,16},{1,9},{9,17},{2,10},{10,18},{3,11},{11,19},{4,12},{12... | collective-permute-start | bytes 1179656 | tf_op jit(solution)/shard_map/ppermute | solution.py:642
  61.1 13.7 %collective-permute-start.5 = (bf16[256,768]{1,0:T(8,128)(2,1)S(1)}, bf16[256,768]{1,0:T(8,128)(2,1)S(1)}, u32[]{:S(2)}, u32[]{:S(2)}) collective-permute-start(bf16[256,768]{1,0:T(8,128)(2,1)S(1)} %get-tuple-element.732), channel_id=1, source_target_pairs={{0,8},{8,16},{16,24},{1,9},{9,17},{17,25},{2,10},{10,18},{18,26},{... | collective-permute-start | bytes 1179656 | tf_op jit(solution)/shard_map/ppermute | solution.py:642
  72.9 13.1 %collective-permute-start.4 = (bf16[256,768]{1,0:T(8,128)(2,1)S(1)}, bf16[256,768]{1,0:T(8,128)(2,1)S(1)}, u32[]{:S(2)}, u32[]{:S(2)}) collective-permute-start(bf16[256,768]{1,0:T(8,128)(2,1)S(1)} %get-tuple-element.731), channel_id=1, source_target_pairs={{0,8},{8,16},{16,24},{1,9},{9,17},{17,25},{2,10},{10,18},{18,26},{... | collective-permute-start | bytes 1179656 | tf_op jit(solution)/shard_map/ppermute | solution.py:642
  84.0 13.8 %collective-permute-start.7 = (bf16[256,768]{1,0:T(8,128)(2,1)S(1)}, bf16[256,768]{1,0:T(8,128)(2,1)S(1)}, u32[]{:S(2)}, u32[]{:S(2)}) collective-permute-start(bf16[256,768]{1,0:T(8,128)(2,1)S(1)} %get-tuple-element.782), channel_id=1, source_target_pairs={{0,8},{8,16},{16,24},{1,9},{9,17},{17,25},{2,10},{10,18},{18,26},{... | collective-permute-start | bytes 1179656 | tf_op jit(solution)/shard_map/ppermute | solution.py:642
  95.9 10.2 %collective-permute-start.6 = (bf16[256,768]{1,0:T(8,128)(2,1)S(1)}, bf16[256,768]{1,0:T(8,128)(2,1)S(1)}, u32[]{:S(2)}, u32[]{:S(2)}) collective-permute-start(bf16[256,768]{1,0:T(8,128)(2,1)S(1)} %get-tuple-element.781), channel_id=1, source_target_pairs={{0,8},{8,16},{16,24},{1,9},{9,17},{17,25},{2,10},{10,18},{18,26},{... | collective-permute-start | bytes 1179656 | tf_op jit(solution)/shard_map/ppermute | solution.py:642
  98.7 14.9 %collective-permute-start.9 = (bf16[256,768]{1,0:T(8,128)(2,1)S(1)}, bf16[256,768]{1,0:T(8,128)(2,1)S(1)}, u32[]{:S(2)}, u32[]{:S(2)}) collective-permute-start(bf16[256,768]{1,0:T(8,128)(2,1)S(1)} %get-tuple-element.832), channel_id=1, source_target_pairs={{8,16},{16,24},{9,17},{17,25},{10,18},{18,26},{11,19},{19,27},{12,... | collective-permute-start | bytes 1179656 | tf_op jit(solution)/shard_map/ppermute | solution.py:642
  112.9 2.3 collective-permute-start.8
  114.5 10.1 %collective-permute-start.11 = (bf16[256,768]{1,0:T(8,128)(2,1)S(1)}, bf16[256,768]{1,0:T(8,128)(2,1)S(1)}, u32[]{:S(2)}, u32[]{:S(2)}) collective-permute-start(bf16[256,768]{1,0:T(8,128)(2,1)S(1)} %get-tuple-element.882), channel_id=1, source_target_pairs={{16,24},{17,25},{18,26},{19,27},{20,28},{21,29},{22,30},{23,31}} | collective-permute-start | bytes 1179656 | tf_op jit(solution)/shard_map/ppermute | solution.py:642
  123.9 2.3 collective-permute-start.10
  138.7 11.0 %collective-permute-start.13 = (bf16[256,768]{1,0:T(8,128)(2,1)S(1)}, bf16[256,768]{1,0:T(8,128)(2,1)S(1)}, u32[]{:S(2)}, u32[]{:S(2)}) collective-permute-start(bf16[256,768]{1,0:T(8,128)(2,1)S(1)} %get-tuple-element.969), channel_id=1, source_target_pairs={{24,16},{25,17},{26,18},{27,19},{28,20},{29,21},{30,22},{31,23}} | collective-permute-start | bytes 1179656 | tf_op jit(solution)/shard_map/ppermute | solution.py:652
  149.0 3.6 collective-permute-start.12
  151.9 10.7 %collective-permute-start.15 = (bf16[256,768]{1,0:T(8,128)(2,1)S(1)}, bf16[256,768]{1,0:T(8,128)(2,1)S(1)}, u32[]{:S(2)}, u32[]{:S(2)}) collective-permute-start(bf16[256,768]{1,0:T(8,128)(2,1)S(1)} %get-tuple-element.1001), channel_id=1, source_target_pairs={{16,8},{24,16},{17,9},{25,17},{18,10},{26,18},{19,11},{27,19},{20,... | collective-permute-start | bytes 1179656 | tf_op jit(solution)/shard_map/ppermute | solution.py:652
  161.9 4.2 collective-permute-start.14
  164.8 64.8 %collective-permute-start.17 = (bf16[256,768]{1,0:T(8,128)(2,1)S(1)}, bf16[256,768]{1,0:T(8,128)(2,1)S(1)}, u32[]{:S(2)}, u32[]{:S(2)}) collective-permute-start(bf16[256,768]{1,0:T(8,128)(2,1)S(1)} %get-tuple-element.1033), channel_id=1, source_target_pairs={{8,0},{16,8},{24,16},{9,1},{17,9},{25,17},{10,2},{18,10},{26,18},{... | collective-permute-start | bytes 1179656 | tf_op jit(solution)/shard_map/ppermute | solution.py:652
  175.0 70.7 %collective-permute-start.16 = (bf16[256,768]{1,0:T(8,128)(2,1)S(1)}, bf16[256,768]{1,0:T(8,128)(2,1)S(1)}, u32[]{:S(2)}, u32[]{:S(2)}) collective-permute-start(bf16[256,768]{1,0:T(8,128)(2,1)S(1)} %get-tuple-element.1032), channel_id=1, source_target_pairs={{8,0},{16,8},{24,16},{9,1},{17,9},{25,17},{10,2},{18,10},{26,18},{... | collective-permute-start | bytes 1179656 | tf_op jit(solution)/shard_map/ppermute | solution.py:652
  243.4 18.1 %collective-permute-start.19 = (bf16[256,768]{1,0:T(8,128)(2,1)S(1)}, bf16[256,768]{1,0:T(8,128)(2,1)S(1)}, u32[]{:S(2)}, u32[]{:S(2)}) collective-permute-start(bf16[256,768]{1,0:T(8,128)(2,1)S(1)} %get-tuple-element.1065), channel_id=1, source_target_pairs={{8,0},{16,8},{24,16},{9,1},{17,9},{25,17},{10,2},{18,10},{26,18},{... | collective-permute-start | bytes 1179656 | tf_op jit(solution)/shard_map/ppermute | solution.py:652
  259.7 17.7 %collective-permute-start.18 = (bf16[256,768]{1,0:T(8,128)(2,1)S(1)}, bf16[256,768]{1,0:T(8,128)(2,1)S(1)}, u32[]{:S(2)}, u32[]{:S(2)}) collective-permute-start(bf16[256,768]{1,0:T(8,128)(2,1)S(1)} %get-tuple-element.1064), channel_id=1, source_target_pairs={{8,0},{16,8},{24,16},{9,1},{17,9},{25,17},{10,2},{18,10},{26,18},{... | collective-permute-start | bytes 1179656 | tf_op jit(solution)/shard_map/ppermute | solution.py:652
  275.2 17.9 %collective-permute-start.21 = (bf16[256,768]{1,0:T(8,128)(2,1)S(1)}, bf16[256,768]{1,0:T(8,128)(2,1)S(1)}, u32[]{:S(2)}, u32[]{:S(2)}) collective-permute-start(bf16[256,768]{1,0:T(8,128)(2,1)S(1)} %get-tuple-element.1097), channel_id=1, source_target_pairs={{8,0},{16,8},{9,1},{17,9},{10,2},{18,10},{11,3},{19,11},{12,4},{20... | collective-permute-start | bytes 1179656 | tf_op jit(solution)/shard_map/ppermute | solution.py:652
  291.3 17.7 %collective-permute-start.20 = (bf16[256,768]{1,0:T(8,128)(2,1)S(1)}, bf16[256,768]{1,0:T(8,128)(2,1)S(1)}, u32[]{:S(2)}, u32[]{:S(2)}) collective-permute-start(bf16[256,768]{1,0:T(8,128)(2,1)S(1)} %get-tuple-element.1096), channel_id=1, source_target_pairs={{8,0},{16,8},{9,1},{17,9},{10,2},{18,10},{11,3},{19,11},{12,4},{20... | collective-permute-start | bytes 1179656 | tf_op jit(solution)/shard_map/ppermute | solution.py:652
  306.8 17.4 %collective-permute-start.23 = (bf16[256,768]{1,0:T(8,128)(2,1)S(1)}, bf16[256,768]{1,0:T(8,128)(2,1)S(1)}, u32[]{:S(2)}, u32[]{:S(2)}) collective-permute-start(bf16[256,768]{1,0:T(8,128)(2,1)S(1)} %get-tuple-element.1129), channel_id=1, source_target_pairs={{8,0},{9,1},{10,2},{11,3},{12,4},{13,5},{14,6},{15,7}} | collective-permute-start | bytes 1179656 | tf_op jit(solution)/shard_map/ppermute | solution.py:652
  322.9 16.5 %collective-permute-start.22 = (bf16[256,768]{1,0:T(8,128)(2,1)S(1)}, bf16[256,768]{1,0:T(8,128)(2,1)S(1)}, u32[]{:S(2)}, u32[]{:S(2)}) collective-permute-start(bf16[256,768]{1,0:T(8,128)(2,1)S(1)} %get-tuple-element.1128), channel_id=1, source_target_pairs={{8,0},{9,1},{10,2},{11,3},{12,4},{13,5},{14,6},{15,7}} | collective-permute-start | bytes 1179656 | tf_op jit(solution)/shard_map/ppermute | solution.py:652
  362.4 7.5 %collective-permute-start.25 = (bf16[2,384,768]{2,1,0:T(8,128)(2,1)}, bf16[2,384,768]{2,1,0:T(8,128)(2,1)S(1)}, u32[]{:S(2)}, u32[]{:S(2)}) collective-permute-start(bf16[2,384,768]{2,1,0:T(8,128)(2,1)} %get-tuple-element.1169), channel_id=1, source_target_pairs={{0,2},{2,0},{4,6},{6,4},{1,3},{3,1},{5,7},{7,5},{8,10},{10,8},{12,... | collective-permute-start | bytes 3538952 | tf_op jit(solution)/shard_map/ppermute | solution.py:574
  362.4 23.2 %slice-start = ((s8[12582912]{0:T(1024)(128)(4,1)}), s8[4194304]{0:T(1024)(128)(4,1)S(1)}, s32[]{:S(2)}) async-start(s8[12582912]{0:T(1024)(128)(4,1)} %bitcast.63), calls=%async_computation | async-start | bytes 8388608
  362.5 23.2 %slice-start.1 = ((s8[12582912]{0:T(1024)(128)(4,1)}), s8[4194304]{0:T(1024)(128)(4,1)S(1)}, s32[]{:S(2)}) async-start(s8[12582912]{0:T(1024)(128)(4,1)} %bitcast.63), calls=%async_computation.1 | async-start | bytes 8388608
  362.5 23.2 %slice-start.2 = ((s8[12582912]{0:T(1024)(128)(4,1)}), s8[4194304]{0:T(1024)(128)(4,1)S(1)}, s32[]{:S(2)}) async-start(s8[12582912]{0:T(1024)(128)(4,1)} %bitcast.63), calls=%async_computation.2 | async-start | bytes 8388608
  369.3 3.2 collective-permute-start.27
  370.3 15.4 %collective-permute-start.26 = (bf16[384,768]{1,0:T(8,128)(2,1)S(1)}, bf16[384,768]{1,0:T(8,128)(2,1)S(1)}, u32[]{:S(2)}, u32[]{:S(2)}) collective-permute-start(bf16[384,768]{1,0:T(8,128)(2,1)S(1)} %add_parts.14), channel_id=1, source_target_pairs={{0,4},{2,6},{4,0},{6,2},{1,5},{3,7},{5,1},{7,3},{8,12},{10,14},{12... | collective-permute-start | bytes 1769480 | tf_op jit(solution)/shard_map/ppermute | solution.py:574
  394.1 11.1 %collective-permute-start.29 = (bf16[2,384,768]{2,1,0:T(8,128)(2,1)}, bf16[2,384,768]{2,1,0:T(8,128)(2,1)S(1)}, u32[]{:S(2)}, u32[]{:S(2)}) collective-permute-start(bf16[2,384,768]{2,1,0:T(8,128)(2,1)} %get-tuple-element.1175), channel_id=1, source_target_pairs={{0,2},{2,0},{4,6},{6,4},{1,3},{3,1},{5,7},{7,5},{8,10},{10,8},{12,... | collective-permute-start | bytes 3538952 | tf_op jit(solution)/shard_map/ppermute | solution.py:574
  394.1 15.7 %collective-permute-start.28 = (bf16[384,768]{1,0:T(8,128)(2,1)S(1)}, bf16[384,768]{1,0:T(8,128)(2,1)S(1)}, u32[]{:S(2)}, u32[]{:S(2)}) collective-permute-start(bf16[384,768]{1,0:T(8,128)(2,1)S(1)} %add_parts.15.refs_2_), channel_id=1, source_target_pairs={{0,4},{2,6},{4,0},{6,2},{1,5},{3,7},{5,1},{7,3},{8,12},{10,14},{12... | collective-permute-start | bytes 1769480 | tf_op jit(solution)/shard_map/ppermute | solution.py:574
  395.3 15.5 %collective-permute-start.33 = (bf16[384,768]{1,0:T(8,128)(2,1)S(1)}, bf16[384,768]{1,0:T(8,128)(2,1)S(1)}, u32[]{:S(2)}, u32[]{:S(2)}) collective-permute-start(bf16[384,768]{1,0:T(8,128)(2,1)S(1)} %add_parts.21), channel_id=1, source_target_pairs={{0,1},{1,0},{2,3},{3,2},{4,5},{5,4},{6,7},{7,6},{8,9},{9,8},{10,11... | collective-permute-start | bytes 1769480 | tf_op jit(solution)/shard_map/ppermute | solution.py:574
  405.1 15.7 %collective-permute-start.24 = (bf16[2,384,768]{2,1,0:T(8,128)(2,1)}, bf16[2,384,768]{2,1,0:T(8,128)(2,1)S(1)}, u32[]{:S(2)}, u32[]{:S(2)}) collective-permute-start(bf16[2,384,768]{2,1,0:T(8,128)(2,1)} %get-tuple-element.1165), channel_id=1, source_target_pairs={{0,2},{2,0},{4,6},{6,4},{1,3},{3,1},{5,7},{7,5},{8,10},{10,8},{12,... | collective-permute-start | bytes 3538952 | tf_op jit(solution)/shard_map/ppermute | solution.py:574
  410.8 16.4 %collective-permute-start.34 = (bf16[384,768]{1,0:T(8,128)(2,1)S(1)}, bf16[384,768]{1,0:T(8,128)(2,1)S(1)}, u32[]{:S(2)}, u32[]{:S(2)}) collective-permute-start(bf16[384,768]{1,0:T(8,128)(2,1)S(1)} %add_parts.22), channel_id=1, source_target_pairs={{0,1},{1,0},{2,3},{3,2},{4,5},{5,4},{6,7},{7,6},{8,9},{9,8},{10,11... | collective-permute-start | bytes 1769480 | tf_op jit(solution)/shard_map/ppermute | solution.py:574
  412.3 14.6 %collective-permute-start.30 = (bf16[384,768]{1,0:T(8,128)(2,1)S(1)}, bf16[384,768]{1,0:T(8,128)(2,1)S(1)}, u32[]{:S(2)}, u32[]{:S(2)}) collective-permute-start(bf16[384,768]{1,0:T(8,128)(2,1)S(1)} %add_parts.16.refs_1_), channel_id=1, source_target_pairs={{0,4},{2,6},{4,0},{6,2},{1,5},{3,7},{5,1},{7,3},{8,12},{10,14},{12... | collective-permute-start | bytes 1769480 | tf_op jit(solution)/shard_map/ppermute | solution.py:574
  420.7 16.2 %collective-permute-start.32 = (bf16[2,384,768]{2,1,0:T(8,128)(2,1)}, bf16[2,384,768]{2,1,0:T(8,128)(2,1)S(1)}, u32[]{:S(2)}, u32[]{:S(2)}) collective-permute-start(bf16[2,384,768]{2,1,0:T(8,128)(2,1)} %get-tuple-element.1181), channel_id=1, source_target_pairs={{0,2},{2,0},{4,6},{6,4},{1,3},{3,1},{5,7},{7,5},{8,10},{10,8},{12,... | collective-permute-start | bytes 3538952 | tf_op jit(solution)/shard_map/ppermute | solution.py:574
  427.2 14.8 %collective-permute-start.35 = (bf16[384,768]{1,0:T(8,128)(2,1)S(1)}, bf16[384,768]{1,0:T(8,128)(2,1)}, u32[]{:S(2)}, u32[]{:S(2)}) collective-permute-start(bf16[384,768]{1,0:T(8,128)(2,1)S(1)} %add_parts.20), channel_id=1, source_target_pairs={{0,1},{1,0},{2,3},{3,2},{4,5},{5,4},{6,7},{7,6},{8,9},{9,8},{10,11... | collective-permute-start | bytes 1769480 | tf_op jit(solution)/shard_map/ppermute | solution.py:574
  427.6 13.4 %collective-permute-start.31 = (bf16[384,768]{1,0:T(8,128)(2,1)S(1)}, bf16[384,768]{1,0:T(8,128)(2,1)S(1)}, u32[]{:S(2)}, u32[]{:S(2)}) collective-permute-start(bf16[384,768]{1,0:T(8,128)(2,1)S(1)} %add_parts.17.refs_1_), channel_id=1, source_target_pairs={{0,4},{2,6},{4,0},{6,2},{1,5},{3,7},{5,1},{7,3},{8,12},{10,14},{12... | collective-permute-start | bytes 1769480 | tf_op jit(solution)/shard_map/ppermute | solution.py:574
  435.6 30.5 %collective-permute-start.38 = (bf16[2,384,768]{2,1,0:T(8,128)(2,1)}, bf16[2,384,768]{2,1,0:T(8,128)(2,1)}, u32[]{:S(2)}, u32[]{:S(2)}) collective-permute-start(bf16[2,384,768]{2,1,0:T(8,128)(2,1)} %get-tuple-element.1193), channel_id=1, source_target_pairs={{0,2},{2,0},{4,6},{6,4},{1,3},{3,1},{5,7},{7,5},{8,10},{10,8},{12,... | collective-permute-start | bytes 3538952 | tf_op jit(solution)/shard_map/ppermute | solution.py:574
  442.2 2.7 collective-permute-start.42
  442.3 27.8 %collective-permute-start.36 = (bf16[384,768]{1,0:T(8,128)(2,1)}, bf16[384,768]{1,0:T(8,128)(2,1)}, u32[]{:S(2)}, u32[]{:S(2)}) collective-permute-start(bf16[384,768]{1,0:T(8,128)(2,1)} %add_parts.19), channel_id=1, source_target_pairs={{0,1},{1,0},{2,3},{3,2},{4,5},{5,4},{6,7},{7,6},{8,9},{9,8},{10,11... | collective-permute-start | bytes 1769480 | tf_op jit(solution)/shard_map/ppermute | solution.py:574
  444.0 24.1 %collective-permute-start.37 = (bf16[384,768]{1,0:T(8,128)(2,1)}, bf16[384,768]{1,0:T(8,128)(2,1)}, u32[]{:S(2)}, u32[]{:S(2)}) collective-permute-start(bf16[384,768]{1,0:T(8,128)(2,1)} %copy-done.11), channel_id=1, source_target_pairs={{0,4},{2,6},{4,0},{6,2},{1,5},{3,7},{5,1},{7,3},{8,12},{10,14},{12... | collective-permute-start | bytes 1769480 | tf_op jit(solution)/shard_map/ppermute | solution.py:574
  445.5 14.3 %collective-permute-start.43 = (f32[1,768]{1,0:T(1,128)}, f32[1,768]{1,0:T(1,128)}, u32[]{:S(2)}, u32[]{:S(2)}) collective-permute-start(f32[1,768]{1,0:T(1,128)} %add_parts.26), channel_id=1, source_target_pairs={{0,4},{2,6},{4,0},{6,2},{1,5},{3,7},{5,1},{7,3},{8,12},{10,14},{12... | collective-permute-start | bytes 9224 | tf_op jit(solution)/shard_map/ppermute | solution.py:574
  461.0 3.8 collective-permute-start.44
  470.1 16.0 %collective-permute-start.39 = (bf16[384,768]{1,0:T(8,128)(2,1)}, bf16[384,768]{1,0:T(8,128)(2,1)}, u32[]{:S(2)}, u32[]{:S(2)}) collective-permute-start(bf16[384,768]{1,0:T(8,128)(2,1)} %add_parts.24), channel_id=1, source_target_pairs={{0,1},{1,0},{2,3},{3,2},{4,5},{5,4},{6,7},{7,6},{8,9},{9,8},{10,11... | collective-permute-start | bytes 1769480 | tf_op jit(solution)/shard_map/ppermute | solution.py:574
  470.7 14.2 %collective-permute-start.40 = (bf16[384,768]{1,0:T(8,128)(2,1)}, bf16[384,768]{1,0:T(8,128)(2,1)S(1)}, u32[]{:S(2)}, u32[]{:S(2)}) collective-permute-start(bf16[384,768]{1,0:T(8,128)(2,1)} %add_parts.23), channel_id=1, source_target_pairs={{0,4},{2,6},{4,0},{6,2},{1,5},{3,7},{5,1},{7,3},{8,12},{10,14},{12... | collective-permute-start | bytes 1769480 | tf_op jit(solution)/shard_map/ppermute | solution.py:574
  486.2 13.3 %collective-permute-start.41 = (bf16[384,768]{1,0:T(8,128)(2,1)S(1)}, bf16[384,768]{1,0:T(8,128)(2,1)S(1)}, u32[]{:S(2)}, u32[]{:S(2)}) collective-permute-start(bf16[384,768]{1,0:T(8,128)(2,1)S(1)} %add_parts.25), channel_id=1, source_target_pairs={{0,1},{1,0},{2,3},{3,2},{4,5},{5,4},{6,7},{7,6},{8,9},{9,8},{10,11... | collective-permute-start | bytes 1769480 | tf_op jit(solution)/shard_map/ppermute | solution.py:574
  (19 other events, 185.2 us)

commit v5 on v4

--- a/solution.py
+++ b/solution.py
@@ -228,7 +228,7 @@
             ((4, D), f32), ((TILES, every, TILE), bf)]
 
 
-def forward_call(rows, n, delta, opening, limit=19):
+def forward_call(rows, n, delta, opening, limit=17):
     V = pl.BlockSpec(memory_space=pltpu.VMEM)
     S = pl.BlockSpec(memory_space=pltpu.SMEM)
     A = pl.BlockSpec(memory_space=pl.ANY)
@@ -276,6 +276,20 @@
             if loads:
                 loads[i].wait()
 
+    quarters = [slice(j, j + D) for j in range(0, 4 * D, D)]
+
+    def early(which):
+        part = pl.ds(pl.multiple_of(which * rows, rows), rows)
+        pairs = [(n2_i.at[part, :], n2_ref), (rs_i.at[part, :], rs_ref)] + [(gp_i.at[part, cols], gp_ref.at[:, cols]) for cols in quarters]
+        return [pltpu.make_async_copy(src, dst, fetch_sems.at[i]) for i, (src, dst) in enumerate(pairs)]
+
+    @pl.when(chunk == n)
+    def _():
+        for copy in early(n - 1):
+            copy.start()
+        for copy in early(n - 1):
+            copy.wait()
+
     @pl.when(jnp.logical_not(valid))
     def _():
         loaded(*range(len(loads)))
@@ -284,15 +298,15 @@
     def _():
         base = pl.multiple_of(chunk * rows, rows)
         here = pl.ds(base, rows)
-        fetched = []
-        quarters = [slice(j, j + D) for j in range(0, 4 * D, D)]
-        pairs = [(n2_i.at[here, :], n2_ref), (rs_i.at[here, :], rs_ref)] + [(gp_i.at[here, cols], gp_ref.at[:, cols]) for cols in quarters]
-        pairs += [(src.at[here, :], dst) for src, dst in ((n1_i, n1_ref), (att_i, att_ref), (v_i, v_ref), (qn_i, qn_ref), (kf_i, kf_ref), (sg_i, sg_ref))]
-        pairs += [(sb_i.at[chunk], sb_ref)]
-        for i, (src, dst) in enumerate(pairs):
-            copy = pltpu.make_async_copy(src, dst, fetch_sems.at[i])
+        fetched = early(chunk) if loads else []
+        for copy in fetched:
             copy.start()
-            fetched.append(copy)
+        needed = []
+        rest = [(src.at[here, :], dst) for src, dst in ((n1_i, n1_ref), (att_i, att_ref), (v_i, v_ref), (qn_i, qn_ref), (kf_i, kf_ref), (sg_i, sg_ref))]
+        for src, dst in rest + [(sb_i.at[chunk], sb_ref)]:
+            copy = pltpu.make_async_copy(src, dst, fetch_sems.at[6 + len(needed)])
+            copy.start()
+            needed.append(copy)
         send = Sender(sems)
         last = meta_ref[2 + n + chunk] != 0
 
@@ -328,8 +342,8 @@
                 ga_out[...] = ga_in[...]
 
         g = g_ref[...].astype(f32)
-        fetched[0].wait()
-        fetched[1].wait()
+        for copy in fetched:
+            copy.wait()
         n2 = n2_ref[...].astype(f32)
         r1 = rs_ref[:, 0:1]
         r2 = rs_ref[:, 64:65]
@@ -340,21 +354,26 @@
         df_ref[...] = df
         send.put(df_ref, df_o.at[here, :])
         total = d_two
-        for cols, copy in zip(quarters, fetched[2:6]):
-            copy.wait()
+        for cols in quarters:
             du = (nt_dot(df, wd_ref[cols, :]) * gp_ref[:, cols].astype(f32)).astype(bf)
             du_ref[:, cols] = du
             for i in range(cols.start // TILE, cols.stop // TILE):
                 send.put(du_ref.at[:, i * TILE:(i + 1) * TILE], du_o.at[i, here, :])
             total = total + nt_dot(du, wu_ref[:, cols])
-        fetched[6].wait()
+        needed[0].wait()
         n1 = n1_ref[...].astype(f32)
         ga_out[0:1, :] += jnp.sum(total * n1, axis=0, keepdims=True)
         ga_out[1:2, :] += jnp.sum(total, axis=0, keepdims=True)
         d_res = norm_back(total, n1, r1, gb_ref[0:1, :])
         dp = d_res.astype(bf)
+
+        @pl.when(chunk > 0)
+        def _():
+            for copy in early(chunk - 1):
+                copy.start()
+
         da_ref[...] = nt_dot(dp, wo_ref[...]).astype(bf)
-        for copy in fetched[7:]:
+        for copy in needed[1:]:
             copy.wait()
         cos = cos_ref[pl.ds(base, rows), :]
         sin = sin_ref[pl.ds(base, rows), :]
@@ -418,6 +437,11 @@
         send.put(ds_ref, all_o.at[here, :])
         send.finish()
 
+        @pl.when(chunk > 0)
+        def _():
+            for copy in early(chunk - 1):
+                copy.wait()
+
 
 def backward_opening(delta, n, rows, stages, groups, *refs):
     t, meta, arr = refs[:3]
@@ -426,12 +450,13 @@
     loads = [pltpu.make_async_copy(cot.at[part, :], cot_v.at[part, :], load_sems.at[i]) for i, part in enumerate((head, tail))]
     for copy in loads:
         copy.start()
-    backward_kernel(delta, n, rows, stages, groups, t, meta, cot_v, arr, *refs[4:11], None, None, *refs[12:22], *refs[23:30], *refs[39:], loads=loads)
+    backward_kernel(delta, n, rows, stages, groups, t, meta, cot_v, arr, *refs[4:11], None, None, *refs[12:22], *refs[23:30],
+                    *refs[42:48], *refs[39:42], *refs[48:], loads=loads)
 
 
 def backward_next(delta, n, rows, stages, groups, *refs):
     t, meta, arr, cot = refs[:4]
-    act, act_v, sem, refs = refs[28], refs[44], refs[-1], refs[:-1]
+    act, act_v, sem, refs = refs[31], refs[47], refs[-1], refs[:-1]
     fill = (t[0] >= 1) & (t[0] <= TILES)
     tile = jnp.clip(t[0] - 1, 0, TILES - 1)
     copy = pltpu.make_async_copy(act.at[tile], act_v.at[tile], sem)
@@ -440,14 +465,15 @@
     def _():
         copy.start()
 
-    backward_kernel(delta, n, rows, stages, groups, t, meta, cot, arr, *refs[4:11], *refs[12:24], *refs[29:36], *refs[45:])
+    backward_kernel(delta, n, rows, stages, groups, t, meta, cot, arr, *refs[4:11], *refs[15:27], *refs[32:39],
+                    *refs[51:57], *refs[48:51], *refs[57:])
 
     @pl.when(fill)
     def _():
         copy.wait()
 
 
-def backward_call(rows, n, delta, stages, groups, opening, limit=19):
+def backward_call(rows, n, delta, stages, groups, opening, limit=17):
     V = pl.BlockSpec(memory_space=pltpu.VMEM)
     S = pl.BlockSpec(memory_space=pltpu.SMEM)
     A = pl.BlockSpec(memory_space=pl.ANY)
@@ -457,17 +483,18 @@
     saved = [((rows, D), bf), ((rows, 128), f32), ((rows, 4 * D), bf), ((rows, D), bf), ((rows, D), bf), ((rows, D), bf),
              ((rows, 2 * D), bf), ((rows, 2 * D), bf), ((rows, 2 * D), bf), ((PAIRS, 256, 256), bf)]
     own = [((rows, 3 * D), bf), ((rows, D), bf), ((rows, D), bf)]
+    early, saved = saved[:3], saved[3:]
     big = [pltpu.HBM((every, D), bf), pltpu.HBM((TILES, every, TILE), bf), pltpu.HBM((TILES, every, TILE), bf), pltpu.HBM((every, D), bf)]
     if opening:
         aliases = {3 + i: 7 + i for i in range(9)}
     else:
-        aliases = {**{3 + i: 7 + i for i in range(9)}, 12: 1, 13: 2, **{24 + i: 3 + i for i in range(4)}}
+        aliases = {**{3 + i: 7 + i for i in range(12)}, 15: 1, 16: 2, **{27 + i: 3 + i for i in range(4)}}
     return pl.pallas_call(
         functools.partial(backward_opening if opening else backward_next, delta, n, rows, stages, groups),
-        in_specs=[S, S] + [V] * 10 + [A] * 11 if opening else [S, S] + [V] * 12 + [A] * 15,
-        out_specs=[V] * 3 + [A] * 4 + [V] * 9,
+        in_specs=[S, S] + [V] * 10 + [A] * 11 if opening else [S, S] + [V] * 15 + [A] * 15,
+        out_specs=[V] * 3 + [A] * 4 + [V] * 12,
         out_shape=[sd((rows, D), bf), sd((PAIRS, 256, 256), f32), sd((8, D), f32)] + big
-        + [pltpu.VMEM(*item) for item in kept_items(every)],
+        + [pltpu.VMEM(*item) for item in kept_items(every) + early],
         scratch_shapes=[pltpu.VMEM(*item) for item in made + own + saved] + [pltpu.SemaphoreType.DMA((30,)), pltpu.SemaphoreType.DMA((13,))]
         + [pltpu.SemaphoreType.DMA((2,)) if opening else pltpu.SemaphoreType.DMA],
         input_output_aliases=aliases,
@@ -546,6 +573,7 @@
     )
 
 
+READY = {2: 0, 3: 1, 4: 2, 5: 3}
 MB_ROWS = 1024
 MICRO = 2
 ROWS = 256
@@ -596,13 +624,13 @@
     )(keep, got, *more)
 
 
-def reduced(keep, send, before):
-    got = exchange(send, "group", 1)
-    away = add_call(1, keep, got)
-    if before:
-        before[0], away = lax.optimization_barrier((before[0], away))
-    back = exchange(away, "group", 2)
-    return [back, keep, got, away]
+def plain_add(*items, limit=12):
+    V = pl.BlockSpec(memory_space=pltpu.VMEM)
+    return pl.pallas_call(
+        add_kernel, in_specs=[V] * len(items), out_specs=V, out_shape=jax.ShapeDtypeStruct(items[0].shape, items[0].dtype),
+        cost_estimate=pl.CostEstimate(flops=items[0].size, bytes_accessed=items[0].size * 4, transcendentals=0),
+        compiler_params=pltpu.CompilerParams(vmem_limit_bytes=limit * 2**20), name="add_vectors",
+    )(*items)
 
 
 def spread(own, before):
@@ -653,30 +681,45 @@
     df, du, de, input_grad = big
     act = resident[8]
     pieces = [(act, df), (de, x, att), (du, hb)]
-    waiting, owns, others, keeps = [], [], [], []
+    vectors = state[1]
+    for flip in (1, 2):
+        vectors = plain_add(vectors, exchange(vectors, "group", flip))
+    aways, keeps, gots, backs, owns, others = [], [], [], [], [], []
+
+    def turn(k):
+        if backs:
+            backs[-1], aways[k] = lax.optimization_barrier((backs[-1], aways[k]))
+        backs.append(exchange(aways[k], "group", 2))
+
     for piece in range(3):
         left, *rights = pieces[piece]
         for half in range(2):
-            fetch = not keeps
-            ready = {2: 1, 4: 2, 5: 3}.get(len(keeps))
-            waits = [] if ready is None else [waiting[ready][3]]
+            k = len(keeps)
+            fetch = k == 0
+            ready = READY.get(k)
+            waits = [] if ready is None else [aways[ready]]
             call = weight_call(n * ROWS, groups, half, len(rights) == 2, len(waits), fetch, [])
             keep, send, *loads = call(meta, left, *(far(rights) if fetch else rights), *waits)
             rights = loads if fetch else rights
             keeps.append(keep)
-            waiting.append(reduced(keep, send, waiting[-1] if waiting else None))
-    for back, keep, got, _ in waiting:
+            gots.append(exchange(send, "group", 1))
+            away = add_call(1, keep, gots[-1])
+            if k == 1:
+                vectors, away = lax.optimization_barrier((vectors, away))
+            aways.append(away)
+            turn(k)
+    for keep, got, back in zip(keeps, gots, backs):
         own = add_call(0, keep, got, back)
         other = spread(own, others)
         owns.append(own)
         others.append(other)
     parts = [finished(*pair) for pair in zip(owns, others)]
-    vectors, me, _ = lax.optimization_barrier((state[1], me, owns[3]))
-    vectors = vectors[:4].reshape(4, groups, D // groups).swapaxes(0, 1).reshape(groups, 1, D)
-    ordered = [lax.dynamic_index_in_dim(vectors, me ^ rel, 0, keepdims=False) for rel in range(4)]
-    small = reduced(jnp.stack(ordered[0::2]), jnp.stack(ordered[1::2]), None)
-    own = add_call(0, *small[1:3], small[0])
-    mine = finished(own, spread(own, [])).reshape(4, D // groups)
+    if lax.axis_size("dp") == 2:
+        vectors = plain_add(vectors, exchange(vectors, "dp", 1))
+    else:
+        vectors = lax.psum(vectors, "dp")
+    vectors, me, _ = lax.optimization_barrier((vectors, me, owns[3]))
+    mine = lax.dynamic_slice_in_dim(vectors, me * (D // groups), D // groups, axis=1)
     g_down, g_mixed, g_up = (jnp.concatenate(parts[i:i + 2], axis=0) for i in (0, 2, 4))
     odd = (me & 1) == 1
     swap = lambda a, b: jnp.concatenate([g_mixed[:, a], g_mixed[:, b]], axis=1)

time: 508 us -> 468 us (0.921)
  waiting for transfers between devices: 112 us -> 89.6 us
  Pallas kernels: 310 us -> 298 us
  other arithmetic: 19 us -> 12.6 us
    ppermute x21, waiting for transfers between devices: 47.2 us -> 29.8 us  [exchange(): return lax.ppermute(block, axis, route)]
    pallas_call x14, Pallas kernels: 147 us -> 134 us  [local(): backward_call(ROWS, n, DELTA, stages, groups, t == 0)]
    unnamed x49 -> x61, local copies, waits for them, and re-layouts: 10.8 us -> 6.78 us
    pallas_call x14 -> x12, Pallas kernels: 9.98 us -> 11.9 us  [add_call(): pl.pallas_call(add_kernel, grid=(rows // step,), in_specs=[pick, pick] +...]
  transfers between devices with their start and end apart: 45 -> 45, of which waited for: 18 -> 17; matrix products, arithmetic and copies ran while one was open for 5% -> 4% of each run, Pallas kernels for 51% -> 55%
where the time goes in v5:
time: 468 us; the launch traced here: 461 us
  Pallas kernels  298 us (64%)
  waiting for transfers between devices  89.6 us (19%)
  starting transfers between devices  47.9 us (10%)
  other arithmetic  12.6 us (3%)
  local copies, waits for them, and re-layouts  10.1 us (2%)
    pallas_call x14, Pallas kernels, local(): backward_call(ROWS, n, DELTA, stages, groups, t == 0)  134 us
    pallas_call x14, Pallas kernels, local(): forward_call(ROWS, n, DELTA, t == 0)  105 us
    ppermute x24, waiting for transfers between devices, local(): arriving.append(lax.ppermute(made[0], 'pipe', route) if route else made[0])  59.8 us
    pallas_call x6, Pallas kernels, local(): call(meta, left, *(far(rights) if fetch else rights), *waits)  45.9 us
    ppermute x24, starting transfers between devices, local(): arriving.append(lax.ppermute(made[0], 'pipe', route) if route else made[0])  31.1 us
    ppermute x21, waiting for transfers between devices, exchange(): return lax.ppermute(block, axis, route)  29.8 us
    ppermute x21, starting transfers between devices, exchange(): return lax.ppermute(block, axis, route)  16.8 us
    pallas_call x12, Pallas kernels, add_call(): pl.pallas_call(add_kernel, grid=(rows // step,), in_specs=[pick, pick] +...  11.9 us
  transfers between devices with their start and end apart: 45, of which 17 were waited for; matrix products, arithmetic and copies ran while one was open for 4% of the time, Pallas kernels for 55%

profile of v5, /device:TPU:0, one launch (start us, length us, event | category | flops | bytes accessed | tf_op | source)
XLA Modules:
  0.0 460.6 jit_solution(8839380383792620203)
XLA Ops:
  4.2 11.4 %layer_forward.14 = (bf16[256,768]{1,0:T(8,128)(2,1)S(1)}, f32[6,256,256]{2,1,0:T(8,128)S(1)}, bf16[2048,768]{1,0:T(8,128)(2,1)}, bf16[2048,768]{1,0:T(8,128)(2,...) custom-call(s32[1]{0:T(128)} %constant.21.clone.1.refs_0_, ...), custom_call_target="tpu_custom_call", output_to_operand_aliasing={{17}: (4, {}), {18}: (5, {}), {23}: (10, {})} | custom-call | flops 4608000000 | bytes 4194304 | tf_op jit(solution)/shard_map/layer_forward/pallas_call | solution.py:667
  16.9 9.5 %layer_forward.15 = (bf16[256,768]{1,0:T(8,128)(2,1)S(1)}, f32[6,256,256]{2,1,0:T(8,128)S(1)}, bf16[2048,768]{1,0:T(8,128)(2,1)}, bf16[2048,768]{1,0:T(8,128)(2,...) custom-call(s32[1]{0:T(128)} %constant.19.clone.1.refs_0_, ...), custom_call_target="tpu_custom_call", output_to_operand_aliasing={{1}: (12, {}), {2}: (13, {}), {3}: (14, {}), {4}: (15, {}),... | custom-call | flops 4608000000 | bytes 4194304 | tf_op jit(solution)/shard_map/layer_forward/pallas_call | solution.py:667
  27.8 9.0 %layer_forward.16 = (bf16[256,768]{1,0:T(8,128)(2,1)S(1)}, f32[6,256,256]{2,1,0:T(8,128)S(1)}, bf16[2048,768]{1,0:T(8,128)(2,1)}, bf16[2048,768]{1,0:T(8,128)(2,...) custom-call(s32[1]{0:T(128)} %constant.23.clone.1.refs_0_, ...), custom_call_target="tpu_custom_call", output_to_operand_aliasing={{1}: (12, {}), {2}: (13, {}), {3}: (14, {}), {4}: (15, {}),... | custom-call | flops 4608000000 | bytes 4194304 | tf_op jit(solution)/shard_map/layer_forward/pallas_call | solution.py:667
  36.8 2.7 collective-permute-start.3
  39.5 9.7 %layer_forward.17 = (bf16[256,768]{1,0:T(8,128)(2,1)S(1)}, f32[6,256,256]{2,1,0:T(8,128)S(1)}, bf16[2048,768]{1,0:T(8,128)(2,1)}, bf16[2048,768]{1,0:T(8,128)(2,...) custom-call(s32[1]{0:T(128)} %constant.18.clone.1.refs_0_, ...), custom_call_target="tpu_custom_call", output_to_operand_aliasing={{1}: (12, {}), {2}: (13, {}), {3}: (14, {}), {4}: (15, {}),... | custom-call | flops 4608000000 | bytes 4194304 | tf_op jit(solution)/shard_map/layer_forward/pallas_call | solution.py:667
  51.1 8.9 %layer_forward.18 = (bf16[256,768]{1,0:T(8,128)(2,1)S(1)}, f32[6,256,256]{2,1,0:T(8,128)S(1)}, bf16[2048,768]{1,0:T(8,128)(2,1)}, bf16[2048,768]{1,0:T(8,128)(2,...) custom-call(s32[1]{0:T(128)} %constant.24.clone.1.refs_0_, ...), custom_call_target="tpu_custom_call", output_to_operand_aliasing={{1}: (12, {}), {2}: (13, {}), {3}: (14, {}), {4}: (15, {}),... | custom-call | flops 4608000000 | bytes 4194304 | tf_op jit(solution)/shard_map/layer_forward/pallas_call | solution.py:667
  60.0 2.0 collective-permute-start.5
  62.1 9.4 %layer_forward.19 = (bf16[256,768]{1,0:T(8,128)(2,1)S(1)}, f32[6,256,256]{2,1,0:T(8,128)S(1)}, bf16[2048,768]{1,0:T(8,128)(2,1)}, bf16[2048,768]{1,0:T(8,128)(2,...) custom-call(s32[1]{0:T(128)} %constant.40.clone.1.refs_0_, ...), custom_call_target="tpu_custom_call", output_to_operand_aliasing={{1}: (12, {}), {2}: (13, {}), {3}: (14, {}), {4}: (15, {}),... | custom-call | flops 4608000000 | bytes 4194304 | tf_op jit(solution)/shard_map/layer_forward/pallas_call | solution.py:667
  71.4 2.0 collective-permute-start.4
  73.5 8.9 %layer_forward.20 = (bf16[256,768]{1,0:T(8,128)(2,1)S(1)}, f32[6,256,256]{2,1,0:T(8,128)S(1)}, bf16[2048,768]{1,0:T(8,128)(2,1)}, bf16[2048,768]{1,0:T(8,128)(2,...) custom-call(s32[1]{0:T(128)} %constant.25.clone.1.refs_0_, ...), custom_call_target="tpu_custom_call", output_to_operand_aliasing={{1}: (12, {}), {2}: (13, {}), {3}: (14, {}), {4}: (15, {}),... | custom-call | flops 4608000000 | bytes 4194304 | tf_op jit(solution)/shard_map/layer_forward/pallas_call | solution.py:667
  82.4 2.0 collective-permute-start.7
  84.4 9.5 %layer_forward.21 = (bf16[256,768]{1,0:T(8,128)(2,1)S(1)}, f32[6,256,256]{2,1,0:T(8,128)S(1)}, bf16[2048,768]{1,0:T(8,128)(2,1)}, bf16[2048,768]{1,0:T(8,128)(2,...) custom-call(s32[1]{0:T(128)} %constant.39.clone.1.refs_0_, ...), custom_call_target="tpu_custom_call", output_to_operand_aliasing={{1}: (12, {}), {2}: (13, {}), {3}: (14, {}), {4}: (15, {}),... | custom-call | flops 4608000000 | bytes 4194304 | tf_op jit(solution)/shard_map/layer_forward/pallas_call | solution.py:667
  94.0 2.0 collective-permute-start.6
  97.6 6.6 %collective-permute-done.6.refs_2_ = bf16[256,768]{1,0:T(8,128)(2,1)S(1)} collective-permute-done((bf16[256,768]{1,0:T(8,128)(2,1)S(1)}, bf16[256,768]{1,0:T(8,128)(2,1)S(1)}, u32[]{:S(2)}, u32[]{:S(2)}) %collective-permute-start.6) | collective-permute-done | bytes 393248 | tf_op jit(solution)/shard_map/ppermute | solution.py:670
  104.2 6.8 %layer_forward.23 = (bf16[256,768]{1,0:T(8,128)(2,1)S(1)}, f32[6,256,256]{2,1,0:T(8,128)S(1)}, bf16[2048,768]{1,0:T(8,128)(2,1)}, bf16[2048,768]{1,0:T(8,128)(2,...) custom-call(s32[1]{0:T(128)} %constant.38.clone.1.refs_0_, ...), custom_call_target="tpu_custom_call", output_to_operand_aliasing={{1}: (12, {}), {2}: (13, {}), {3}: (14, {}), {4}: (15, {}),... | custom-call | flops 4608000000 | bytes 4194304 | tf_op jit(solution)/shard_map/layer_forward/pallas_call | solution.py:667
  113.3 8.7 %layer_forward.25 = (bf16[256,768]{1,0:T(8,128)(2,1)S(1)}, f32[6,256,256]{2,1,0:T(8,128)S(1)}, bf16[2048,768]{1,0:T(8,128)(2,1)}, bf16[2048,768]{1,0:T(8,128)(2,...) custom-call(s32[1]{0:T(128)} %constant.17.clone.1.refs_0_, ...), custom_call_target="tpu_custom_call", output_to_operand_aliasing={{1}: (12, {}), {2}: (13, {}), {3}: (14, {}), {4}: (15, {}),... | custom-call | flops 4608000000 | bytes 4194304 | tf_op jit(solution)/shard_map/layer_forward/pallas_call | solution.py:667
  124.4 9.5 %layer_forward.27 = (bf16[256,768]{1,0:T(8,128)(2,1)S(1)}, f32[6,256,256]{2,1,0:T(8,128)S(1)}, bf16[2048,768]{1,0:T(8,128)(2,1)}, bf16[2048,768]{1,0:T(8,128)(2,...) custom-call(s32[1]{0:T(128)} %constant.29.clone.1.refs_0_, ...), custom_call_target="tpu_custom_call", output_to_operand_aliasing={{1}: (12, {}), {2}: (13, {}), {3}: (14, {}), {4}: (15, {}),... | custom-call | flops 4608000000 | bytes 4194304 | tf_op jit(solution)/shard_map/layer_forward/pallas_call | solution.py:667
  133.9 2.9 layer_backward.14
  137.5 9.6 %layer_backward.15 = (bf16[256,768]{1,0:T(8,128)(2,1)S(1)}, f32[6,256,256]{2,1,0:T(8,128)S(1)}, f32[8,768]{1,0:T(8,128)S(1)}, bf16[2048,768]{1,0:T(8,128)(2,1)},...) custom-call(s32[1]{0:T(128)} %constant.19.clone.1.refs_0_, ...), custom_call_target="tpu_custom_call", output_to_operand_aliasing={{7}: (3, {}), {8}: (4, {}), {9}: (5, {}), {10}: (6, {}), {1... | custom-call | flops 5120000000 | bytes 4194304 | tf_op jit(solution)/shard_map/layer_backward/pallas_call | solution.py:675
  147.8 2.2 layer_backward.16
  150.7 9.2 %layer_backward.17 = (bf16[256,768]{1,0:T(8,128)(2,1)S(1)}, f32[6,256,256]{2,1,0:T(8,128)S(1)}, f32[8,768]{1,0:T(8,128)S(1)}, bf16[2048,768]{1,0:T(8,128)(2,1)},...) custom-call(s32[1]{0:T(128)} %constant.18.clone.1.refs_0_, ...), custom_call_target="tpu_custom_call", output_to_operand_aliasing={{7}: (3, {}), {8}: (4, {}), {9}: (5, {}), {10}: (6, {}), {1... | custom-call | flops 5120000000 | bytes 4194304 | tf_op jit(solution)/shard_map/layer_backward/pallas_call | solution.py:675
  160.7 2.2 layer_backward.18
  164.2 10.1 %layer_backward.19 = (bf16[256,768]{1,0:T(8,128)(2,1)S(1)}, f32[6,256,256]{2,1,0:T(8,128)S(1)}, f32[8,768]{1,0:T(8,128)S(1)}, bf16[2048,768]{1,0:T(8,128)(2,1)},...) custom-call(s32[1]{0:T(128)} %constant.40.clone.1.refs_0_, ...), custom_call_target="tpu_custom_call", output_to_operand_aliasing={{7}: (3, {}), {8}: (4, {}), {9}: (5, {}), {10}: (6, {}), {1... | custom-call | flops 5120000000 | bytes 4194304 | tf_op jit(solution)/shard_map/layer_backward/pallas_call | solution.py:675
  175.6 47.1 %collective-permute-done.17.refs_2_ = bf16[256,768]{1,0:T(8,128)(2,1)S(1)} collective-permute-done((bf16[256,768]{1,0:T(8,128)(2,1)S(1)}, bf16[256,768]{1,0:T(8,128)(2,1)S(1)}, u32[]{:S(2)}, u32[]{:S(2)}) %collective-permute-start.17) | collective-permute-done | bytes 393248 | tf_op jit(solution)/shard_map/ppermute | solution.py:680
  222.7 11.8 %layer_backward.20 = (bf16[256,768]{1,0:T(8,128)(2,1)S(1)}, f32[6,256,256]{2,1,0:T(8,128)S(1)}, f32[8,768]{1,0:T(8,128)S(1)}, bf16[2048,768]{1,0:T(8,128)(2,1)},...) custom-call(s32[1]{0:T(128)} %constant.25.clone.1.refs_0_, ...), custom_call_target="tpu_custom_call", output_to_operand_aliasing={{7}: (3, {}), {8}: (4, {}), {9}: (5, {}), {10}: (6, {}), {1... | custom-call | flops 5120000000 | bytes 4194304 | tf_op jit(solution)/shard_map/layer_backward/pallas_call | solution.py:675
  235.7 2.3 collective-permute-done.16.refs_2_
  238.1 12.2 %layer_backward.21 = (bf16[256,768]{1,0:T(8,128)(2,1)S(1)}, f32[6,256,256]{2,1,0:T(8,128)S(1)}, f32[8,768]{1,0:T(8,128)S(1)}, bf16[2048,768]{1,0:T(8,128)(2,1)},...) custom-call(s32[1]{0:T(128)} %constant.39.clone.1.refs_0_, ...), custom_call_target="tpu_custom_call", output_to_operand_aliasing={{7}: (3, {}), {8}: (4, {}), {9}: (5, {}), {10}: (6, {}), {1... | custom-call | flops 5120000000 | bytes 4194304 | tf_op jit(solution)/shard_map/layer_backward/pallas_call | solution.py:675
  251.9 11.8 %layer_backward.22 = (bf16[256,768]{1,0:T(8,128)(2,1)S(1)}, f32[6,256,256]{2,1,0:T(8,128)S(1)}, f32[8,768]{1,0:T(8,128)S(1)}, bf16[2048,768]{1,0:T(8,128)(2,1)},...) custom-call(s32[1]{0:T(128)} %constant.26.clone.1.refs_0_, ...), custom_call_target="tpu_custom_call", output_to_operand_aliasing={{7}: (3, {}), {8}: (4, {}), {9}: (5, {}), {10}: (6, {}), {1... | custom-call | flops 5120000000 | bytes 4194304 | tf_op jit(solution)/shard_map/layer_backward/pallas_call | solution.py:675
  266.4 12.4 %layer_backward.23 = (bf16[256,768]{1,0:T(8,128)(2,1)S(1)}, f32[6,256,256]{2,1,0:T(8,128)S(1)}, f32[8,768]{1,0:T(8,128)S(1)}, bf16[2048,768]{1,0:T(8,128)(2,1)},...) custom-call(s32[1]{0:T(128)} %constant.38.clone.1.refs_0_, ...), custom_call_target="tpu_custom_call", output_to_operand_aliasing={{7}: (3, {}), {8}: (4, {}), {9}: (5, {}), {10}: (6, {}), {1... | custom-call | flops 5120000000 | bytes 4194304 | tf_op jit(solution)/shard_map/layer_backward/pallas_call | solution.py:675
  280.2 11.8 %layer_backward.24 = (bf16[256,768]{1,0:T(8,128)(2,1)S(1)}, f32[6,256,256]{2,1,0:T(8,128)S(1)}, f32[8,768]{1,0:T(8,128)S(1)}, bf16[2048,768]{1,0:T(8,128)(2,1)},...) custom-call(s32[1]{0:T(128)} %constant.27.clone.1.refs_0_, ...), custom_call_target="tpu_custom_call", output_to_operand_aliasing={{7}: (3, {}), {8}: (4, {}), {9}: (5, {}), {10}: (6, {}), {1... | custom-call | flops 5120000000 | bytes 4194304 | tf_op jit(solution)/shard_map/layer_backward/pallas_call | solution.py:675
  294.6 12.3 %layer_backward.25 = (bf16[256,768]{1,0:T(8,128)(2,1)S(1)}, f32[6,256,256]{2,1,0:T(8,128)S(1)}, f32[8,768]{1,0:T(8,128)S(1)}, bf16[2048,768]{1,0:T(8,128)(2,1)},...) custom-call(s32[1]{0:T(128)} %constant.17.clone.1.refs_0_, ...), custom_call_target="tpu_custom_call", output_to_operand_aliasing={{7}: (3, {}), {8}: (4, {}), {9}: (5, {}), {10}: (6, {}), {1... | custom-call | flops 5120000000 | bytes 4194304 | tf_op jit(solution)/shard_map/layer_backward/pallas_call | solution.py:675
  308.3 12.7 %layer_backward.26 = (bf16[256,768]{1,0:T(8,128)(2,1)}, f32[6,256,256]{2,1,0:T(8,128)S(1)}, f32[8,768]{1,0:T(8,128)S(1)}, bf16[2048,768]{1,0:T(8,128)(2,1)}, bf1...) custom-call(s32[1]{0:T(128)} %constant.28.clone.1.refs_0_, ...), custom_call_target="tpu_custom_call", output_to_operand_aliasing={{7}: (3, {}), {8}: (4, {}), {9}: (5, {}), {10}: (6, {}), {1... | custom-call | flops 5120000000 | bytes 4194304 | tf_op jit(solution)/shard_map/layer_backward/pallas_call | solution.py:675
  321.5 13.2 %layer_backward.27 = (bf16[256,768]{1,0:T(8,128)(2,1)}, f32[6,256,256]{2,1,0:T(8,128)S(1)}, f32[8,768]{1,0:T(8,128)S(1)}, bf16[2048,768]{1,0:T(8,128)(2,1)}, bf1...) custom-call(s32[1]{0:T(128)} %constant.29.clone.1.refs_0_, ...), custom_call_target="tpu_custom_call", output_to_operand_aliasing={{7}: (3, {}), {8}: (4, {}), {9}: (5, {}), {10}: (6, {}), {1... | custom-call | flops 5120000000 | bytes 4194304 | tf_op jit(solution)/shard_map/layer_backward/pallas_call | solution.py:675
  334.7 8.8 %weight_grad.6 = (bf16[2,384,768]{2,1,0:T(8,128)(2,1)}, bf16[2,384,768]{2,1,0:T(8,128)(2,1)}, bf16[2048,768]{1,0:T(8,128)(2,1)S(1)}) custom-call(s32[18]{0:T(128)S(1)} %pad_add_fusion.refs_1_.meta_ref, bf16[12,2048,256]{2,1,0:T(8,128)(2,1)S(1)} %get-tuple-element.1242.left, bf16[2048,768]{1,0:T(8,128)(2,1)} %get-tuple-element.1243.refs_0_), custom_call_target="tpu_custom_call" | custom-call | flops 4831838208 | bytes 15728640 | tf_op jit(solution)/shard_map/weight_grad/pallas_call | solution.py:702
  343.6 6.8 %weight_grad.7 = (bf16[2,384,768]{2,1,0:T(8,128)(2,1)}, bf16[2,384,768]{2,1,0:T(8,128)(2,1)}) custom-call(s32[18]{0:T(128)S(1)} %pad_add_fusion.refs_1_.meta_ref, bf16[12,2048,256]{2,1,0:T(8,128)(2,1)S(1)} %get-tuple-element.1242.left, bf16[2048,768]{1,0:T(8,128)(2,1)S(1)} %get-tuple-element.1244.refs_0_), custom_call_target="tpu_custom_call" | custom-call | flops 4831838208 | bytes 15728640 | tf_op jit(solution)/shard_map/weight_grad/pallas_call | solution.py:702
  351.6 8.3 %weight_grad.9 = (bf16[2,384,768]{2,1,0:T(8,128)(2,1)}, bf16[2,384,768]{2,1,0:T(8,128)(2,1)}) custom-call(s32[18]{0:T(128)S(1)} %pad_add_fusion.refs_1_.meta_ref, bf16[12,2048,256]{2,1,0:T(8,128)(2,1)S(1)} %bitcast.61, bf16[2048,768]{1,0:T(8,128)(2,1)S(1)} %copy-done.1, bf16[2048,768]{1,0:T(8,128)(2,1)S(1)} %copy-done, bf16[384,768]{1,0:T(8,128)(2,1)S(1)} %add_parts.13.refs_2_), custom_call_target="tpu_custom_call" | custom-call | flops 4831838208 | bytes 15728640 | tf_op jit(solution)/shard_map/weight_grad/pallas_call | solution.py:702
  364.4 2.8 collective-permute-done.25.refs_1_
  371.2 8.3 %weight_grad.8 = (bf16[2,384,768]{2,1,0:T(8,128)(2,1)}, bf16[2,384,768]{2,1,0:T(8,128)(2,1)}) custom-call(s32[18]{0:T(128)S(1)} %pad_add_fusion.refs_1_.meta_ref, bf16[12,2048,256]{2,1,0:T(8,128)(2,1)S(1)} %bitcast.61, bf16[2048,768]{1,0:T(8,128)(2,1)S(1)} %copy-done.1, bf16[2048,768]{1,0:T(8,128)(2,1)S(1)} %copy-done, bf16[384,768]{1,0:T(8,128)(2,1)S(1)} %add_parts.12.refs_2_), custom_call_target="tpu_custom_call" | custom-call | flops 4831838208 | bytes 15728640 | tf_op jit(solution)/shard_map/weight_grad/pallas_call | solution.py:702
  379.8 2.6 collective-permute-done.31.refs_2_
  385.9 6.8 %weight_grad.10 = (bf16[2,384,768]{2,1,0:T(8,128)(2,1)}, bf16[2,384,768]{2,1,0:T(8,128)(2,1)}) custom-call(s32[18]{0:T(128)S(1)} %pad_add_fusion.refs_1_.meta_ref, bf16[12,2048,256]{2,1,0:T(8,128)(2,1)S(1)} %bitcast.63, bf16[2048,768]{1,0:T(8,128)(2,1)S(1)} %copy-done.2, bf16[384,768]{1,0:T(8,128)(2,1)S(1)} %add_parts.14.refs_1_), custom_call_target="tpu_custom_call" | custom-call | flops 4831838208 | bytes 15728640 | tf_op jit(solution)/shard_map/weight_grad/pallas_call | solution.py:702
  394.0 2.0 collective-permute-done.33.refs_2_
  399.8 6.8 %weight_grad.11 = (bf16[2,384,768]{2,1,0:T(8,128)(2,1)}, bf16[2,384,768]{2,1,0:T(8,128)(2,1)}) custom-call(s32[18]{0:T(128)S(1)} %pad_add_fusion.refs_1_.meta_ref, bf16[12,2048,256]{2,1,0:T(8,128)(2,1)S(1)} %bitcast.63, bf16[2048,768]{1,0:T(8,128)(2,1)S(1)} %copy-done.2, bf16[384,768]{1,0:T(8,128)(2,1)} %add_parts.15.refs_1_), custom_call_target="tpu_custom_call" | custom-call | flops 4831838208 | bytes 15728640 | tf_op jit(solution)/shard_map/weight_grad/pallas_call | solution.py:702
  407.1 5.2 %collective-permute-done.27.refs_1_ = f32[8,768]{1,0:T(8,128)} collective-permute-done((f32[8,768]{1,0:T(8,128)}, f32[8,768]{1,0:T(8,128)}, u32[]{:S(2)}, u32[]{:S(2)}) %collective-permute-start.27) | collective-permute-done | bytes 24608 | tf_op jit(solution)/shard_map/ppermute | solution.py:602
  421.3 3.1 copy.584
  427.4 2.3 add_parts.21
  437.9 5.5 %collective-permute-done.43.refs_2_ = bf16[384,768]{1,0:T(8,128)(2,1)} collective-permute-done((bf16[384,768]{1,0:T(8,128)(2,1)}, bf16[384,768]{1,0:T(8,128)(2,1)}, u32[]{:S(2)}, u32[]{:S(2)}) %collective-permute-start.43) | collective-permute-done | bytes 589856 | tf_op jit(solution)/shard_map/ppermute | solution.py:602
  444.7 2.0 collective-permute-done.42
  451.5 7.0 %collective-permute-done.44 = bf16[384,768]{1,0:T(8,128)(2,1)S(1)} collective-permute-done((bf16[384,768]{1,0:T(8,128)(2,1)S(1)}, bf16[384,768]{1,0:T(8,128)(2,1)S(1)}, u32[]{:S(2)}, u32[]{:S(2)}) %collective-permute-start.44) | collective-permute-done | bytes 589856 | tf_op jit(solution)/shard_map/ppermute | solution.py:602
  (188 shorter events, 77.5 us)
Async XLA Ops:
  15.6 12.1 %collective-permute-start.1 = (bf16[256,768]{1,0:T(8,128)(2,1)S(1)}, bf16[256,768]{1,0:T(8,128)(2,1)S(1)}, u32[]{:S(2)}, u32[]{:S(2)}) collective-permute-start(bf16[256,768]{1,0:T(8,128)(2,1)S(1)} %get-tuple-element.673), channel_id=1, source_target_pairs={{0,8},{1,9},{2,10},{3,11},{4,12},{5,13},{6,14},{7,15}} | collective-permute-start | bytes 1179656 | tf_op jit(solution)/shard_map/ppermute | solution.py:670
  26.4 13.1 %collective-permute-start = (bf16[256,768]{1,0:T(8,128)(2,1)S(1)}, bf16[256,768]{1,0:T(8,128)(2,1)S(1)}, u32[]{:S(2)}, u32[]{:S(2)}) collective-permute-start(bf16[256,768]{1,0:T(8,128)(2,1)S(1)} %get-tuple-element.672), channel_id=1, source_target_pairs={{0,8},{1,9},{2,10},{3,11},{4,12},{5,13},{6,14},{7,15}} | collective-permute-start | bytes 1179656 | tf_op jit(solution)/shard_map/ppermute | solution.py:670
  36.8 14.3 %collective-permute-start.3 = (bf16[256,768]{1,0:T(8,128)(2,1)S(1)}, bf16[256,768]{1,0:T(8,128)(2,1)S(1)}, u32[]{:S(2)}, u32[]{:S(2)}) collective-permute-start(bf16[256,768]{1,0:T(8,128)(2,1)S(1)} %get-tuple-element.723), channel_id=1, source_target_pairs={{0,8},{8,16},{1,9},{9,17},{2,10},{10,18},{3,11},{11,19},{4,12},{12... | collective-permute-start | bytes 1179656 | tf_op jit(solution)/shard_map/ppermute | solution.py:670
  49.1 12.9 %collective-permute-start.2 = (bf16[256,768]{1,0:T(8,128)(2,1)S(1)}, bf16[256,768]{1,0:T(8,128)(2,1)S(1)}, u32[]{:S(2)}, u32[]{:S(2)}) collective-permute-start(bf16[256,768]{1,0:T(8,128)(2,1)S(1)} %get-tuple-element.722), channel_id=1, source_target_pairs={{0,8},{8,16},{1,9},{9,17},{2,10},{10,18},{3,11},{11,19},{4,12},{12... | collective-permute-start | bytes 1179656 | tf_op jit(solution)/shard_map/ppermute | solution.py:670
  60.0 13.4 %collective-permute-start.5 = (bf16[256,768]{1,0:T(8,128)(2,1)S(1)}, bf16[256,768]{1,0:T(8,128)(2,1)S(1)}, u32[]{:S(2)}, u32[]{:S(2)}) collective-permute-start(bf16[256,768]{1,0:T(8,128)(2,1)S(1)} %get-tuple-element.773), channel_id=1, source_target_pairs={{0,8},{8,16},{16,24},{1,9},{9,17},{17,25},{2,10},{10,18},{18,26},{... | collective-permute-start | bytes 1179656 | tf_op jit(solution)/shard_map/ppermute | solution.py:670
  71.4 13.0 %collective-permute-start.4 = (bf16[256,768]{1,0:T(8,128)(2,1)S(1)}, bf16[256,768]{1,0:T(8,128)(2,1)S(1)}, u32[]{:S(2)}, u32[]{:S(2)}) collective-permute-start(bf16[256,768]{1,0:T(8,128)(2,1)S(1)} %get-tuple-element.772), channel_id=1, source_target_pairs={{0,8},{8,16},{16,24},{1,9},{9,17},{17,25},{2,10},{10,18},{18,26},{... | collective-permute-start | bytes 1179656 | tf_op jit(solution)/shard_map/ppermute | solution.py:670
  82.4 13.6 %collective-permute-start.7 = (bf16[256,768]{1,0:T(8,128)(2,1)S(1)}, bf16[256,768]{1,0:T(8,128)(2,1)S(1)}, u32[]{:S(2)}, u32[]{:S(2)}) collective-permute-start(bf16[256,768]{1,0:T(8,128)(2,1)S(1)} %get-tuple-element.823), channel_id=1, source_target_pairs={{0,8},{8,16},{16,24},{1,9},{9,17},{17,25},{2,10},{10,18},{18,26},{... | collective-permute-start | bytes 1179656 | tf_op jit(solution)/shard_map/ppermute | solution.py:670
  94.0 10.2 %collective-permute-start.6 = (bf16[256,768]{1,0:T(8,128)(2,1)S(1)}, bf16[256,768]{1,0:T(8,128)(2,1)S(1)}, u32[]{:S(2)}, u32[]{:S(2)}) collective-permute-start(bf16[256,768]{1,0:T(8,128)(2,1)S(1)} %get-tuple-element.822), channel_id=1, source_target_pairs={{0,8},{8,16},{16,24},{1,9},{9,17},{17,25},{2,10},{10,18},{18,26},{... | collective-permute-start | bytes 1179656 | tf_op jit(solution)/shard_map/ppermute | solution.py:670
  96.9 14.8 %collective-permute-start.9 = (bf16[256,768]{1,0:T(8,128)(2,1)S(1)}, bf16[256,768]{1,0:T(8,128)(2,1)S(1)}, u32[]{:S(2)}, u32[]{:S(2)}) collective-permute-start(bf16[256,768]{1,0:T(8,128)(2,1)S(1)} %get-tuple-element.873), channel_id=1, source_target_pairs={{8,16},{16,24},{9,17},{17,25},{10,18},{18,26},{11,19},{19,27},{12,... | collective-permute-start | bytes 1179656 | tf_op jit(solution)/shard_map/ppermute | solution.py:670
  111.0 2.3 collective-permute-start.8
  112.6 10.1 %collective-permute-start.11 = (bf16[256,768]{1,0:T(8,128)(2,1)S(1)}, bf16[256,768]{1,0:T(8,128)(2,1)S(1)}, u32[]{:S(2)}, u32[]{:S(2)}) collective-permute-start(bf16[256,768]{1,0:T(8,128)(2,1)S(1)} %get-tuple-element.923), channel_id=1, source_target_pairs={{16,24},{17,25},{18,26},{19,27},{20,28},{21,29},{22,30},{23,31}} | collective-permute-start | bytes 1179656 | tf_op jit(solution)/shard_map/ppermute | solution.py:670
  122.0 2.3 collective-permute-start.10
  136.8 11.0 %collective-permute-start.13 = (bf16[256,768]{1,0:T(8,128)(2,1)S(1)}, bf16[256,768]{1,0:T(8,128)(2,1)S(1)}, u32[]{:S(2)}, u32[]{:S(2)}) collective-permute-start(bf16[256,768]{1,0:T(8,128)(2,1)S(1)} %get-tuple-element.1013), channel_id=1, source_target_pairs={{24,16},{25,17},{26,18},{27,19},{28,20},{29,21},{30,22},{31,23}} | collective-permute-start | bytes 1179656 | tf_op jit(solution)/shard_map/ppermute | solution.py:680
  147.1 3.6 collective-permute-start.12
  150.0 10.6 %collective-permute-start.15 = (bf16[256,768]{1,0:T(8,128)(2,1)S(1)}, bf16[256,768]{1,0:T(8,128)(2,1)S(1)}, u32[]{:S(2)}, u32[]{:S(2)}) collective-permute-start(bf16[256,768]{1,0:T(8,128)(2,1)S(1)} %get-tuple-element.1051), channel_id=1, source_target_pairs={{16,8},{24,16},{17,9},{25,17},{18,10},{26,18},{19,11},{27,19},{20,... | collective-permute-start | bytes 1179656 | tf_op jit(solution)/shard_map/ppermute | solution.py:680
  160.0 4.2 collective-permute-start.14
  162.9 59.8 %collective-permute-start.17 = (bf16[256,768]{1,0:T(8,128)(2,1)S(1)}, bf16[256,768]{1,0:T(8,128)(2,1)S(1)}, u32[]{:S(2)}, u32[]{:S(2)}) collective-permute-start(bf16[256,768]{1,0:T(8,128)(2,1)S(1)} %get-tuple-element.1089), channel_id=1, source_target_pairs={{8,0},{16,8},{24,16},{9,1},{17,9},{25,17},{10,2},{18,10},{26,18},{... | collective-permute-start | bytes 1179656 | tf_op jit(solution)/shard_map/ppermute | solution.py:680
  174.3 63.8 %collective-permute-start.16 = (bf16[256,768]{1,0:T(8,128)(2,1)S(1)}, bf16[256,768]{1,0:T(8,128)(2,1)S(1)}, u32[]{:S(2)}, u32[]{:S(2)}) collective-permute-start(bf16[256,768]{1,0:T(8,128)(2,1)S(1)} %get-tuple-element.1088), channel_id=1, source_target_pairs={{8,0},{16,8},{24,16},{9,1},{17,9},{25,17},{10,2},{18,10},{26,18},{... | collective-permute-start | bytes 1179656 | tf_op jit(solution)/shard_map/ppermute | solution.py:680
  234.4 17.5 %collective-permute-start.19 = (bf16[256,768]{1,0:T(8,128)(2,1)S(1)}, bf16[256,768]{1,0:T(8,128)(2,1)S(1)}, u32[]{:S(2)}, u32[]{:S(2)}) collective-permute-start(bf16[256,768]{1,0:T(8,128)(2,1)S(1)} %get-tuple-element.1127), channel_id=1, source_target_pairs={{8,0},{16,8},{24,16},{9,1},{17,9},{25,17},{10,2},{18,10},{26,18},{... | collective-permute-start | bytes 1179656 | tf_op jit(solution)/shard_map/ppermute | solution.py:680
  250.3 16.1 %collective-permute-start.18 = (bf16[256,768]{1,0:T(8,128)(2,1)S(1)}, bf16[256,768]{1,0:T(8,128)(2,1)S(1)}, u32[]{:S(2)}, u32[]{:S(2)}) collective-permute-start(bf16[256,768]{1,0:T(8,128)(2,1)S(1)} %get-tuple-element.1126), channel_id=1, source_target_pairs={{8,0},{16,8},{24,16},{9,1},{17,9},{25,17},{10,2},{18,10},{26,18},{... | collective-permute-start | bytes 1179656 | tf_op jit(solution)/shard_map/ppermute | solution.py:680
  263.7 16.5 %collective-permute-start.21 = (bf16[256,768]{1,0:T(8,128)(2,1)S(1)}, bf16[256,768]{1,0:T(8,128)(2,1)S(1)}, u32[]{:S(2)}, u32[]{:S(2)}) collective-permute-start(bf16[256,768]{1,0:T(8,128)(2,1)S(1)} %get-tuple-element.1165), channel_id=1, source_target_pairs={{8,0},{16,8},{9,1},{17,9},{10,2},{18,10},{11,3},{19,11},{12,4},{20... | collective-permute-start | bytes 1179656 | tf_op jit(solution)/shard_map/ppermute | solution.py:680
  278.8 15.9 %collective-permute-start.20 = (bf16[256,768]{1,0:T(8,128)(2,1)S(1)}, bf16[256,768]{1,0:T(8,128)(2,1)S(1)}, u32[]{:S(2)}, u32[]{:S(2)}) collective-permute-start(bf16[256,768]{1,0:T(8,128)(2,1)S(1)} %get-tuple-element.1164), channel_id=1, source_target_pairs={{8,0},{16,8},{9,1},{17,9},{10,2},{18,10},{11,3},{19,11},{12,4},{20... | collective-permute-start | bytes 1179656 | tf_op jit(solution)/shard_map/ppermute | solution.py:680
  291.9 16.3 %collective-permute-start.23 = (bf16[256,768]{1,0:T(8,128)(2,1)S(1)}, bf16[256,768]{1,0:T(8,128)(2,1)S(1)}, u32[]{:S(2)}, u32[]{:S(2)}) collective-permute-start(bf16[256,768]{1,0:T(8,128)(2,1)S(1)} %get-tuple-element.1203), channel_id=1, source_target_pairs={{8,0},{9,1},{10,2},{11,3},{12,4},{13,5},{14,6},{15,7}} | collective-permute-start | bytes 1179656 | tf_op jit(solution)/shard_map/ppermute | solution.py:680
  306.9 14.5 %collective-permute-start.22 = (bf16[256,768]{1,0:T(8,128)(2,1)S(1)}, bf16[256,768]{1,0:T(8,128)(2,1)S(1)}, u32[]{:S(2)}, u32[]{:S(2)}) collective-permute-start(bf16[256,768]{1,0:T(8,128)(2,1)S(1)} %get-tuple-element.1202), channel_id=1, source_target_pairs={{8,0},{9,1},{10,2},{11,3},{12,4},{13,5},{14,6},{15,7}} | collective-permute-start | bytes 1179656 | tf_op jit(solution)/shard_map/ppermute | solution.py:680
  334.7 16.9 %slice-start = ((s8[12582912]{0:T(1024)(128)(4,1)}), s8[4194304]{0:T(1024)(128)(4,1)S(1)}, s32[]{:S(2)}) async-start(s8[12582912]{0:T(1024)(128)(4,1)} %bitcast.60), calls=%async_computation | async-start | bytes 8388608
  334.7 16.9 %slice-start.1 = ((s8[12582912]{0:T(1024)(128)(4,1)}), s8[4194304]{0:T(1024)(128)(4,1)S(1)}, s32[]{:S(2)}) async-start(s8[12582912]{0:T(1024)(128)(4,1)} %bitcast.60), calls=%async_computation.1 | async-start | bytes 8388608
  343.5 7.4 %collective-permute-start.28 = (bf16[2,384,768]{2,1,0:T(8,128)(2,1)}, bf16[2,384,768]{2,1,0:T(8,128)(2,1)S(1)}, u32[]{:S(2)}, u32[]{:S(2)}) collective-permute-start(bf16[2,384,768]{2,1,0:T(8,128)(2,1)} %get-tuple-element.1251), channel_id=1, source_target_pairs={{0,2},{2,0},{4,6},{6,4},{1,3},{3,1},{5,7},{7,5},{8,10},{10,8},{12,... | collective-permute-start | bytes 3538952 | tf_op jit(solution)/shard_map/ppermute | solution.py:602
  350.4 17.4 %collective-permute-start.26 = (bf16[2,384,768]{2,1,0:T(8,128)(2,1)}, bf16[2,384,768]{2,1,0:T(8,128)(2,1)S(1)}, u32[]{:S(2)}, u32[]{:S(2)}) collective-permute-start(bf16[2,384,768]{2,1,0:T(8,128)(2,1)} %get-tuple-element.1246), channel_id=1, source_target_pairs={{0,2},{2,0},{4,6},{6,4},{1,3},{3,1},{5,7},{7,5},{8,10},{10,8},{12,... | collective-permute-start | bytes 3538952 | tf_op jit(solution)/shard_map/ppermute | solution.py:602
  351.3 16.7 %collective-permute-start.29 = (bf16[384,768]{1,0:T(8,128)(2,1)S(1)}, bf16[384,768]{1,0:T(8,128)(2,1)S(1)}, u32[]{:S(2)}, u32[]{:S(2)}) collective-permute-start(bf16[384,768]{1,0:T(8,128)(2,1)S(1)} %add_parts.13.refs_2_), channel_id=1, source_target_pairs={{0,4},{2,6},{4,0},{6,2},{1,5},{3,7},{5,1},{7,3},{8,12},{10,14},{12... | collective-permute-start | bytes 1769480 | tf_op jit(solution)/shard_map/ppermute | solution.py:602
  359.9 19.7 %collective-permute-start.32 = (bf16[2,384,768]{2,1,0:T(8,128)(2,1)}, bf16[2,384,768]{2,1,0:T(8,128)(2,1)S(1)}, u32[]{:S(2)}, u32[]{:S(2)}) collective-permute-start(bf16[2,384,768]{2,1,0:T(8,128)(2,1)} %get-tuple-element.1257), channel_id=1, source_target_pairs={{0,2},{2,0},{4,6},{6,4},{1,3},{3,1},{5,7},{7,5},{8,10},{10,8},{12,... | collective-permute-start | bytes 3538952 | tf_op jit(solution)/shard_map/ppermute | solution.py:602
  360.0 2.5 collective-permute-start.24
  362.5 4.7 %collective-permute-start.25 = (f32[8,768]{1,0:T(8,128)S(1)}, f32[8,768]{1,0:T(8,128)S(1)}, u32[]{:S(2)}, u32[]{:S(2)}) collective-permute-start(f32[8,768]{1,0:T(8,128)S(1)} %add_vectors.3.refs_0_), channel_id=1, source_target_pairs={{0,4},{2,6},{4,0},{6,2},{1,5},{3,7},{5,1},{7,3},{8,12},{10,14},{12... | collective-permute-start | bytes 73736 | tf_op jit(solution)/shard_map/ppermute | solution.py:602
  368.0 14.5 %collective-permute-start.31 = (bf16[384,768]{1,0:T(8,128)(2,1)S(1)}, bf16[384,768]{1,0:T(8,128)(2,1)S(1)}, u32[]{:S(2)}, u32[]{:S(2)}) collective-permute-start(bf16[384,768]{1,0:T(8,128)(2,1)S(1)} %add_parts.12.refs_2_), channel_id=1, source_target_pairs={{0,4},{2,6},{4,0},{6,2},{1,5},{3,7},{5,1},{7,3},{8,12},{10,14},{12... | collective-permute-start | bytes 1769480 | tf_op jit(solution)/shard_map/ppermute | solution.py:602
  369.1 16.8 %slice-start.3 = ((s8[12582912]{0:T(1024)(128)(4,1)}), s8[4194304]{0:T(1024)(128)(4,1)S(1)}, s32[]{:S(2)}) async-start(s8[12582912]{0:T(1024)(128)(4,1)} %bitcast.62), calls=%async_computation.3 | async-start | bytes 8388608
  369.4 14.7 %collective-permute-start.36 = (bf16[384,768]{1,0:T(8,128)(2,1)S(1)}, bf16[384,768]{1,0:T(8,128)(2,1)S(1)}, u32[]{:S(2)}, u32[]{:S(2)}) collective-permute-start(bf16[384,768]{1,0:T(8,128)(2,1)S(1)} %add_parts.19), channel_id=1, source_target_pairs={{0,1},{1,0},{2,3},{3,2},{4,5},{5,4},{6,7},{7,6},{8,9},{9,8},{10,11... | collective-permute-start | bytes 1769480 | tf_op jit(solution)/shard_map/ppermute | solution.py:602
  379.5 13.3 %collective-permute-start.30 = (bf16[2,384,768]{2,1,0:T(8,128)(2,1)}, bf16[2,384,768]{2,1,0:T(8,128)(2,1)S(1)}, u32[]{:S(2)}, u32[]{:S(2)}) collective-permute-start(bf16[2,384,768]{2,1,0:T(8,128)(2,1)} %get-tuple-element.1255), channel_id=1, source_target_pairs={{0,2},{2,0},{4,6},{6,4},{1,3},{3,1},{5,7},{7,5},{8,10},{10,8},{12,... | collective-permute-start | bytes 3538952 | tf_op jit(solution)/shard_map/ppermute | solution.py:602
  382.5 13.5 %collective-permute-start.33 = (bf16[384,768]{1,0:T(8,128)(2,1)S(1)}, bf16[384,768]{1,0:T(8,128)(2,1)S(1)}, u32[]{:S(2)}, u32[]{:S(2)}) collective-permute-start(bf16[384,768]{1,0:T(8,128)(2,1)S(1)} %add_parts.14.refs_1_), channel_id=1, source_target_pairs={{0,4},{2,6},{4,0},{6,2},{1,5},{3,7},{5,1},{7,3},{8,12},{10,14},{12... | collective-permute-start | bytes 1769480 | tf_op jit(solution)/shard_map/ppermute | solution.py:602
  384.0 13.9 %collective-permute-start.37 = (bf16[384,768]{1,0:T(8,128)(2,1)S(1)}, bf16[384,768]{1,0:T(8,128)(2,1)S(1)}, u32[]{:S(2)}, u32[]{:S(2)}) collective-permute-start(bf16[384,768]{1,0:T(8,128)(2,1)S(1)} %add_parts.20), channel_id=1, source_target_pairs={{0,1},{1,0},{2,3},{3,2},{4,5},{5,4},{6,7},{7,6},{8,9},{9,8},{10,11... | collective-permute-start | bytes 1769480 | tf_op jit(solution)/shard_map/ppermute | solution.py:602
  392.8 22.3 %collective-permute-start.35 = (bf16[2,384,768]{2,1,0:T(8,128)(2,1)}, bf16[2,384,768]{2,1,0:T(8,128)(2,1)S(1)}, u32[]{:S(2)}, u32[]{:S(2)}) collective-permute-start(bf16[2,384,768]{2,1,0:T(8,128)(2,1)} %get-tuple-element.1263), channel_id=1, source_target_pairs={{0,2},{2,0},{4,6},{6,4},{1,3},{3,1},{5,7},{7,5},{8,10},{10,8},{12,... | collective-permute-start | bytes 3538952 | tf_op jit(solution)/shard_map/ppermute | solution.py:602
  396.0 20.0 %collective-permute-start.34 = (bf16[384,768]{1,0:T(8,128)(2,1)}, bf16[384,768]{1,0:T(8,128)(2,1)}, u32[]{:S(2)}, u32[]{:S(2)}) collective-permute-start(bf16[384,768]{1,0:T(8,128)(2,1)} %add_parts.15.refs_1_), channel_id=1, source_target_pairs={{0,4},{2,6},{4,0},{6,2},{1,5},{3,7},{5,1},{7,3},{8,12},{10,14},{12... | collective-permute-start | bytes 1769480 | tf_op jit(solution)/shard_map/ppermute | solution.py:602
  398.0 21.0 %collective-permute-start.38 = (bf16[384,768]{1,0:T(8,128)(2,1)}, bf16[384,768]{1,0:T(8,128)(2,1)}, u32[]{:S(2)}, u32[]{:S(2)}) collective-permute-start(bf16[384,768]{1,0:T(8,128)(2,1)} %add_parts.18), channel_id=1, source_target_pairs={{0,1},{1,0},{2,3},{3,2},{4,5},{5,4},{6,7},{7,6},{8,9},{9,8},{10,11... | collective-permute-start | bytes 1769480 | tf_op jit(solution)/shard_map/ppermute | solution.py:602
  406.7 20.7 %collective-permute-start.41 = (bf16[2,384,768]{2,1,0:T(8,128)(2,1)}, bf16[2,384,768]{2,1,0:T(8,128)(2,1)}, u32[]{:S(2)}, u32[]{:S(2)}) collective-permute-start(bf16[2,384,768]{2,1,0:T(8,128)(2,1)} %get-tuple-element.1275), channel_id=1, source_target_pairs={{0,2},{2,0},{4,6},{6,4},{1,3},{3,1},{5,7},{7,5},{8,10},{10,8},{12,... | collective-permute-start | bytes 3538952 | tf_op jit(solution)/shard_map/ppermute | solution.py:602
  406.8 5.5 %collective-permute-start.27 = (f32[8,768]{1,0:T(8,128)}, f32[8,768]{1,0:T(8,128)}, u32[]{:S(2)}, u32[]{:S(2)}) collective-permute-start(f32[8,768]{1,0:T(8,128)} %add_vectors.4.refs_0_), channel_id=1, source_target_pairs={{0,1},{1,0},{2,3},{3,2},{4,5},{5,4},{6,7},{7,6},{8,9},{9,8},{10,11... | collective-permute-start | bytes 73736 | tf_op jit(solution)/shard_map/ppermute | solution.py:602
  416.0 14.1 %collective-permute-start.40 = (bf16[384,768]{1,0:T(8,128)(2,1)}, bf16[384,768]{1,0:T(8,128)(2,1)}, u32[]{:S(2)}, u32[]{:S(2)}) collective-permute-start(bf16[384,768]{1,0:T(8,128)(2,1)} %add_parts.16), channel_id=1, source_target_pairs={{0,4},{2,6},{4,0},{6,2},{1,5},{3,7},{5,1},{7,3},{8,12},{10,14},{12... | collective-permute-start | bytes 1769480 | tf_op jit(solution)/shard_map/ppermute | solution.py:602
  419.0 14.1 %collective-permute-start.39 = (bf16[384,768]{1,0:T(8,128)(2,1)}, bf16[384,768]{1,0:T(8,128)(2,1)}, u32[]{:S(2)}, u32[]{:S(2)}) collective-permute-start(bf16[384,768]{1,0:T(8,128)(2,1)} %add_parts.17), channel_id=1, source_target_pairs={{0,1},{1,0},{2,3},{3,2},{4,5},{5,4},{6,7},{7,6},{8,9},{9,8},{10,11... | collective-permute-start | bytes 1769480 | tf_op jit(solution)/shard_map/ppermute | solution.py:602
  430.1 13.2 %collective-permute-start.43 = (bf16[384,768]{1,0:T(8,128)(2,1)}, bf16[384,768]{1,0:T(8,128)(2,1)}, u32[]{:S(2)}, u32[]{:S(2)}) collective-permute-start(bf16[384,768]{1,0:T(8,128)(2,1)} %add_parts.21), channel_id=1, source_target_pairs={{0,4},{2,6},{4,0},{6,2},{1,5},{3,7},{5,1},{7,3},{8,12},{10,14},{12... | collective-permute-start | bytes 1769480 | tf_op jit(solution)/shard_map/ppermute | solution.py:602
  433.0 13.7 %collective-permute-start.42 = (bf16[384,768]{1,0:T(8,128)(2,1)}, bf16[384,768]{1,0:T(8,128)(2,1)}, u32[]{:S(2)}, u32[]{:S(2)}) collective-permute-start(bf16[384,768]{1,0:T(8,128)(2,1)} %add_parts.22), channel_id=1, source_target_pairs={{0,1},{1,0},{2,3},{3,2},{4,5},{5,4},{6,7},{7,6},{8,9},{9,8},{10,11... | collective-permute-start | bytes 1769480 | tf_op jit(solution)/shard_map/ppermute | solution.py:602
  446.8 11.8 %collective-permute-start.44 = (bf16[384,768]{1,0:T(8,128)(2,1)S(1)}, bf16[384,768]{1,0:T(8,128)(2,1)S(1)}, u32[]{:S(2)}, u32[]{:S(2)}) collective-permute-start(bf16[384,768]{1,0:T(8,128)(2,1)S(1)} %add_parts.23), channel_id=1, source_target_pairs={{0,1},{1,0},{2,3},{3,2},{4,5},{5,4},{6,7},{7,6},{8,9},{9,8},{10,11... | collective-permute-start | bytes 1769480 | tf_op jit(solution)/shard_map/ppermute | solution.py:602
  (25 other events, 209.8 us)

commit v6 on v5

--- a/solution.py
+++ b/solution.py
@@ -265,7 +265,7 @@
                     wq_ref, wo_ref, wu_ref, wd_ref, gb_ref, t_in, ga_in,
                     n2_i, rs_i, gp_i, n1_i, att_i, v_i, qn_i, kf_i, sg_i, sb_i,
                     ds_ref, t_out, ga_out, df_o, du_o, de_o, all_o,
-                    df_ref, du_ref, de_ref, dm_ref, da_ref, g_ref,
+                    df_ref, du_ref, mix_ref, dm_ref, da_ref, g_ref, dp_ref,
                     n2_ref, rs_ref, gp_ref, n1_ref, att_ref, v_ref, qn_ref, kf_ref, sg_ref, sb_ref, sems, fetch_sems, loads=()):
     stage = meta_ref[0]
     chunk = n - 1 - t_ref[0] + delta * (stages - 1 - stage)
@@ -308,6 +308,10 @@
             copy.start()
             needed.append(copy)
         send = Sender(sems)
+
+        def place(part, g, spot):
+            send.put(part, de_o.at[3 * g + spot // 2, here, spot % 2 * 128:spot % 2 * 128 + 128])
+
         last = meta_ref[2 + n + chunk] != 0
 
         loaded(0)
@@ -366,15 +370,18 @@
         ga_out[1:2, :] += jnp.sum(total, axis=0, keepdims=True)
         d_res = norm_back(total, n1, r1, gb_ref[0:1, :])
         dp = d_res.astype(bf)
+        dp_ref[...] = dp
+        for g, j in enumerate((0, 2, 3, 5)):
+            place(dp_ref.at[:, 128 * j:128 * j + 128], g, 5)
 
         @pl.when(chunk > 0)
         def _():
             for copy in early(chunk - 1):
                 copy.start()
 
-        da_ref[...] = nt_dot(dp, wo_ref[...]).astype(bf)
         for copy in needed[1:]:
             copy.wait()
+        da_ref[...] = nt_dot(dp, wo_ref[...]).astype(bf)
         cos = cos_ref[pl.ds(base, rows), :]
         sin = sin_ref[pl.ds(base, rows), :]
         m_a = head_lanes(rows, 256)
@@ -386,6 +393,7 @@
         diag = block_diag(256)
         ones = jnp.ones((rows, 128), bf)
         zero = jnp.zeros((), bf)
+        d_state = d_res
         for p in range(PAIRS):
             lanes = slice(128 * p, 128 * p + 128)
             wide = slice(256 * p, 256 * p + 256)
@@ -416,24 +424,24 @@
             dm_ref[:, lanes] = ((dq[:, :128] * cos + dq[:, 128:] * sin) * sq).astype(bf)
             dm_ref[:, D + 128 * p:D + 128 * p + 128] = ((dk[:, :128] * cos + dk[:, 128:] * sin) * sk).astype(bf)
             dm_ref[:, 2 * D + 128 * p:2 * D + 128 * p + 128] = dv.astype(bf)
+            for j in (p, 6 + p, 12 + p):
+                column = slice(128 * j, 128 * j + 128)
+                if j in (4, 13):
+                    below = (dp_ref[:, 128:256] if j == 4 else dp_ref[:, 512:640]).astype(f32)
+                    above = dm_ref[:, column].astype(f32)
+                    for g in ((0, 1) if j == 4 else (2, 3)):
+                        one, two = (pltpu.roll(above, 64, 1), below) if g & 1 else (above, pltpu.roll(below, 64, 1))
+                        mix_ref[g] = jnp.where(lane < 64, one, two).astype(bf)
+                        place(mix_ref.at[g], g, 4)
+                else:
+                    g = sum(j >= first for first in (5, 9, 14))
+                    place(dm_ref.at[:, column], g, j - (0, 5, 9, 14)[g])
+            if p % 2 == 1:
+                for j in (0, D, 2 * D):
+                    both = slice(j + 128 * (p - 1), j + 128 * (p + 1))
+                    d_state = d_state + nt_dot(dm_ref[:, both], wq_ref[:, both])
         loaded(1)
-        dm = dm_ref[...]
-        for g in range(groups):
-            odd = g & 1
-            part, rest = 9 * g, 3 * g
-            inner, outer = part + odd, rest + odd
-            de_ref[:, g * D:g * D + 4 * 128] = dm[:, inner * 64:inner * 64 + 4 * 128]
-            de_ref[:, g * D + 5 * 128:(g + 1) * D] = dp[:, outer * 64:outer * 64 + 128]
-            one = dm[:, (part if odd else part + 8) // 2 * 128:][:, :128].astype(f32)
-            two = dp[:, (rest if odd else rest + 2) // 2 * 128:][:, :128].astype(f32)
-            if odd:
-                one = pltpu.roll(one, 64, 1)
-            else:
-                two = pltpu.roll(two, 64, 1)
-            de_ref[:, g * D + 4 * 128:g * D + 5 * 128] = jnp.where(lane < 64, one, two).astype(bf)
-        for i in range(TILES):
-            send.put(de_ref.at[:, i * TILE:(i + 1) * TILE], de_o.at[i, here, :])
-        ds_ref[...] = (d_res + nt_dot(dm, wq_ref[...])).astype(bf)
+        ds_ref[...] = d_state.astype(bf)
         send.put(ds_ref, all_o.at[here, :])
         send.finish()
 
@@ -451,7 +459,7 @@
     for copy in loads:
         copy.start()
     backward_kernel(delta, n, rows, stages, groups, t, meta, cot_v, arr, *refs[4:11], None, None, *refs[12:22], *refs[23:30],
-                    *refs[42:48], *refs[39:42], *refs[48:], loads=loads)
+                    *refs[42:49], *refs[39:42], *refs[49:], loads=loads)
 
 
 def backward_next(delta, n, rows, stages, groups, *refs):
@@ -466,7 +474,7 @@
         copy.start()
 
     backward_kernel(delta, n, rows, stages, groups, t, meta, cot, arr, *refs[4:11], *refs[15:27], *refs[32:39],
-                    *refs[51:57], *refs[48:51], *refs[57:])
+                    *refs[51:58], *refs[48:51], *refs[58:])
 
     @pl.when(fill)
     def _():
@@ -479,10 +487,10 @@
     A = pl.BlockSpec(memory_space=pl.ANY)
     sd = jax.ShapeDtypeStruct
     every = n * rows
-    made = [((rows, D), bf), ((rows, 4 * D), bf), ((rows, 4 * D), bf)]
+    made = [((rows, D), bf), ((rows, 4 * D), bf), ((4, rows, 128), bf)]
     saved = [((rows, D), bf), ((rows, 128), f32), ((rows, 4 * D), bf), ((rows, D), bf), ((rows, D), bf), ((rows, D), bf),
              ((rows, 2 * D), bf), ((rows, 2 * D), bf), ((rows, 2 * D), bf), ((PAIRS, 256, 256), bf)]
-    own = [((rows, 3 * D), bf), ((rows, D), bf), ((rows, D), bf)]
+    own = [((rows, 3 * D), bf), ((rows, D), bf), ((rows, D), bf), ((rows, D), bf)]
     early, saved = saved[:3], saved[3:]
     big = [pltpu.HBM((every, D), bf), pltpu.HBM((TILES, every, TILE), bf), pltpu.HBM((TILES, every, TILE), bf), pltpu.HBM((every, D), bf)]
     if opening:
@@ -495,7 +503,7 @@
         out_specs=[V] * 3 + [A] * 4 + [V] * 12,
         out_shape=[sd((rows, D), bf), sd((PAIRS, 256, 256), f32), sd((8, D), f32)] + big
         + [pltpu.VMEM(*item) for item in kept_items(every) + early],
-        scratch_shapes=[pltpu.VMEM(*item) for item in made + own + saved] + [pltpu.SemaphoreType.DMA((30,)), pltpu.SemaphoreType.DMA((13,))]
+        scratch_shapes=[pltpu.VMEM(*item) for item in made + own + saved] + [pltpu.SemaphoreType.DMA((40,)), pltpu.SemaphoreType.DMA((13,))]
         + [pltpu.SemaphoreType.DMA((2,)) if opening else pltpu.SemaphoreType.DMA],
         input_output_aliases=aliases,
         cost_estimate=pl.CostEstimate(flops=rows * 2 * 10 * 10**6, bytes_accessed=4 * 2**20, transcendentals=0),

time: 468 us -> 457 us (0.976)
  Pallas kernels: 298 us -> 291 us
    pallas_call x14, Pallas kernels: 134 us -> 127 us  [local(): backward_call(ROWS, n, DELTA, stages, groups, t == 0)]
  transfers between devices with their start and end apart: 45 -> 45, of which waited for: 17 -> 15; matrix products, arithmetic and copies ran while one was open for 4% -> 4% of each run, Pallas kernels for 55% -> 55%
where the time goes in v6:
time: 457 us; the launch traced here: 449 us
  Pallas kernels  291 us (64%)
  waiting for transfers between devices  87.7 us (19%)
  starting transfers between devices  45.8 us (10%)
  other arithmetic  12.6 us (3%)
  local copies, waits for them, and re-layouts  10.1 us (2%)
    pallas_call x14, Pallas kernels, local(): backward_call(ROWS, n, DELTA, stages, groups, t == 0)  127 us
    pallas_call x14, Pallas kernels, local(): forward_call(ROWS, n, DELTA, t == 0)  105 us
    ppermute x24, waiting for transfers between devices, local(): arriving.append(lax.ppermute(made[0], 'pipe', route) if route else made[0])  56.5 us
    pallas_call x6, Pallas kernels, local(): call(meta, left, *(far(rights) if fetch else rights), *waits)  45.9 us
    ppermute x21, waiting for transfers between devices, exchange(): return lax.ppermute(block, axis, route)  31.2 us
    ppermute x24, starting transfers between devices, local(): arriving.append(lax.ppermute(made[0], 'pipe', route) if route else made[0])  31 us
    ppermute x21, starting transfers between devices, exchange(): return lax.ppermute(block, axis, route)  14.8 us
    pallas_call x12, Pallas kernels, add_call(): pl.pallas_call(add_kernel, grid=(rows // step,), in_specs=[pick, pick] +...  11.9 us
  transfers between devices with their start and end apart: 45, of which 15 were waited for; matrix products, arithmetic and copies ran while one was open for 4% of the time, Pallas kernels for 55%

profile of v6, /device:TPU:0, one launch (start us, length us, event | category | flops | bytes accessed | tf_op | source)
XLA Modules:
  0.0 449.5 jit_solution(12675255620862952914)
XLA Ops:
  4.2 11.4 %layer_forward.14 = (bf16[256,768]{1,0:T(8,128)(2,1)S(1)}, f32[6,256,256]{2,1,0:T(8,128)S(1)}, bf16[2048,768]{1,0:T(8,128)(2,1)}, bf16[2048,768]{1,0:T(8,128)(2,...) custom-call(s32[1]{0:T(128)} %constant.21.clone.1.refs_0_, ...), custom_call_target="tpu_custom_call", output_to_operand_aliasing={{17}: (4, {}), {18}: (5, {}), {23}: (10, {})} | custom-call | flops 4608000000 | bytes 4194304 | tf_op jit(solution)/shard_map/layer_forward/pallas_call | solution.py:675
  16.9 9.5 %layer_forward.15 = (bf16[256,768]{1,0:T(8,128)(2,1)S(1)}, f32[6,256,256]{2,1,0:T(8,128)S(1)}, bf16[2048,768]{1,0:T(8,128)(2,1)}, bf16[2048,768]{1,0:T(8,128)(2,...) custom-call(s32[1]{0:T(128)} %constant.19.clone.1.refs_0_, ...), custom_call_target="tpu_custom_call", output_to_operand_aliasing={{1}: (12, {}), {2}: (13, {}), {3}: (14, {}), {4}: (15, {}),... | custom-call | flops 4608000000 | bytes 4194304 | tf_op jit(solution)/shard_map/layer_forward/pallas_call | solution.py:675
  27.8 8.9 %layer_forward.16 = (bf16[256,768]{1,0:T(8,128)(2,1)S(1)}, f32[6,256,256]{2,1,0:T(8,128)S(1)}, bf16[2048,768]{1,0:T(8,128)(2,1)}, bf16[2048,768]{1,0:T(8,128)(2,...) custom-call(s32[1]{0:T(128)} %constant.23.clone.1.refs_0_, ...), custom_call_target="tpu_custom_call", output_to_operand_aliasing={{1}: (12, {}), {2}: (13, {}), {3}: (14, {}), {4}: (15, {}),... | custom-call | flops 4608000000 | bytes 4194304 | tf_op jit(solution)/shard_map/layer_forward/pallas_call | solution.py:675
  36.7 2.8 collective-permute-start.3
  39.5 9.7 %layer_forward.17 = (bf16[256,768]{1,0:T(8,128)(2,1)S(1)}, f32[6,256,256]{2,1,0:T(8,128)S(1)}, bf16[2048,768]{1,0:T(8,128)(2,1)}, bf16[2048,768]{1,0:T(8,128)(2,...) custom-call(s32[1]{0:T(128)} %constant.18.clone.1.refs_0_, ...), custom_call_target="tpu_custom_call", output_to_operand_aliasing={{1}: (12, {}), {2}: (13, {}), {3}: (14, {}), {4}: (15, {}),... | custom-call | flops 4608000000 | bytes 4194304 | tf_op jit(solution)/shard_map/layer_forward/pallas_call | solution.py:675
  51.1 8.9 %layer_forward.18 = (bf16[256,768]{1,0:T(8,128)(2,1)S(1)}, f32[6,256,256]{2,1,0:T(8,128)S(1)}, bf16[2048,768]{1,0:T(8,128)(2,1)}, bf16[2048,768]{1,0:T(8,128)(2,...) custom-call(s32[1]{0:T(128)} %constant.24.clone.1.refs_0_, ...), custom_call_target="tpu_custom_call", output_to_operand_aliasing={{1}: (12, {}), {2}: (13, {}), {3}: (14, {}), {4}: (15, {}),... | custom-call | flops 4608000000 | bytes 4194304 | tf_op jit(solution)/shard_map/layer_forward/pallas_call | solution.py:675
  60.0 1.9 collective-permute-start.5
  62.0 9.5 %layer_forward.19 = (bf16[256,768]{1,0:T(8,128)(2,1)S(1)}, f32[6,256,256]{2,1,0:T(8,128)S(1)}, bf16[2048,768]{1,0:T(8,128)(2,1)}, bf16[2048,768]{1,0:T(8,128)(2,...) custom-call(s32[1]{0:T(128)} %constant.40.clone.1.refs_0_, ...), custom_call_target="tpu_custom_call", output_to_operand_aliasing={{1}: (12, {}), {2}: (13, {}), {3}: (14, {}), {4}: (15, {}),... | custom-call | flops 4608000000 | bytes 4194304 | tf_op jit(solution)/shard_map/layer_forward/pallas_call | solution.py:675
  73.4 8.9 %layer_forward.20 = (bf16[256,768]{1,0:T(8,128)(2,1)S(1)}, f32[6,256,256]{2,1,0:T(8,128)S(1)}, bf16[2048,768]{1,0:T(8,128)(2,1)}, bf16[2048,768]{1,0:T(8,128)(2,...) custom-call(s32[1]{0:T(128)} %constant.25.clone.1.refs_0_, ...), custom_call_target="tpu_custom_call", output_to_operand_aliasing={{1}: (12, {}), {2}: (13, {}), {3}: (14, {}), {4}: (15, {}),... | custom-call | flops 4608000000 | bytes 4194304 | tf_op jit(solution)/shard_map/layer_forward/pallas_call | solution.py:675
  82.3 2.1 collective-permute-start.7
  84.4 9.6 %layer_forward.21 = (bf16[256,768]{1,0:T(8,128)(2,1)S(1)}, f32[6,256,256]{2,1,0:T(8,128)S(1)}, bf16[2048,768]{1,0:T(8,128)(2,1)}, bf16[2048,768]{1,0:T(8,128)(2,...) custom-call(s32[1]{0:T(128)} %constant.39.clone.1.refs_0_, ...), custom_call_target="tpu_custom_call", output_to_operand_aliasing={{1}: (12, {}), {2}: (13, {}), {3}: (14, {}), {4}: (15, {}),... | custom-call | flops 4608000000 | bytes 4194304 | tf_op jit(solution)/shard_map/layer_forward/pallas_call | solution.py:675
  97.6 6.6 %collective-permute-done.6.refs_2_ = bf16[256,768]{1,0:T(8,128)(2,1)S(1)} collective-permute-done((bf16[256,768]{1,0:T(8,128)(2,1)S(1)}, bf16[256,768]{1,0:T(8,128)(2,1)S(1)}, u32[]{:S(2)}, u32[]{:S(2)}) %collective-permute-start.6) | collective-permute-done | bytes 393248 | tf_op jit(solution)/shard_map/ppermute | solution.py:678
  104.2 6.8 %layer_forward.23 = (bf16[256,768]{1,0:T(8,128)(2,1)S(1)}, f32[6,256,256]{2,1,0:T(8,128)S(1)}, bf16[2048,768]{1,0:T(8,128)(2,1)}, bf16[2048,768]{1,0:T(8,128)(2,...) custom-call(s32[1]{0:T(128)} %constant.38.clone.1.refs_0_, ...), custom_call_target="tpu_custom_call", output_to_operand_aliasing={{1}: (12, {}), {2}: (13, {}), {3}: (14, {}), {4}: (15, {}),... | custom-call | flops 4608000000 | bytes 4194304 | tf_op jit(solution)/shard_map/layer_forward/pallas_call | solution.py:675
  113.3 8.7 %layer_forward.25 = (bf16[256,768]{1,0:T(8,128)(2,1)S(1)}, f32[6,256,256]{2,1,0:T(8,128)S(1)}, bf16[2048,768]{1,0:T(8,128)(2,1)}, bf16[2048,768]{1,0:T(8,128)(2,...) custom-call(s32[1]{0:T(128)} %constant.17.clone.1.refs_0_, ...), custom_call_target="tpu_custom_call", output_to_operand_aliasing={{1}: (12, {}), {2}: (13, {}), {3}: (14, {}), {4}: (15, {}),... | custom-call | flops 4608000000 | bytes 4194304 | tf_op jit(solution)/shard_map/layer_forward/pallas_call | solution.py:675
  124.4 9.4 %layer_forward.27 = (bf16[256,768]{1,0:T(8,128)(2,1)S(1)}, f32[6,256,256]{2,1,0:T(8,128)S(1)}, bf16[2048,768]{1,0:T(8,128)(2,1)}, bf16[2048,768]{1,0:T(8,128)(2,...) custom-call(s32[1]{0:T(128)} %constant.29.clone.1.refs_0_, ...), custom_call_target="tpu_custom_call", output_to_operand_aliasing={{1}: (12, {}), {2}: (13, {}), {3}: (14, {}), {4}: (15, {}),... | custom-call | flops 4608000000 | bytes 4194304 | tf_op jit(solution)/shard_map/layer_forward/pallas_call | solution.py:675
  133.7 3.0 layer_backward.14
  137.4 9.5 %layer_backward.15 = (bf16[256,768]{1,0:T(8,128)(2,1)S(1)}, f32[6,256,256]{2,1,0:T(8,128)S(1)}, f32[8,768]{1,0:T(8,128)S(1)}, bf16[2048,768]{1,0:T(8,128)(2,1)},...) custom-call(s32[1]{0:T(128)} %constant.19.clone.1.refs_0_, ...), custom_call_target="tpu_custom_call", output_to_operand_aliasing={{7}: (3, {}), {8}: (4, {}), {9}: (5, {}), {10}: (6, {}), {1... | custom-call | flops 5120000000 | bytes 4194304 | tf_op jit(solution)/shard_map/layer_backward/pallas_call | solution.py:683
  147.6 2.3 layer_backward.16
  150.7 9.1 %layer_backward.17 = (bf16[256,768]{1,0:T(8,128)(2,1)S(1)}, f32[6,256,256]{2,1,0:T(8,128)S(1)}, f32[8,768]{1,0:T(8,128)S(1)}, bf16[2048,768]{1,0:T(8,128)(2,1)},...) custom-call(s32[1]{0:T(128)} %constant.18.clone.1.refs_0_, ...), custom_call_target="tpu_custom_call", output_to_operand_aliasing={{7}: (3, {}), {8}: (4, {}), {9}: (5, {}), {10}: (6, {}), {1... | custom-call | flops 5120000000 | bytes 4194304 | tf_op jit(solution)/shard_map/layer_backward/pallas_call | solution.py:683
  160.5 2.3 layer_backward.18
  164.1 10.1 %layer_backward.19 = (bf16[256,768]{1,0:T(8,128)(2,1)S(1)}, f32[6,256,256]{2,1,0:T(8,128)S(1)}, f32[8,768]{1,0:T(8,128)S(1)}, bf16[2048,768]{1,0:T(8,128)(2,1)},...) custom-call(s32[1]{0:T(128)} %constant.40.clone.1.refs_0_, ...), custom_call_target="tpu_custom_call", output_to_operand_aliasing={{7}: (3, {}), {8}: (4, {}), {9}: (5, {}), {10}: (6, {}), {1... | custom-call | flops 5120000000 | bytes 4194304 | tf_op jit(solution)/shard_map/layer_backward/pallas_call | solution.py:683
  175.5 44.3 %collective-permute-done.17.refs_2_ = bf16[256,768]{1,0:T(8,128)(2,1)S(1)} collective-permute-done((bf16[256,768]{1,0:T(8,128)(2,1)S(1)}, bf16[256,768]{1,0:T(8,128)(2,1)S(1)}, u32[]{:S(2)}, u32[]{:S(2)}) %collective-permute-start.17) | collective-permute-done | bytes 393248 | tf_op jit(solution)/shard_map/ppermute | solution.py:688
  219.8 10.8 %layer_backward.20 = (bf16[256,768]{1,0:T(8,128)(2,1)S(1)}, f32[6,256,256]{2,1,0:T(8,128)S(1)}, f32[8,768]{1,0:T(8,128)S(1)}, bf16[2048,768]{1,0:T(8,128)(2,1)},...) custom-call(s32[1]{0:T(128)} %constant.25.clone.1.refs_0_, ...), custom_call_target="tpu_custom_call", output_to_operand_aliasing={{7}: (3, {}), {8}: (4, {}), {9}: (5, {}), {10}: (6, {}), {1... | custom-call | flops 5120000000 | bytes 4194304 | tf_op jit(solution)/shard_map/layer_backward/pallas_call | solution.py:683
  231.9 2.0 collective-permute-done.16.refs_2_
  234.0 11.4 %layer_backward.21 = (bf16[256,768]{1,0:T(8,128)(2,1)S(1)}, f32[6,256,256]{2,1,0:T(8,128)S(1)}, f32[8,768]{1,0:T(8,128)S(1)}, bf16[2048,768]{1,0:T(8,128)(2,1)},...) custom-call(s32[1]{0:T(128)} %constant.39.clone.1.refs_0_, ...), custom_call_target="tpu_custom_call", output_to_operand_aliasing={{7}: (3, {}), {8}: (4, {}), {9}: (5, {}), {10}: (6, {}), {1... | custom-call | flops 5120000000 | bytes 4194304 | tf_op jit(solution)/shard_map/layer_backward/pallas_call | solution.py:683
  246.9 10.8 %layer_backward.22 = (bf16[256,768]{1,0:T(8,128)(2,1)S(1)}, f32[6,256,256]{2,1,0:T(8,128)S(1)}, f32[8,768]{1,0:T(8,128)S(1)}, bf16[2048,768]{1,0:T(8,128)(2,1)},...) custom-call(s32[1]{0:T(128)} %constant.26.clone.1.refs_0_, ...), custom_call_target="tpu_custom_call", output_to_operand_aliasing={{7}: (3, {}), {8}: (4, {}), {9}: (5, {}), {10}: (6, {}), {1... | custom-call | flops 5120000000 | bytes 4194304 | tf_op jit(solution)/shard_map/layer_backward/pallas_call | solution.py:683
  260.4 11.6 %layer_backward.23 = (bf16[256,768]{1,0:T(8,128)(2,1)S(1)}, f32[6,256,256]{2,1,0:T(8,128)S(1)}, f32[8,768]{1,0:T(8,128)S(1)}, bf16[2048,768]{1,0:T(8,128)(2,1)},...) custom-call(s32[1]{0:T(128)} %constant.38.clone.1.refs_0_, ...), custom_call_target="tpu_custom_call", output_to_operand_aliasing={{7}: (3, {}), {8}: (4, {}), {9}: (5, {}), {10}: (6, {}), {1... | custom-call | flops 5120000000 | bytes 4194304 | tf_op jit(solution)/shard_map/layer_backward/pallas_call | solution.py:683
  273.3 10.9 %layer_backward.24 = (bf16[256,768]{1,0:T(8,128)(2,1)S(1)}, f32[6,256,256]{2,1,0:T(8,128)S(1)}, f32[8,768]{1,0:T(8,128)S(1)}, bf16[2048,768]{1,0:T(8,128)(2,1)},...) custom-call(s32[1]{0:T(128)} %constant.27.clone.1.refs_0_, ...), custom_call_target="tpu_custom_call", output_to_operand_aliasing={{7}: (3, {}), {8}: (4, {}), {9}: (5, {}), {10}: (6, {}), {1... | custom-call | flops 5120000000 | bytes 4194304 | tf_op jit(solution)/shard_map/layer_backward/pallas_call | solution.py:683
  286.8 11.4 %layer_backward.25 = (bf16[256,768]{1,0:T(8,128)(2,1)S(1)}, f32[6,256,256]{2,1,0:T(8,128)S(1)}, f32[8,768]{1,0:T(8,128)S(1)}, bf16[2048,768]{1,0:T(8,128)(2,1)},...) custom-call(s32[1]{0:T(128)} %constant.17.clone.1.refs_0_, ...), custom_call_target="tpu_custom_call", output_to_operand_aliasing={{7}: (3, {}), {8}: (4, {}), {9}: (5, {}), {10}: (6, {}), {1... | custom-call | flops 5120000000 | bytes 4194304 | tf_op jit(solution)/shard_map/layer_backward/pallas_call | solution.py:683
  299.5 11.7 %layer_backward.26 = (bf16[256,768]{1,0:T(8,128)(2,1)}, f32[6,256,256]{2,1,0:T(8,128)S(1)}, f32[8,768]{1,0:T(8,128)S(1)}, bf16[2048,768]{1,0:T(8,128)(2,1)}, bf1...) custom-call(s32[1]{0:T(128)} %constant.28.clone.1.refs_0_, ...), custom_call_target="tpu_custom_call", output_to_operand_aliasing={{7}: (3, {}), {8}: (4, {}), {9}: (5, {}), {10}: (6, {}), {1... | custom-call | flops 5120000000 | bytes 4194304 | tf_op jit(solution)/shard_map/layer_backward/pallas_call | solution.py:683
  311.8 12.3 %layer_backward.27 = (bf16[256,768]{1,0:T(8,128)(2,1)}, f32[6,256,256]{2,1,0:T(8,128)S(1)}, f32[8,768]{1,0:T(8,128)S(1)}, bf16[2048,768]{1,0:T(8,128)(2,1)}, bf1...) custom-call(s32[1]{0:T(128)} %constant.29.clone.1.refs_0_, ...), custom_call_target="tpu_custom_call", output_to_operand_aliasing={{7}: (3, {}), {8}: (4, {}), {9}: (5, {}), {10}: (6, {}), {1... | custom-call | flops 5120000000 | bytes 4194304 | tf_op jit(solution)/shard_map/layer_backward/pallas_call | solution.py:683
  324.1 8.8 %weight_grad.6 = (bf16[2,384,768]{2,1,0:T(8,128)(2,1)}, bf16[2,384,768]{2,1,0:T(8,128)(2,1)}, bf16[2048,768]{1,0:T(8,128)(2,1)S(1)}) custom-call(s32[18]{0:T(128)S(1)} %pad_add_fusion.refs_1_.meta_ref, bf16[12,2048,256]{2,1,0:T(8,128)(2,1)S(1)} %get-tuple-element.1242.left, bf16[2048,768]{1,0:T(8,128)(2,1)} %get-tuple-element.1243.refs_0_), custom_call_target="tpu_custom_call" | custom-call | flops 4831838208 | bytes 15728640 | tf_op jit(solution)/shard_map/weight_grad/pallas_call | solution.py:710
  333.1 6.8 %weight_grad.7 = (bf16[2,384,768]{2,1,0:T(8,128)(2,1)}, bf16[2,384,768]{2,1,0:T(8,128)(2,1)}) custom-call(s32[18]{0:T(128)S(1)} %pad_add_fusion.refs_1_.meta_ref, bf16[12,2048,256]{2,1,0:T(8,128)(2,1)S(1)} %get-tuple-element.1242.left, bf16[2048,768]{1,0:T(8,128)(2,1)S(1)} %get-tuple-element.1244.refs_0_), custom_call_target="tpu_custom_call" | custom-call | flops 4831838208 | bytes 15728640 | tf_op jit(solution)/shard_map/weight_grad/pallas_call | solution.py:710
  340.9 8.3 %weight_grad.9 = (bf16[2,384,768]{2,1,0:T(8,128)(2,1)}, bf16[2,384,768]{2,1,0:T(8,128)(2,1)}) custom-call(s32[18]{0:T(128)S(1)} %pad_add_fusion.refs_1_.meta_ref, bf16[12,2048,256]{2,1,0:T(8,128)(2,1)S(1)} %bitcast.61, bf16[2048,768]{1,0:T(8,128)(2,1)S(1)} %copy-done.1, bf16[2048,768]{1,0:T(8,128)(2,1)S(1)} %copy-done, bf16[384,768]{1,0:T(8,128)(2,1)S(1)} %add_parts.13.refs_2_), custom_call_target="tpu_custom_call" | custom-call | flops 4831838208 | bytes 15728640 | tf_op jit(solution)/shard_map/weight_grad/pallas_call | solution.py:710
  349.8 2.0 collective-permute-done.24.refs_1_
  351.9 1.9 collective-permute-start.25
  353.8 2.8 collective-permute-done.25.refs_1_
  358.9 8.3 %weight_grad.8 = (bf16[2,384,768]{2,1,0:T(8,128)(2,1)}, bf16[2,384,768]{2,1,0:T(8,128)(2,1)}) custom-call(s32[18]{0:T(128)S(1)} %pad_add_fusion.refs_1_.meta_ref, bf16[12,2048,256]{2,1,0:T(8,128)(2,1)S(1)} %bitcast.61, bf16[2048,768]{1,0:T(8,128)(2,1)S(1)} %copy-done.1, bf16[2048,768]{1,0:T(8,128)(2,1)S(1)} %copy-done, bf16[384,768]{1,0:T(8,128)(2,1)S(1)} %add_parts.12.refs_2_), custom_call_target="tpu_custom_call" | custom-call | flops 4831838208 | bytes 15728640 | tf_op jit(solution)/shard_map/weight_grad/pallas_call | solution.py:710
  367.5 4.4 collective-permute-done.31.refs_2_
  373.8 6.8 %weight_grad.10 = (bf16[2,384,768]{2,1,0:T(8,128)(2,1)}, bf16[2,384,768]{2,1,0:T(8,128)(2,1)}) custom-call(s32[18]{0:T(128)S(1)} %pad_add_fusion.refs_1_.meta_ref, bf16[12,2048,256]{2,1,0:T(8,128)(2,1)S(1)} %bitcast.63, bf16[2048,768]{1,0:T(8,128)(2,1)S(1)} %copy-done.2, bf16[384,768]{1,0:T(8,128)(2,1)S(1)} %add_parts.14.refs_1_), custom_call_target="tpu_custom_call" | custom-call | flops 4831838208 | bytes 15728640 | tf_op jit(solution)/shard_map/weight_grad/pallas_call | solution.py:710
  381.9 3.5 collective-permute-done.33.refs_2_
  388.0 6.8 %weight_grad.11 = (bf16[2,384,768]{2,1,0:T(8,128)(2,1)}, bf16[2,384,768]{2,1,0:T(8,128)(2,1)}) custom-call(s32[18]{0:T(128)S(1)} %pad_add_fusion.refs_1_.meta_ref, bf16[12,2048,256]{2,1,0:T(8,128)(2,1)S(1)} %bitcast.63, bf16[2048,768]{1,0:T(8,128)(2,1)S(1)} %copy-done.2, bf16[384,768]{1,0:T(8,128)(2,1)} %add_parts.15.refs_1_), custom_call_target="tpu_custom_call" | custom-call | flops 4831838208 | bytes 15728640 | tf_op jit(solution)/shard_map/weight_grad/pallas_call | solution.py:710
  396.5 4.1 collective-permute-done.27.refs_1_
  405.4 2.0 add_parts.17
  410.3 3.1 copy.584
  416.4 2.3 add_parts.21
  426.7 5.5 %collective-permute-done.43.refs_2_ = bf16[384,768]{1,0:T(8,128)(2,1)} collective-permute-done((bf16[384,768]{1,0:T(8,128)(2,1)}, bf16[384,768]{1,0:T(8,128)(2,1)}, u32[]{:S(2)}, u32[]{:S(2)}) %collective-permute-start.43) | collective-permute-done | bytes 589856 | tf_op jit(solution)/shard_map/ppermute | solution.py:610
  440.3 7.1 %collective-permute-done.44 = bf16[384,768]{1,0:T(8,128)(2,1)S(1)} collective-permute-done((bf16[384,768]{1,0:T(8,128)(2,1)S(1)}, bf16[384,768]{1,0:T(8,128)(2,1)S(1)}, u32[]{:S(2)}, u32[]{:S(2)}) %collective-permute-start.44) | collective-permute-done | bytes 589856 | tf_op jit(solution)/shard_map/ppermute | solution.py:610
  (188 shorter events, 74.3 us)
Async XLA Ops:
  15.6 12.1 %collective-permute-start.1 = (bf16[256,768]{1,0:T(8,128)(2,1)S(1)}, bf16[256,768]{1,0:T(8,128)(2,1)S(1)}, u32[]{:S(2)}, u32[]{:S(2)}) collective-permute-start(bf16[256,768]{1,0:T(8,128)(2,1)S(1)} %get-tuple-element.673), channel_id=1, source_target_pairs={{0,8},{1,9},{2,10},{3,11},{4,12},{5,13},{6,14},{7,15}} | collective-permute-start | bytes 1179656 | tf_op jit(solution)/shard_map/ppermute | solution.py:678
  26.4 13.1 %collective-permute-start = (bf16[256,768]{1,0:T(8,128)(2,1)S(1)}, bf16[256,768]{1,0:T(8,128)(2,1)S(1)}, u32[]{:S(2)}, u32[]{:S(2)}) collective-permute-start(bf16[256,768]{1,0:T(8,128)(2,1)S(1)} %get-tuple-element.672), channel_id=1, source_target_pairs={{0,8},{1,9},{2,10},{3,11},{4,12},{5,13},{6,14},{7,15}} | collective-permute-start | bytes 1179656 | tf_op jit(solution)/shard_map/ppermute | solution.py:678
  36.7 14.4 %collective-permute-start.3 = (bf16[256,768]{1,0:T(8,128)(2,1)S(1)}, bf16[256,768]{1,0:T(8,128)(2,1)S(1)}, u32[]{:S(2)}, u32[]{:S(2)}) collective-permute-start(bf16[256,768]{1,0:T(8,128)(2,1)S(1)} %get-tuple-element.723), channel_id=1, source_target_pairs={{0,8},{8,16},{1,9},{9,17},{2,10},{10,18},{3,11},{11,19},{4,12},{12... | collective-permute-start | bytes 1179656 | tf_op jit(solution)/shard_map/ppermute | solution.py:678
  49.1 12.8 %collective-permute-start.2 = (bf16[256,768]{1,0:T(8,128)(2,1)S(1)}, bf16[256,768]{1,0:T(8,128)(2,1)S(1)}, u32[]{:S(2)}, u32[]{:S(2)}) collective-permute-start(bf16[256,768]{1,0:T(8,128)(2,1)S(1)} %get-tuple-element.722), channel_id=1, source_target_pairs={{0,8},{8,16},{1,9},{9,17},{2,10},{10,18},{3,11},{11,19},{4,12},{12... | collective-permute-start | bytes 1179656 | tf_op jit(solution)/shard_map/ppermute | solution.py:678
  60.0 13.4 %collective-permute-start.5 = (bf16[256,768]{1,0:T(8,128)(2,1)S(1)}, bf16[256,768]{1,0:T(8,128)(2,1)S(1)}, u32[]{:S(2)}, u32[]{:S(2)}) collective-permute-start(bf16[256,768]{1,0:T(8,128)(2,1)S(1)} %get-tuple-element.773), channel_id=1, source_target_pairs={{0,8},{8,16},{16,24},{1,9},{9,17},{17,25},{2,10},{10,18},{18,26},{... | collective-permute-start | bytes 1179656 | tf_op jit(solution)/shard_map/ppermute | solution.py:678
  71.5 13.0 %collective-permute-start.4 = (bf16[256,768]{1,0:T(8,128)(2,1)S(1)}, bf16[256,768]{1,0:T(8,128)(2,1)S(1)}, u32[]{:S(2)}, u32[]{:S(2)}) collective-permute-start(bf16[256,768]{1,0:T(8,128)(2,1)S(1)} %get-tuple-element.772), channel_id=1, source_target_pairs={{0,8},{8,16},{16,24},{1,9},{9,17},{17,25},{2,10},{10,18},{18,26},{... | collective-permute-start | bytes 1179656 | tf_op jit(solution)/shard_map/ppermute | solution.py:678
  82.3 13.7 %collective-permute-start.7 = (bf16[256,768]{1,0:T(8,128)(2,1)S(1)}, bf16[256,768]{1,0:T(8,128)(2,1)S(1)}, u32[]{:S(2)}, u32[]{:S(2)}) collective-permute-start(bf16[256,768]{1,0:T(8,128)(2,1)S(1)} %get-tuple-element.823), channel_id=1, source_target_pairs={{0,8},{8,16},{16,24},{1,9},{9,17},{17,25},{2,10},{10,18},{18,26},{... | collective-permute-start | bytes 1179656 | tf_op jit(solution)/shard_map/ppermute | solution.py:678
  94.1 10.1 %collective-permute-start.6 = (bf16[256,768]{1,0:T(8,128)(2,1)S(1)}, bf16[256,768]{1,0:T(8,128)(2,1)S(1)}, u32[]{:S(2)}, u32[]{:S(2)}) collective-permute-start(bf16[256,768]{1,0:T(8,128)(2,1)S(1)} %get-tuple-element.822), channel_id=1, source_target_pairs={{0,8},{8,16},{16,24},{1,9},{9,17},{17,25},{2,10},{10,18},{18,26},{... | collective-permute-start | bytes 1179656 | tf_op jit(solution)/shard_map/ppermute | solution.py:678
  96.9 14.8 %collective-permute-start.9 = (bf16[256,768]{1,0:T(8,128)(2,1)S(1)}, bf16[256,768]{1,0:T(8,128)(2,1)S(1)}, u32[]{:S(2)}, u32[]{:S(2)}) collective-permute-start(bf16[256,768]{1,0:T(8,128)(2,1)S(1)} %get-tuple-element.873), channel_id=1, source_target_pairs={{8,16},{16,24},{9,17},{17,25},{10,18},{18,26},{11,19},{19,27},{12,... | collective-permute-start | bytes 1179656 | tf_op jit(solution)/shard_map/ppermute | solution.py:678
  111.0 2.3 collective-permute-start.8
  112.6 10.1 %collective-permute-start.11 = (bf16[256,768]{1,0:T(8,128)(2,1)S(1)}, bf16[256,768]{1,0:T(8,128)(2,1)S(1)}, u32[]{:S(2)}, u32[]{:S(2)}) collective-permute-start(bf16[256,768]{1,0:T(8,128)(2,1)S(1)} %get-tuple-element.923), channel_id=1, source_target_pairs={{16,24},{17,25},{18,26},{19,27},{20,28},{21,29},{22,30},{23,31}} | collective-permute-start | bytes 1179656 | tf_op jit(solution)/shard_map/ppermute | solution.py:678
  122.0 2.3 collective-permute-start.10
  136.7 10.9 %collective-permute-start.13 = (bf16[256,768]{1,0:T(8,128)(2,1)S(1)}, bf16[256,768]{1,0:T(8,128)(2,1)S(1)}, u32[]{:S(2)}, u32[]{:S(2)}) collective-permute-start(bf16[256,768]{1,0:T(8,128)(2,1)S(1)} %get-tuple-element.1013), channel_id=1, source_target_pairs={{24,16},{25,17},{26,18},{27,19},{28,20},{29,21},{30,22},{31,23}} | collective-permute-start | bytes 1179656 | tf_op jit(solution)/shard_map/ppermute | solution.py:688
  146.9 3.7 collective-permute-start.12
  150.0 10.5 %collective-permute-start.15 = (bf16[256,768]{1,0:T(8,128)(2,1)S(1)}, bf16[256,768]{1,0:T(8,128)(2,1)S(1)}, u32[]{:S(2)}, u32[]{:S(2)}) collective-permute-start(bf16[256,768]{1,0:T(8,128)(2,1)S(1)} %get-tuple-element.1051), channel_id=1, source_target_pairs={{16,8},{24,16},{17,9},{25,17},{18,10},{26,18},{19,11},{27,19},{20,... | collective-permute-start | bytes 1179656 | tf_op jit(solution)/shard_map/ppermute | solution.py:688
  159.8 4.3 collective-permute-start.14
  162.8 57.0 %collective-permute-start.17 = (bf16[256,768]{1,0:T(8,128)(2,1)S(1)}, bf16[256,768]{1,0:T(8,128)(2,1)S(1)}, u32[]{:S(2)}, u32[]{:S(2)}) collective-permute-start(bf16[256,768]{1,0:T(8,128)(2,1)S(1)} %get-tuple-element.1089), channel_id=1, source_target_pairs={{8,0},{16,8},{24,16},{9,1},{17,9},{25,17},{10,2},{18,10},{26,18},{... | collective-permute-start | bytes 1179656 | tf_op jit(solution)/shard_map/ppermute | solution.py:688
  174.2 59.7 %collective-permute-start.16 = (bf16[256,768]{1,0:T(8,128)(2,1)S(1)}, bf16[256,768]{1,0:T(8,128)(2,1)S(1)}, u32[]{:S(2)}, u32[]{:S(2)}) collective-permute-start(bf16[256,768]{1,0:T(8,128)(2,1)S(1)} %get-tuple-element.1088), channel_id=1, source_target_pairs={{8,0},{16,8},{24,16},{9,1},{17,9},{25,17},{10,2},{18,10},{26,18},{... | collective-permute-start | bytes 1179656 | tf_op jit(solution)/shard_map/ppermute | solution.py:688
  230.6 16.3 %collective-permute-start.19 = (bf16[256,768]{1,0:T(8,128)(2,1)S(1)}, bf16[256,768]{1,0:T(8,128)(2,1)S(1)}, u32[]{:S(2)}, u32[]{:S(2)}) collective-permute-start(bf16[256,768]{1,0:T(8,128)(2,1)S(1)} %get-tuple-element.1127), channel_id=1, source_target_pairs={{8,0},{16,8},{24,16},{9,1},{17,9},{25,17},{10,2},{18,10},{26,18},{... | collective-permute-start | bytes 1179656 | tf_op jit(solution)/shard_map/ppermute | solution.py:688
  245.4 15.0 %collective-permute-start.18 = (bf16[256,768]{1,0:T(8,128)(2,1)S(1)}, bf16[256,768]{1,0:T(8,128)(2,1)S(1)}, u32[]{:S(2)}, u32[]{:S(2)}) collective-permute-start(bf16[256,768]{1,0:T(8,128)(2,1)S(1)} %get-tuple-element.1126), channel_id=1, source_target_pairs={{8,0},{16,8},{24,16},{9,1},{17,9},{25,17},{10,2},{18,10},{26,18},{... | collective-permute-start | bytes 1179656 | tf_op jit(solution)/shard_map/ppermute | solution.py:688
  257.8 15.5 %collective-permute-start.21 = (bf16[256,768]{1,0:T(8,128)(2,1)S(1)}, bf16[256,768]{1,0:T(8,128)(2,1)S(1)}, u32[]{:S(2)}, u32[]{:S(2)}) collective-permute-start(bf16[256,768]{1,0:T(8,128)(2,1)S(1)} %get-tuple-element.1165), channel_id=1, source_target_pairs={{8,0},{16,8},{9,1},{17,9},{10,2},{18,10},{11,3},{19,11},{12,4},{20... | collective-permute-start | bytes 1179656 | tf_op jit(solution)/shard_map/ppermute | solution.py:688
  272.0 14.8 %collective-permute-start.20 = (bf16[256,768]{1,0:T(8,128)(2,1)S(1)}, bf16[256,768]{1,0:T(8,128)(2,1)S(1)}, u32[]{:S(2)}, u32[]{:S(2)}) collective-permute-start(bf16[256,768]{1,0:T(8,128)(2,1)S(1)} %get-tuple-element.1164), channel_id=1, source_target_pairs={{8,0},{16,8},{9,1},{17,9},{10,2},{18,10},{11,3},{19,11},{12,4},{20... | collective-permute-start | bytes 1179656 | tf_op jit(solution)/shard_map/ppermute | solution.py:688
  284.2 15.3 %collective-permute-start.23 = (bf16[256,768]{1,0:T(8,128)(2,1)S(1)}, bf16[256,768]{1,0:T(8,128)(2,1)S(1)}, u32[]{:S(2)}, u32[]{:S(2)}) collective-permute-start(bf16[256,768]{1,0:T(8,128)(2,1)S(1)} %get-tuple-element.1203), channel_id=1, source_target_pairs={{8,0},{9,1},{10,2},{11,3},{12,4},{13,5},{14,6},{15,7}} | collective-permute-start | bytes 1179656 | tf_op jit(solution)/shard_map/ppermute | solution.py:688
  298.2 13.6 %collective-permute-start.22 = (bf16[256,768]{1,0:T(8,128)(2,1)S(1)}, bf16[256,768]{1,0:T(8,128)(2,1)S(1)}, u32[]{:S(2)}, u32[]{:S(2)}) collective-permute-start(bf16[256,768]{1,0:T(8,128)(2,1)S(1)} %get-tuple-element.1202), channel_id=1, source_target_pairs={{8,0},{9,1},{10,2},{11,3},{12,4},{13,5},{14,6},{15,7}} | collective-permute-start | bytes 1179656 | tf_op jit(solution)/shard_map/ppermute | solution.py:688
  324.1 16.7 %slice-start = ((s8[12582912]{0:T(1024)(128)(4,1)}), s8[4194304]{0:T(1024)(128)(4,1)S(1)}, s32[]{:S(2)}) async-start(s8[12582912]{0:T(1024)(128)(4,1)} %bitcast.60), calls=%async_computation | async-start | bytes 8388608
  324.1 16.7 %slice-start.1 = ((s8[12582912]{0:T(1024)(128)(4,1)}), s8[4194304]{0:T(1024)(128)(4,1)S(1)}, s32[]{:S(2)}) async-start(s8[12582912]{0:T(1024)(128)(4,1)} %bitcast.60), calls=%async_computation.1 | async-start | bytes 8388608
  332.9 7.4 %collective-permute-start.28 = (bf16[2,384,768]{2,1,0:T(8,128)(2,1)}, bf16[2,384,768]{2,1,0:T(8,128)(2,1)S(1)}, u32[]{:S(2)}, u32[]{:S(2)}) collective-permute-start(bf16[2,384,768]{2,1,0:T(8,128)(2,1)} %get-tuple-element.1251), channel_id=1, source_target_pairs={{0,2},{2,0},{4,6},{6,4},{1,3},{3,1},{5,7},{7,5},{8,10},{10,8},{12,... | collective-permute-start | bytes 3538952 | tf_op jit(solution)/shard_map/ppermute | solution.py:610
  339.8 17.4 %collective-permute-start.26 = (bf16[2,384,768]{2,1,0:T(8,128)(2,1)}, bf16[2,384,768]{2,1,0:T(8,128)(2,1)S(1)}, u32[]{:S(2)}, u32[]{:S(2)}) collective-permute-start(bf16[2,384,768]{2,1,0:T(8,128)(2,1)} %get-tuple-element.1246), channel_id=1, source_target_pairs={{0,2},{2,0},{4,6},{6,4},{1,3},{3,1},{5,7},{7,5},{8,10},{10,8},{12,... | collective-permute-start | bytes 3538952 | tf_op jit(solution)/shard_map/ppermute | solution.py:610
  340.7 16.7 %collective-permute-start.29 = (bf16[384,768]{1,0:T(8,128)(2,1)S(1)}, bf16[384,768]{1,0:T(8,128)(2,1)S(1)}, u32[]{:S(2)}, u32[]{:S(2)}) collective-permute-start(bf16[384,768]{1,0:T(8,128)(2,1)S(1)} %add_parts.13.refs_2_), channel_id=1, source_target_pairs={{0,4},{2,6},{4,0},{6,2},{1,5},{3,7},{5,1},{7,3},{8,12},{10,14},{12... | collective-permute-start | bytes 1769480 | tf_op jit(solution)/shard_map/ppermute | solution.py:610
  340.9 16.3 %copy-start.9 = (bf16[2,384,768]{2,1,0:T(8,128)(2,1)S(1)}, bf16[2,384,768]{2,1,0:T(8,128)(2,1)}, u32[]{:S(2)}) copy-start(bf16[2,384,768]{2,1,0:T(8,128)(2,1)} %get-tuple-element.1245.refs_0_) | copy-start | bytes 3538948
  349.2 18.1 %collective-permute-start.32 = (bf16[2,384,768]{2,1,0:T(8,128)(2,1)}, bf16[2,384,768]{2,1,0:T(8,128)(2,1)S(1)}, u32[]{:S(2)}, u32[]{:S(2)}) collective-permute-start(bf16[2,384,768]{2,1,0:T(8,128)(2,1)} %get-tuple-element.1257), channel_id=1, source_target_pairs={{0,2},{2,0},{4,6},{6,4},{1,3},{3,1},{5,7},{7,5},{8,10},{10,8},{12,... | collective-permute-start | bytes 3538952 | tf_op jit(solution)/shard_map/ppermute | solution.py:610
  349.3 2.5 collective-permute-start.24
  351.9 4.8 %collective-permute-start.25 = (f32[8,768]{1,0:T(8,128)S(1)}, f32[8,768]{1,0:T(8,128)S(1)}, u32[]{:S(2)}, u32[]{:S(2)}) collective-permute-start(f32[8,768]{1,0:T(8,128)S(1)} %add_vectors.3.refs_0_), channel_id=1, source_target_pairs={{0,4},{2,6},{4,0},{6,2},{1,5},{3,7},{5,1},{7,3},{8,12},{10,14},{12... | collective-permute-start | bytes 73736 | tf_op jit(solution)/shard_map/ppermute | solution.py:610
  357.4 14.5 %collective-permute-start.31 = (bf16[384,768]{1,0:T(8,128)(2,1)S(1)}, bf16[384,768]{1,0:T(8,128)(2,1)S(1)}, u32[]{:S(2)}, u32[]{:S(2)}) collective-permute-start(bf16[384,768]{1,0:T(8,128)(2,1)S(1)} %add_parts.12.refs_2_), channel_id=1, source_target_pairs={{0,4},{2,6},{4,0},{6,2},{1,5},{3,7},{5,1},{7,3},{8,12},{10,14},{12... | collective-permute-start | bytes 1769480 | tf_op jit(solution)/shard_map/ppermute | solution.py:610
  358.8 14.7 %collective-permute-start.36 = (bf16[384,768]{1,0:T(8,128)(2,1)S(1)}, bf16[384,768]{1,0:T(8,128)(2,1)S(1)}, u32[]{:S(2)}, u32[]{:S(2)}) collective-permute-start(bf16[384,768]{1,0:T(8,128)(2,1)S(1)} %add_parts.19), channel_id=1, source_target_pairs={{0,1},{1,0},{2,3},{3,2},{4,5},{5,4},{6,7},{7,6},{8,9},{9,8},{10,11... | collective-permute-start | bytes 1769480 | tf_op jit(solution)/shard_map/ppermute | solution.py:610
  367.2 13.5 %collective-permute-start.30 = (bf16[2,384,768]{2,1,0:T(8,128)(2,1)}, bf16[2,384,768]{2,1,0:T(8,128)(2,1)S(1)}, u32[]{:S(2)}, u32[]{:S(2)}) collective-permute-start(bf16[2,384,768]{2,1,0:T(8,128)(2,1)} %get-tuple-element.1255), channel_id=1, source_target_pairs={{0,2},{2,0},{4,6},{6,4},{1,3},{3,1},{5,7},{7,5},{8,10},{10,8},{12,... | collective-permute-start | bytes 3538952 | tf_op jit(solution)/shard_map/ppermute | solution.py:610
  371.9 13.5 %collective-permute-start.33 = (bf16[384,768]{1,0:T(8,128)(2,1)S(1)}, bf16[384,768]{1,0:T(8,128)(2,1)S(1)}, u32[]{:S(2)}, u32[]{:S(2)}) collective-permute-start(bf16[384,768]{1,0:T(8,128)(2,1)S(1)} %add_parts.14.refs_1_), channel_id=1, source_target_pairs={{0,4},{2,6},{4,0},{6,2},{1,5},{3,7},{5,1},{7,3},{8,12},{10,14},{12... | collective-permute-start | bytes 1769480 | tf_op jit(solution)/shard_map/ppermute | solution.py:610
  373.5 13.9 %collective-permute-start.37 = (bf16[384,768]{1,0:T(8,128)(2,1)S(1)}, bf16[384,768]{1,0:T(8,128)(2,1)S(1)}, u32[]{:S(2)}, u32[]{:S(2)}) collective-permute-start(bf16[384,768]{1,0:T(8,128)(2,1)S(1)} %add_parts.20), channel_id=1, source_target_pairs={{0,1},{1,0},{2,3},{3,2},{4,5},{5,4},{6,7},{7,6},{8,9},{9,8},{10,11... | collective-permute-start | bytes 1769480 | tf_op jit(solution)/shard_map/ppermute | solution.py:610
  380.7 22.7 %collective-permute-start.35 = (bf16[2,384,768]{2,1,0:T(8,128)(2,1)}, bf16[2,384,768]{2,1,0:T(8,128)(2,1)S(1)}, u32[]{:S(2)}, u32[]{:S(2)}) collective-permute-start(bf16[2,384,768]{2,1,0:T(8,128)(2,1)} %get-tuple-element.1263), channel_id=1, source_target_pairs={{0,2},{2,0},{4,6},{6,4},{1,3},{3,1},{5,7},{7,5},{8,10},{10,8},{12,... | collective-permute-start | bytes 3538952 | tf_op jit(solution)/shard_map/ppermute | solution.py:610
  385.4 18.9 %collective-permute-start.34 = (bf16[384,768]{1,0:T(8,128)(2,1)}, bf16[384,768]{1,0:T(8,128)(2,1)}, u32[]{:S(2)}, u32[]{:S(2)}) collective-permute-start(bf16[384,768]{1,0:T(8,128)(2,1)} %add_parts.15.refs_1_), channel_id=1, source_target_pairs={{0,4},{2,6},{4,0},{6,2},{1,5},{3,7},{5,1},{7,3},{8,12},{10,14},{12... | collective-permute-start | bytes 1769480 | tf_op jit(solution)/shard_map/ppermute | solution.py:610
  387.4 19.9 %collective-permute-start.38 = (bf16[384,768]{1,0:T(8,128)(2,1)}, bf16[384,768]{1,0:T(8,128)(2,1)}, u32[]{:S(2)}, u32[]{:S(2)}) collective-permute-start(bf16[384,768]{1,0:T(8,128)(2,1)} %add_parts.18), channel_id=1, source_target_pairs={{0,1},{1,0},{2,3},{3,2},{4,5},{5,4},{6,7},{7,6},{8,9},{9,8},{10,11... | collective-permute-start | bytes 1769480 | tf_op jit(solution)/shard_map/ppermute | solution.py:610
  394.8 21.5 %collective-permute-start.41 = (bf16[2,384,768]{2,1,0:T(8,128)(2,1)}, bf16[2,384,768]{2,1,0:T(8,128)(2,1)}, u32[]{:S(2)}, u32[]{:S(2)}) collective-permute-start(bf16[2,384,768]{2,1,0:T(8,128)(2,1)} %get-tuple-element.1275), channel_id=1, source_target_pairs={{0,2},{2,0},{4,6},{6,4},{1,3},{3,1},{5,7},{7,5},{8,10},{10,8},{12,... | collective-permute-start | bytes 3538952 | tf_op jit(solution)/shard_map/ppermute | solution.py:610
  394.9 5.7 %collective-permute-start.27 = (f32[8,768]{1,0:T(8,128)}, f32[8,768]{1,0:T(8,128)}, u32[]{:S(2)}, u32[]{:S(2)}) collective-permute-start(f32[8,768]{1,0:T(8,128)} %add_vectors.4.refs_0_), channel_id=1, source_target_pairs={{0,1},{1,0},{2,3},{3,2},{4,5},{5,4},{6,7},{7,6},{8,9},{9,8},{10,11... | collective-permute-start | bytes 73736 | tf_op jit(solution)/shard_map/ppermute | solution.py:610
  404.3 14.3 %collective-permute-start.40 = (bf16[384,768]{1,0:T(8,128)(2,1)}, bf16[384,768]{1,0:T(8,128)(2,1)}, u32[]{:S(2)}, u32[]{:S(2)}) collective-permute-start(bf16[384,768]{1,0:T(8,128)(2,1)} %add_parts.16), channel_id=1, source_target_pairs={{0,4},{2,6},{4,0},{6,2},{1,5},{3,7},{5,1},{7,3},{8,12},{10,14},{12... | collective-permute-start | bytes 1769480 | tf_op jit(solution)/shard_map/ppermute | solution.py:610
  407.3 14.3 %collective-permute-start.39 = (bf16[384,768]{1,0:T(8,128)(2,1)}, bf16[384,768]{1,0:T(8,128)(2,1)}, u32[]{:S(2)}, u32[]{:S(2)}) collective-permute-start(bf16[384,768]{1,0:T(8,128)(2,1)} %add_parts.17), channel_id=1, source_target_pairs={{0,1},{1,0},{2,3},{3,2},{4,5},{5,4},{6,7},{7,6},{8,9},{9,8},{10,11... | collective-permute-start | bytes 1769480 | tf_op jit(solution)/shard_map/ppermute | solution.py:610
  418.6 13.6 %collective-permute-start.43 = (bf16[384,768]{1,0:T(8,128)(2,1)}, bf16[384,768]{1,0:T(8,128)(2,1)}, u32[]{:S(2)}, u32[]{:S(2)}) collective-permute-start(bf16[384,768]{1,0:T(8,128)(2,1)} %add_parts.21), channel_id=1, source_target_pairs={{0,4},{2,6},{4,0},{6,2},{1,5},{3,7},{5,1},{7,3},{8,12},{10,14},{12... | collective-permute-start | bytes 1769480 | tf_op jit(solution)/shard_map/ppermute | solution.py:610
  421.6 13.7 %collective-permute-start.42 = (bf16[384,768]{1,0:T(8,128)(2,1)}, bf16[384,768]{1,0:T(8,128)(2,1)}, u32[]{:S(2)}, u32[]{:S(2)}) collective-permute-start(bf16[384,768]{1,0:T(8,128)(2,1)} %add_parts.22), channel_id=1, source_target_pairs={{0,1},{1,0},{2,3},{3,2},{4,5},{5,4},{6,7},{7,6},{8,9},{9,8},{10,11... | collective-permute-start | bytes 1769480 | tf_op jit(solution)/shard_map/ppermute | solution.py:610
  435.3 12.1 %collective-permute-start.44 = (bf16[384,768]{1,0:T(8,128)(2,1)S(1)}, bf16[384,768]{1,0:T(8,128)(2,1)S(1)}, u32[]{:S(2)}, u32[]{:S(2)}) collective-permute-start(bf16[384,768]{1,0:T(8,128)(2,1)S(1)} %add_parts.23), channel_id=1, source_target_pairs={{0,1},{1,0},{2,3},{3,2},{4,5},{5,4},{6,7},{7,6},{8,9},{9,8},{10,11... | collective-permute-start | bytes 1769480 | tf_op jit(solution)/shard_map/ppermute | solution.py:610
  (25 other events, 199.5 us)

commit v7 on v6

--- a/solution.py
+++ b/solution.py
@@ -74,7 +74,7 @@
                    t_ref, meta_ref, tok_ref, arr_ref, cos_ref, sin_ref,
                    wq_ref, wo_ref, wu_ref, wd_ref, gb_ref, s_in,
                    y_ref, s_out, all_o, x_o, att_o, hb_o, act_o, qn_o, kf_o, v_o, sg_o, n1_o, gp_o, n2_o, rs_o, sb_o,
-                   x_ref, att_ref, hb_ref, act_ref, qn_ref, kf_ref, v_ref, sg_ref, n1_ref, gp_ref, n2_ref, rs_ref, sb_ref, sems, loads=()):
+                   x_ref, att_ref, hb_ref, act_ref, qn_ref, kf_ref, v_ref, sg_ref, n1_ref, gp_ref, n2_ref, rs_ref, sb_ref, sems, loads=(), final=False):
     stage = meta_ref[0]
     chunk = t_ref[0] - delta * stage
     valid = (chunk >= 0) & (chunk < n)
@@ -184,10 +184,11 @@
         n2_ref[...] = n2.astype(bf)
         lane = lax.broadcasted_iota(jnp.int32, (rows, 128), 1)
         rs_ref[...] = jnp.where(lane < 64, r1, r2)
-        send.put(n2_ref, n2_o.at[here, :])
-        send.put(rs_ref, rs_o.at[here, :])
         y_ref[...] = (n2 * gb_ref[2:3, :] + gb_ref[3:4, :]).astype(bf)
-        send.put(y_ref, all_o.at[here, :])
+        if final:
+            send.put(n2_ref, n2_o.at[here, :])
+            send.put(rs_ref, rs_o.at[here, :])
+            send.put(y_ref, all_o.at[here, :])
         loaded(5)
         send.finish()
 
@@ -201,8 +202,7 @@
 
 
 def forward_opening(delta, n, rows, *refs):
-    ins, refs = refs[:11], refs[11:]
-    outs, kept, scratch, load_sems = refs[:16], refs[16:25], refs[25:-1], refs[-1]
+    ins, outs, big, kept, scratch, sems, load_sems = refs[:11], refs[11:15], refs[15:29], refs[29:38], refs[38:49], refs[49], refs[50]
     tok, cos, sin, *weights, gb = ins[3:]
     tok_v, _, _, *weights_v = kept[:7]
     head, tail = pl.ds(0, rows), pl.ds(rows, (n - 1) * rows)
@@ -210,12 +210,30 @@
     loads = [pltpu.make_async_copy(src, dst, load_sems.at[i]) for i, (src, dst) in enumerate(pairs)]
     for copy in loads:
         copy.start()
-    forward_kernel(delta, n, rows, *ins[:2], tok_v, ins[2], cos, sin, *weights_v, gb, None, *outs, *scratch, loads=loads)
-
-
-def forward_next(delta, n, rows, *refs):
-    t, meta, arr, tok, cos, sin, wq, wo, wu, wd, gb, _, s_in = refs[:13]
-    forward_kernel(delta, n, rows, t, meta, tok, arr, cos, sin, wq, wo, wu, wd, gb, s_in, *refs[27:43], *refs[52:])
+    forward_kernel(delta, n, rows, *ins[:2], tok_v, ins[2], cos, sin, *weights_v, gb, None, *outs[:2], *big,
+                   *scratch[:10], *outs[2:], scratch[10], sems, loads=loads)
+
+
+def forward_next(delta, n, rows, final, *refs):
+    t, meta, arr, tok = refs[:4]
+    outs, big, scratch, sems, before_sems = refs[30:34], refs[34:48], refs[57:68], refs[68], refs[69]
+    before = t[0] - 1 - delta * meta[0]
+    there = pl.ds(pl.multiple_of(jnp.clip(before, 0, n - 1) * rows, rows), rows)
+    copies = [pltpu.make_async_copy(src, big[i].at[there, :], before_sems.at[j]) for j, (src, i) in enumerate(zip(refs[13:16], (0, 11, 12)))]
+    pending = (before >= 0) & (before < n)
+
+    @pl.when(pending)
+    def _():
+        for copy in copies:
+            copy.start()
+
+    forward_kernel(delta, n, rows, t, meta, tok, arr, *refs[4:11], refs[12], *outs[:2], *big,
+                   *scratch[:10], *outs[2:], scratch[10], sems, final=final)
+
+    @pl.when(pending)
+    def _():
+        for copy in copies:
+            copy.wait()
 
 
 def saved_items(rows):
@@ -228,7 +246,7 @@
             ((4, D), f32), ((TILES, every, TILE), bf)]
 
 
-def forward_call(rows, n, delta, opening, limit=17):
+def forward_call(rows, n, delta, opening, final, limit=17):
     V = pl.BlockSpec(memory_space=pltpu.VMEM)
     S = pl.BlockSpec(memory_space=pltpu.SMEM)
     A = pl.BlockSpec(memory_space=pl.ANY)
@@ -237,15 +255,18 @@
     big = [pltpu.HBM((every, D), bf)] + [pltpu.HBM(*item) for item in saved_items(every)]
     big[4] = pltpu.HBM((TILES, every, TILE), bf)
     big[13] = pltpu.HBM((n, PAIRS, 256, 256), bf)
-    aliases = {4: 17, 5: 18, 10: 23}
+    own = saved_items(rows)
+    handed = [sd((rows, D), bf), sd((PAIRS, 256, 256), f32), sd(*own[10]), sd(*own[11])]
+    aliases = {4: 19, 5: 20, 10: 25}
     if not opening:
-        aliases = {12: 1, **{13 + i: 2 + i for i in range(14)}, **{3 + i: 16 + i for i in range(9)}}
+        aliases = {12: 1, **{16 + i: 4 + i for i in range(14)}, **{3 + i: 18 + i for i in range(9)}}
     return pl.pallas_call(
-        functools.partial(forward_opening if opening else forward_next, delta, n, rows),
-        in_specs=[S, S, V, A, V, V, A, A, A, A, V] if opening else [S, S] + [V] * 11 + [A] * 14,
-        out_specs=[V, V] + [A] * 14 + [V] * 9,
-        out_shape=[sd((rows, D), bf), sd((PAIRS, 256, 256), f32)] + big + [pltpu.VMEM(*item) for item in kept_items(every)],
-        scratch_shapes=[pltpu.VMEM(*item) for item in saved_items(rows)] + [pltpu.SemaphoreType.DMA((30,))] + [pltpu.SemaphoreType.DMA((6,))] * opening,
+        functools.partial(forward_opening, delta, n, rows) if opening else functools.partial(forward_next, delta, n, rows, final),
+        in_specs=[S, S, V, A, V, V, A, A, A, A, V] if opening else [S, S] + [V] * 14 + [A] * 14,
+        out_specs=[V] * 4 + [A] * 14 + [V] * 9,
+        out_shape=handed + big + [pltpu.VMEM(*item) for item in kept_items(every)],
+        scratch_shapes=[pltpu.VMEM(*item) for item in own[:10] + own[12:]]
+        + [pltpu.SemaphoreType.DMA((30,)), pltpu.SemaphoreType.DMA((6 if opening else 3,))],
         input_output_aliases=aliases,
         cost_estimate=pl.CostEstimate(flops=rows * 2 * 9 * 10**6, bytes_accessed=4 * 2**20, transcendentals=0),
         compiler_params=pltpu.CompilerParams(vmem_limit_bytes=limit * 2**20),
@@ -672,8 +693,8 @@
     resident = resident + [gb]
     state, big = (), ()
     for t in range(ticks):
-        made = forward_call(ROWS, n, DELTA, t == 0)(jnp.full((1,), t, jnp.int32), meta, arriving.pop(0), *resident, *state, *big)
-        state, big, resident = made[1:2], made[2:16], made[16:]
+        made = forward_call(ROWS, n, DELTA, t == 0, t == ticks - 1)(jnp.full((1,), t, jnp.int32), meta, arriving.pop(0), *resident, *state, *big)
+        state, big, resident = [made[1], made[0], made[2], made[3]], made[4:18], made[18:]
         route = [(a, a + 1) for a in range(stages - 1) if 0 <= t - a * DELTA < n]
         arriving.append(lax.ppermute(made[0], "pipe", route) if route else made[0])
     block_out, x, att, hb, act, qn, kf, v, sg, n1, gp, n2, rs, sb = big

time: 457 us -> 452 us (0.989)
  no operation moved by 1% of the time
where the time goes in v7:
time: 452 us; the launch traced here: 444 us
  Pallas kernels  288 us (64%)
  waiting for transfers between devices  83.3 us (18%)
  starting transfers between devices  47.8 us (11%)
  other arithmetic  12.6 us (3%)
  local copies, waits for them, and re-layouts  10.1 us (2%)
    pallas_call x14, Pallas kernels, local(): backward_call(ROWS, n, DELTA, stages, groups, t == 0)  126 us
    pallas_call x14, Pallas kernels, local(): forward_call(ROWS, n, DELTA, t == 0, t == ticks - 1)  102 us
    ppermute x24, waiting for transfers between devices, local(): arriving.append(lax.ppermute(made[0], 'pipe', route) if route else made[0])  52.1 us
    pallas_call x6, Pallas kernels, local(): call(meta, left, *(far(rights) if fetch else rights), *waits)  45.9 us
    ppermute x24, starting transfers between devices, local(): arriving.append(lax.ppermute(made[0], 'pipe', route) if route else made[0])  31.9 us
    ppermute x21, waiting for transfers between devices, exchange(): return lax.ppermute(block, axis, route)  31.2 us
    ppermute x21, starting transfers between devices, exchange(): return lax.ppermute(block, axis, route)  15.9 us
    pallas_call x12, Pallas kernels, add_call(): pl.pallas_call(add_kernel, grid=(rows // step,), in_specs=[pick, pick] +...  11.9 us
  transfers between devices with their start and end apart: 45, of which 15 were waited for; matrix products, arithmetic and copies ran while one was open for 4% of the time, Pallas kernels for 55%

profile of v7, /device:TPU:0, one launch (start us, length us, event | category | flops | bytes accessed | tf_op | source)
XLA Modules:
  0.0 443.9 jit_solution(8405796720981163275)
XLA Ops:
  4.2 10.8 %layer_forward.14 = (bf16[256,768]{1,0:T(8,128)(2,1)S(1)}, f32[6,256,256]{2,1,0:T(8,128)S(1)}, bf16[256,768]{1,0:T(8,128)(2,1)S(1)}, f32[256,128]{1,0:T(8,128)S(...) custom-call(s32[1]{0:T(128)} %constant.21.clone.1.refs_0_, ...), custom_call_target="tpu_custom_call", output_to_operand_aliasing={{19}: (4, {}), {20}: (5, {}), {25}: (10, {})} | custom-call | flops 4608000000 | bytes 4194304 | tf_op jit(solution)/shard_map/layer_forward/pallas_call | solution.py:696
  16.4 8.9 %layer_forward.15 = (bf16[256,768]{1,0:T(8,128)(2,1)S(1)}, f32[6,256,256]{2,1,0:T(8,128)S(1)}, bf16[256,768]{1,0:T(8,128)(2,1)S(1)}, f32[256,128]{1,0:T(8,128)S(...) custom-call(s32[1]{0:T(128)} %constant.19.clone.1.refs_0_, ...), custom_call_target="tpu_custom_call", output_to_operand_aliasing={{1}: (12, {}), {4}: (16, {}), {5}: (17, {}), {6}: (18, {}),... | custom-call | flops 4608000000 | bytes 4194304 | tf_op jit(solution)/shard_map/layer_forward/pallas_call | solution.py:696
  26.6 8.5 %layer_forward.16 = (bf16[256,768]{1,0:T(8,128)(2,1)S(1)}, f32[6,256,256]{2,1,0:T(8,128)S(1)}, bf16[256,768]{1,0:T(8,128)(2,1)S(1)}, f32[256,128]{1,0:T(8,128)S(...) custom-call(s32[1]{0:T(128)} %constant.23.clone.1.refs_0_, ...), custom_call_target="tpu_custom_call", output_to_operand_aliasing={{1}: (12, {}), {4}: (16, {}), {5}: (17, {}), {6}: (18, {}),... | custom-call | flops 4608000000 | bytes 4194304 | tf_op jit(solution)/shard_map/layer_forward/pallas_call | solution.py:696
  35.1 3.3 collective-permute-start.3
  38.4 9.1 %layer_forward.17 = (bf16[256,768]{1,0:T(8,128)(2,1)S(1)}, f32[6,256,256]{2,1,0:T(8,128)S(1)}, bf16[256,768]{1,0:T(8,128)(2,1)S(1)}, f32[256,128]{1,0:T(8,128)S(...) custom-call(s32[1]{0:T(128)} %constant.18.clone.1.refs_0_, ...), custom_call_target="tpu_custom_call", output_to_operand_aliasing={{1}: (12, {}), {4}: (16, {}), {5}: (17, {}), {6}: (18, {}),... | custom-call | flops 4608000000 | bytes 4194304 | tf_op jit(solution)/shard_map/layer_forward/pallas_call | solution.py:696
  47.5 1.9 collective-permute-start.2
  49.4 8.5 %layer_forward.18 = (bf16[256,768]{1,0:T(8,128)(2,1)S(1)}, f32[6,256,256]{2,1,0:T(8,128)S(1)}, bf16[256,768]{1,0:T(8,128)(2,1)S(1)}, f32[256,128]{1,0:T(8,128)S(...) custom-call(s32[1]{0:T(128)} %constant.24.clone.1.refs_0_, ...), custom_call_target="tpu_custom_call", output_to_operand_aliasing={{1}: (12, {}), {4}: (16, {}), {5}: (17, {}), {6}: (18, {}),... | custom-call | flops 4608000000 | bytes 4194304 | tf_op jit(solution)/shard_map/layer_forward/pallas_call | solution.py:696
  59.8 9.0 %layer_forward.19 = (bf16[256,768]{1,0:T(8,128)(2,1)S(1)}, f32[6,256,256]{2,1,0:T(8,128)S(1)}, bf16[256,768]{1,0:T(8,128)(2,1)S(1)}, f32[256,128]{1,0:T(8,128)S(...) custom-call(s32[1]{0:T(128)} %constant.40.clone.1.refs_0_, ...), custom_call_target="tpu_custom_call", output_to_operand_aliasing={{1}: (12, {}), {4}: (16, {}), {5}: (17, {}), {6}: (18, {}),... | custom-call | flops 4608000000 | bytes 4194304 | tf_op jit(solution)/shard_map/layer_forward/pallas_call | solution.py:696
  68.8 2.2 collective-permute-start.4
  71.0 8.4 %layer_forward.20 = (bf16[256,768]{1,0:T(8,128)(2,1)S(1)}, f32[6,256,256]{2,1,0:T(8,128)S(1)}, bf16[256,768]{1,0:T(8,128)(2,1)S(1)}, f32[256,128]{1,0:T(8,128)S(...) custom-call(s32[1]{0:T(128)} %constant.25.clone.1.refs_0_, ...), custom_call_target="tpu_custom_call", output_to_operand_aliasing={{1}: (12, {}), {4}: (16, {}), {5}: (17, {}), {6}: (18, {}),... | custom-call | flops 4608000000 | bytes 4194304 | tf_op jit(solution)/shard_map/layer_forward/pallas_call | solution.py:696
  79.5 2.3 collective-permute-start.7
  81.7 9.2 %layer_forward.21 = (bf16[256,768]{1,0:T(8,128)(2,1)S(1)}, f32[6,256,256]{2,1,0:T(8,128)S(1)}, bf16[256,768]{1,0:T(8,128)(2,1)S(1)}, f32[256,128]{1,0:T(8,128)S(...) custom-call(s32[1]{0:T(128)} %constant.39.clone.1.refs_0_, ...), custom_call_target="tpu_custom_call", output_to_operand_aliasing={{1}: (12, {}), {4}: (16, {}), {5}: (17, {}), {6}: (18, {}),... | custom-call | flops 4608000000 | bytes 4194304 | tf_op jit(solution)/shard_map/layer_forward/pallas_call | solution.py:696
  95.4 5.2 %collective-permute-done.6.refs_2_ = bf16[256,768]{1,0:T(8,128)(2,1)S(1)} collective-permute-done((bf16[256,768]{1,0:T(8,128)(2,1)S(1)}, bf16[256,768]{1,0:T(8,128)(2,1)S(1)}, u32[]{:S(2)}, u32[]{:S(2)}) %collective-permute-start.6) | collective-permute-done | bytes 393248 | tf_op jit(solution)/shard_map/ppermute | solution.py:699
  100.5 6.9 %layer_forward.23 = (bf16[256,768]{1,0:T(8,128)(2,1)S(1)}, f32[6,256,256]{2,1,0:T(8,128)S(1)}, bf16[256,768]{1,0:T(8,128)(2,1)S(1)}, f32[256,128]{1,0:T(8,128)S(...) custom-call(s32[1]{0:T(128)} %constant.38.clone.1.refs_0_, ...), custom_call_target="tpu_custom_call", output_to_operand_aliasing={{1}: (12, {}), {4}: (16, {}), {5}: (17, {}), {6}: (18, {}),... | custom-call | flops 4608000000 | bytes 4194304 | tf_op jit(solution)/shard_map/layer_forward/pallas_call | solution.py:696
  109.7 8.7 %layer_forward.25 = (bf16[256,768]{1,0:T(8,128)(2,1)S(1)}, f32[6,256,256]{2,1,0:T(8,128)S(1)}, bf16[256,768]{1,0:T(8,128)(2,1)S(1)}, f32[256,128]{1,0:T(8,128)S(...) custom-call(s32[1]{0:T(128)} %constant.17.clone.1.refs_0_, ...), custom_call_target="tpu_custom_call", output_to_operand_aliasing={{1}: (12, {}), {4}: (16, {}), {5}: (17, {}), {6}: (18, {}),... | custom-call | flops 4608000000 | bytes 4194304 | tf_op jit(solution)/shard_map/layer_forward/pallas_call | solution.py:696
  120.1 10.9 %layer_forward.27 = (bf16[256,768]{1,0:T(8,128)(2,1)S(1)}, f32[6,256,256]{2,1,0:T(8,128)S(1)}, bf16[256,768]{1,0:T(8,128)(2,1)}, f32[256,128]{1,0:T(8,128)}, bf1...) custom-call(s32[1]{0:T(128)} %constant.29.clone.1.refs_0_, ...), custom_call_target="tpu_custom_call", output_to_operand_aliasing={{1}: (12, {}), {4}: (16, {}), {5}: (17, {}), {6}: (18, {}),... | custom-call | flops 4608000000 | bytes 4194304 | tf_op jit(solution)/shard_map/layer_forward/pallas_call | solution.py:696
  130.9 3.0 layer_backward.14
  134.6 8.7 %layer_backward.15 = (bf16[256,768]{1,0:T(8,128)(2,1)S(1)}, f32[6,256,256]{2,1,0:T(8,128)S(1)}, f32[8,768]{1,0:T(8,128)S(1)}, bf16[2048,768]{1,0:T(8,128)(2,1)},...) custom-call(s32[1]{0:T(128)} %constant.19.clone.1.refs_0_, ...), custom_call_target="tpu_custom_call", output_to_operand_aliasing={{7}: (3, {}), {8}: (4, {}), {9}: (5, {}), {10}: (6, {}), {1... | custom-call | flops 5120000000 | bytes 4194304 | tf_op jit(solution)/shard_map/layer_backward/pallas_call | solution.py:704
  144.0 2.3 layer_backward.16
  147.1 9.1 %layer_backward.17 = (bf16[256,768]{1,0:T(8,128)(2,1)S(1)}, f32[6,256,256]{2,1,0:T(8,128)S(1)}, f32[8,768]{1,0:T(8,128)S(1)}, bf16[2048,768]{1,0:T(8,128)(2,1)},...) custom-call(s32[1]{0:T(128)} %constant.18.clone.1.refs_0_, ...), custom_call_target="tpu_custom_call", output_to_operand_aliasing={{7}: (3, {}), {8}: (4, {}), {9}: (5, {}), {10}: (6, {}), {1... | custom-call | flops 5120000000 | bytes 4194304 | tf_op jit(solution)/shard_map/layer_backward/pallas_call | solution.py:704
  156.9 2.3 layer_backward.18
  160.5 10.1 %layer_backward.19 = (bf16[256,768]{1,0:T(8,128)(2,1)S(1)}, f32[6,256,256]{2,1,0:T(8,128)S(1)}, f32[8,768]{1,0:T(8,128)S(1)}, bf16[2048,768]{1,0:T(8,128)(2,1)},...) custom-call(s32[1]{0:T(128)} %constant.40.clone.1.refs_0_, ...), custom_call_target="tpu_custom_call", output_to_operand_aliasing={{7}: (3, {}), {8}: (4, {}), {9}: (5, {}), {10}: (6, {}), {1... | custom-call | flops 5120000000 | bytes 4194304 | tf_op jit(solution)/shard_map/layer_backward/pallas_call | solution.py:704
  171.9 41.8 %collective-permute-done.17.refs_2_ = bf16[256,768]{1,0:T(8,128)(2,1)S(1)} collective-permute-done((bf16[256,768]{1,0:T(8,128)(2,1)S(1)}, bf16[256,768]{1,0:T(8,128)(2,1)S(1)}, u32[]{:S(2)}, u32[]{:S(2)}) %collective-permute-start.17) | collective-permute-done | bytes 393248 | tf_op jit(solution)/shard_map/ppermute | solution.py:709
  213.7 10.8 %layer_backward.20 = (bf16[256,768]{1,0:T(8,128)(2,1)S(1)}, f32[6,256,256]{2,1,0:T(8,128)S(1)}, f32[8,768]{1,0:T(8,128)S(1)}, bf16[2048,768]{1,0:T(8,128)(2,1)},...) custom-call(s32[1]{0:T(128)} %constant.25.clone.1.refs_0_, ...), custom_call_target="tpu_custom_call", output_to_operand_aliasing={{7}: (3, {}), {8}: (4, {}), {9}: (5, {}), {10}: (6, {}), {1... | custom-call | flops 5120000000 | bytes 4194304 | tf_op jit(solution)/shard_map/layer_backward/pallas_call | solution.py:704
  227.7 11.4 %layer_backward.21 = (bf16[256,768]{1,0:T(8,128)(2,1)S(1)}, f32[6,256,256]{2,1,0:T(8,128)S(1)}, f32[8,768]{1,0:T(8,128)S(1)}, bf16[2048,768]{1,0:T(8,128)(2,1)},...) custom-call(s32[1]{0:T(128)} %constant.39.clone.1.refs_0_, ...), custom_call_target="tpu_custom_call", output_to_operand_aliasing={{7}: (3, {}), {8}: (4, {}), {9}: (5, {}), {10}: (6, {}), {1... | custom-call | flops 5120000000 | bytes 4194304 | tf_op jit(solution)/shard_map/layer_backward/pallas_call | solution.py:704
  240.6 10.8 %layer_backward.22 = (bf16[256,768]{1,0:T(8,128)(2,1)S(1)}, f32[6,256,256]{2,1,0:T(8,128)S(1)}, f32[8,768]{1,0:T(8,128)S(1)}, bf16[2048,768]{1,0:T(8,128)(2,1)},...) custom-call(s32[1]{0:T(128)} %constant.26.clone.1.refs_0_, ...), custom_call_target="tpu_custom_call", output_to_operand_aliasing={{7}: (3, {}), {8}: (4, {}), {9}: (5, {}), {10}: (6, {}), {1... | custom-call | flops 5120000000 | bytes 4194304 | tf_op jit(solution)/shard_map/layer_backward/pallas_call | solution.py:704
  253.9 11.6 %layer_backward.23 = (bf16[256,768]{1,0:T(8,128)(2,1)S(1)}, f32[6,256,256]{2,1,0:T(8,128)S(1)}, f32[8,768]{1,0:T(8,128)S(1)}, bf16[2048,768]{1,0:T(8,128)(2,1)},...) custom-call(s32[1]{0:T(128)} %constant.38.clone.1.refs_0_, ...), custom_call_target="tpu_custom_call", output_to_operand_aliasing={{7}: (3, {}), {8}: (4, {}), {9}: (5, {}), {10}: (6, {}), {1... | custom-call | flops 5120000000 | bytes 4194304 | tf_op jit(solution)/shard_map/layer_backward/pallas_call | solution.py:704
  266.8 10.9 %layer_backward.24 = (bf16[256,768]{1,0:T(8,128)(2,1)S(1)}, f32[6,256,256]{2,1,0:T(8,128)S(1)}, f32[8,768]{1,0:T(8,128)S(1)}, bf16[2048,768]{1,0:T(8,128)(2,1)},...) custom-call(s32[1]{0:T(128)} %constant.27.clone.1.refs_0_, ...), custom_call_target="tpu_custom_call", output_to_operand_aliasing={{7}: (3, {}), {8}: (4, {}), {9}: (5, {}), {10}: (6, {}), {1... | custom-call | flops 5120000000 | bytes 4194304 | tf_op jit(solution)/shard_map/layer_backward/pallas_call | solution.py:704
  280.3 11.3 %layer_backward.25 = (bf16[256,768]{1,0:T(8,128)(2,1)S(1)}, f32[6,256,256]{2,1,0:T(8,128)S(1)}, f32[8,768]{1,0:T(8,128)S(1)}, bf16[2048,768]{1,0:T(8,128)(2,1)},...) custom-call(s32[1]{0:T(128)} %constant.17.clone.1.refs_0_, ...), custom_call_target="tpu_custom_call", output_to_operand_aliasing={{7}: (3, {}), {8}: (4, {}), {9}: (5, {}), {10}: (6, {}), {1... | custom-call | flops 5120000000 | bytes 4194304 | tf_op jit(solution)/shard_map/layer_backward/pallas_call | solution.py:704
  292.9 11.6 %layer_backward.26 = (bf16[256,768]{1,0:T(8,128)(2,1)}, f32[6,256,256]{2,1,0:T(8,128)S(1)}, f32[8,768]{1,0:T(8,128)S(1)}, bf16[2048,768]{1,0:T(8,128)(2,1)}, bf1...) custom-call(s32[1]{0:T(128)} %constant.28.clone.1.refs_0_, ...), custom_call_target="tpu_custom_call", output_to_operand_aliasing={{7}: (3, {}), {8}: (4, {}), {9}: (5, {}), {10}: (6, {}), {1... | custom-call | flops 5120000000 | bytes 4194304 | tf_op jit(solution)/shard_map/layer_backward/pallas_call | solution.py:704
  305.2 12.2 %layer_backward.27 = (bf16[256,768]{1,0:T(8,128)(2,1)}, f32[6,256,256]{2,1,0:T(8,128)S(1)}, f32[8,768]{1,0:T(8,128)S(1)}, bf16[2048,768]{1,0:T(8,128)(2,1)}, bf1...) custom-call(s32[1]{0:T(128)} %constant.29.clone.1.refs_0_, ...), custom_call_target="tpu_custom_call", output_to_operand_aliasing={{7}: (3, {}), {8}: (4, {}), {9}: (5, {}), {10}: (6, {}), {1... | custom-call | flops 5120000000 | bytes 4194304 | tf_op jit(solution)/shard_map/layer_backward/pallas_call | solution.py:704
  317.4 8.8 %weight_grad.6 = (bf16[2,384,768]{2,1,0:T(8,128)(2,1)}, bf16[2,384,768]{2,1,0:T(8,128)(2,1)}, bf16[2048,768]{1,0:T(8,128)(2,1)S(1)}) custom-call(s32[18]{0:T(128)S(1)} %pad_add_fusion.refs_1_.meta_ref, bf16[12,2048,256]{2,1,0:T(8,128)(2,1)S(1)} %get-tuple-element.1296.left, bf16[2048,768]{1,0:T(8,128)(2,1)} %get-tuple-element.1297.refs_0_), custom_call_target="tpu_custom_call" | custom-call | flops 4831838208 | bytes 15728640 | tf_op jit(solution)/shard_map/weight_grad/pallas_call | solution.py:731
  326.3 6.8 %weight_grad.7 = (bf16[2,384,768]{2,1,0:T(8,128)(2,1)}, bf16[2,384,768]{2,1,0:T(8,128)(2,1)}) custom-call(s32[18]{0:T(128)S(1)} %pad_add_fusion.refs_1_.meta_ref, bf16[12,2048,256]{2,1,0:T(8,128)(2,1)S(1)} %get-tuple-element.1296.left, bf16[2048,768]{1,0:T(8,128)(2,1)S(1)} %get-tuple-element.1298.refs_0_), custom_call_target="tpu_custom_call" | custom-call | flops 4831838208 | bytes 15728640 | tf_op jit(solution)/shard_map/weight_grad/pallas_call | solution.py:731
  334.0 2.2 collective-permute-start.29
  336.2 8.3 %weight_grad.9 = (bf16[2,384,768]{2,1,0:T(8,128)(2,1)}, bf16[2,384,768]{2,1,0:T(8,128)(2,1)}) custom-call(s32[18]{0:T(128)S(1)} %pad_add_fusion.refs_1_.meta_ref, bf16[12,2048,256]{2,1,0:T(8,128)(2,1)S(1)} %bitcast.61, bf16[2048,768]{1,0:T(8,128)(2,1)S(1)} %copy-done.1, bf16[2048,768]{1,0:T(8,128)(2,1)S(1)} %copy-done, bf16[384,768]{1,0:T(8,128)(2,1)S(1)} %add_parts.13.refs_2_), custom_call_target="tpu_custom_call" | custom-call | flops 4831838208 | bytes 15728640 | tf_op jit(solution)/shard_map/weight_grad/pallas_call | solution.py:731
  345.1 2.0 collective-permute-done.24.refs_1_
  347.3 3.7 collective-permute-done.25.refs_1_
  353.8 8.3 %weight_grad.8 = (bf16[2,384,768]{2,1,0:T(8,128)(2,1)}, bf16[2,384,768]{2,1,0:T(8,128)(2,1)}) custom-call(s32[18]{0:T(128)S(1)} %pad_add_fusion.refs_1_.meta_ref, bf16[12,2048,256]{2,1,0:T(8,128)(2,1)S(1)} %bitcast.61, bf16[2048,768]{1,0:T(8,128)(2,1)S(1)} %copy-done.1, bf16[2048,768]{1,0:T(8,128)(2,1)S(1)} %copy-done, bf16[384,768]{1,0:T(8,128)(2,1)S(1)} %add_parts.12.refs_2_), custom_call_target="tpu_custom_call" | custom-call | flops 4831838208 | bytes 15728640 | tf_op jit(solution)/shard_map/weight_grad/pallas_call | solution.py:731
  362.5 3.8 collective-permute-done.31.refs_2_
  368.5 6.8 %weight_grad.10 = (bf16[2,384,768]{2,1,0:T(8,128)(2,1)}, bf16[2,384,768]{2,1,0:T(8,128)(2,1)}) custom-call(s32[18]{0:T(128)S(1)} %pad_add_fusion.refs_1_.meta_ref, bf16[12,2048,256]{2,1,0:T(8,128)(2,1)S(1)} %bitcast.63, bf16[2048,768]{1,0:T(8,128)(2,1)S(1)} %copy-done.2, bf16[384,768]{1,0:T(8,128)(2,1)S(1)} %add_parts.14.refs_1_), custom_call_target="tpu_custom_call" | custom-call | flops 4831838208 | bytes 15728640 | tf_op jit(solution)/shard_map/weight_grad/pallas_call | solution.py:731
  376.6 3.2 collective-permute-done.33.refs_2_
  382.4 6.8 %weight_grad.11 = (bf16[2,384,768]{2,1,0:T(8,128)(2,1)}, bf16[2,384,768]{2,1,0:T(8,128)(2,1)}) custom-call(s32[18]{0:T(128)S(1)} %pad_add_fusion.refs_1_.meta_ref, bf16[12,2048,256]{2,1,0:T(8,128)(2,1)S(1)} %bitcast.63, bf16[2048,768]{1,0:T(8,128)(2,1)S(1)} %copy-done.2, bf16[384,768]{1,0:T(8,128)(2,1)} %add_parts.15.refs_1_), custom_call_target="tpu_custom_call" | custom-call | flops 4831838208 | bytes 15728640 | tf_op jit(solution)/shard_map/weight_grad/pallas_call | solution.py:731
  390.9 4.1 collective-permute-done.27.refs_1_
  399.7 2.0 add_parts.17
  404.7 3.1 copy.584
  410.8 2.3 add_parts.21
  421.1 5.5 %collective-permute-done.43.refs_2_ = bf16[384,768]{1,0:T(8,128)(2,1)} collective-permute-done((bf16[384,768]{1,0:T(8,128)(2,1)}, bf16[384,768]{1,0:T(8,128)(2,1)}, u32[]{:S(2)}, u32[]{:S(2)}) %collective-permute-start.43) | collective-permute-done | bytes 589856 | tf_op jit(solution)/shard_map/ppermute | solution.py:631
  434.7 7.1 %collective-permute-done.44 = bf16[384,768]{1,0:T(8,128)(2,1)S(1)} collective-permute-done((bf16[384,768]{1,0:T(8,128)(2,1)S(1)}, bf16[384,768]{1,0:T(8,128)(2,1)S(1)}, u32[]{:S(2)}, u32[]{:S(2)}) %collective-permute-start.44) | collective-permute-done | bytes 589856 | tf_op jit(solution)/shard_map/ppermute | solution.py:631
  (188 shorter events, 75.1 us)
Async XLA Ops:
  15.1 11.5 %collective-permute-start.1 = (bf16[256,768]{1,0:T(8,128)(2,1)S(1)}, bf16[256,768]{1,0:T(8,128)(2,1)S(1)}, u32[]{:S(2)}, u32[]{:S(2)}) collective-permute-start(bf16[256,768]{1,0:T(8,128)(2,1)S(1)} %get-tuple-element.685.refs_13_), channel_id=1, source_target_pairs={{0,8},{1,9},{2,10},{3,11},{4,12},{5,13},{6,14},{7,15}} | collective-permute-start | bytes 1179656 | tf_op jit(solution)/shard_map/ppermute | solution.py:699
  25.3 13.1 %collective-permute-start = (bf16[256,768]{1,0:T(8,128)(2,1)S(1)}, bf16[256,768]{1,0:T(8,128)(2,1)S(1)}, u32[]{:S(2)}, u32[]{:S(2)}) collective-permute-start(bf16[256,768]{1,0:T(8,128)(2,1)S(1)} %get-tuple-element.702.refs_13_), channel_id=1, source_target_pairs={{0,8},{1,9},{2,10},{3,11},{4,12},{5,13},{6,14},{7,15}} | collective-permute-start | bytes 1179656 | tf_op jit(solution)/shard_map/ppermute | solution.py:699
  35.1 14.3 %collective-permute-start.3 = (bf16[256,768]{1,0:T(8,128)(2,1)S(1)}, bf16[256,768]{1,0:T(8,128)(2,1)S(1)}, u32[]{:S(2)}, u32[]{:S(2)}) collective-permute-start(bf16[256,768]{1,0:T(8,128)(2,1)S(1)} %get-tuple-element.739.refs_13_), channel_id=1, source_target_pairs={{0,8},{8,16},{1,9},{9,17},{2,10},{10,18},{3,11},{11,19},{4,12},{12... | collective-permute-start | bytes 1179656 | tf_op jit(solution)/shard_map/ppermute | solution.py:699
  47.5 12.4 %collective-permute-start.2 = (bf16[256,768]{1,0:T(8,128)(2,1)S(1)}, bf16[256,768]{1,0:T(8,128)(2,1)S(1)}, u32[]{:S(2)}, u32[]{:S(2)}) collective-permute-start(bf16[256,768]{1,0:T(8,128)(2,1)S(1)} %get-tuple-element.756.refs_13_), channel_id=1, source_target_pairs={{0,8},{8,16},{1,9},{9,17},{2,10},{10,18},{3,11},{11,19},{4,12},{12... | collective-permute-start | bytes 1179656 | tf_op jit(solution)/shard_map/ppermute | solution.py:699
  57.9 13.1 %collective-permute-start.5 = (bf16[256,768]{1,0:T(8,128)(2,1)S(1)}, bf16[256,768]{1,0:T(8,128)(2,1)S(1)}, u32[]{:S(2)}, u32[]{:S(2)}) collective-permute-start(bf16[256,768]{1,0:T(8,128)(2,1)S(1)} %get-tuple-element.793.refs_13_), channel_id=1, source_target_pairs={{0,8},{8,16},{16,24},{1,9},{9,17},{17,25},{2,10},{10,18},{18,26},{... | collective-permute-start | bytes 1179656 | tf_op jit(solution)/shard_map/ppermute | solution.py:699
  68.8 12.9 %collective-permute-start.4 = (bf16[256,768]{1,0:T(8,128)(2,1)S(1)}, bf16[256,768]{1,0:T(8,128)(2,1)S(1)}, u32[]{:S(2)}, u32[]{:S(2)}) collective-permute-start(bf16[256,768]{1,0:T(8,128)(2,1)S(1)} %get-tuple-element.810.refs_13_), channel_id=1, source_target_pairs={{0,8},{8,16},{16,24},{1,9},{9,17},{17,25},{2,10},{10,18},{18,26},{... | collective-permute-start | bytes 1179656 | tf_op jit(solution)/shard_map/ppermute | solution.py:699
  79.5 13.4 %collective-permute-start.7 = (bf16[256,768]{1,0:T(8,128)(2,1)S(1)}, bf16[256,768]{1,0:T(8,128)(2,1)S(1)}, u32[]{:S(2)}, u32[]{:S(2)}) collective-permute-start(bf16[256,768]{1,0:T(8,128)(2,1)S(1)} %get-tuple-element.847.refs_13_), channel_id=1, source_target_pairs={{0,8},{8,16},{16,24},{1,9},{9,17},{17,25},{2,10},{10,18},{18,26},{... | collective-permute-start | bytes 1179656 | tf_op jit(solution)/shard_map/ppermute | solution.py:699
  90.9 9.6 %collective-permute-start.6 = (bf16[256,768]{1,0:T(8,128)(2,1)S(1)}, bf16[256,768]{1,0:T(8,128)(2,1)S(1)}, u32[]{:S(2)}, u32[]{:S(2)}) collective-permute-start(bf16[256,768]{1,0:T(8,128)(2,1)S(1)} %get-tuple-element.864.refs_13_), channel_id=1, source_target_pairs={{0,8},{8,16},{16,24},{1,9},{9,17},{17,25},{2,10},{10,18},{18,26},{... | collective-permute-start | bytes 1179656 | tf_op jit(solution)/shard_map/ppermute | solution.py:699
  94.7 13.4 %collective-permute-start.9 = (bf16[256,768]{1,0:T(8,128)(2,1)S(1)}, bf16[256,768]{1,0:T(8,128)(2,1)S(1)}, u32[]{:S(2)}, u32[]{:S(2)}) collective-permute-start(bf16[256,768]{1,0:T(8,128)(2,1)S(1)} %get-tuple-element.901.refs_13_), channel_id=1, source_target_pairs={{8,16},{16,24},{9,17},{17,25},{10,18},{18,26},{11,19},{19,27},{12,... | collective-permute-start | bytes 1179656 | tf_op jit(solution)/shard_map/ppermute | solution.py:699
  107.4 2.3 collective-permute-start.8
  109.0 10.1 %collective-permute-start.11 = (bf16[256,768]{1,0:T(8,128)(2,1)S(1)}, bf16[256,768]{1,0:T(8,128)(2,1)S(1)}, u32[]{:S(2)}, u32[]{:S(2)}) collective-permute-start(bf16[256,768]{1,0:T(8,128)(2,1)S(1)} %get-tuple-element.955.refs_13_), channel_id=1, source_target_pairs={{16,24},{17,25},{18,26},{19,27},{20,28},{21,29},{22,30},{23,31}} | collective-permute-start | bytes 1179656 | tf_op jit(solution)/shard_map/ppermute | solution.py:699
  118.4 1.6 collective-permute-start.10
  134.0 10.1 %collective-permute-start.13 = (bf16[256,768]{1,0:T(8,128)(2,1)S(1)}, bf16[256,768]{1,0:T(8,128)(2,1)S(1)}, u32[]{:S(2)}, u32[]{:S(2)}) collective-permute-start(bf16[256,768]{1,0:T(8,128)(2,1)S(1)} %get-tuple-element.1067), channel_id=1, source_target_pairs={{24,16},{25,17},{26,18},{27,19},{28,20},{29,21},{30,22},{31,23}} | collective-permute-start | bytes 1179656 | tf_op jit(solution)/shard_map/ppermute | solution.py:709
  143.3 3.7 collective-permute-start.12
  146.4 10.5 %collective-permute-start.15 = (bf16[256,768]{1,0:T(8,128)(2,1)S(1)}, bf16[256,768]{1,0:T(8,128)(2,1)S(1)}, u32[]{:S(2)}, u32[]{:S(2)}) collective-permute-start(bf16[256,768]{1,0:T(8,128)(2,1)S(1)} %get-tuple-element.1105), channel_id=1, source_target_pairs={{16,8},{24,16},{17,9},{25,17},{18,10},{26,18},{19,11},{27,19},{20,... | collective-permute-start | bytes 1179656 | tf_op jit(solution)/shard_map/ppermute | solution.py:709
  156.2 4.3 collective-permute-start.14
  159.2 54.5 %collective-permute-start.17 = (bf16[256,768]{1,0:T(8,128)(2,1)S(1)}, bf16[256,768]{1,0:T(8,128)(2,1)S(1)}, u32[]{:S(2)}, u32[]{:S(2)}) collective-permute-start(bf16[256,768]{1,0:T(8,128)(2,1)S(1)} %get-tuple-element.1143), channel_id=1, source_target_pairs={{8,0},{16,8},{24,16},{9,1},{17,9},{25,17},{10,2},{18,10},{26,18},{... | collective-permute-start | bytes 1179656 | tf_op jit(solution)/shard_map/ppermute | solution.py:709
  170.6 57.1 %collective-permute-start.16 = (bf16[256,768]{1,0:T(8,128)(2,1)S(1)}, bf16[256,768]{1,0:T(8,128)(2,1)S(1)}, u32[]{:S(2)}, u32[]{:S(2)}) collective-permute-start(bf16[256,768]{1,0:T(8,128)(2,1)S(1)} %get-tuple-element.1142), channel_id=1, source_target_pairs={{8,0},{16,8},{24,16},{9,1},{17,9},{25,17},{10,2},{18,10},{26,18},{... | collective-permute-start | bytes 1179656 | tf_op jit(solution)/shard_map/ppermute | solution.py:709
  224.6 16.0 %collective-permute-start.19 = (bf16[256,768]{1,0:T(8,128)(2,1)S(1)}, bf16[256,768]{1,0:T(8,128)(2,1)S(1)}, u32[]{:S(2)}, u32[]{:S(2)}) collective-permute-start(bf16[256,768]{1,0:T(8,128)(2,1)S(1)} %get-tuple-element.1181), channel_id=1, source_target_pairs={{8,0},{16,8},{24,16},{9,1},{17,9},{25,17},{10,2},{18,10},{26,18},{... | collective-permute-start | bytes 1179656 | tf_op jit(solution)/shard_map/ppermute | solution.py:709
  239.1 14.9 %collective-permute-start.18 = (bf16[256,768]{1,0:T(8,128)(2,1)S(1)}, bf16[256,768]{1,0:T(8,128)(2,1)S(1)}, u32[]{:S(2)}, u32[]{:S(2)}) collective-permute-start(bf16[256,768]{1,0:T(8,128)(2,1)S(1)} %get-tuple-element.1180), channel_id=1, source_target_pairs={{8,0},{16,8},{24,16},{9,1},{17,9},{25,17},{10,2},{18,10},{26,18},{... | collective-permute-start | bytes 1179656 | tf_op jit(solution)/shard_map/ppermute | solution.py:709
  251.4 15.4 %collective-permute-start.21 = (bf16[256,768]{1,0:T(8,128)(2,1)S(1)}, bf16[256,768]{1,0:T(8,128)(2,1)S(1)}, u32[]{:S(2)}, u32[]{:S(2)}) collective-permute-start(bf16[256,768]{1,0:T(8,128)(2,1)S(1)} %get-tuple-element.1219), channel_id=1, source_target_pairs={{8,0},{16,8},{9,1},{17,9},{10,2},{18,10},{11,3},{19,11},{12,4},{20... | collective-permute-start | bytes 1179656 | tf_op jit(solution)/shard_map/ppermute | solution.py:709
  265.5 14.8 %collective-permute-start.20 = (bf16[256,768]{1,0:T(8,128)(2,1)S(1)}, bf16[256,768]{1,0:T(8,128)(2,1)S(1)}, u32[]{:S(2)}, u32[]{:S(2)}) collective-permute-start(bf16[256,768]{1,0:T(8,128)(2,1)S(1)} %get-tuple-element.1218), channel_id=1, source_target_pairs={{8,0},{16,8},{9,1},{17,9},{10,2},{18,10},{11,3},{19,11},{12,4},{20... | collective-permute-start | bytes 1179656 | tf_op jit(solution)/shard_map/ppermute | solution.py:709
  277.7 15.1 %collective-permute-start.23 = (bf16[256,768]{1,0:T(8,128)(2,1)S(1)}, bf16[256,768]{1,0:T(8,128)(2,1)S(1)}, u32[]{:S(2)}, u32[]{:S(2)}) collective-permute-start(bf16[256,768]{1,0:T(8,128)(2,1)S(1)} %get-tuple-element.1257), channel_id=1, source_target_pairs={{8,0},{9,1},{10,2},{11,3},{12,4},{13,5},{14,6},{15,7}} | collective-permute-start | bytes 1179656 | tf_op jit(solution)/shard_map/ppermute | solution.py:709
  291.5 13.6 %collective-permute-start.22 = (bf16[256,768]{1,0:T(8,128)(2,1)S(1)}, bf16[256,768]{1,0:T(8,128)(2,1)S(1)}, u32[]{:S(2)}, u32[]{:S(2)}) collective-permute-start(bf16[256,768]{1,0:T(8,128)(2,1)S(1)} %get-tuple-element.1256), channel_id=1, source_target_pairs={{8,0},{9,1},{10,2},{11,3},{12,4},{13,5},{14,6},{15,7}} | collective-permute-start | bytes 1179656 | tf_op jit(solution)/shard_map/ppermute | solution.py:709
  317.4 18.8 %slice-start = ((s8[12582912]{0:T(1024)(128)(4,1)}), s8[4194304]{0:T(1024)(128)(4,1)S(1)}, s32[]{:S(2)}) async-start(s8[12582912]{0:T(1024)(128)(4,1)} %bitcast.60), calls=%async_computation | async-start | bytes 8388608
  317.4 18.8 %slice-start.1 = ((s8[12582912]{0:T(1024)(128)(4,1)}), s8[4194304]{0:T(1024)(128)(4,1)S(1)}, s32[]{:S(2)}) async-start(s8[12582912]{0:T(1024)(128)(4,1)} %bitcast.60), calls=%async_computation.1 | async-start | bytes 8388608
  326.2 7.4 %collective-permute-start.28 = (bf16[2,384,768]{2,1,0:T(8,128)(2,1)}, bf16[2,384,768]{2,1,0:T(8,128)(2,1)S(1)}, u32[]{:S(2)}, u32[]{:S(2)}) collective-permute-start(bf16[2,384,768]{2,1,0:T(8,128)(2,1)} %get-tuple-element.1305), channel_id=1, source_target_pairs={{0,2},{2,0},{4,6},{6,4},{1,3},{3,1},{5,7},{7,5},{8,10},{10,8},{12,... | collective-permute-start | bytes 3538952 | tf_op jit(solution)/shard_map/ppermute | solution.py:631
  333.1 18.5 %collective-permute-start.26 = (bf16[2,384,768]{2,1,0:T(8,128)(2,1)}, bf16[2,384,768]{2,1,0:T(8,128)(2,1)S(1)}, u32[]{:S(2)}, u32[]{:S(2)}) collective-permute-start(bf16[2,384,768]{2,1,0:T(8,128)(2,1)} %get-tuple-element.1300), channel_id=1, source_target_pairs={{0,2},{2,0},{4,6},{6,4},{1,3},{3,1},{5,7},{7,5},{8,10},{10,8},{12,... | collective-permute-start | bytes 3538952 | tf_op jit(solution)/shard_map/ppermute | solution.py:631
  334.0 17.8 %collective-permute-start.29 = (bf16[384,768]{1,0:T(8,128)(2,1)S(1)}, bf16[384,768]{1,0:T(8,128)(2,1)S(1)}, u32[]{:S(2)}, u32[]{:S(2)}) collective-permute-start(bf16[384,768]{1,0:T(8,128)(2,1)S(1)} %add_parts.13.refs_2_), channel_id=1, source_target_pairs={{0,4},{2,6},{4,0},{6,2},{1,5},{3,7},{5,1},{7,3},{8,12},{10,14},{12... | collective-permute-start | bytes 1769480 | tf_op jit(solution)/shard_map/ppermute | solution.py:631
  344.6 17.7 %collective-permute-start.32 = (bf16[2,384,768]{2,1,0:T(8,128)(2,1)}, bf16[2,384,768]{2,1,0:T(8,128)(2,1)S(1)}, u32[]{:S(2)}, u32[]{:S(2)}) collective-permute-start(bf16[2,384,768]{2,1,0:T(8,128)(2,1)} %get-tuple-element.1311), channel_id=1, source_target_pairs={{0,2},{2,0},{4,6},{6,4},{1,3},{3,1},{5,7},{7,5},{8,10},{10,8},{12,... | collective-permute-start | bytes 3538952 | tf_op jit(solution)/shard_map/ppermute | solution.py:631
  344.7 2.5 collective-permute-start.24
  347.2 3.8 collective-permute-start.25
  351.8 14.5 %collective-permute-start.31 = (bf16[384,768]{1,0:T(8,128)(2,1)S(1)}, bf16[384,768]{1,0:T(8,128)(2,1)S(1)}, u32[]{:S(2)}, u32[]{:S(2)}) collective-permute-start(bf16[384,768]{1,0:T(8,128)(2,1)S(1)} %add_parts.12.refs_2_), channel_id=1, source_target_pairs={{0,4},{2,6},{4,0},{6,2},{1,5},{3,7},{5,1},{7,3},{8,12},{10,14},{12... | collective-permute-start | bytes 1769480 | tf_op jit(solution)/shard_map/ppermute | solution.py:631
  352.9 15.6 %slice-start.3 = ((s8[12582912]{0:T(1024)(128)(4,1)}), s8[4194304]{0:T(1024)(128)(4,1)S(1)}, s32[]{:S(2)}) async-start(s8[12582912]{0:T(1024)(128)(4,1)} %bitcast.62), calls=%async_computation.3 | async-start | bytes 8388608
  353.2 14.7 %collective-permute-start.36 = (bf16[384,768]{1,0:T(8,128)(2,1)S(1)}, bf16[384,768]{1,0:T(8,128)(2,1)S(1)}, u32[]{:S(2)}, u32[]{:S(2)}) collective-permute-start(bf16[384,768]{1,0:T(8,128)(2,1)S(1)} %add_parts.19), channel_id=1, source_target_pairs={{0,1},{1,0},{2,3},{3,2},{4,5},{5,4},{6,7},{7,6},{8,9},{9,8},{10,11... | collective-permute-start | bytes 1769480 | tf_op jit(solution)/shard_map/ppermute | solution.py:631
  362.2 13.3 %collective-permute-start.30 = (bf16[2,384,768]{2,1,0:T(8,128)(2,1)}, bf16[2,384,768]{2,1,0:T(8,128)(2,1)S(1)}, u32[]{:S(2)}, u32[]{:S(2)}) collective-permute-start(bf16[2,384,768]{2,1,0:T(8,128)(2,1)} %get-tuple-element.1309), channel_id=1, source_target_pairs={{0,2},{2,0},{4,6},{6,4},{1,3},{3,1},{5,7},{7,5},{8,10},{10,8},{12,... | collective-permute-start | bytes 3538952 | tf_op jit(solution)/shard_map/ppermute | solution.py:631
  366.3 13.5 %collective-permute-start.33 = (bf16[384,768]{1,0:T(8,128)(2,1)S(1)}, bf16[384,768]{1,0:T(8,128)(2,1)S(1)}, u32[]{:S(2)}, u32[]{:S(2)}) collective-permute-start(bf16[384,768]{1,0:T(8,128)(2,1)S(1)} %add_parts.14.refs_1_), channel_id=1, source_target_pairs={{0,4},{2,6},{4,0},{6,2},{1,5},{3,7},{5,1},{7,3},{8,12},{10,14},{12... | collective-permute-start | bytes 1769480 | tf_op jit(solution)/shard_map/ppermute | solution.py:631
  367.8 13.9 %collective-permute-start.37 = (bf16[384,768]{1,0:T(8,128)(2,1)S(1)}, bf16[384,768]{1,0:T(8,128)(2,1)S(1)}, u32[]{:S(2)}, u32[]{:S(2)}) collective-permute-start(bf16[384,768]{1,0:T(8,128)(2,1)S(1)} %add_parts.20), channel_id=1, source_target_pairs={{0,1},{1,0},{2,3},{3,2},{4,5},{5,4},{6,7},{7,6},{8,9},{9,8},{10,11... | collective-permute-start | bytes 1769480 | tf_op jit(solution)/shard_map/ppermute | solution.py:631
  375.4 22.4 %collective-permute-start.35 = (bf16[2,384,768]{2,1,0:T(8,128)(2,1)}, bf16[2,384,768]{2,1,0:T(8,128)(2,1)S(1)}, u32[]{:S(2)}, u32[]{:S(2)}) collective-permute-start(bf16[2,384,768]{2,1,0:T(8,128)(2,1)} %get-tuple-element.1317), channel_id=1, source_target_pairs={{0,2},{2,0},{4,6},{6,4},{1,3},{3,1},{5,7},{7,5},{8,10},{10,8},{12,... | collective-permute-start | bytes 3538952 | tf_op jit(solution)/shard_map/ppermute | solution.py:631
  379.8 18.9 %collective-permute-start.34 = (bf16[384,768]{1,0:T(8,128)(2,1)}, bf16[384,768]{1,0:T(8,128)(2,1)}, u32[]{:S(2)}, u32[]{:S(2)}) collective-permute-start(bf16[384,768]{1,0:T(8,128)(2,1)} %add_parts.15.refs_1_), channel_id=1, source_target_pairs={{0,4},{2,6},{4,0},{6,2},{1,5},{3,7},{5,1},{7,3},{8,12},{10,14},{12... | collective-permute-start | bytes 1769480 | tf_op jit(solution)/shard_map/ppermute | solution.py:631
  381.8 19.9 %collective-permute-start.38 = (bf16[384,768]{1,0:T(8,128)(2,1)}, bf16[384,768]{1,0:T(8,128)(2,1)}, u32[]{:S(2)}, u32[]{:S(2)}) collective-permute-start(bf16[384,768]{1,0:T(8,128)(2,1)} %add_parts.18), channel_id=1, source_target_pairs={{0,1},{1,0},{2,3},{3,2},{4,5},{5,4},{6,7},{7,6},{8,9},{9,8},{10,11... | collective-permute-start | bytes 1769480 | tf_op jit(solution)/shard_map/ppermute | solution.py:631
  389.3 21.4 %collective-permute-start.41 = (bf16[2,384,768]{2,1,0:T(8,128)(2,1)}, bf16[2,384,768]{2,1,0:T(8,128)(2,1)}, u32[]{:S(2)}, u32[]{:S(2)}) collective-permute-start(bf16[2,384,768]{2,1,0:T(8,128)(2,1)} %get-tuple-element.1329), channel_id=1, source_target_pairs={{0,2},{2,0},{4,6},{6,4},{1,3},{3,1},{5,7},{7,5},{8,10},{10,8},{12,... | collective-permute-start | bytes 3538952 | tf_op jit(solution)/shard_map/ppermute | solution.py:631
  389.4 5.6 %collective-permute-start.27 = (f32[8,768]{1,0:T(8,128)}, f32[8,768]{1,0:T(8,128)}, u32[]{:S(2)}, u32[]{:S(2)}) collective-permute-start(f32[8,768]{1,0:T(8,128)} %add_vectors.4.refs_0_), channel_id=1, source_target_pairs={{0,1},{1,0},{2,3},{3,2},{4,5},{5,4},{6,7},{7,6},{8,9},{9,8},{10,11... | collective-permute-start | bytes 73736 | tf_op jit(solution)/shard_map/ppermute | solution.py:631
  398.7 14.3 %collective-permute-start.40 = (bf16[384,768]{1,0:T(8,128)(2,1)}, bf16[384,768]{1,0:T(8,128)(2,1)}, u32[]{:S(2)}, u32[]{:S(2)}) collective-permute-start(bf16[384,768]{1,0:T(8,128)(2,1)} %add_parts.16), channel_id=1, source_target_pairs={{0,4},{2,6},{4,0},{6,2},{1,5},{3,7},{5,1},{7,3},{8,12},{10,14},{12... | collective-permute-start | bytes 1769480 | tf_op jit(solution)/shard_map/ppermute | solution.py:631
  401.7 14.3 %collective-permute-start.39 = (bf16[384,768]{1,0:T(8,128)(2,1)}, bf16[384,768]{1,0:T(8,128)(2,1)}, u32[]{:S(2)}, u32[]{:S(2)}) collective-permute-start(bf16[384,768]{1,0:T(8,128)(2,1)} %add_parts.17), channel_id=1, source_target_pairs={{0,1},{1,0},{2,3},{3,2},{4,5},{5,4},{6,7},{7,6},{8,9},{9,8},{10,11... | collective-permute-start | bytes 1769480 | tf_op jit(solution)/shard_map/ppermute | solution.py:631
  413.0 13.6 %collective-permute-start.43 = (bf16[384,768]{1,0:T(8,128)(2,1)}, bf16[384,768]{1,0:T(8,128)(2,1)}, u32[]{:S(2)}, u32[]{:S(2)}) collective-permute-start(bf16[384,768]{1,0:T(8,128)(2,1)} %add_parts.21), channel_id=1, source_target_pairs={{0,4},{2,6},{4,0},{6,2},{1,5},{3,7},{5,1},{7,3},{8,12},{10,14},{12... | collective-permute-start | bytes 1769480 | tf_op jit(solution)/shard_map/ppermute | solution.py:631
  416.0 13.7 %collective-permute-start.42 = (bf16[384,768]{1,0:T(8,128)(2,1)}, bf16[384,768]{1,0:T(8,128)(2,1)}, u32[]{:S(2)}, u32[]{:S(2)}) collective-permute-start(bf16[384,768]{1,0:T(8,128)(2,1)} %add_parts.22), channel_id=1, source_target_pairs={{0,1},{1,0},{2,3},{3,2},{4,5},{5,4},{6,7},{7,6},{8,9},{9,8},{10,11... | collective-permute-start | bytes 1769480 | tf_op jit(solution)/shard_map/ppermute | solution.py:631
  429.7 12.1 %collective-permute-start.44 = (bf16[384,768]{1,0:T(8,128)(2,1)S(1)}, bf16[384,768]{1,0:T(8,128)(2,1)S(1)}, u32[]{:S(2)}, u32[]{:S(2)}) collective-permute-start(bf16[384,768]{1,0:T(8,128)(2,1)S(1)} %add_parts.23), channel_id=1, source_target_pairs={{0,1},{1,0},{2,3},{3,2},{4,5},{5,4},{6,7},{7,6},{8,9},{9,8},{10,11... | collective-permute-start | bytes 1769480 | tf_op jit(solution)/shard_map/ppermute | solution.py:631
  (25 other events, 207.9 us)

commit v8 on v7

--- a/solution.py
+++ b/solution.py
@@ -733,7 +733,7 @@
             keeps.append(keep)
             gots.append(exchange(send, "group", 1))
             away = add_call(1, keep, gots[-1])
-            if k == 1:
+            if k in (1, 5):
                 vectors, away = lax.optimization_barrier((vectors, away))
             aways.append(away)
             turn(k)

time: 452 us -> 450 us (level)
  waiting for transfers between devices: 83.3 us -> 74.1 us
  other arithmetic: 12.6 us -> 20.1 us
    ppermute x21, waiting for transfers between devices: 31.2 us -> 21.1 us  [exchange(): return lax.ppermute(block, axis, route)]
  transfers between devices with their start and end apart: 45 -> 45, of which waited for: 15 -> 16; matrix products, arithmetic and copies ran while one was open for 4% -> 6% of each run, Pallas kernels for 55% -> 54%
where the time goes in v8:
time: 450 us; the launch traced here: 443 us
  Pallas kernels  287 us (64%)
  waiting for transfers between devices  74.1 us (16%)
  starting transfers between devices  48.4 us (11%)
  other arithmetic  20.1 us (4%)
  local copies, waits for them, and re-layouts  10.8 us (2%)
    pallas_call x14, Pallas kernels, local(): backward_call(ROWS, n, DELTA, stages, groups, t == 0)  126 us
    pallas_call x14, Pallas kernels, local(): forward_call(ROWS, n, DELTA, t == 0, t == ticks - 1)  103 us
    ppermute x24, waiting for transfers between devices, local(): arriving.append(lax.ppermute(made[0], 'pipe', route) if route else made[0])  53.1 us
    pallas_call x6, Pallas kernels, local(): call(meta, left, *(far(rights) if fetch else rights), *waits)  45.9 us
    ppermute x24, starting transfers between devices, local(): arriving.append(lax.ppermute(made[0], 'pipe', route) if route else made[0])  31.9 us
    ppermute x21, waiting for transfers between devices, exchange(): return lax.ppermute(block, axis, route)  21.1 us
    ppermute x21, starting transfers between devices, exchange(): return lax.ppermute(block, axis, route)  16.5 us
    pallas_call x12, Pallas kernels, add_call(): pl.pallas_call(add_kernel, grid=(rows // step,), in_specs=[pick, pick] +...  11.9 us
  transfers between devices with their start and end apart: 45, of which 16 were waited for; matrix products, arithmetic and copies ran while one was open for 6% of the time, Pallas kernels for 54%

profile of v8, /device:TPU:0, one launch (start us, length us, event | category | flops | bytes accessed | tf_op | source)
XLA Modules:
  0.0 442.8 jit_solution(18134745085702179046)
XLA Ops:
  4.2 10.9 %layer_forward.14 = (bf16[256,768]{1,0:T(8,128)(2,1)S(1)}, f32[6,256,256]{2,1,0:T(8,128)S(1)}, bf16[256,768]{1,0:T(8,128)(2,1)S(1)}, f32[256,128]{1,0:T(8,128)S(...) custom-call(s32[1]{0:T(128)} %constant.21.clone.1.refs_0_, ...), custom_call_target="tpu_custom_call", output_to_operand_aliasing={{19}: (4, {}), {20}: (5, {}), {25}: (10, {})} | custom-call | flops 4608000000 | bytes 4194304 | tf_op jit(solution)/shard_map/layer_forward/pallas_call | solution.py:696
  16.4 9.0 %layer_forward.15 = (bf16[256,768]{1,0:T(8,128)(2,1)S(1)}, f32[6,256,256]{2,1,0:T(8,128)S(1)}, bf16[256,768]{1,0:T(8,128)(2,1)S(1)}, f32[256,128]{1,0:T(8,128)S(...) custom-call(s32[1]{0:T(128)} %constant.19.clone.1.refs_0_, ...), custom_call_target="tpu_custom_call", output_to_operand_aliasing={{1}: (12, {}), {4}: (16, {}), {5}: (17, {}), {6}: (18, {}),... | custom-call | flops 4608000000 | bytes 4194304 | tf_op jit(solution)/shard_map/layer_forward/pallas_call | solution.py:696
  26.7 8.6 %layer_forward.16 = (bf16[256,768]{1,0:T(8,128)(2,1)S(1)}, f32[6,256,256]{2,1,0:T(8,128)S(1)}, bf16[256,768]{1,0:T(8,128)(2,1)S(1)}, f32[256,128]{1,0:T(8,128)S(...) custom-call(s32[1]{0:T(128)} %constant.23.clone.1.refs_0_, ...), custom_call_target="tpu_custom_call", output_to_operand_aliasing={{1}: (12, {}), {4}: (16, {}), {5}: (17, {}), {6}: (18, {}),... | custom-call | flops 4608000000 | bytes 4194304 | tf_op jit(solution)/shard_map/layer_forward/pallas_call | solution.py:696
  35.3 3.1 collective-permute-start.3
  38.4 9.1 %layer_forward.17 = (bf16[256,768]{1,0:T(8,128)(2,1)S(1)}, f32[6,256,256]{2,1,0:T(8,128)S(1)}, bf16[256,768]{1,0:T(8,128)(2,1)S(1)}, f32[256,128]{1,0:T(8,128)S(...) custom-call(s32[1]{0:T(128)} %constant.18.clone.1.refs_0_, ...), custom_call_target="tpu_custom_call", output_to_operand_aliasing={{1}: (12, {}), {4}: (16, {}), {5}: (17, {}), {6}: (18, {}),... | custom-call | flops 4608000000 | bytes 4194304 | tf_op jit(solution)/shard_map/layer_forward/pallas_call | solution.py:696
  49.5 8.5 %layer_forward.18 = (bf16[256,768]{1,0:T(8,128)(2,1)S(1)}, f32[6,256,256]{2,1,0:T(8,128)S(1)}, bf16[256,768]{1,0:T(8,128)(2,1)S(1)}, f32[256,128]{1,0:T(8,128)S(...) custom-call(s32[1]{0:T(128)} %constant.24.clone.1.refs_0_, ...), custom_call_target="tpu_custom_call", output_to_operand_aliasing={{1}: (12, {}), {4}: (16, {}), {5}: (17, {}), {6}: (18, {}),... | custom-call | flops 4608000000 | bytes 4194304 | tf_op jit(solution)/shard_map/layer_forward/pallas_call | solution.py:696
  60.1 9.0 %layer_forward.19 = (bf16[256,768]{1,0:T(8,128)(2,1)S(1)}, f32[6,256,256]{2,1,0:T(8,128)S(1)}, bf16[256,768]{1,0:T(8,128)(2,1)S(1)}, f32[256,128]{1,0:T(8,128)S(...) custom-call(s32[1]{0:T(128)} %constant.40.clone.1.refs_0_, ...), custom_call_target="tpu_custom_call", output_to_operand_aliasing={{1}: (12, {}), {4}: (16, {}), {5}: (17, {}), {6}: (18, {}),... | custom-call | flops 4608000000 | bytes 4194304 | tf_op jit(solution)/shard_map/layer_forward/pallas_call | solution.py:696
  69.1 2.2 collective-permute-start.4
  71.2 8.4 %layer_forward.20 = (bf16[256,768]{1,0:T(8,128)(2,1)S(1)}, f32[6,256,256]{2,1,0:T(8,128)S(1)}, bf16[256,768]{1,0:T(8,128)(2,1)S(1)}, f32[256,128]{1,0:T(8,128)S(...) custom-call(s32[1]{0:T(128)} %constant.25.clone.1.refs_0_, ...), custom_call_target="tpu_custom_call", output_to_operand_aliasing={{1}: (12, {}), {4}: (16, {}), {5}: (17, {}), {6}: (18, {}),... | custom-call | flops 4608000000 | bytes 4194304 | tf_op jit(solution)/shard_map/layer_forward/pallas_call | solution.py:696
  79.6 2.3 collective-permute-start.7
  82.0 9.2 %layer_forward.21 = (bf16[256,768]{1,0:T(8,128)(2,1)S(1)}, f32[6,256,256]{2,1,0:T(8,128)S(1)}, bf16[256,768]{1,0:T(8,128)(2,1)S(1)}, f32[256,128]{1,0:T(8,128)S(...) custom-call(s32[1]{0:T(128)} %constant.39.clone.1.refs_0_, ...), custom_call_target="tpu_custom_call", output_to_operand_aliasing={{1}: (12, {}), {4}: (16, {}), {5}: (17, {}), {6}: (18, {}),... | custom-call | flops 4608000000 | bytes 4194304 | tf_op jit(solution)/shard_map/layer_forward/pallas_call | solution.py:696
  95.6 5.1 %collective-permute-done.6.refs_2_ = bf16[256,768]{1,0:T(8,128)(2,1)S(1)} collective-permute-done((bf16[256,768]{1,0:T(8,128)(2,1)S(1)}, bf16[256,768]{1,0:T(8,128)(2,1)S(1)}, u32[]{:S(2)}, u32[]{:S(2)}) %collective-permute-start.6) | collective-permute-done | bytes 393248 | tf_op jit(solution)/shard_map/ppermute | solution.py:699
  100.7 6.9 %layer_forward.23 = (bf16[256,768]{1,0:T(8,128)(2,1)S(1)}, f32[6,256,256]{2,1,0:T(8,128)S(1)}, bf16[256,768]{1,0:T(8,128)(2,1)S(1)}, f32[256,128]{1,0:T(8,128)S(...) custom-call(s32[1]{0:T(128)} %constant.38.clone.1.refs_0_, ...), custom_call_target="tpu_custom_call", output_to_operand_aliasing={{1}: (12, {}), {4}: (16, {}), {5}: (17, {}), {6}: (18, {}),... | custom-call | flops 4608000000 | bytes 4194304 | tf_op jit(solution)/shard_map/layer_forward/pallas_call | solution.py:696
  109.9 8.7 %layer_forward.25 = (bf16[256,768]{1,0:T(8,128)(2,1)S(1)}, f32[6,256,256]{2,1,0:T(8,128)S(1)}, bf16[256,768]{1,0:T(8,128)(2,1)S(1)}, f32[256,128]{1,0:T(8,128)S(...) custom-call(s32[1]{0:T(128)} %constant.17.clone.1.refs_0_, ...), custom_call_target="tpu_custom_call", output_to_operand_aliasing={{1}: (12, {}), {4}: (16, {}), {5}: (17, {}), {6}: (18, {}),... | custom-call | flops 4608000000 | bytes 4194304 | tf_op jit(solution)/shard_map/layer_forward/pallas_call | solution.py:696
  120.3 10.9 %layer_forward.27 = (bf16[256,768]{1,0:T(8,128)(2,1)S(1)}, f32[6,256,256]{2,1,0:T(8,128)S(1)}, bf16[256,768]{1,0:T(8,128)(2,1)}, f32[256,128]{1,0:T(8,128)}, bf1...) custom-call(s32[1]{0:T(128)} %constant.29.clone.1.refs_0_, ...), custom_call_target="tpu_custom_call", output_to_operand_aliasing={{1}: (12, {}), {4}: (16, {}), {5}: (17, {}), {6}: (18, {}),... | custom-call | flops 4608000000 | bytes 4194304 | tf_op jit(solution)/shard_map/layer_forward/pallas_call | solution.py:696
  131.1 3.0 layer_backward.14
  134.9 8.7 %layer_backward.15 = (bf16[256,768]{1,0:T(8,128)(2,1)S(1)}, f32[6,256,256]{2,1,0:T(8,128)S(1)}, f32[8,768]{1,0:T(8,128)S(1)}, bf16[2048,768]{1,0:T(8,128)(2,1)},...) custom-call(s32[1]{0:T(128)} %constant.19.clone.1.refs_0_, ...), custom_call_target="tpu_custom_call", output_to_operand_aliasing={{7}: (3, {}), {8}: (4, {}), {9}: (5, {}), {10}: (6, {}), {1... | custom-call | flops 5120000000 | bytes 4194304 | tf_op jit(solution)/shard_map/layer_backward/pallas_call | solution.py:704
  144.3 2.3 layer_backward.16
  147.3 9.1 %layer_backward.17 = (bf16[256,768]{1,0:T(8,128)(2,1)S(1)}, f32[6,256,256]{2,1,0:T(8,128)S(1)}, f32[8,768]{1,0:T(8,128)S(1)}, bf16[2048,768]{1,0:T(8,128)(2,1)},...) custom-call(s32[1]{0:T(128)} %constant.18.clone.1.refs_0_, ...), custom_call_target="tpu_custom_call", output_to_operand_aliasing={{7}: (3, {}), {8}: (4, {}), {9}: (5, {}), {10}: (6, {}), {1... | custom-call | flops 5120000000 | bytes 4194304 | tf_op jit(solution)/shard_map/layer_backward/pallas_call | solution.py:704
  157.1 2.3 layer_backward.18
  160.7 10.1 %layer_backward.19 = (bf16[256,768]{1,0:T(8,128)(2,1)S(1)}, f32[6,256,256]{2,1,0:T(8,128)S(1)}, f32[8,768]{1,0:T(8,128)S(1)}, bf16[2048,768]{1,0:T(8,128)(2,1)},...) custom-call(s32[1]{0:T(128)} %constant.40.clone.1.refs_0_, ...), custom_call_target="tpu_custom_call", output_to_operand_aliasing={{7}: (3, {}), {8}: (4, {}), {9}: (5, {}), {10}: (6, {}), {1... | custom-call | flops 5120000000 | bytes 4194304 | tf_op jit(solution)/shard_map/layer_backward/pallas_call | solution.py:704
  172.1 42.5 %collective-permute-done.17.refs_2_ = bf16[256,768]{1,0:T(8,128)(2,1)S(1)} collective-permute-done((bf16[256,768]{1,0:T(8,128)(2,1)S(1)}, bf16[256,768]{1,0:T(8,128)(2,1)S(1)}, u32[]{:S(2)}, u32[]{:S(2)}) %collective-permute-start.17) | collective-permute-done | bytes 393248 | tf_op jit(solution)/shard_map/ppermute | solution.py:709
  214.7 10.8 %layer_backward.20 = (bf16[256,768]{1,0:T(8,128)(2,1)S(1)}, f32[6,256,256]{2,1,0:T(8,128)S(1)}, f32[8,768]{1,0:T(8,128)S(1)}, bf16[2048,768]{1,0:T(8,128)(2,1)},...) custom-call(s32[1]{0:T(128)} %constant.25.clone.1.refs_0_, ...), custom_call_target="tpu_custom_call", output_to_operand_aliasing={{7}: (3, {}), {8}: (4, {}), {9}: (5, {}), {10}: (6, {}), {1... | custom-call | flops 5120000000 | bytes 4194304 | tf_op jit(solution)/shard_map/layer_backward/pallas_call | solution.py:704
  226.8 2.0 collective-permute-done.16.refs_2_
  228.9 11.4 %layer_backward.21 = (bf16[256,768]{1,0:T(8,128)(2,1)S(1)}, f32[6,256,256]{2,1,0:T(8,128)S(1)}, f32[8,768]{1,0:T(8,128)S(1)}, bf16[2048,768]{1,0:T(8,128)(2,1)},...) custom-call(s32[1]{0:T(128)} %constant.39.clone.1.refs_0_, ...), custom_call_target="tpu_custom_call", output_to_operand_aliasing={{7}: (3, {}), {8}: (4, {}), {9}: (5, {}), {10}: (6, {}), {1... | custom-call | flops 5120000000 | bytes 4194304 | tf_op jit(solution)/shard_map/layer_backward/pallas_call | solution.py:704
  241.7 10.8 %layer_backward.22 = (bf16[256,768]{1,0:T(8,128)(2,1)S(1)}, f32[6,256,256]{2,1,0:T(8,128)S(1)}, f32[8,768]{1,0:T(8,128)S(1)}, bf16[2048,768]{1,0:T(8,128)(2,1)},...) custom-call(s32[1]{0:T(128)} %constant.26.clone.1.refs_0_, ...), custom_call_target="tpu_custom_call", output_to_operand_aliasing={{7}: (3, {}), {8}: (4, {}), {9}: (5, {}), {10}: (6, {}), {1... | custom-call | flops 5120000000 | bytes 4194304 | tf_op jit(solution)/shard_map/layer_backward/pallas_call | solution.py:704
  255.1 11.6 %layer_backward.23 = (bf16[256,768]{1,0:T(8,128)(2,1)S(1)}, f32[6,256,256]{2,1,0:T(8,128)S(1)}, f32[8,768]{1,0:T(8,128)S(1)}, bf16[2048,768]{1,0:T(8,128)(2,1)},...) custom-call(s32[1]{0:T(128)} %constant.38.clone.1.refs_0_, ...), custom_call_target="tpu_custom_call", output_to_operand_aliasing={{7}: (3, {}), {8}: (4, {}), {9}: (5, {}), {10}: (6, {}), {1... | custom-call | flops 5120000000 | bytes 4194304 | tf_op jit(solution)/shard_map/layer_backward/pallas_call | solution.py:704
  268.0 10.9 %layer_backward.24 = (bf16[256,768]{1,0:T(8,128)(2,1)S(1)}, f32[6,256,256]{2,1,0:T(8,128)S(1)}, f32[8,768]{1,0:T(8,128)S(1)}, bf16[2048,768]{1,0:T(8,128)(2,1)},...) custom-call(s32[1]{0:T(128)} %constant.27.clone.1.refs_0_, ...), custom_call_target="tpu_custom_call", output_to_operand_aliasing={{7}: (3, {}), {8}: (4, {}), {9}: (5, {}), {10}: (6, {}), {1... | custom-call | flops 5120000000 | bytes 4194304 | tf_op jit(solution)/shard_map/layer_backward/pallas_call | solution.py:704
  281.5 11.4 %layer_backward.25 = (bf16[256,768]{1,0:T(8,128)(2,1)S(1)}, f32[6,256,256]{2,1,0:T(8,128)S(1)}, f32[8,768]{1,0:T(8,128)S(1)}, bf16[2048,768]{1,0:T(8,128)(2,1)},...) custom-call(s32[1]{0:T(128)} %constant.17.clone.1.refs_0_, ...), custom_call_target="tpu_custom_call", output_to_operand_aliasing={{7}: (3, {}), {8}: (4, {}), {9}: (5, {}), {10}: (6, {}), {1... | custom-call | flops 5120000000 | bytes 4194304 | tf_op jit(solution)/shard_map/layer_backward/pallas_call | solution.py:704
  294.2 11.7 %layer_backward.26 = (bf16[256,768]{1,0:T(8,128)(2,1)}, f32[6,256,256]{2,1,0:T(8,128)S(1)}, f32[8,768]{1,0:T(8,128)S(1)}, bf16[2048,768]{1,0:T(8,128)(2,1)}, bf1...) custom-call(s32[1]{0:T(128)} %constant.28.clone.1.refs_0_, ...), custom_call_target="tpu_custom_call", output_to_operand_aliasing={{7}: (3, {}), {8}: (4, {}), {9}: (5, {}), {10}: (6, {}), {1... | custom-call | flops 5120000000 | bytes 4194304 | tf_op jit(solution)/shard_map/layer_backward/pallas_call | solution.py:704
  306.6 12.3 %layer_backward.27 = (bf16[256,768]{1,0:T(8,128)(2,1)}, f32[6,256,256]{2,1,0:T(8,128)S(1)}, f32[8,768]{1,0:T(8,128)S(1)}, bf16[2048,768]{1,0:T(8,128)(2,1)}, bf1...) custom-call(s32[1]{0:T(128)} %constant.29.clone.1.refs_0_, ...), custom_call_target="tpu_custom_call", output_to_operand_aliasing={{7}: (3, {}), {8}: (4, {}), {9}: (5, {}), {10}: (6, {}), {1... | custom-call | flops 5120000000 | bytes 4194304 | tf_op jit(solution)/shard_map/layer_backward/pallas_call | solution.py:704
  318.9 8.8 %weight_grad.6 = (bf16[2,384,768]{2,1,0:T(8,128)(2,1)}, bf16[2,384,768]{2,1,0:T(8,128)(2,1)}, bf16[2048,768]{1,0:T(8,128)(2,1)S(1)}) custom-call(s32[18]{0:T(128)S(1)} %pad_add_fusion.refs_1_.meta_ref, bf16[12,2048,256]{2,1,0:T(8,128)(2,1)S(1)} %get-tuple-element.1298.left, bf16[2048,768]{1,0:T(8,128)(2,1)} %get-tuple-element.1299.refs_0_), custom_call_target="tpu_custom_call" | custom-call | flops 4831838208 | bytes 15728640 | tf_op jit(solution)/shard_map/weight_grad/pallas_call | solution.py:731
  327.9 6.8 %weight_grad.7 = (bf16[2,384,768]{2,1,0:T(8,128)(2,1)}, bf16[2,384,768]{2,1,0:T(8,128)(2,1)}) custom-call(s32[18]{0:T(128)S(1)} %pad_add_fusion.refs_1_.meta_ref, bf16[12,2048,256]{2,1,0:T(8,128)(2,1)S(1)} %get-tuple-element.1298.left, bf16[2048,768]{1,0:T(8,128)(2,1)S(1)} %get-tuple-element.1300.refs_0_), custom_call_target="tpu_custom_call" | custom-call | flops 4831838208 | bytes 15728640 | tf_op jit(solution)/shard_map/weight_grad/pallas_call | solution.py:731
  335.7 8.3 %weight_grad.8 = (bf16[2,384,768]{2,1,0:T(8,128)(2,1)}, bf16[2,384,768]{2,1,0:T(8,128)(2,1)}) custom-call(s32[18]{0:T(128)S(1)} %pad_add_fusion.refs_1_.meta_ref, bf16[12,2048,256]{2,1,0:T(8,128)(2,1)S(1)} %bitcast.61, bf16[2048,768]{1,0:T(8,128)(2,1)S(1)} %copy-done.1, bf16[2048,768]{1,0:T(8,128)(2,1)S(1)} %copy-done, bf16[384,768]{1,0:T(8,128)(2,1)S(1)} %add_parts.13.refs_2_), custom_call_target="tpu_custom_call" | custom-call | flops 4831838208 | bytes 15728640 | tf_op jit(solution)/shard_map/weight_grad/pallas_call | solution.py:731
  344.6 2.1 collective-permute-done.24.refs_1_
  348.6 2.8 collective-permute-done.25.refs_1_
  354.6 8.3 %weight_grad.9 = (bf16[2,384,768]{2,1,0:T(8,128)(2,1)}, bf16[2,384,768]{2,1,0:T(8,128)(2,1)}) custom-call(s32[18]{0:T(128)S(1)} %pad_add_fusion.refs_1_.meta_ref, bf16[12,2048,256]{2,1,0:T(8,128)(2,1)S(1)} %bitcast.61, bf16[2048,768]{1,0:T(8,128)(2,1)S(1)} %copy-done.1, bf16[2048,768]{1,0:T(8,128)(2,1)S(1)} %copy-done, bf16[384,768]{1,0:T(8,128)(2,1)S(1)} %add_parts.12.refs_2_), custom_call_target="tpu_custom_call" | custom-call | flops 4831838208 | bytes 15728640 | tf_op jit(solution)/shard_map/weight_grad/pallas_call | solution.py:731
  363.2 2.9 collective-permute-done.29.refs_2_
  369.3 6.8 %weight_grad.11 = (bf16[2,384,768]{2,1,0:T(8,128)(2,1)}, bf16[2,384,768]{2,1,0:T(8,128)(2,1)}) custom-call(s32[18]{0:T(128)S(1)} %pad_add_fusion.refs_1_.meta_ref, bf16[12,2048,256]{2,1,0:T(8,128)(2,1)S(1)} %bitcast.63, bf16[2048,768]{1,0:T(8,128)(2,1)S(1)} %copy-done.2, bf16[384,768]{1,0:T(8,128)(2,1)S(1)} %add_parts.14.refs_1_), custom_call_target="tpu_custom_call" | custom-call | flops 4831838208 | bytes 15728640 | tf_op jit(solution)/shard_map/weight_grad/pallas_call | solution.py:731
  377.4 2.3 collective-permute-done.31.refs_2_
  383.2 6.8 %weight_grad.10 = (bf16[2,384,768]{2,1,0:T(8,128)(2,1)}, bf16[2,384,768]{2,1,0:T(8,128)(2,1)}) custom-call(s32[18]{0:T(128)S(1)} %pad_add_fusion.refs_1_.meta_ref, bf16[12,2048,256]{2,1,0:T(8,128)(2,1)S(1)} %bitcast.63, bf16[2048,768]{1,0:T(8,128)(2,1)S(1)} %copy-done.2, bf16[384,768]{1,0:T(8,128)(2,1)} %add_parts.15.refs_1_), custom_call_target="tpu_custom_call" | custom-call | flops 4831838208 | bytes 15728640 | tf_op jit(solution)/shard_map/weight_grad/pallas_call | solution.py:731
  398.8 3.1 copy.584
  403.3 2.2 add_parts.16
  416.7 6.3 %collective-permute-done.43.refs_2_ = bf16[384,768]{1,0:T(8,128)(2,1)} collective-permute-done((bf16[384,768]{1,0:T(8,128)(2,1)}, bf16[384,768]{1,0:T(8,128)(2,1)}, u32[]{:S(2)}, u32[]{:S(2)}) %collective-permute-start.43) | collective-permute-done | bytes 589856 | tf_op jit(solution)/shard_map/ppermute | solution.py:631
  426.7 2.3 fusion.6
  428.9 2.2 copy.583
  431.1 3.3 fusion.2
  434.4 2.8 copy.582
  (194 shorter events, 79.4 us)
Async XLA Ops:
  15.1 11.6 %collective-permute-start.1 = (bf16[256,768]{1,0:T(8,128)(2,1)S(1)}, bf16[256,768]{1,0:T(8,128)(2,1)S(1)}, u32[]{:S(2)}, u32[]{:S(2)}) collective-permute-start(bf16[256,768]{1,0:T(8,128)(2,1)S(1)} %get-tuple-element.687.refs_13_), channel_id=1, source_target_pairs={{0,8},{1,9},{2,10},{3,11},{4,12},{5,13},{6,14},{7,15}} | collective-permute-start | bytes 1179656 | tf_op jit(solution)/shard_map/ppermute | solution.py:699
  25.4 13.1 %collective-permute-start = (bf16[256,768]{1,0:T(8,128)(2,1)S(1)}, bf16[256,768]{1,0:T(8,128)(2,1)S(1)}, u32[]{:S(2)}, u32[]{:S(2)}) collective-permute-start(bf16[256,768]{1,0:T(8,128)(2,1)S(1)} %get-tuple-element.704.refs_13_), channel_id=1, source_target_pairs={{0,8},{1,9},{2,10},{3,11},{4,12},{5,13},{6,14},{7,15}} | collective-permute-start | bytes 1179656 | tf_op jit(solution)/shard_map/ppermute | solution.py:699
  35.3 14.2 %collective-permute-start.3 = (bf16[256,768]{1,0:T(8,128)(2,1)S(1)}, bf16[256,768]{1,0:T(8,128)(2,1)S(1)}, u32[]{:S(2)}, u32[]{:S(2)}) collective-permute-start(bf16[256,768]{1,0:T(8,128)(2,1)S(1)} %get-tuple-element.741.refs_13_), channel_id=1, source_target_pairs={{0,8},{8,16},{1,9},{9,17},{2,10},{10,18},{3,11},{11,19},{4,12},{12... | collective-permute-start | bytes 1179656 | tf_op jit(solution)/shard_map/ppermute | solution.py:699
  47.6 12.5 %collective-permute-start.2 = (bf16[256,768]{1,0:T(8,128)(2,1)S(1)}, bf16[256,768]{1,0:T(8,128)(2,1)S(1)}, u32[]{:S(2)}, u32[]{:S(2)}) collective-permute-start(bf16[256,768]{1,0:T(8,128)(2,1)S(1)} %get-tuple-element.758.refs_13_), channel_id=1, source_target_pairs={{0,8},{8,16},{1,9},{9,17},{2,10},{10,18},{3,11},{11,19},{4,12},{12... | collective-permute-start | bytes 1179656 | tf_op jit(solution)/shard_map/ppermute | solution.py:699
  58.1 13.2 %collective-permute-start.5 = (bf16[256,768]{1,0:T(8,128)(2,1)S(1)}, bf16[256,768]{1,0:T(8,128)(2,1)S(1)}, u32[]{:S(2)}, u32[]{:S(2)}) collective-permute-start(bf16[256,768]{1,0:T(8,128)(2,1)S(1)} %get-tuple-element.795.refs_13_), channel_id=1, source_target_pairs={{0,8},{8,16},{16,24},{1,9},{9,17},{17,25},{2,10},{10,18},{18,26},{... | collective-permute-start | bytes 1179656 | tf_op jit(solution)/shard_map/ppermute | solution.py:699
  69.1 12.9 %collective-permute-start.4 = (bf16[256,768]{1,0:T(8,128)(2,1)S(1)}, bf16[256,768]{1,0:T(8,128)(2,1)S(1)}, u32[]{:S(2)}, u32[]{:S(2)}) collective-permute-start(bf16[256,768]{1,0:T(8,128)(2,1)S(1)} %get-tuple-element.812.refs_13_), channel_id=1, source_target_pairs={{0,8},{8,16},{16,24},{1,9},{9,17},{17,25},{2,10},{10,18},{18,26},{... | collective-permute-start | bytes 1179656 | tf_op jit(solution)/shard_map/ppermute | solution.py:699
  79.6 13.5 %collective-permute-start.7 = (bf16[256,768]{1,0:T(8,128)(2,1)S(1)}, bf16[256,768]{1,0:T(8,128)(2,1)S(1)}, u32[]{:S(2)}, u32[]{:S(2)}) collective-permute-start(bf16[256,768]{1,0:T(8,128)(2,1)S(1)} %get-tuple-element.849.refs_13_), channel_id=1, source_target_pairs={{0,8},{8,16},{16,24},{1,9},{9,17},{17,25},{2,10},{10,18},{18,26},{... | collective-permute-start | bytes 1179656 | tf_op jit(solution)/shard_map/ppermute | solution.py:699
  91.2 9.5 %collective-permute-start.6 = (bf16[256,768]{1,0:T(8,128)(2,1)S(1)}, bf16[256,768]{1,0:T(8,128)(2,1)S(1)}, u32[]{:S(2)}, u32[]{:S(2)}) collective-permute-start(bf16[256,768]{1,0:T(8,128)(2,1)S(1)} %get-tuple-element.866.refs_13_), channel_id=1, source_target_pairs={{0,8},{8,16},{16,24},{1,9},{9,17},{17,25},{2,10},{10,18},{18,26},{... | collective-permute-start | bytes 1179656 | tf_op jit(solution)/shard_map/ppermute | solution.py:699
  95.0 13.3 %collective-permute-start.9 = (bf16[256,768]{1,0:T(8,128)(2,1)S(1)}, bf16[256,768]{1,0:T(8,128)(2,1)S(1)}, u32[]{:S(2)}, u32[]{:S(2)}) collective-permute-start(bf16[256,768]{1,0:T(8,128)(2,1)S(1)} %get-tuple-element.903.refs_13_), channel_id=1, source_target_pairs={{8,16},{16,24},{9,17},{17,25},{10,18},{18,26},{11,19},{19,27},{12,... | collective-permute-start | bytes 1179656 | tf_op jit(solution)/shard_map/ppermute | solution.py:699
  107.6 2.3 collective-permute-start.8
  109.2 10.1 %collective-permute-start.11 = (bf16[256,768]{1,0:T(8,128)(2,1)S(1)}, bf16[256,768]{1,0:T(8,128)(2,1)S(1)}, u32[]{:S(2)}, u32[]{:S(2)}) collective-permute-start(bf16[256,768]{1,0:T(8,128)(2,1)S(1)} %get-tuple-element.957.refs_13_), channel_id=1, source_target_pairs={{16,24},{17,25},{18,26},{19,27},{20,28},{21,29},{22,30},{23,31}} | collective-permute-start | bytes 1179656 | tf_op jit(solution)/shard_map/ppermute | solution.py:699
  118.6 1.6 collective-permute-start.10
  134.2 10.1 %collective-permute-start.13 = (bf16[256,768]{1,0:T(8,128)(2,1)S(1)}, bf16[256,768]{1,0:T(8,128)(2,1)S(1)}, u32[]{:S(2)}, u32[]{:S(2)}) collective-permute-start(bf16[256,768]{1,0:T(8,128)(2,1)S(1)} %get-tuple-element.1069), channel_id=1, source_target_pairs={{24,16},{25,17},{26,18},{27,19},{28,20},{29,21},{30,22},{31,23}} | collective-permute-start | bytes 1179656 | tf_op jit(solution)/shard_map/ppermute | solution.py:709
  143.5 3.7 collective-permute-start.12
  146.6 10.5 %collective-permute-start.15 = (bf16[256,768]{1,0:T(8,128)(2,1)S(1)}, bf16[256,768]{1,0:T(8,128)(2,1)S(1)}, u32[]{:S(2)}, u32[]{:S(2)}) collective-permute-start(bf16[256,768]{1,0:T(8,128)(2,1)S(1)} %get-tuple-element.1107), channel_id=1, source_target_pairs={{16,8},{24,16},{17,9},{25,17},{18,10},{26,18},{19,11},{27,19},{20,... | collective-permute-start | bytes 1179656 | tf_op jit(solution)/shard_map/ppermute | solution.py:709
  156.4 4.3 collective-permute-start.14
  159.4 55.3 %collective-permute-start.17 = (bf16[256,768]{1,0:T(8,128)(2,1)S(1)}, bf16[256,768]{1,0:T(8,128)(2,1)S(1)}, u32[]{:S(2)}, u32[]{:S(2)}) collective-permute-start(bf16[256,768]{1,0:T(8,128)(2,1)S(1)} %get-tuple-element.1145), channel_id=1, source_target_pairs={{8,0},{16,8},{24,16},{9,1},{17,9},{25,17},{10,2},{18,10},{26,18},{... | collective-permute-start | bytes 1179656 | tf_op jit(solution)/shard_map/ppermute | solution.py:709
  170.8 58.0 %collective-permute-start.16 = (bf16[256,768]{1,0:T(8,128)(2,1)S(1)}, bf16[256,768]{1,0:T(8,128)(2,1)S(1)}, u32[]{:S(2)}, u32[]{:S(2)}) collective-permute-start(bf16[256,768]{1,0:T(8,128)(2,1)S(1)} %get-tuple-element.1144), channel_id=1, source_target_pairs={{8,0},{16,8},{24,16},{9,1},{17,9},{25,17},{10,2},{18,10},{26,18},{... | collective-permute-start | bytes 1179656 | tf_op jit(solution)/shard_map/ppermute | solution.py:709
  225.5 16.2 %collective-permute-start.19 = (bf16[256,768]{1,0:T(8,128)(2,1)S(1)}, bf16[256,768]{1,0:T(8,128)(2,1)S(1)}, u32[]{:S(2)}, u32[]{:S(2)}) collective-permute-start(bf16[256,768]{1,0:T(8,128)(2,1)S(1)} %get-tuple-element.1183), channel_id=1, source_target_pairs={{8,0},{16,8},{24,16},{9,1},{17,9},{25,17},{10,2},{18,10},{26,18},{... | collective-permute-start | bytes 1179656 | tf_op jit(solution)/shard_map/ppermute | solution.py:709
  240.3 14.9 %collective-permute-start.18 = (bf16[256,768]{1,0:T(8,128)(2,1)S(1)}, bf16[256,768]{1,0:T(8,128)(2,1)S(1)}, u32[]{:S(2)}, u32[]{:S(2)}) collective-permute-start(bf16[256,768]{1,0:T(8,128)(2,1)S(1)} %get-tuple-element.1182), channel_id=1, source_target_pairs={{8,0},{16,8},{24,16},{9,1},{17,9},{25,17},{10,2},{18,10},{26,18},{... | collective-permute-start | bytes 1179656 | tf_op jit(solution)/shard_map/ppermute | solution.py:709
  252.6 15.4 %collective-permute-start.21 = (bf16[256,768]{1,0:T(8,128)(2,1)S(1)}, bf16[256,768]{1,0:T(8,128)(2,1)S(1)}, u32[]{:S(2)}, u32[]{:S(2)}) collective-permute-start(bf16[256,768]{1,0:T(8,128)(2,1)S(1)} %get-tuple-element.1221), channel_id=1, source_target_pairs={{8,0},{16,8},{9,1},{17,9},{10,2},{18,10},{11,3},{19,11},{12,4},{20... | collective-permute-start | bytes 1179656 | tf_op jit(solution)/shard_map/ppermute | solution.py:709
  266.7 14.8 %collective-permute-start.20 = (bf16[256,768]{1,0:T(8,128)(2,1)S(1)}, bf16[256,768]{1,0:T(8,128)(2,1)S(1)}, u32[]{:S(2)}, u32[]{:S(2)}) collective-permute-start(bf16[256,768]{1,0:T(8,128)(2,1)S(1)} %get-tuple-element.1220), channel_id=1, source_target_pairs={{8,0},{16,8},{9,1},{17,9},{10,2},{18,10},{11,3},{19,11},{12,4},{20... | collective-permute-start | bytes 1179656 | tf_op jit(solution)/shard_map/ppermute | solution.py:709
  278.9 15.3 %collective-permute-start.23 = (bf16[256,768]{1,0:T(8,128)(2,1)S(1)}, bf16[256,768]{1,0:T(8,128)(2,1)S(1)}, u32[]{:S(2)}, u32[]{:S(2)}) collective-permute-start(bf16[256,768]{1,0:T(8,128)(2,1)S(1)} %get-tuple-element.1259), channel_id=1, source_target_pairs={{8,0},{9,1},{10,2},{11,3},{12,4},{13,5},{14,6},{15,7}} | collective-permute-start | bytes 1179656 | tf_op jit(solution)/shard_map/ppermute | solution.py:709
  292.9 13.7 %collective-permute-start.22 = (bf16[256,768]{1,0:T(8,128)(2,1)S(1)}, bf16[256,768]{1,0:T(8,128)(2,1)S(1)}, u32[]{:S(2)}, u32[]{:S(2)}) collective-permute-start(bf16[256,768]{1,0:T(8,128)(2,1)S(1)} %get-tuple-element.1258), channel_id=1, source_target_pairs={{8,0},{9,1},{10,2},{11,3},{12,4},{13,5},{14,6},{15,7}} | collective-permute-start | bytes 1179656 | tf_op jit(solution)/shard_map/ppermute | solution.py:709
  318.9 16.7 %slice-start = ((s8[12582912]{0:T(1024)(128)(4,1)}), s8[4194304]{0:T(1024)(128)(4,1)S(1)}, s32[]{:S(2)}) async-start(s8[12582912]{0:T(1024)(128)(4,1)} %bitcast.60), calls=%async_computation | async-start | bytes 8388608
  318.9 16.7 %slice-start.1 = ((s8[12582912]{0:T(1024)(128)(4,1)}), s8[4194304]{0:T(1024)(128)(4,1)S(1)}, s32[]{:S(2)}) async-start(s8[12582912]{0:T(1024)(128)(4,1)} %bitcast.60), calls=%async_computation.1 | async-start | bytes 8388608
  327.7 7.4 %collective-permute-start.27 = (bf16[2,384,768]{2,1,0:T(8,128)(2,1)}, bf16[2,384,768]{2,1,0:T(8,128)(2,1)S(1)}, u32[]{:S(2)}, u32[]{:S(2)}) collective-permute-start(bf16[2,384,768]{2,1,0:T(8,128)(2,1)} %get-tuple-element.1307), channel_id=1, source_target_pairs={{0,2},{2,0},{4,6},{6,4},{1,3},{3,1},{5,7},{7,5},{8,10},{10,8},{12,... | collective-permute-start | bytes 3538952 | tf_op jit(solution)/shard_map/ppermute | solution.py:631
  334.6 16.8 %collective-permute-start.26 = (bf16[2,384,768]{2,1,0:T(8,128)(2,1)}, bf16[2,384,768]{2,1,0:T(8,128)(2,1)S(1)}, u32[]{:S(2)}, u32[]{:S(2)}) collective-permute-start(bf16[2,384,768]{2,1,0:T(8,128)(2,1)} %get-tuple-element.1302), channel_id=1, source_target_pairs={{0,2},{2,0},{4,6},{6,4},{1,3},{3,1},{5,7},{7,5},{8,10},{10,8},{12,... | collective-permute-start | bytes 3538952 | tf_op jit(solution)/shard_map/ppermute | solution.py:631
  335.5 16.1 %collective-permute-start.28 = (bf16[384,768]{1,0:T(8,128)(2,1)S(1)}, bf16[384,768]{1,0:T(8,128)(2,1)S(1)}, u32[]{:S(2)}, u32[]{:S(2)}) collective-permute-start(bf16[384,768]{1,0:T(8,128)(2,1)S(1)} %add_parts.13.refs_2_), channel_id=1, source_target_pairs={{0,4},{2,6},{4,0},{6,2},{1,5},{3,7},{5,1},{7,3},{8,12},{10,14},{12... | collective-permute-start | bytes 1769480 | tf_op jit(solution)/shard_map/ppermute | solution.py:631
  344.0 19.0 %collective-permute-start.30 = (bf16[2,384,768]{2,1,0:T(8,128)(2,1)}, bf16[2,384,768]{2,1,0:T(8,128)(2,1)S(1)}, u32[]{:S(2)}, u32[]{:S(2)}) collective-permute-start(bf16[2,384,768]{2,1,0:T(8,128)(2,1)} %get-tuple-element.1313), channel_id=1, source_target_pairs={{0,2},{2,0},{4,6},{6,4},{1,3},{3,1},{5,7},{7,5},{8,10},{10,8},{12,... | collective-permute-start | bytes 3538952 | tf_op jit(solution)/shard_map/ppermute | solution.py:631
  344.1 2.5 collective-permute-start.24
  346.7 4.8 %collective-permute-start.25 = (f32[8,768]{1,0:T(8,128)S(1)}, f32[8,768]{1,0:T(8,128)S(1)}, u32[]{:S(2)}, u32[]{:S(2)}) collective-permute-start(f32[8,768]{1,0:T(8,128)S(1)} %add_vectors.3.refs_0_), channel_id=1, source_target_pairs={{0,4},{2,6},{4,0},{6,2},{1,5},{3,7},{5,1},{7,3},{8,12},{10,14},{12... | collective-permute-start | bytes 73736 | tf_op jit(solution)/shard_map/ppermute | solution.py:631
  351.6 14.5 %collective-permute-start.29 = (bf16[384,768]{1,0:T(8,128)(2,1)S(1)}, bf16[384,768]{1,0:T(8,128)(2,1)S(1)}, u32[]{:S(2)}, u32[]{:S(2)}) collective-permute-start(bf16[384,768]{1,0:T(8,128)(2,1)S(1)} %add_parts.12.refs_2_), channel_id=1, source_target_pairs={{0,4},{2,6},{4,0},{6,2},{1,5},{3,7},{5,1},{7,3},{8,12},{10,14},{12... | collective-permute-start | bytes 1769480 | tf_op jit(solution)/shard_map/ppermute | solution.py:631
  352.7 16.5 %slice-start.3 = ((s8[12582912]{0:T(1024)(128)(4,1)}), s8[4194304]{0:T(1024)(128)(4,1)S(1)}, s32[]{:S(2)}) async-start(s8[12582912]{0:T(1024)(128)(4,1)} %bitcast.62), calls=%async_computation.3 | async-start | bytes 8388608
  353.0 14.7 %collective-permute-start.37 = (bf16[384,768]{1,0:T(8,128)(2,1)S(1)}, bf16[384,768]{1,0:T(8,128)(2,1)S(1)}, u32[]{:S(2)}, u32[]{:S(2)}) collective-permute-start(bf16[384,768]{1,0:T(8,128)(2,1)S(1)} %add_parts.20), channel_id=1, source_target_pairs={{0,1},{1,0},{2,3},{3,2},{4,5},{5,4},{6,7},{7,6},{8,9},{9,8},{10,11... | collective-permute-start | bytes 1769480 | tf_op jit(solution)/shard_map/ppermute | solution.py:631
  362.9 13.3 %collective-permute-start.32 = (bf16[2,384,768]{2,1,0:T(8,128)(2,1)}, bf16[2,384,768]{2,1,0:T(8,128)(2,1)S(1)}, u32[]{:S(2)}, u32[]{:S(2)}) collective-permute-start(bf16[2,384,768]{2,1,0:T(8,128)(2,1)} %get-tuple-element.1316), channel_id=1, source_target_pairs={{0,2},{2,0},{4,6},{6,4},{1,3},{3,1},{5,7},{7,5},{8,10},{10,8},{12,... | collective-permute-start | bytes 3538952 | tf_op jit(solution)/shard_map/ppermute | solution.py:631
  366.2 13.5 %collective-permute-start.31 = (bf16[384,768]{1,0:T(8,128)(2,1)S(1)}, bf16[384,768]{1,0:T(8,128)(2,1)S(1)}, u32[]{:S(2)}, u32[]{:S(2)}) collective-permute-start(bf16[384,768]{1,0:T(8,128)(2,1)S(1)} %add_parts.14.refs_1_), channel_id=1, source_target_pairs={{0,4},{2,6},{4,0},{6,2},{1,5},{3,7},{5,1},{7,3},{8,12},{10,14},{12... | collective-permute-start | bytes 1769480 | tf_op jit(solution)/shard_map/ppermute | solution.py:631
  367.7 13.9 %collective-permute-start.38 = (bf16[384,768]{1,0:T(8,128)(2,1)S(1)}, bf16[384,768]{1,0:T(8,128)(2,1)S(1)}, u32[]{:S(2)}, u32[]{:S(2)}) collective-permute-start(bf16[384,768]{1,0:T(8,128)(2,1)S(1)} %add_parts.21), channel_id=1, source_target_pairs={{0,1},{1,0},{2,3},{3,2},{4,5},{5,4},{6,7},{7,6},{8,9},{9,8},{10,11... | collective-permute-start | bytes 1769480 | tf_op jit(solution)/shard_map/ppermute | solution.py:631
  376.2 15.5 %collective-permute-start.36 = (bf16[2,384,768]{2,1,0:T(8,128)(2,1)}, bf16[2,384,768]{2,1,0:T(8,128)(2,1)S(1)}, u32[]{:S(2)}, u32[]{:S(2)}) collective-permute-start(bf16[2,384,768]{2,1,0:T(8,128)(2,1)} %get-tuple-element.1322), channel_id=1, source_target_pairs={{0,2},{2,0},{4,6},{6,4},{1,3},{3,1},{5,7},{7,5},{8,10},{10,8},{12,... | collective-permute-start | bytes 3538952 | tf_op jit(solution)/shard_map/ppermute | solution.py:631
  379.7 13.7 %collective-permute-start.35 = (bf16[384,768]{1,0:T(8,128)(2,1)}, bf16[384,768]{1,0:T(8,128)(2,1)}, u32[]{:S(2)}, u32[]{:S(2)}) collective-permute-start(bf16[384,768]{1,0:T(8,128)(2,1)} %add_parts.15.refs_1_), channel_id=1, source_target_pairs={{0,4},{2,6},{4,0},{6,2},{1,5},{3,7},{5,1},{7,3},{8,12},{10,14},{12... | collective-permute-start | bytes 1769480 | tf_op jit(solution)/shard_map/ppermute | solution.py:631
  381.6 15.0 %collective-permute-start.39 = (bf16[384,768]{1,0:T(8,128)(2,1)}, bf16[384,768]{1,0:T(8,128)(2,1)}, u32[]{:S(2)}, u32[]{:S(2)}) collective-permute-start(bf16[384,768]{1,0:T(8,128)(2,1)} %add_parts.19), channel_id=1, source_target_pairs={{0,1},{1,0},{2,3},{3,2},{4,5},{5,4},{6,7},{7,6},{8,9},{9,8},{10,11... | collective-permute-start | bytes 1769480 | tf_op jit(solution)/shard_map/ppermute | solution.py:631
  390.1 13.2 %collective-permute-start.33 = (bf16[2,384,768]{2,1,0:T(8,128)(2,1)}, bf16[2,384,768]{2,1,0:T(8,128)(2,1)}, u32[]{:S(2)}, u32[]{:S(2)}) collective-permute-start(bf16[2,384,768]{2,1,0:T(8,128)(2,1)} %get-tuple-element.1319), channel_id=1, source_target_pairs={{0,2},{2,0},{4,6},{6,4},{1,3},{3,1},{5,7},{7,5},{8,10},{10,8},{12,... | collective-permute-start | bytes 3538952 | tf_op jit(solution)/shard_map/ppermute | solution.py:631
  393.4 15.2 %collective-permute-start.41 = (bf16[384,768]{1,0:T(8,128)(2,1)}, bf16[384,768]{1,0:T(8,128)(2,1)}, u32[]{:S(2)}, u32[]{:S(2)}) collective-permute-start(bf16[384,768]{1,0:T(8,128)(2,1)} %add_parts.17), channel_id=1, source_target_pairs={{0,4},{2,6},{4,0},{6,2},{1,5},{3,7},{5,1},{7,3},{8,12},{10,14},{12... | collective-permute-start | bytes 1769480 | tf_op jit(solution)/shard_map/ppermute | solution.py:631
  396.6 15.4 %collective-permute-start.40 = (bf16[384,768]{1,0:T(8,128)(2,1)}, bf16[384,768]{1,0:T(8,128)(2,1)}, u32[]{:S(2)}, u32[]{:S(2)}) collective-permute-start(bf16[384,768]{1,0:T(8,128)(2,1)} %add_parts.18), channel_id=1, source_target_pairs={{0,1},{1,0},{2,3},{3,2},{4,5},{5,4},{6,7},{7,6},{8,9},{9,8},{10,11... | collective-permute-start | bytes 1769480 | tf_op jit(solution)/shard_map/ppermute | solution.py:631
  405.6 11.1 %collective-permute-start.34 = (f32[8,768]{1,0:T(8,128)S(1)}, f32[8,768]{1,0:T(8,128)S(1)}, u32[]{:S(2)}, u32[]{:S(2)}) collective-permute-start(f32[8,768]{1,0:T(8,128)S(1)} %copy-done.15), channel_id=1, source_target_pairs={{0,1},{1,0},{2,3},{3,2},{4,5},{5,4},{6,7},{7,6},{8,9},{9,8},{10,11... | collective-permute-start | bytes 73736 | tf_op jit(solution)/shard_map/ppermute | solution.py:631
  408.6 14.4 %collective-permute-start.43 = (bf16[384,768]{1,0:T(8,128)(2,1)}, bf16[384,768]{1,0:T(8,128)(2,1)}, u32[]{:S(2)}, u32[]{:S(2)}) collective-permute-start(bf16[384,768]{1,0:T(8,128)(2,1)} %add_parts.16), channel_id=1, source_target_pairs={{0,4},{2,6},{4,0},{6,2},{1,5},{3,7},{5,1},{7,3},{8,12},{10,14},{12... | collective-permute-start | bytes 1769480 | tf_op jit(solution)/shard_map/ppermute | solution.py:631
  412.1 14.3 %collective-permute-start.42 = (bf16[384,768]{1,0:T(8,128)(2,1)}, bf16[384,768]{1,0:T(8,128)(2,1)}, u32[]{:S(2)}, u32[]{:S(2)}) collective-permute-start(bf16[384,768]{1,0:T(8,128)(2,1)} %add_parts.22), channel_id=1, source_target_pairs={{0,1},{1,0},{2,3},{3,2},{4,5},{5,4},{6,7},{7,6},{8,9},{9,8},{10,11... | collective-permute-start | bytes 1769480 | tf_op jit(solution)/shard_map/ppermute | solution.py:631
  426.4 13.2 %collective-permute-start.44 = (bf16[384,768]{1,0:T(8,128)(2,1)S(1)}, bf16[384,768]{1,0:T(8,128)(2,1)}, u32[]{:S(2)}, u32[]{:S(2)}) collective-permute-start(bf16[384,768]{1,0:T(8,128)(2,1)S(1)} %add_parts.23), channel_id=1, source_target_pairs={{0,1},{1,0},{2,3},{3,2},{4,5},{5,4},{6,7},{7,6},{8,9},{9,8},{10,11... | collective-permute-start | bytes 1769480 | tf_op jit(solution)/shard_map/ppermute | solution.py:631
  (28 other events, 217.9 us)

commit v9 on v8

--- a/solution.py
+++ b/solution.py
@@ -676,6 +676,22 @@
     return other.astype(f32)
 
 
+def join_half(own, other, half, before, limit=12):
+    step = HALF // 2
+    flat = pl.BlockSpec((step, D), lambda i: (i, 0))
+    return pl.pallas_call(
+        lambda *refs: add_kernel(refs[0], refs[1], refs[-1]),
+        grid=(2,),
+        in_specs=[flat, flat] + [pl.BlockSpec(memory_space=pl.ANY)] * len(before),
+        out_specs=pl.BlockSpec((step, D), lambda i: (2 * half + i, 0)),
+        out_shape=jax.ShapeDtypeStruct((D, D), f32),
+        input_output_aliases={2: 0} if before else {},
+        cost_estimate=pl.CostEstimate(flops=HALF * D, bytes_accessed=HALF * D * 8, transcendentals=0),
+        compiler_params=pltpu.CompilerParams(vmem_limit_bytes=limit * 2**20),
+        name="join_half",
+    )(own, other, *before)
+
+
 def local(tokens, doc_ids, cotangent, w_qkv, w_out, w_up, w_down,
           first_gain, first_bias, second_gain, second_bias):
     stages = lax.axis_size("pipe")
@@ -750,6 +766,8 @@
     vectors, me, _ = lax.optimization_barrier((vectors, me, owns[3]))
     mine = lax.dynamic_slice_in_dim(vectors, me * (D // groups), D // groups, axis=1)
     g_down, g_mixed, g_up = (jnp.concatenate(parts[i:i + 2], axis=0) for i in (0, 2, 4))
+    if lax.axis_size("dp") == 2:
+        g_up = join_half(owns[5], others[5], 1, [join_half(owns[4], others[4], 0, [])])
     odd = (me & 1) == 1
     swap = lambda a, b: jnp.concatenate([g_mixed[:, a], g_mixed[:, b]], axis=1)
     low, one, two, high = slice(0, 512), slice(512, 576), slice(576, 640), slice(640, 768)

time: 450 us -> 447 us (level)
  other arithmetic: 20.1 us -> 14.7 us
  transfers between devices with their start and end apart: 45 -> 45, of which waited for: 16 -> 16; matrix products, arithmetic and copies ran while one was open for 6% -> 5% of each run, Pallas kernels for 54% -> 55%
where the time goes in v9:
time: 447 us; the launch traced here: 439 us
  Pallas kernels  287 us (64%)
  waiting for transfers between devices  75.4 us (17%)
  starting transfers between devices  48.2 us (11%)
  other arithmetic  14.7 us (3%)
  local copies, waits for them, and re-layouts  10.9 us (2%)
    pallas_call x14, Pallas kernels, local(): backward_call(ROWS, n, DELTA, stages, groups, t == 0)  126 us
    pallas_call x14, Pallas kernels, local(): forward_call(ROWS, n, DELTA, t == 0, t == ticks - 1)  103 us
    ppermute x24, waiting for transfers between devices, local(): arriving.append(lax.ppermute(made[0], 'pipe', route) if route else made[0])  51.4 us
    pallas_call x6, Pallas kernels, local(): call(meta, left, *(far(rights) if fetch else rights), *waits)  45.9 us
    ppermute x24, starting transfers between devices, local(): arriving.append(lax.ppermute(made[0], 'pipe', route) if route else made[0])  31.7 us
    ppermute x21, waiting for transfers between devices, exchange(): return lax.ppermute(block, axis, route)  24 us
    ppermute x21, starting transfers between devices, exchange(): return lax.ppermute(block, axis, route)  16.5 us
    pallas_call x12, Pallas kernels, add_call(): pl.pallas_call(add_kernel, grid=(rows // step,), in_specs=[pick, pick] +...  10 us
  transfers between devices with their start and end apart: 45, of which 16 were waited for; matrix products, arithmetic and copies ran while one was open for 5% of the time, Pallas kernels for 55%

profile of v9, /device:TPU:0, one launch (start us, length us, event | category | flops | bytes accessed | tf_op | source)
XLA Modules:
  0.0 438.8 jit_solution(13794264668171137430)
XLA Ops:
  4.2 10.9 %layer_forward.14 = (bf16[256,768]{1,0:T(8,128)(2,1)S(1)}, f32[6,256,256]{2,1,0:T(8,128)S(1)}, bf16[256,768]{1,0:T(8,128)(2,1)S(1)}, f32[256,128]{1,0:T(8,128)S(...) custom-call(s32[1]{0:T(128)} %constant.21.clone.1.refs_0_, ...), custom_call_target="tpu_custom_call", output_to_operand_aliasing={{19}: (4, {}), {20}: (5, {}), {25}: (10, {})} | custom-call | flops 4608000000 | bytes 4194304 | tf_op jit(solution)/shard_map/layer_forward/pallas_call | solution.py:712
  16.4 9.0 %layer_forward.15 = (bf16[256,768]{1,0:T(8,128)(2,1)S(1)}, f32[6,256,256]{2,1,0:T(8,128)S(1)}, bf16[256,768]{1,0:T(8,128)(2,1)S(1)}, f32[256,128]{1,0:T(8,128)S(...) custom-call(s32[1]{0:T(128)} %constant.19.clone.1.refs_0_, ...), custom_call_target="tpu_custom_call", output_to_operand_aliasing={{1}: (12, {}), {4}: (16, {}), {5}: (17, {}), {6}: (18, {}),... | custom-call | flops 4608000000 | bytes 4194304 | tf_op jit(solution)/shard_map/layer_forward/pallas_call | solution.py:712
  26.7 8.5 %layer_forward.16 = (bf16[256,768]{1,0:T(8,128)(2,1)S(1)}, f32[6,256,256]{2,1,0:T(8,128)S(1)}, bf16[256,768]{1,0:T(8,128)(2,1)S(1)}, f32[256,128]{1,0:T(8,128)S(...) custom-call(s32[1]{0:T(128)} %constant.23.clone.1.refs_0_, ...), custom_call_target="tpu_custom_call", output_to_operand_aliasing={{1}: (12, {}), {4}: (16, {}), {5}: (17, {}), {6}: (18, {}),... | custom-call | flops 4608000000 | bytes 4194304 | tf_op jit(solution)/shard_map/layer_forward/pallas_call | solution.py:712
  35.2 3.2 collective-permute-start.3
  38.5 9.2 %layer_forward.17 = (bf16[256,768]{1,0:T(8,128)(2,1)S(1)}, f32[6,256,256]{2,1,0:T(8,128)S(1)}, bf16[256,768]{1,0:T(8,128)(2,1)S(1)}, f32[256,128]{1,0:T(8,128)S(...) custom-call(s32[1]{0:T(128)} %constant.18.clone.1.refs_0_, ...), custom_call_target="tpu_custom_call", output_to_operand_aliasing={{1}: (12, {}), {4}: (16, {}), {5}: (17, {}), {6}: (18, {}),... | custom-call | flops 4608000000 | bytes 4194304 | tf_op jit(solution)/shard_map/layer_forward/pallas_call | solution.py:712
  49.5 8.4 %layer_forward.18 = (bf16[256,768]{1,0:T(8,128)(2,1)S(1)}, f32[6,256,256]{2,1,0:T(8,128)S(1)}, bf16[256,768]{1,0:T(8,128)(2,1)S(1)}, f32[256,128]{1,0:T(8,128)S(...) custom-call(s32[1]{0:T(128)} %constant.24.clone.1.refs_0_, ...), custom_call_target="tpu_custom_call", output_to_operand_aliasing={{1}: (12, {}), {4}: (16, {}), {5}: (17, {}), {6}: (18, {}),... | custom-call | flops 4608000000 | bytes 4194304 | tf_op jit(solution)/shard_map/layer_forward/pallas_call | solution.py:712
  60.0 9.0 %layer_forward.19 = (bf16[256,768]{1,0:T(8,128)(2,1)S(1)}, f32[6,256,256]{2,1,0:T(8,128)S(1)}, bf16[256,768]{1,0:T(8,128)(2,1)S(1)}, f32[256,128]{1,0:T(8,128)S(...) custom-call(s32[1]{0:T(128)} %constant.40.clone.1.refs_0_, ...), custom_call_target="tpu_custom_call", output_to_operand_aliasing={{1}: (12, {}), {4}: (16, {}), {5}: (17, {}), {6}: (18, {}),... | custom-call | flops 4608000000 | bytes 4194304 | tf_op jit(solution)/shard_map/layer_forward/pallas_call | solution.py:712
  69.0 2.2 collective-permute-start.4
  71.2 8.5 %layer_forward.20 = (bf16[256,768]{1,0:T(8,128)(2,1)S(1)}, f32[6,256,256]{2,1,0:T(8,128)S(1)}, bf16[256,768]{1,0:T(8,128)(2,1)S(1)}, f32[256,128]{1,0:T(8,128)S(...) custom-call(s32[1]{0:T(128)} %constant.25.clone.1.refs_0_, ...), custom_call_target="tpu_custom_call", output_to_operand_aliasing={{1}: (12, {}), {4}: (16, {}), {5}: (17, {}), {6}: (18, {}),... | custom-call | flops 4608000000 | bytes 4194304 | tf_op jit(solution)/shard_map/layer_forward/pallas_call | solution.py:712
  79.7 2.1 collective-permute-start.7
  81.8 9.2 %layer_forward.21 = (bf16[256,768]{1,0:T(8,128)(2,1)S(1)}, f32[6,256,256]{2,1,0:T(8,128)S(1)}, bf16[256,768]{1,0:T(8,128)(2,1)S(1)}, f32[256,128]{1,0:T(8,128)S(...) custom-call(s32[1]{0:T(128)} %constant.39.clone.1.refs_0_, ...), custom_call_target="tpu_custom_call", output_to_operand_aliasing={{1}: (12, {}), {4}: (16, {}), {5}: (17, {}), {6}: (18, {}),... | custom-call | flops 4608000000 | bytes 4194304 | tf_op jit(solution)/shard_map/layer_forward/pallas_call | solution.py:712
  95.5 5.0 %collective-permute-done.6.refs_2_ = bf16[256,768]{1,0:T(8,128)(2,1)S(1)} collective-permute-done((bf16[256,768]{1,0:T(8,128)(2,1)S(1)}, bf16[256,768]{1,0:T(8,128)(2,1)S(1)}, u32[]{:S(2)}, u32[]{:S(2)}) %collective-permute-start.6) | collective-permute-done | bytes 393248 | tf_op jit(solution)/shard_map/ppermute | solution.py:715
  100.5 6.9 %layer_forward.23 = (bf16[256,768]{1,0:T(8,128)(2,1)S(1)}, f32[6,256,256]{2,1,0:T(8,128)S(1)}, bf16[256,768]{1,0:T(8,128)(2,1)S(1)}, f32[256,128]{1,0:T(8,128)S(...) custom-call(s32[1]{0:T(128)} %constant.38.clone.1.refs_0_, ...), custom_call_target="tpu_custom_call", output_to_operand_aliasing={{1}: (12, {}), {4}: (16, {}), {5}: (17, {}), {6}: (18, {}),... | custom-call | flops 4608000000 | bytes 4194304 | tf_op jit(solution)/shard_map/layer_forward/pallas_call | solution.py:712
  109.7 8.7 %layer_forward.25 = (bf16[256,768]{1,0:T(8,128)(2,1)S(1)}, f32[6,256,256]{2,1,0:T(8,128)S(1)}, bf16[256,768]{1,0:T(8,128)(2,1)S(1)}, f32[256,128]{1,0:T(8,128)S(...) custom-call(s32[1]{0:T(128)} %constant.17.clone.1.refs_0_, ...), custom_call_target="tpu_custom_call", output_to_operand_aliasing={{1}: (12, {}), {4}: (16, {}), {5}: (17, {}), {6}: (18, {}),... | custom-call | flops 4608000000 | bytes 4194304 | tf_op jit(solution)/shard_map/layer_forward/pallas_call | solution.py:712
  120.0 10.9 %layer_forward.27 = (bf16[256,768]{1,0:T(8,128)(2,1)S(1)}, f32[6,256,256]{2,1,0:T(8,128)S(1)}, bf16[256,768]{1,0:T(8,128)(2,1)}, f32[256,128]{1,0:T(8,128)}, bf1...) custom-call(s32[1]{0:T(128)} %constant.29.clone.1.refs_0_, ...), custom_call_target="tpu_custom_call", output_to_operand_aliasing={{1}: (12, {}), {4}: (16, {}), {5}: (17, {}), {6}: (18, {}),... | custom-call | flops 4608000000 | bytes 4194304 | tf_op jit(solution)/shard_map/layer_forward/pallas_call | solution.py:712
  130.9 3.0 layer_backward.14
  134.6 8.7 %layer_backward.15 = (bf16[256,768]{1,0:T(8,128)(2,1)S(1)}, f32[6,256,256]{2,1,0:T(8,128)S(1)}, f32[8,768]{1,0:T(8,128)S(1)}, bf16[2048,768]{1,0:T(8,128)(2,1)},...) custom-call(s32[1]{0:T(128)} %constant.19.clone.1.refs_0_, ...), custom_call_target="tpu_custom_call", output_to_operand_aliasing={{7}: (3, {}), {8}: (4, {}), {9}: (5, {}), {10}: (6, {}), {1... | custom-call | flops 5120000000 | bytes 4194304 | tf_op jit(solution)/shard_map/layer_backward/pallas_call | solution.py:720
  144.0 2.3 layer_backward.16
  147.0 9.1 %layer_backward.17 = (bf16[256,768]{1,0:T(8,128)(2,1)S(1)}, f32[6,256,256]{2,1,0:T(8,128)S(1)}, f32[8,768]{1,0:T(8,128)S(1)}, bf16[2048,768]{1,0:T(8,128)(2,1)},...) custom-call(s32[1]{0:T(128)} %constant.18.clone.1.refs_0_, ...), custom_call_target="tpu_custom_call", output_to_operand_aliasing={{7}: (3, {}), {8}: (4, {}), {9}: (5, {}), {10}: (6, {}), {1... | custom-call | flops 5120000000 | bytes 4194304 | tf_op jit(solution)/shard_map/layer_backward/pallas_call | solution.py:720
  156.8 2.3 layer_backward.18
  160.5 10.1 %layer_backward.19 = (bf16[256,768]{1,0:T(8,128)(2,1)S(1)}, f32[6,256,256]{2,1,0:T(8,128)S(1)}, f32[8,768]{1,0:T(8,128)S(1)}, bf16[2048,768]{1,0:T(8,128)(2,1)},...) custom-call(s32[1]{0:T(128)} %constant.40.clone.1.refs_0_, ...), custom_call_target="tpu_custom_call", output_to_operand_aliasing={{7}: (3, {}), {8}: (4, {}), {9}: (5, {}), {10}: (6, {}), {1... | custom-call | flops 5120000000 | bytes 4194304 | tf_op jit(solution)/shard_map/layer_backward/pallas_call | solution.py:720
  171.9 41.2 %collective-permute-done.17.refs_2_ = bf16[256,768]{1,0:T(8,128)(2,1)S(1)} collective-permute-done((bf16[256,768]{1,0:T(8,128)(2,1)S(1)}, bf16[256,768]{1,0:T(8,128)(2,1)S(1)}, u32[]{:S(2)}, u32[]{:S(2)}) %collective-permute-start.17) | collective-permute-done | bytes 393248 | tf_op jit(solution)/shard_map/ppermute | solution.py:725
  213.1 10.8 %layer_backward.20 = (bf16[256,768]{1,0:T(8,128)(2,1)S(1)}, f32[6,256,256]{2,1,0:T(8,128)S(1)}, f32[8,768]{1,0:T(8,128)S(1)}, bf16[2048,768]{1,0:T(8,128)(2,1)},...) custom-call(s32[1]{0:T(128)} %constant.25.clone.1.refs_0_, ...), custom_call_target="tpu_custom_call", output_to_operand_aliasing={{7}: (3, {}), {8}: (4, {}), {9}: (5, {}), {10}: (6, {}), {1... | custom-call | flops 5120000000 | bytes 4194304 | tf_op jit(solution)/shard_map/layer_backward/pallas_call | solution.py:720
  227.1 11.4 %layer_backward.21 = (bf16[256,768]{1,0:T(8,128)(2,1)S(1)}, f32[6,256,256]{2,1,0:T(8,128)S(1)}, f32[8,768]{1,0:T(8,128)S(1)}, bf16[2048,768]{1,0:T(8,128)(2,1)},...) custom-call(s32[1]{0:T(128)} %constant.39.clone.1.refs_0_, ...), custom_call_target="tpu_custom_call", output_to_operand_aliasing={{7}: (3, {}), {8}: (4, {}), {9}: (5, {}), {10}: (6, {}), {1... | custom-call | flops 5120000000 | bytes 4194304 | tf_op jit(solution)/shard_map/layer_backward/pallas_call | solution.py:720
  240.0 10.9 %layer_backward.22 = (bf16[256,768]{1,0:T(8,128)(2,1)S(1)}, f32[6,256,256]{2,1,0:T(8,128)S(1)}, f32[8,768]{1,0:T(8,128)S(1)}, bf16[2048,768]{1,0:T(8,128)(2,1)},...) custom-call(s32[1]{0:T(128)} %constant.26.clone.1.refs_0_, ...), custom_call_target="tpu_custom_call", output_to_operand_aliasing={{7}: (3, {}), {8}: (4, {}), {9}: (5, {}), {10}: (6, {}), {1... | custom-call | flops 5120000000 | bytes 4194304 | tf_op jit(solution)/shard_map/layer_backward/pallas_call | solution.py:720
  253.4 11.6 %layer_backward.23 = (bf16[256,768]{1,0:T(8,128)(2,1)S(1)}, f32[6,256,256]{2,1,0:T(8,128)S(1)}, f32[8,768]{1,0:T(8,128)S(1)}, bf16[2048,768]{1,0:T(8,128)(2,1)},...) custom-call(s32[1]{0:T(128)} %constant.38.clone.1.refs_0_, ...), custom_call_target="tpu_custom_call", output_to_operand_aliasing={{7}: (3, {}), {8}: (4, {}), {9}: (5, {}), {10}: (6, {}), {1... | custom-call | flops 5120000000 | bytes 4194304 | tf_op jit(solution)/shard_map/layer_backward/pallas_call | solution.py:720
  266.3 10.9 %layer_backward.24 = (bf16[256,768]{1,0:T(8,128)(2,1)S(1)}, f32[6,256,256]{2,1,0:T(8,128)S(1)}, f32[8,768]{1,0:T(8,128)S(1)}, bf16[2048,768]{1,0:T(8,128)(2,1)},...) custom-call(s32[1]{0:T(128)} %constant.27.clone.1.refs_0_, ...), custom_call_target="tpu_custom_call", output_to_operand_aliasing={{7}: (3, {}), {8}: (4, {}), {9}: (5, {}), {10}: (6, {}), {1... | custom-call | flops 5120000000 | bytes 4194304 | tf_op jit(solution)/shard_map/layer_backward/pallas_call | solution.py:720
  279.8 11.4 %layer_backward.25 = (bf16[256,768]{1,0:T(8,128)(2,1)S(1)}, f32[6,256,256]{2,1,0:T(8,128)S(1)}, f32[8,768]{1,0:T(8,128)S(1)}, bf16[2048,768]{1,0:T(8,128)(2,1)},...) custom-call(s32[1]{0:T(128)} %constant.17.clone.1.refs_0_, ...), custom_call_target="tpu_custom_call", output_to_operand_aliasing={{7}: (3, {}), {8}: (4, {}), {9}: (5, {}), {10}: (6, {}), {1... | custom-call | flops 5120000000 | bytes 4194304 | tf_op jit(solution)/shard_map/layer_backward/pallas_call | solution.py:720
  292.5 11.6 %layer_backward.26 = (bf16[256,768]{1,0:T(8,128)(2,1)}, f32[6,256,256]{2,1,0:T(8,128)S(1)}, f32[8,768]{1,0:T(8,128)S(1)}, bf16[2048,768]{1,0:T(8,128)(2,1)}, bf1...) custom-call(s32[1]{0:T(128)} %constant.28.clone.1.refs_0_, ...), custom_call_target="tpu_custom_call", output_to_operand_aliasing={{7}: (3, {}), {8}: (4, {}), {9}: (5, {}), {10}: (6, {}), {1... | custom-call | flops 5120000000 | bytes 4194304 | tf_op jit(solution)/shard_map/layer_backward/pallas_call | solution.py:720
  304.8 12.3 %layer_backward.27 = (bf16[256,768]{1,0:T(8,128)(2,1)}, f32[6,256,256]{2,1,0:T(8,128)S(1)}, f32[8,768]{1,0:T(8,128)S(1)}, bf16[2048,768]{1,0:T(8,128)(2,1)}, bf1...) custom-call(s32[1]{0:T(128)} %constant.29.clone.1.refs_0_, ...), custom_call_target="tpu_custom_call", output_to_operand_aliasing={{7}: (3, {}), {8}: (4, {}), {9}: (5, {}), {10}: (6, {}), {1... | custom-call | flops 5120000000 | bytes 4194304 | tf_op jit(solution)/shard_map/layer_backward/pallas_call | solution.py:720
  317.1 8.8 %weight_grad.6 = (bf16[2,384,768]{2,1,0:T(8,128)(2,1)}, bf16[2,384,768]{2,1,0:T(8,128)(2,1)}, bf16[2048,768]{1,0:T(8,128)(2,1)S(1)}) custom-call(s32[18]{0:T(128)S(1)} %pad_add_fusion.refs_1_.meta_ref, bf16[12,2048,256]{2,1,0:T(8,128)(2,1)S(1)} %get-tuple-element.1298.left, bf16[2048,768]{1,0:T(8,128)(2,1)} %get-tuple-element.1299.refs_0_), custom_call_target="tpu_custom_call" | custom-call | flops 4831838208 | bytes 15728640 | tf_op jit(solution)/shard_map/weight_grad/pallas_call | solution.py:747
  326.1 6.8 %weight_grad.7 = (bf16[2,384,768]{2,1,0:T(8,128)(2,1)}, bf16[2,384,768]{2,1,0:T(8,128)(2,1)}) custom-call(s32[18]{0:T(128)S(1)} %pad_add_fusion.refs_1_.meta_ref, bf16[12,2048,256]{2,1,0:T(8,128)(2,1)S(1)} %get-tuple-element.1298.left, bf16[2048,768]{1,0:T(8,128)(2,1)S(1)} %get-tuple-element.1300.refs_0_), custom_call_target="tpu_custom_call" | custom-call | flops 4831838208 | bytes 15728640 | tf_op jit(solution)/shard_map/weight_grad/pallas_call | solution.py:747
  335.2 8.3 %weight_grad.8 = (bf16[2,384,768]{2,1,0:T(8,128)(2,1)}, bf16[2,384,768]{2,1,0:T(8,128)(2,1)}) custom-call(s32[18]{0:T(128)S(1)} %pad_add_fusion.refs_1_.meta_ref, bf16[12,2048,256]{2,1,0:T(8,128)(2,1)S(1)} %bitcast.60, bf16[2048,768]{1,0:T(8,128)(2,1)S(1)} %copy-done.1, bf16[2048,768]{1,0:T(8,128)(2,1)S(1)} %copy-done, bf16[384,768]{1,0:T(8,128)(2,1)S(1)} %add_parts.13.refs_2_), custom_call_target="tpu_custom_call" | custom-call | flops 4831838208 | bytes 15728640 | tf_op jit(solution)/shard_map/weight_grad/pallas_call | solution.py:747
  346.8 3.2 collective-permute-done.25.refs_1_
  353.1 8.3 %weight_grad.9 = (bf16[2,384,768]{2,1,0:T(8,128)(2,1)}, bf16[2,384,768]{2,1,0:T(8,128)(2,1)}) custom-call(s32[18]{0:T(128)S(1)} %pad_add_fusion.refs_1_.meta_ref, bf16[12,2048,256]{2,1,0:T(8,128)(2,1)S(1)} %bitcast.60, bf16[2048,768]{1,0:T(8,128)(2,1)S(1)} %copy-done.1, bf16[2048,768]{1,0:T(8,128)(2,1)S(1)} %copy-done, bf16[384,768]{1,0:T(8,128)(2,1)S(1)} %add_parts.12.refs_2_), custom_call_target="tpu_custom_call" | custom-call | flops 4831838208 | bytes 15728640 | tf_op jit(solution)/shard_map/weight_grad/pallas_call | solution.py:747
  361.8 3.0 collective-permute-done.29.refs_2_
  367.8 6.8 %weight_grad.11 = (bf16[2,384,768]{2,1,0:T(8,128)(2,1)}, bf16[2,384,768]{2,1,0:T(8,128)(2,1)}) custom-call(s32[18]{0:T(128)S(1)} %pad_add_fusion.refs_1_.meta_ref, bf16[12,2048,256]{2,1,0:T(8,128)(2,1)S(1)} %bitcast.62, bf16[2048,768]{1,0:T(8,128)(2,1)S(1)} %copy-done.2, bf16[384,768]{1,0:T(8,128)(2,1)S(1)} %add_parts.14.refs_1_), custom_call_target="tpu_custom_call" | custom-call | flops 4831838208 | bytes 15728640 | tf_op jit(solution)/shard_map/weight_grad/pallas_call | solution.py:747
  375.9 2.4 collective-permute-done.31.refs_2_
  381.7 6.8 %weight_grad.10 = (bf16[2,384,768]{2,1,0:T(8,128)(2,1)}, bf16[2,384,768]{2,1,0:T(8,128)(2,1)}) custom-call(s32[18]{0:T(128)S(1)} %pad_add_fusion.refs_1_.meta_ref, bf16[12,2048,256]{2,1,0:T(8,128)(2,1)S(1)} %bitcast.62, bf16[2048,768]{1,0:T(8,128)(2,1)S(1)} %copy-done.2, bf16[384,768]{1,0:T(8,128)(2,1)} %add_parts.15.refs_1_), custom_call_target="tpu_custom_call" | custom-call | flops 4831838208 | bytes 15728640 | tf_op jit(solution)/shard_map/weight_grad/pallas_call | solution.py:747
  389.6 2.3 collective-permute-done.35.refs_2_
  397.4 3.1 copy.585
  401.7 4.0 collective-permute-done.41.refs_2_
  415.0 3.3 collective-permute-done.42.refs_2_
  419.5 3.1 collective-permute-done.43.refs_1_
  424.1 2.8 fusion.6
  426.9 2.2 copy.584
  429.1 3.6 fusion.2
  432.7 2.8 copy.583
  (195 shorter events, 75.5 us)
Async XLA Ops:
  15.1 11.6 %collective-permute-start.1 = (bf16[256,768]{1,0:T(8,128)(2,1)S(1)}, bf16[256,768]{1,0:T(8,128)(2,1)S(1)}, u32[]{:S(2)}, u32[]{:S(2)}) collective-permute-start(bf16[256,768]{1,0:T(8,128)(2,1)S(1)} %get-tuple-element.687.refs_13_), channel_id=1, source_target_pairs={{0,8},{1,9},{2,10},{3,11},{4,12},{5,13},{6,14},{7,15}} | collective-permute-start | bytes 1179656 | tf_op jit(solution)/shard_map/ppermute | solution.py:715
  25.4 13.1 %collective-permute-start = (bf16[256,768]{1,0:T(8,128)(2,1)S(1)}, bf16[256,768]{1,0:T(8,128)(2,1)S(1)}, u32[]{:S(2)}, u32[]{:S(2)}) collective-permute-start(bf16[256,768]{1,0:T(8,128)(2,1)S(1)} %get-tuple-element.704.refs_13_), channel_id=1, source_target_pairs={{0,8},{1,9},{2,10},{3,11},{4,12},{5,13},{6,14},{7,15}} | collective-permute-start | bytes 1179656 | tf_op jit(solution)/shard_map/ppermute | solution.py:715
  35.2 14.3 %collective-permute-start.3 = (bf16[256,768]{1,0:T(8,128)(2,1)S(1)}, bf16[256,768]{1,0:T(8,128)(2,1)S(1)}, u32[]{:S(2)}, u32[]{:S(2)}) collective-permute-start(bf16[256,768]{1,0:T(8,128)(2,1)S(1)} %get-tuple-element.741.refs_13_), channel_id=1, source_target_pairs={{0,8},{8,16},{1,9},{9,17},{2,10},{10,18},{3,11},{11,19},{4,12},{12... | collective-permute-start | bytes 1179656 | tf_op jit(solution)/shard_map/ppermute | solution.py:715
  47.6 12.3 %collective-permute-start.2 = (bf16[256,768]{1,0:T(8,128)(2,1)S(1)}, bf16[256,768]{1,0:T(8,128)(2,1)S(1)}, u32[]{:S(2)}, u32[]{:S(2)}) collective-permute-start(bf16[256,768]{1,0:T(8,128)(2,1)S(1)} %get-tuple-element.758.refs_13_), channel_id=1, source_target_pairs={{0,8},{8,16},{1,9},{9,17},{2,10},{10,18},{3,11},{11,19},{4,12},{12... | collective-permute-start | bytes 1179656 | tf_op jit(solution)/shard_map/ppermute | solution.py:715
  58.0 13.2 %collective-permute-start.5 = (bf16[256,768]{1,0:T(8,128)(2,1)S(1)}, bf16[256,768]{1,0:T(8,128)(2,1)S(1)}, u32[]{:S(2)}, u32[]{:S(2)}) collective-permute-start(bf16[256,768]{1,0:T(8,128)(2,1)S(1)} %get-tuple-element.795.refs_13_), channel_id=1, source_target_pairs={{0,8},{8,16},{16,24},{1,9},{9,17},{17,25},{2,10},{10,18},{18,26},{... | collective-permute-start | bytes 1179656 | tf_op jit(solution)/shard_map/ppermute | solution.py:715
  69.0 12.8 %collective-permute-start.4 = (bf16[256,768]{1,0:T(8,128)(2,1)S(1)}, bf16[256,768]{1,0:T(8,128)(2,1)S(1)}, u32[]{:S(2)}, u32[]{:S(2)}) collective-permute-start(bf16[256,768]{1,0:T(8,128)(2,1)S(1)} %get-tuple-element.812.refs_13_), channel_id=1, source_target_pairs={{0,8},{8,16},{16,24},{1,9},{9,17},{17,25},{2,10},{10,18},{18,26},{... | collective-permute-start | bytes 1179656 | tf_op jit(solution)/shard_map/ppermute | solution.py:715
  79.7 13.3 %collective-permute-start.7 = (bf16[256,768]{1,0:T(8,128)(2,1)S(1)}, bf16[256,768]{1,0:T(8,128)(2,1)S(1)}, u32[]{:S(2)}, u32[]{:S(2)}) collective-permute-start(bf16[256,768]{1,0:T(8,128)(2,1)S(1)} %get-tuple-element.849.refs_13_), channel_id=1, source_target_pairs={{0,8},{8,16},{16,24},{1,9},{9,17},{17,25},{2,10},{10,18},{18,26},{... | collective-permute-start | bytes 1179656 | tf_op jit(solution)/shard_map/ppermute | solution.py:715
  91.0 9.5 %collective-permute-start.6 = (bf16[256,768]{1,0:T(8,128)(2,1)S(1)}, bf16[256,768]{1,0:T(8,128)(2,1)S(1)}, u32[]{:S(2)}, u32[]{:S(2)}) collective-permute-start(bf16[256,768]{1,0:T(8,128)(2,1)S(1)} %get-tuple-element.866.refs_13_), channel_id=1, source_target_pairs={{0,8},{8,16},{16,24},{1,9},{9,17},{17,25},{2,10},{10,18},{18,26},{... | collective-permute-start | bytes 1179656 | tf_op jit(solution)/shard_map/ppermute | solution.py:715
  94.8 13.2 %collective-permute-start.9 = (bf16[256,768]{1,0:T(8,128)(2,1)S(1)}, bf16[256,768]{1,0:T(8,128)(2,1)S(1)}, u32[]{:S(2)}, u32[]{:S(2)}) collective-permute-start(bf16[256,768]{1,0:T(8,128)(2,1)S(1)} %get-tuple-element.903.refs_13_), channel_id=1, source_target_pairs={{8,16},{16,24},{9,17},{17,25},{10,18},{18,26},{11,19},{19,27},{12,... | collective-permute-start | bytes 1179656 | tf_op jit(solution)/shard_map/ppermute | solution.py:715
  107.4 2.3 collective-permute-start.8
  109.0 10.1 %collective-permute-start.11 = (bf16[256,768]{1,0:T(8,128)(2,1)S(1)}, bf16[256,768]{1,0:T(8,128)(2,1)S(1)}, u32[]{:S(2)}, u32[]{:S(2)}) collective-permute-start(bf16[256,768]{1,0:T(8,128)(2,1)S(1)} %get-tuple-element.957.refs_13_), channel_id=1, source_target_pairs={{16,24},{17,25},{18,26},{19,27},{20,28},{21,29},{22,30},{23,31}} | collective-permute-start | bytes 1179656 | tf_op jit(solution)/shard_map/ppermute | solution.py:715
  118.4 1.6 collective-permute-start.10
  133.9 10.1 %collective-permute-start.13 = (bf16[256,768]{1,0:T(8,128)(2,1)S(1)}, bf16[256,768]{1,0:T(8,128)(2,1)S(1)}, u32[]{:S(2)}, u32[]{:S(2)}) collective-permute-start(bf16[256,768]{1,0:T(8,128)(2,1)S(1)} %get-tuple-element.1069), channel_id=1, source_target_pairs={{24,16},{25,17},{26,18},{27,19},{28,20},{29,21},{30,22},{31,23}} | collective-permute-start | bytes 1179656 | tf_op jit(solution)/shard_map/ppermute | solution.py:725
  143.3 3.7 collective-permute-start.12
  146.3 10.5 %collective-permute-start.15 = (bf16[256,768]{1,0:T(8,128)(2,1)S(1)}, bf16[256,768]{1,0:T(8,128)(2,1)S(1)}, u32[]{:S(2)}, u32[]{:S(2)}) collective-permute-start(bf16[256,768]{1,0:T(8,128)(2,1)S(1)} %get-tuple-element.1107), channel_id=1, source_target_pairs={{16,8},{24,16},{17,9},{25,17},{18,10},{26,18},{19,11},{27,19},{20,... | collective-permute-start | bytes 1179656 | tf_op jit(solution)/shard_map/ppermute | solution.py:725
  156.1 4.3 collective-permute-start.14
  159.2 53.9 %collective-permute-start.17 = (bf16[256,768]{1,0:T(8,128)(2,1)S(1)}, bf16[256,768]{1,0:T(8,128)(2,1)S(1)}, u32[]{:S(2)}, u32[]{:S(2)}) collective-permute-start(bf16[256,768]{1,0:T(8,128)(2,1)S(1)} %get-tuple-element.1145), channel_id=1, source_target_pairs={{8,0},{16,8},{24,16},{9,1},{17,9},{25,17},{10,2},{18,10},{26,18},{... | collective-permute-start | bytes 1179656 | tf_op jit(solution)/shard_map/ppermute | solution.py:725
  170.6 56.5 %collective-permute-start.16 = (bf16[256,768]{1,0:T(8,128)(2,1)S(1)}, bf16[256,768]{1,0:T(8,128)(2,1)S(1)}, u32[]{:S(2)}, u32[]{:S(2)}) collective-permute-start(bf16[256,768]{1,0:T(8,128)(2,1)S(1)} %get-tuple-element.1144), channel_id=1, source_target_pairs={{8,0},{16,8},{24,16},{9,1},{17,9},{25,17},{10,2},{18,10},{26,18},{... | collective-permute-start | bytes 1179656 | tf_op jit(solution)/shard_map/ppermute | solution.py:725
  223.9 16.1 %collective-permute-start.19 = (bf16[256,768]{1,0:T(8,128)(2,1)S(1)}, bf16[256,768]{1,0:T(8,128)(2,1)S(1)}, u32[]{:S(2)}, u32[]{:S(2)}) collective-permute-start(bf16[256,768]{1,0:T(8,128)(2,1)S(1)} %get-tuple-element.1183), channel_id=1, source_target_pairs={{8,0},{16,8},{24,16},{9,1},{17,9},{25,17},{10,2},{18,10},{26,18},{... | collective-permute-start | bytes 1179656 | tf_op jit(solution)/shard_map/ppermute | solution.py:725
  238.5 14.9 %collective-permute-start.18 = (bf16[256,768]{1,0:T(8,128)(2,1)S(1)}, bf16[256,768]{1,0:T(8,128)(2,1)S(1)}, u32[]{:S(2)}, u32[]{:S(2)}) collective-permute-start(bf16[256,768]{1,0:T(8,128)(2,1)S(1)} %get-tuple-element.1182), channel_id=1, source_target_pairs={{8,0},{16,8},{24,16},{9,1},{17,9},{25,17},{10,2},{18,10},{26,18},{... | collective-permute-start | bytes 1179656 | tf_op jit(solution)/shard_map/ppermute | solution.py:725
  251.0 15.3 %collective-permute-start.21 = (bf16[256,768]{1,0:T(8,128)(2,1)S(1)}, bf16[256,768]{1,0:T(8,128)(2,1)S(1)}, u32[]{:S(2)}, u32[]{:S(2)}) collective-permute-start(bf16[256,768]{1,0:T(8,128)(2,1)S(1)} %get-tuple-element.1221), channel_id=1, source_target_pairs={{8,0},{16,8},{9,1},{17,9},{10,2},{18,10},{11,3},{19,11},{12,4},{20... | collective-permute-start | bytes 1179656 | tf_op jit(solution)/shard_map/ppermute | solution.py:725
  265.0 14.8 %collective-permute-start.20 = (bf16[256,768]{1,0:T(8,128)(2,1)S(1)}, bf16[256,768]{1,0:T(8,128)(2,1)S(1)}, u32[]{:S(2)}, u32[]{:S(2)}) collective-permute-start(bf16[256,768]{1,0:T(8,128)(2,1)S(1)} %get-tuple-element.1220), channel_id=1, source_target_pairs={{8,0},{16,8},{9,1},{17,9},{10,2},{18,10},{11,3},{19,11},{12,4},{20... | collective-permute-start | bytes 1179656 | tf_op jit(solution)/shard_map/ppermute | solution.py:725
  277.2 15.3 %collective-permute-start.23 = (bf16[256,768]{1,0:T(8,128)(2,1)S(1)}, bf16[256,768]{1,0:T(8,128)(2,1)S(1)}, u32[]{:S(2)}, u32[]{:S(2)}) collective-permute-start(bf16[256,768]{1,0:T(8,128)(2,1)S(1)} %get-tuple-element.1259), channel_id=1, source_target_pairs={{8,0},{9,1},{10,2},{11,3},{12,4},{13,5},{14,6},{15,7}} | collective-permute-start | bytes 1179656 | tf_op jit(solution)/shard_map/ppermute | solution.py:725
  291.2 13.6 %collective-permute-start.22 = (bf16[256,768]{1,0:T(8,128)(2,1)S(1)}, bf16[256,768]{1,0:T(8,128)(2,1)S(1)}, u32[]{:S(2)}, u32[]{:S(2)}) collective-permute-start(bf16[256,768]{1,0:T(8,128)(2,1)S(1)} %get-tuple-element.1258), channel_id=1, source_target_pairs={{8,0},{9,1},{10,2},{11,3},{12,4},{13,5},{14,6},{15,7}} | collective-permute-start | bytes 1179656 | tf_op jit(solution)/shard_map/ppermute | solution.py:725
  317.1 18.1 %slice-start = ((s8[12582912]{0:T(1024)(128)(4,1)}), s8[4194304]{0:T(1024)(128)(4,1)S(1)}, s32[]{:S(2)}) async-start(s8[12582912]{0:T(1024)(128)(4,1)} %bitcast.59), calls=%async_computation | async-start | bytes 8388608
  317.1 18.0 %slice-start.1 = ((s8[12582912]{0:T(1024)(128)(4,1)}), s8[4194304]{0:T(1024)(128)(4,1)S(1)}, s32[]{:S(2)}) async-start(s8[12582912]{0:T(1024)(128)(4,1)} %bitcast.59), calls=%async_computation.1 | async-start | bytes 8388608
  325.9 7.4 %collective-permute-start.27 = (bf16[2,384,768]{2,1,0:T(8,128)(2,1)}, bf16[2,384,768]{2,1,0:T(8,128)(2,1)S(1)}, u32[]{:S(2)}, u32[]{:S(2)}) collective-permute-start(bf16[2,384,768]{2,1,0:T(8,128)(2,1)} %get-tuple-element.1307), channel_id=1, source_target_pairs={{0,2},{2,0},{4,6},{6,4},{1,3},{3,1},{5,7},{7,5},{8,10},{10,8},{12,... | collective-permute-start | bytes 3538952 | tf_op jit(solution)/shard_map/ppermute | solution.py:631
  332.8 17.1 %collective-permute-start.26 = (bf16[2,384,768]{2,1,0:T(8,128)(2,1)}, bf16[2,384,768]{2,1,0:T(8,128)(2,1)S(1)}, u32[]{:S(2)}, u32[]{:S(2)}) collective-permute-start(bf16[2,384,768]{2,1,0:T(8,128)(2,1)} %get-tuple-element.1302), channel_id=1, source_target_pairs={{0,2},{2,0},{4,6},{6,4},{1,3},{3,1},{5,7},{7,5},{8,10},{10,8},{12,... | collective-permute-start | bytes 3538952 | tf_op jit(solution)/shard_map/ppermute | solution.py:631
  333.7 16.5 %collective-permute-start.28 = (bf16[384,768]{1,0:T(8,128)(2,1)S(1)}, bf16[384,768]{1,0:T(8,128)(2,1)S(1)}, u32[]{:S(2)}, u32[]{:S(2)}) collective-permute-start(bf16[384,768]{1,0:T(8,128)(2,1)S(1)} %add_parts.13.refs_2_), channel_id=1, source_target_pairs={{0,4},{2,6},{4,0},{6,2},{1,5},{3,7},{5,1},{7,3},{8,12},{10,14},{12... | collective-permute-start | bytes 1769480 | tf_op jit(solution)/shard_map/ppermute | solution.py:631
  343.5 18.0 %collective-permute-start.30 = (bf16[2,384,768]{2,1,0:T(8,128)(2,1)}, bf16[2,384,768]{2,1,0:T(8,128)(2,1)S(1)}, u32[]{:S(2)}, u32[]{:S(2)}) collective-permute-start(bf16[2,384,768]{2,1,0:T(8,128)(2,1)} %get-tuple-element.1313), channel_id=1, source_target_pairs={{0,2},{2,0},{4,6},{6,4},{1,3},{3,1},{5,7},{7,5},{8,10},{10,8},{12,... | collective-permute-start | bytes 3538952 | tf_op jit(solution)/shard_map/ppermute | solution.py:631
  343.6 2.5 collective-permute-start.24
  346.1 3.8 collective-permute-start.25
  350.2 14.5 %collective-permute-start.29 = (bf16[384,768]{1,0:T(8,128)(2,1)S(1)}, bf16[384,768]{1,0:T(8,128)(2,1)S(1)}, u32[]{:S(2)}, u32[]{:S(2)}) collective-permute-start(bf16[384,768]{1,0:T(8,128)(2,1)S(1)} %add_parts.12.refs_2_), channel_id=1, source_target_pairs={{0,4},{2,6},{4,0},{6,2},{1,5},{3,7},{5,1},{7,3},{8,12},{10,14},{12... | collective-permute-start | bytes 1769480 | tf_op jit(solution)/shard_map/ppermute | solution.py:631
  351.3 16.5 %slice-start.3 = ((s8[12582912]{0:T(1024)(128)(4,1)}), s8[4194304]{0:T(1024)(128)(4,1)S(1)}, s32[]{:S(2)}) async-start(s8[12582912]{0:T(1024)(128)(4,1)} %bitcast.61), calls=%async_computation.3 | async-start | bytes 8388608
  351.6 14.9 %collective-permute-start.37 = (bf16[384,768]{1,0:T(8,128)(2,1)S(1)}, bf16[384,768]{1,0:T(8,128)(2,1)S(1)}, u32[]{:S(2)}, u32[]{:S(2)}) collective-permute-start(bf16[384,768]{1,0:T(8,128)(2,1)S(1)} %add_parts.20), channel_id=1, source_target_pairs={{0,1},{1,0},{2,3},{3,2},{4,5},{5,4},{6,7},{7,6},{8,9},{9,8},{10,11... | collective-permute-start | bytes 1769480 | tf_op jit(solution)/shard_map/ppermute | solution.py:631
  361.5 13.3 %collective-permute-start.32 = (bf16[2,384,768]{2,1,0:T(8,128)(2,1)}, bf16[2,384,768]{2,1,0:T(8,128)(2,1)S(1)}, u32[]{:S(2)}, u32[]{:S(2)}) collective-permute-start(bf16[2,384,768]{2,1,0:T(8,128)(2,1)} %get-tuple-element.1316), channel_id=1, source_target_pairs={{0,2},{2,0},{4,6},{6,4},{1,3},{3,1},{5,7},{7,5},{8,10},{10,8},{12,... | collective-permute-start | bytes 3538952 | tf_op jit(solution)/shard_map/ppermute | solution.py:631
  364.7 13.6 %collective-permute-start.31 = (bf16[384,768]{1,0:T(8,128)(2,1)S(1)}, bf16[384,768]{1,0:T(8,128)(2,1)S(1)}, u32[]{:S(2)}, u32[]{:S(2)}) collective-permute-start(bf16[384,768]{1,0:T(8,128)(2,1)S(1)} %add_parts.14.refs_1_), channel_id=1, source_target_pairs={{0,4},{2,6},{4,0},{6,2},{1,5},{3,7},{5,1},{7,3},{8,12},{10,14},{12... | collective-permute-start | bytes 1769480 | tf_op jit(solution)/shard_map/ppermute | solution.py:631
  366.5 14.2 %collective-permute-start.38 = (bf16[384,768]{1,0:T(8,128)(2,1)S(1)}, bf16[384,768]{1,0:T(8,128)(2,1)S(1)}, u32[]{:S(2)}, u32[]{:S(2)}) collective-permute-start(bf16[384,768]{1,0:T(8,128)(2,1)S(1)} %add_parts.21), channel_id=1, source_target_pairs={{0,1},{1,0},{2,3},{3,2},{4,5},{5,4},{6,7},{7,6},{8,9},{9,8},{10,11... | collective-permute-start | bytes 1769480 | tf_op jit(solution)/shard_map/ppermute | solution.py:631
  374.7 14.0 %collective-permute-start.36 = (bf16[2,384,768]{2,1,0:T(8,128)(2,1)}, bf16[2,384,768]{2,1,0:T(8,128)(2,1)S(1)}, u32[]{:S(2)}, u32[]{:S(2)}) collective-permute-start(bf16[2,384,768]{2,1,0:T(8,128)(2,1)} %get-tuple-element.1322), channel_id=1, source_target_pairs={{0,2},{2,0},{4,6},{6,4},{1,3},{3,1},{5,7},{7,5},{8,10},{10,8},{12,... | collective-permute-start | bytes 3538952 | tf_op jit(solution)/shard_map/ppermute | solution.py:631
  378.3 13.6 %collective-permute-start.35 = (bf16[384,768]{1,0:T(8,128)(2,1)}, bf16[384,768]{1,0:T(8,128)(2,1)}, u32[]{:S(2)}, u32[]{:S(2)}) collective-permute-start(bf16[384,768]{1,0:T(8,128)(2,1)} %add_parts.15.refs_1_), channel_id=1, source_target_pairs={{0,4},{2,6},{4,0},{6,2},{1,5},{3,7},{5,1},{7,3},{8,12},{10,14},{12... | collective-permute-start | bytes 1769480 | tf_op jit(solution)/shard_map/ppermute | solution.py:631
  380.8 14.2 %collective-permute-start.39 = (bf16[384,768]{1,0:T(8,128)(2,1)}, bf16[384,768]{1,0:T(8,128)(2,1)}, u32[]{:S(2)}, u32[]{:S(2)}) collective-permute-start(bf16[384,768]{1,0:T(8,128)(2,1)} %add_parts.19), channel_id=1, source_target_pairs={{0,1},{1,0},{2,3},{3,2},{4,5},{5,4},{6,7},{7,6},{8,9},{9,8},{10,11... | collective-permute-start | bytes 1769480 | tf_op jit(solution)/shard_map/ppermute | solution.py:631
  388.6 11.9 %collective-permute-start.33 = (bf16[2,384,768]{2,1,0:T(8,128)(2,1)}, bf16[2,384,768]{2,1,0:T(8,128)(2,1)}, u32[]{:S(2)}, u32[]{:S(2)}) collective-permute-start(bf16[2,384,768]{2,1,0:T(8,128)(2,1)} %get-tuple-element.1319), channel_id=1, source_target_pairs={{0,2},{2,0},{4,6},{6,4},{1,3},{3,1},{5,7},{7,5},{8,10},{10,8},{12,... | collective-permute-start | bytes 3538952 | tf_op jit(solution)/shard_map/ppermute | solution.py:631
  391.9 13.8 %collective-permute-start.41 = (bf16[384,768]{1,0:T(8,128)(2,1)}, bf16[384,768]{1,0:T(8,128)(2,1)}, u32[]{:S(2)}, u32[]{:S(2)}) collective-permute-start(bf16[384,768]{1,0:T(8,128)(2,1)} %add_parts.17), channel_id=1, source_target_pairs={{0,4},{2,6},{4,0},{6,2},{1,5},{3,7},{5,1},{7,3},{8,12},{10,14},{12... | collective-permute-start | bytes 1769480 | tf_op jit(solution)/shard_map/ppermute | solution.py:631
  394.9 13.7 %collective-permute-start.40 = (bf16[384,768]{1,0:T(8,128)(2,1)}, bf16[384,768]{1,0:T(8,128)(2,1)}, u32[]{:S(2)}, u32[]{:S(2)}) collective-permute-start(bf16[384,768]{1,0:T(8,128)(2,1)} %add_parts.18), channel_id=1, source_target_pairs={{0,1},{1,0},{2,3},{3,2},{4,5},{5,4},{6,7},{7,6},{8,9},{9,8},{10,11... | collective-permute-start | bytes 1769480 | tf_op jit(solution)/shard_map/ppermute | solution.py:631
  405.7 12.6 %collective-permute-start.42 = (bf16[384,768]{1,0:T(8,128)(2,1)S(1)}, bf16[384,768]{1,0:T(8,128)(2,1)S(1)}, u32[]{:S(2)}, u32[]{:S(2)}) collective-permute-start(bf16[384,768]{1,0:T(8,128)(2,1)S(1)} %add_parts.16), channel_id=1, source_target_pairs={{0,4},{2,6},{4,0},{6,2},{1,5},{3,7},{5,1},{7,3},{8,12},{10,14},{12... | collective-permute-start | bytes 1769480 | tf_op jit(solution)/shard_map/ppermute | solution.py:631
  408.6 14.0 %collective-permute-start.43 = (bf16[384,768]{1,0:T(8,128)(2,1)S(1)}, bf16[384,768]{1,0:T(8,128)(2,1)S(1)}, u32[]{:S(2)}, u32[]{:S(2)}) collective-permute-start(bf16[384,768]{1,0:T(8,128)(2,1)S(1)} %add_parts.22.refs_0_), channel_id=1, source_target_pairs={{0,1},{1,0},{2,3},{3,2},{4,5},{5,4},{6,7},{7,6},{8,9},{9,8},{10,11... | collective-permute-start | bytes 1769480 | tf_op jit(solution)/shard_map/ppermute | solution.py:631
  410.6 13.5 %collective-permute-start.34 = (f32[8,768]{1,0:T(8,128)S(1)}, f32[8,768]{1,0:T(8,128)S(1)}, u32[]{:S(2)}, u32[]{:S(2)}) collective-permute-start(f32[8,768]{1,0:T(8,128)S(1)} %copy-done.18), channel_id=1, source_target_pairs={{0,1},{1,0},{2,3},{3,2},{4,5},{5,4},{6,7},{7,6},{8,9},{9,8},{10,11... | collective-permute-start | bytes 73736 | tf_op jit(solution)/shard_map/ppermute | solution.py:631
  422.7 14.6 %collective-permute-start.44 = (bf16[384,768]{1,0:T(8,128)(2,1)S(1)}, bf16[384,768]{1,0:T(8,128)(2,1)S(1)}, u32[]{:S(2)}, u32[]{:S(2)}) collective-permute-start(bf16[384,768]{1,0:T(8,128)(2,1)S(1)} %add_parts.23.refs_0_), channel_id=1, source_target_pairs={{0,1},{1,0},{2,3},{3,2},{4,5},{5,4},{6,7},{7,6},{8,9},{9,8},{10,11... | collective-permute-start | bytes 1769480 | tf_op jit(solution)/shard_map/ppermute | solution.py:631
  (29 other events, 236.2 us)
